TPU v7x, 32 devices: a whole 2x2x4 slice. The times are simulated.
32 devices in a mesh: rep: 2 (over y), pool: 8 (over z, x), tp: 2 (over core).
Axes of the slice: x: 2, y: 2, z: 4, core: 2. Of those that a mesh axis runs over, the one named last changes fastest.
Arguments:
- hidden: bfloat16 [2048, 8192], P(('rep', 'pool'), 'tp'), parts along dimension 0, may hold values from -6 to 6
- adapter_ids: int32 [2048, 1], P(('rep', 'pool')), parts along dimension 0, may hold values from 0 to 7, as said below
- owner_map: int32 [8], replicated, may hold values from 0 to 7, each once
- shrink_factors: bfloat16 [8, 8192, 64], P('pool', 'tp'), may hold values from -0.0625 to 0.0625
- expand_factors: bfloat16 [8, 64, 4096], P('pool', None, 'tp'), may hold values from -0.75 to 0.75
- query_base: bfloat16 [2048, 4096], P(('rep', 'pool'), 'tp'), parts along dimension 0, may hold values from -3 to 3
- new_key: bfloat16 [2048, 512], P(('rep', 'pool'), 'tp'), parts along dimension 0, may hold values from -6 to 6
- new_value: bfloat16 [2048, 512], P(('rep', 'pool'), 'tp'), parts along dimension 0, may hold values from -6 to 6
- cache_keys: bfloat16 [2048, 16, 512], P(('rep', 'pool'), None, 'tp'), parts along dimension 0, may hold values from -12 to 12
- cache_values: bfloat16 [2048, 16, 512], P(('rep', 'pool'), None, 'tp'), parts along dimension 0, may hold values from -6 to 6
- lengths: int32 [2048], P(('rep', 'pool')), parts along dimension 0, may hold values from 1 to 16, as said below
Outputs:
- attended: bfloat16 [2048, 4096], P(('rep', 'pool'), 'tp'), parts along dimension 0
There are 2 independent parts, one for each index of `rep`. A program takes and returns all parts, laid end to end along the dimension named above; an argument that names none is the same for every part. Nothing has to cross between parts.
Inputs may be any that keep to these rules, and one draw needn't show every extreme that they name: `adapter_ids`: among the 128 requests of one pool index no adapter is named more than 32 times, and one adapter is named exactly 32 times by the requests of every pool index. `owner_map`: each storage index appears once. `lengths`: some request has all 16 slots live.
All inputs are finite; a program needn't handle non-finite values.
Results may differ from a plain program's by a relative error of at most 0.006.
Values may be sent and summed in bfloat16 or wider, within the bound.
No kernel may reach another device: no remote copies, remote signals or barrier semaphores. Data moves between devices by JAX's collectives and lax.ppermute only.
A program may use at most 64 MiB of HBM per device.

v0:
```python
import math

import jax
import jax.numpy as jnp
from jax import lax
from jax.sharding import PartitionSpec as P

HEAD = 128


def attend_requests(queries, new_key, new_value, cache_keys, cache_values, lengths):
    requests = queries.shape[0]
    key_heads = new_key.shape[1] // HEAD
    query_heads = queries.shape[1] // HEAD
    group_size = query_heads // key_heads
    slot_total = cache_keys.shape[1]
    grouped_queries = queries.reshape(requests, key_heads, group_size, HEAD)
    cached_keys = cache_keys.reshape(requests, slot_total, key_heads, HEAD)
    cached_values = cache_values.reshape(requests, slot_total, key_heads, HEAD)
    cache_scores = jnp.einsum(
        "rgqd,rjgd->rgqj", grouped_queries, cached_keys, preferred_element_type=jnp.float32
    ) / math.sqrt(HEAD)
    own_scores = jnp.einsum(
        "rgqd,rgd->rgq",
        grouped_queries,
        new_key.reshape(requests, key_heads, HEAD),
        preferred_element_type=jnp.float32,
    ) / math.sqrt(HEAD)
    live_mask = jnp.arange(slot_total, dtype=jnp.int32)[None, :] < lengths[:, None]
    cache_scores = jnp.where(live_mask[:, None, None, :], cache_scores, -jnp.inf)
    row_top = jnp.maximum(jnp.max(cache_scores, axis=-1), own_scores)
    cache_exp = jnp.exp(cache_scores - row_top[..., None])
    own_exp = jnp.exp(own_scores - row_top)
    denominator = jnp.sum(cache_exp, axis=-1) + own_exp
    cache_probs = (cache_exp / denominator[..., None]).astype(jnp.bfloat16)
    own_probs = (own_exp / denominator).astype(jnp.bfloat16)
    mixed_values = jnp.einsum(
        "rgqj,rjgd->rgqd", cache_probs, cached_values, preferred_element_type=jnp.float32
    )
    own_values = new_value.reshape(requests, key_heads, 1, HEAD).astype(jnp.float32)
    mixed_values = mixed_values + own_probs[..., None].astype(jnp.float32) * own_values
    return mixed_values.reshape(requests, query_heads * HEAD).astype(jnp.bfloat16)


def per_device(
    hidden,
    adapter_ids,
    owner_map,
    shrink_factors,
    expand_factors,
    query_base,
    new_key,
    new_value,
    cache_keys,
    cache_values,
    lengths,
):
    requests = hidden.shape[0]
    pool_size = lax.axis_size("pool")
    capacity = max(2, 2 * requests // pool_size)
    slot_count = pool_size * capacity
    chosen_ids = adapter_ids[:, 0]
    adapter_index = jnp.arange(owner_map.shape[0], dtype=jnp.int32)
    owners = jnp.sum(
        jnp.where(chosen_ids[:, None] == adapter_index[None, :], owner_map[None, :], 0), axis=1
    )
    positions = jnp.arange(requests, dtype=jnp.int32)
    earlier = (owners[:, None] == owners[None, :]) & (positions[None, :] < positions[:, None])
    rank_in = jnp.sum(earlier.astype(jnp.int32), axis=1)
    target = owners * capacity + rank_in
    slot_ids = jnp.arange(slot_count, dtype=jnp.int32)
    place_rows = (slot_ids[:, None] == target[None, :]).astype(jnp.bfloat16)
    pick_rows = (target[:, None] == slot_ids[None, :]).astype(jnp.bfloat16)
    outgoing = jnp.dot(place_rows, hidden, preferred_element_type=jnp.float32).astype(jnp.bfloat16)
    outgoing = outgoing.reshape(pool_size, capacity, hidden.shape[1])
    shrink_weight = shrink_factors[0]
    expand_weight = expand_factors[0]
    received = lax.all_to_all(outgoing, "pool", split_axis=0, concat_axis=0, tiled=True)
    item_count = received.shape[1]
    flattened = received.reshape(pool_size * item_count, received.shape[2])
    partial_sum = jnp.dot(flattened, shrink_weight, preferred_element_type=jnp.float32)
    rank_total = lax.psum(partial_sum, "tp")
    query_delta = jnp.dot(
        rank_total.astype(jnp.bfloat16), expand_weight, preferred_element_type=jnp.float32
    ).astype(jnp.bfloat16)
    returned = lax.all_to_all(
        query_delta.reshape(pool_size, item_count, query_delta.shape[1]),
        "pool",
        split_axis=0,
        concat_axis=0,
        tiled=True,
    )
    delta_rows = returned.reshape(slot_count, returned.shape[2])
    request_delta = jnp.dot(pick_rows, delta_rows, preferred_element_type=jnp.float32).astype(
        jnp.bfloat16
    )
    queries = (query_base.astype(jnp.float32) + request_delta.astype(jnp.float32)).astype(
        jnp.bfloat16
    )
    return attend_requests(queries, new_key, new_value, cache_keys, cache_values, lengths)


def solution(mesh):
    in_specs = (
        P(("rep", "pool"), "tp"),
        P(("rep", "pool"), None),
        P(),
        P("pool", "tp", None),
        P("pool", None, "tp"),
        P(("rep", "pool"), "tp"),
        P(("rep", "pool"), "tp"),
        P(("rep", "pool"), "tp"),
        P(("rep", "pool"), None, "tp"),
        P(("rep", "pool"), None, "tp"),
        P(("rep", "pool")),
    )
    out_specs = P(("rep", "pool"), "tp")
    return jax.shard_map(
        per_device, mesh=mesh, in_specs=in_specs, out_specs=out_specs, check_vma=False
    )
```

profile of v0, /device:TPU:0, one launch (start us, length us, event | category | flops | bytes accessed | tf_op | source)
XLA Modules:
  0.0 101.0 jit_solution(7686514862897897679)
XLA Ops:
  0.0 0.8 select_reduce_fusion
  0.8 0.2 convert_reduce_fusion
  1.0 0.2 copy-done
  1.3 0.7 convolution_convert_fusion
  2.0 55.4 %all_to_all.10 = bf16[8,32,4096]{2,1,0:T(8,128)(2,1)S(1)} all-to-all(bf16[8,32,4096]{2,1,0:T(8,128)(2,1)S(1)} %bitcast.60), channel_id=1, replica_groups=mesh['rep'=2,'pool'=8,'tp'=2] {'pool'}, dimensions={0} | all-to-all | bytes 4194304 | tf_op jit(solution)/shard_map/all_to_all | solution.py:78
  57.4 0.8 fusion.11
  58.2 3.7 %psum.7 = bf16[256,64]{0,1:T(8,128)(2,1)S(1)} all-reduce(f32[256,64]{0,1:T(8,128)S(1)} %fusion.11), channel_id=1, replica_groups=mesh['rep'=2,'pool'=8,'tp'=2] {'tp'}, use_global_device_ids=true, to_apply=%region_2.3 | all-reduce | flops 16384 | bytes 98304 | tf_op jit(solution)/shard_map/psum | solution.py:82
  62.0 1.4 %convolution_convert_fusion.1 = bf16[256,2048]{1,0:T(8,128)(2,1)} fusion(bf16[1,64,2048]{2,1,0:T(8,128)(2,1)S(1)} %copy-done.3, bf16[256,64]{0,1:T(8,128)(2,1)S(1)} %psum.7), kind=kOutput, calls=%fused_computation.1 | convolution fusion | flops 67633152 | bytes 1343488 | tf_op jit(solution)/shard_map/dot_general | solution.py:83
  63.4 3.6 %all-to-all-start.1 = ((bf16[8,32,2048]{2,1,0:T(8,128)(2,1)}), bf16[8,32,2048]{2,1,0:T(8,128)(2,1)S(1)}, u32[]{:S(2)}, u32[]{:S(2)}) async-start(bf16[8,32,2048]{2,1,0:T(8,128)(2,1)} %bitcast.5), calls=%async_computation.1 | async-start | bytes 2097152 | tf_op jit(solution)/shard_map/all_to_all | solution.py:86
  67.1 0.1 reshape.80
  67.1 0.1 iota_compare_fusion.5
  67.2 26.2 %all-to-all-done.1 = bf16[8,32,2048]{2,1,0:T(8,128)(2,1)S(1)} async-done(((bf16[8,32,2048]{2,1,0:T(8,128)(2,1)}), bf16[8,32,2048]{2,1,0:T(8,128)(2,1)S(1)}, u32[]{:S(2)}, u32[]{:S(2)}) %all-to-all-start.1) | async-done | bytes 1048608 | tf_op jit(solution)/shard_map/all_to_all | solution.py:86
  93.5 0.4 fusion.5
  93.8 0.1 copy.32
  93.9 2.0 %fusion.23 = (f32[128,2,8]{2,1,0:T(2,128)S(1)}, f32[128,2,8,16]{3,2,1,0:T(8,128)S(1)}) fusion(bf16[128,2,8,128]{3,2,1,0:T(8,128)(2,1)S(1)} %bitcast.62, pred[128,16]{1,0:T(8,128)(4,1)S(1)} %iota_compare_fusion.5, bf16[128,16,256]{2,1,0:T(8,128)(2,1)} %param.19), kind=kOutput, calls=%fused_computation.42 | convolution fusion | flops 8484864 | bytes 1714176 | tf_op jit(solution)/shard_map/rgqd,rjgd->rgqj/dot_general | solution.py:20
  96.0 0.1 copy.22
  96.1 0.4 fusion.24
  96.5 0.1 copy.29
  96.5 0.2 copy.23
  96.7 0.8 fusion.10
  97.6 0.1 copy.25
  97.7 0.1 copy.27
  97.9 2.1 %fusion.4 = bf16[128,2,8,128]{3,2,1,0:T(8,128)(2,1)S(1)} fusion(f32[128,2,8,16]{3,2,1,0:T(8,128)S(1)} %get-tuple-element.8, f32[128,2,128]{2,1,0:T(2,128)S(1)} %reshape.80, f32[128,2,8]{2,1,0:T(2,128)S(1)} %copy.27, f32[128,2,8]{2,1,0:T(2,128)S(1)} %copy.25, f32[128,2,8]{2,1,0:T(2,128)S(1)} %copy.23, bf16[128,16,256]{2,1,0:T(8,128)(2,1)} %param.20), kind=kOutput, calls=%fused_computation.9 | convolution fusion | flops 9273344 | bytes 1859584 | tf_op jit(solution)/shard_map/rgqj,rjgd->rgqd/dot_general | solution.py:37
  100.0 0.9 copy.45
  (18 shorter events, 0.2 us)
Async XLA Ops:
  0.0 1.3 %copy-start = (bf16[128,4096]{1,0:T(8,128)(2,1)S(1)}, bf16[128,4096]{1,0:T(8,128)(2,1)}, u32[]{:S(2)}) copy-start(bf16[128,4096]{1,0:T(8,128)(2,1)} %param.11) | copy-start | bytes 3145732
  2.0 55.4 %copy-start.2 = (bf16[1,4096,64]{1,2,0:T(8,128)(2,1)S(1)}, bf16[1,4096,64]{1,2,0:T(8,128)(2,1)}, u32[]{:S(2)}) copy-start(bf16[1,4096,64]{1,2,0:T(8,128)(2,1)} %param.14) | copy-start | bytes 1572868
  57.4 4.6 %copy-start.3 = (bf16[1,64,2048]{2,1,0:T(8,128)(2,1)S(1)}, bf16[1,64,2048]{2,1,0:T(8,128)(2,1)}, u32[]{:S(2)}) copy-start(bf16[1,64,2048]{2,1,0:T(8,128)(2,1)} %param.15) | copy-start | bytes 786436
  58.2 8.9 %copy-start.4 = (bf16[128,256]{1,0:T(8,128)(2,1)S(1)}, bf16[128,256]{1,0:T(8,128)(2,1)}, u32[]{:S(2)}) copy-start(bf16[128,256]{1,0:T(8,128)(2,1)} %param.17) | copy-start | bytes 196612
  58.2 8.9 %copy-start.5 = (bf16[128,256]{1,0:T(8,128)(2,1)S(1)}, bf16[128,256]{1,0:T(8,128)(2,1)}, u32[]{:S(2)}) copy-start(bf16[128,256]{1,0:T(8,128)(2,1)} %param.18) | copy-start | bytes 196612
  58.2 8.9 %copy-start.6 = (s32[128]{0:T(128)S(1)}, s32[128]{0:T(128)}, u32[]{:S(2)}) copy-start(s32[128]{0:T(128)} %param.21) | copy-start | bytes 1540
  58.2 35.3 %copy-start.1 = (bf16[128,2048]{1,0:T(8,128)(2,1)S(1)}, bf16[128,2048]{1,0:T(8,128)(2,1)}, u32[]{:S(2)}) copy-start(bf16[128,2048]{1,0:T(8,128)(2,1)} %param.16) | copy-start | bytes 1572868
  63.4 30.0 %all-to-all-start.1 = ((bf16[8,32,2048]{2,1,0:T(8,128)(2,1)}), bf16[8,32,2048]{2,1,0:T(8,128)(2,1)S(1)}, u32[]{:S(2)}, u32[]{:S(2)}) async-start(bf16[8,32,2048]{2,1,0:T(8,128)(2,1)} %bitcast.5), calls=%async_computation.1 | async-start | bytes 2097152 | tf_op jit(solution)/shard_map/all_to_all | solution.py:86
where the time goes:
time: 101 us
  blocking collectives  59.2 us (59%)
  waiting for transfers between devices  26.2 us (26%)
  matrix products  7.84 us (8%)
  starting transfers between devices  3.59 us (4%)
  local copies, waits for them, and re-layouts  2.04 us (2%)
  other arithmetic  1.9 us (2%)
    all_to_all x1, blocking collectives, per_device(): lax.all_to_all(outgoing, 'pool', split_axis=0, concat_axis=0, tiled=True)  55.4 us
    all_to_all x1, waiting for transfers between devices, per_device(): lax.all_to_all(query_delta.reshape(pool_size, item_count, query_delta.sha...  26.2 us
    psum x1, blocking collectives, per_device(): rank_total = lax.psum(partial_sum, 'tp')  3.75 us
    all_to_all x1, starting transfers between devices, per_device(): lax.all_to_all(query_delta.reshape(pool_size, item_count, query_delta.sha...  3.59 us
    dot_general x1, matrix products, attend_requests(): jnp.einsum('rgqj,rjgd->rgqd', cache_probs, cached_values, preferred_eleme...  2.13 us
    dot_general x1, matrix products, attend_requests(): jnp.einsum('rgqd,rjgd->rgqj', grouped_queries, cached_keys, preferred_ele...  2.04 us
  transfers between devices with their start and end apart: 1, of which 1 were waited for; matrix products, arithmetic and copies ran while one was open for 0% of the time, Pallas kernels for 0%

commit v1 on v0

v1 whole, which is shorter than its diff:
```python
import functools
import math

import jax
import jax.numpy as jnp
from jax import lax
from jax.experimental import pallas as pl
from jax.experimental.pallas import tpu as pltpu
from jax.sharding import PartitionSpec as P

HEAD = 128
ROWS = 16
DEAD = -1e30


def attend_kernel(parts, me_ref, base_ref, nk_ref, nv_ref, ck_ref, cv_ref, len_ref, *rest):
    delta_refs, out_ref = rest[:parts], rest[parts]
    me = me_ref[0]
    width = delta_refs[0].shape[1]
    groups = nk_ref.shape[1] // HEAD
    slots = ck_ref.shape[1]
    heads = width // HEAD
    span = parts // groups
    rows = span * heads * ROWS
    row_req = lax.broadcasted_iota(jnp.int32, (rows, ROWS * slots), 0) % ROWS
    col = lax.broadcasted_iota(jnp.int32, (rows, ROWS * slots), 1)
    lens = jnp.concatenate([len_ref[...]] * (span * heads), axis=0)
    live = (row_req == col // slots) & (col % slots < lens)
    own_live = lax.broadcasted_iota(jnp.int32, (rows, ROWS), 0) % ROWS == lax.broadcasted_iota(
        jnp.int32, (rows, ROWS), 1
    )
    scale = 1.0 / math.sqrt(HEAD)
    for first in range(0, parts, span):
        group = (me ^ first) // span
        lanes = pl.ds(pl.multiple_of(group * HEAD, HEAD), HEAD)
        pieces = []
        for s in range(first, first + span):
            at = pl.ds(pl.multiple_of((me ^ s) * width, width), width)
            q = base_ref[:, at].astype(jnp.float32) + delta_refs[s][...].astype(jnp.float32)
            q = q.astype(jnp.bfloat16)
            pieces += [q[:, h * HEAD : (h + 1) * HEAD] for h in range(heads)]
        q = jnp.concatenate(pieces, axis=0)
        keys = ck_ref[:, :, lanes].reshape(ROWS * slots, HEAD)
        values = cv_ref[:, :, lanes].reshape(ROWS * slots, HEAD)
        dims = (((1,), (1,)), ((), ()))
        scores = lax.dot_general(q, keys, dims, preferred_element_type=jnp.float32) * scale
        own = lax.dot_general(q, nk_ref[:, lanes], dims, preferred_element_type=jnp.float32) * scale
        own = jnp.sum(jnp.where(own_live, own, 0.0), axis=1, keepdims=True)
        scores = jnp.where(live, scores, DEAD)
        top = jnp.maximum(jnp.max(scores, axis=1, keepdims=True), own)
        exps = jnp.exp(scores - top)
        own_exp = jnp.exp(own - top)
        total = jnp.sum(exps, axis=1, keepdims=True) + own_exp
        probs = (exps / total).astype(jnp.bfloat16)
        own_prob = (own_exp / total).astype(jnp.bfloat16).astype(jnp.float32)
        mixed = jnp.dot(probs, values, preferred_element_type=jnp.float32)
        own_value = jnp.concatenate([nv_ref[:, lanes].astype(jnp.float32)] * (span * heads), axis=0)
        mixed = (mixed + own_prob * own_value).astype(jnp.bfloat16)
        for i, s in enumerate(range(first, first + span)):
            at = pl.ds(pl.multiple_of((me ^ s) * width, width), width)
            out_ref[:, at] = jnp.concatenate(
                [mixed[(i * heads + h) * ROWS : (i * heads + h + 1) * ROWS] for h in range(heads)],
                axis=1,
            )


def attend(me, base, new_key, new_value, cache_keys, cache_values, lengths, deltas):
    requests, columns = base.shape
    kv = new_key.shape[1]
    slots = cache_keys.shape[1]
    row2 = lambda w: pl.BlockSpec((ROWS, w), lambda i, me: (i, 0))
    row3 = pl.BlockSpec((ROWS, slots, kv), lambda i, me: (i, 0, 0))
    parts = len(deltas)
    return pl.pallas_call(
        functools.partial(attend_kernel, parts),
        out_shape=jax.ShapeDtypeStruct((requests, columns), jnp.bfloat16),
        grid_spec=pltpu.PrefetchScalarGridSpec(
            num_scalar_prefetch=1,
            grid=(requests // ROWS,),
            in_specs=[row2(columns), row2(kv), row2(kv), row3, row3, row2(1)]
            + [row2(columns // parts)] * parts,
            out_specs=row2(columns),
        ),
        compiler_params=pltpu.CompilerParams(vmem_limit_bytes=24 * 1024 * 1024),
        cost_estimate=pl.CostEstimate(
            flops=4 * requests * ROWS * slots * columns,
            bytes_accessed=4 * requests * (columns + slots * kv),
            transcendentals=requests * slots * columns // 8,
        ),
    )(me, base, new_key, new_value, cache_keys, cache_values, lengths, *deltas)


def per_device(
    hidden,
    adapter_ids,
    owner_map,
    shrink_factors,
    expand_factors,
    query_base,
    new_key,
    new_value,
    cache_keys,
    cache_values,
    lengths,
):
    reps, pool, tp = (lax.axis_size(a) for a in ("rep", "pool", "tp"))
    requests = hidden.shape[0]
    rank = shrink_factors.shape[2]
    square = 2 * reps
    column = pool // 2
    features = hidden.shape[1] // square
    outputs = query_base.shape[1] // square
    place = lax.axis_index("pool")
    side, level = place % 2, place // 2
    me = lax.axis_index("rep") * 2 + side
    core = me * tp + lax.axis_index("tp")

    def swap(a, s):
        pairs = [
            (r * pool + p, (r ^ (s // 2)) * pool + (p ^ (s % 2)))
            for r in range(reps)
            for p in range(pool)
        ]
        return lax.ppermute(a, ("rep", "pool"), pairs)

    def swap_core(a, s):
        chip, c = s // tp, s % tp
        pairs = [
            (
                (r * pool + p) * tp + t,
                ((r ^ (chip // 2)) * pool + (p ^ (chip % 2))) * tp + (t ^ c),
            )
            for r in range(reps)
            for p in range(pool)
            for t in range(tp)
        ]
        return lax.ppermute(a, ("rep", "pool", "tp"), pairs)

    def along(a, moves):
        return lax.ppermute(a, "pool", [(i * 2 + s, j * 2 + s) for i, j in moves for s in range(2)])

    def gather_column(a):
        if column == 1:
            return [a]
        near = along(a, [(i, i ^ 1) for i in range(column)])
        if column == 2:
            return [a, near]
        far = along(a, [(i, i ^ 2) for i in range(4)])
        inner = along(a, [(1, 2), (2, 1)])
        outer = along(far, [(2, 3), (1, 0)])
        last = jnp.where((level == 1) | (level == 2), inner, outer)
        return [a, near, far, last]

    ids = adapter_ids[:, 0]
    adapters = jnp.arange(owner_map.shape[0], dtype=jnp.int32)
    owners = jnp.sum(jnp.where(ids[None, :] == adapters[:, None], owner_map[:, None], 0), axis=0)
    owners = owners[None, :]
    all_owners = jnp.concatenate([owners] + [swap(owners, s) for s in range(1, square)], axis=1)

    shrink = shrink_factors[0].T
    expand = expand_factors[0]

    def cut(a, width, at):
        return lax.dynamic_slice_in_dim(a, at * width, width, 1)

    rows = [cut(hidden, features, me)]
    shrink_next = swap(cut(shrink, features, me ^ 1), 1)
    expand_next = swap(cut(expand, outputs, me ^ 1), 1)
    rows += [swap(cut(hidden, features, me ^ s), s) for s in range(1, square)]
    shrink_own = cut(shrink, features, me)
    expand_own = cut(expand, outputs, me)
    all_rows = jnp.concatenate(rows, axis=0)

    def shrink_by(weight, owner):
        sums = lax.dot_general(
            weight, all_rows, (((1,), (1,)), ((), ())), preferred_element_type=jnp.float32
        )
        return jnp.where(all_owners == owner, sums, 0.0)

    small = column in (1, 2, 4)
    if small:
        own_blocks = gather_column(shrink_own)
        next_blocks = gather_column(shrink_next)
        expand_blocks = gather_column(jnp.concatenate([expand_own, expand_next], axis=0))
        partial = 0.0
        for k in range(column):
            partial = partial + shrink_by(own_blocks[k], (level ^ k) * 2 + side)
            partial = partial + shrink_by(next_blocks[k], (level ^ k) * 2 + 1 - side)
    else:
        ring = [(i, (i + 1) % column) for i in range(column)]

        def shrink_step(k, carry):
            total, own, other = carry
            at = (level - k) % column
            total = total + shrink_by(own, at * 2 + side) + shrink_by(other, at * 2 + 1 - side)
            return total, along(own, ring), along(other, ring)

        start = jnp.zeros((rank, square * requests), jnp.float32)
        partial = lax.fori_loop(0, column, shrink_step, (start, shrink_own, shrink_next))[0]

    devices = square * tp
    share = rank // devices
    pieces = partial.reshape(devices, share, square * requests)

    def reorder(a, chip):
        blocks = [a[:, (s ^ chip) * requests : ((s ^ chip) + 1) * requests] for s in range(square)]
        return jnp.concatenate(blocks, axis=1)

    def piece(at):
        return lax.dynamic_index_in_dim(pieces, at, 0, keepdims=False)

    total = piece(core)
    for s in range(1, devices):
        total = total + reorder(swap_core(piece(core ^ s), s), s // tp)
    low = total.astype(jnp.bfloat16)
    lows = [low] + [reorder(swap_core(low, s), s // tp) for s in range(1, devices)]
    low_rank = jnp.stack(lows)[core ^ jnp.arange(devices)]
    low_rank = low_rank.reshape(rank, square * requests)

    def masked(owner):
        return jnp.where(all_owners == owner, low_rank, jnp.zeros_like(low_rank))

    dims = (((0,), (0,)), ((), ()))
    if small:
        picked = []
        for k in range(column):
            picked += [masked((level ^ k) * 2 + side), masked((level ^ k) * 2 + 1 - side)]
        delta = lax.dot_general(
            jnp.concatenate(picked, axis=0),
            jnp.concatenate(expand_blocks, axis=0),
            dims,
            preferred_element_type=jnp.float32,
        ).astype(jnp.bfloat16)
    else:

        def expand_step(k, carry):
            total, block = carry
            at = (level - k) % column
            picked = jnp.concatenate([masked(at * 2 + side), masked(at * 2 + 1 - side)], axis=0)
            total = total + lax.dot_general(
                picked, block, dims, preferred_element_type=jnp.float32
            )
            return total, along(block, ring)

        start = jnp.zeros((square * requests, outputs), jnp.float32)
        block = jnp.concatenate([expand_own, expand_next], axis=0)
        delta = lax.fori_loop(0, column, expand_step, (start, block))[0].astype(jnp.bfloat16)

    deltas = [delta[:requests]]
    deltas += [swap(delta[s * requests : (s + 1) * requests], s) for s in range(1, square)]
    return attend(
        me[None],
        query_base,
        new_key,
        new_value,
        cache_keys,
        cache_values,
        lengths[:, None],
        deltas,
    )


def solution(mesh):
    in_specs = (
        P(("rep", "pool"), "tp"),
        P(("rep", "pool"), None),
        P(),
        P("pool", "tp", None),
        P("pool", None, "tp"),
        P(("rep", "pool"), "tp"),
        P(("rep", "pool"), "tp"),
        P(("rep", "pool"), "tp"),
        P(("rep", "pool"), None, "tp"),
        P(("rep", "pool"), None, "tp"),
        P(("rep", "pool")),
    )
    out_specs = P(("rep", "pool"), "tp")
    return jax.shard_map(
        per_device, mesh=mesh, in_specs=in_specs, out_specs=out_specs, check_vma=False
    )
```

time: 101 us -> 97.1 us (0.961)
  blocking collectives: 59.2 us -> 0 us
  starting transfers between devices: 3.59 us -> 47.4 us
  Pallas kernels: 0 us -> 7.52 us
  waiting for transfers between devices: 26.2 us -> 33.4 us
  matrix products: 7.84 us -> 4.06 us
    all_to_all x1 -> x0, blocking collectives: 55.4 us -> none  [per_device(): lax.all_to_all(outgoing, 'pool', split_axis=0, concat_axis=0, tiled=True)]
    ppermute x0 -> x37, starting transfers between devices: none -> 47.4 us  [the longest x12 19.8 us: along(): lax.ppermute(a, 'pool', [(i * 2 + s, j * 2 + s) for i, j in moves for s i...]
    ppermute x0 -> x37, waiting for transfers between devices: none -> 33.4 us  [the longest x11 16 us: swap(): return lax.ppermute(a, ('rep', 'pool'), pairs)]
    all_to_all x1 -> x0, waiting for transfers between devices: 26.2 us -> none  [per_device(): lax.all_to_all(query_delta.reshape(pool_size, item_count, query_delta.sha...]
    pallas_call x0 -> x1, Pallas kernels: none -> 7.52 us  [attend(): pl.pallas_call(functools.partial(attend_kernel, parts), out_shape=jax.Sha...]
    dot_general x7 -> x9, matrix products: 7.84 us -> 4.06 us  [the longest x8 3.59 us: shrink_by(): lax.dot_general(weight, all_rows, (((1,), (1,)), ((), ())), preferred_ele...]
    psum x1 -> x0, blocking collectives: 3.75 us -> none  [per_device(): rank_total = lax.psum(partial_sum, 'tp')]
    all_to_all x1 -> x0, starting transfers between devices: 3.59 us -> none  [per_device(): lax.all_to_all(query_delta.reshape(pool_size, item_count, query_delta.sha...]
  transfers between devices with their start and end apart: 1 -> 37, of which waited for: 1 -> 16; matrix products, arithmetic and copies ran while one was open for 0% -> 6% of each run, Pallas kernels for 0% -> 0%
where the time goes in v1:
time: 97.1 us; the launch traced here: 96.9 us
  starting transfers between devices  47.4 us (49%)
  waiting for transfers between devices  33.4 us (34%)
  Pallas kernels  7.52 us (8%)
  matrix products  4.06 us (4%)
  local copies, waits for them, and re-layouts  2.91 us (3%)
  other arithmetic  1.1 us (1%)
    ppermute x12, starting transfers between devices, along(): lax.ppermute(a, 'pool', [(i * 2 + s, j * 2 + s) for i, j in moves for s i...  19.8 us
    ppermute x11, waiting for transfers between devices, swap(): return lax.ppermute(a, ('rep', 'pool'), pairs)  16 us
    ppermute x11, starting transfers between devices, swap(): return lax.ppermute(a, ('rep', 'pool'), pairs)  15 us
    ppermute x14, starting transfers between devices, swap_core(): return lax.ppermute(a, ('rep', 'pool', 'tp'), pairs)  12.5 us
    ppermute x12, waiting for transfers between devices, along(): lax.ppermute(a, 'pool', [(i * 2 + s, j * 2 + s) for i, j in moves for s i...  11.4 us
    pallas_call x1, Pallas kernels, attend(): pl.pallas_call(functools.partial(attend_kernel, parts), out_shape=jax.Sha...  7.52 us
    ppermute x14, waiting for transfers between devices, swap_core(): return lax.ppermute(a, ('rep', 'pool', 'tp'), pairs)  6 us
    dot_general x8, matrix products, shrink_by(): lax.dot_general(weight, all_rows, (((1,), (1,)), ((), ())), preferred_ele...  3.59 us
  transfers between devices with their start and end apart: 37, of which 16 were waited for; matrix products, arithmetic and copies ran while one was open for 6% of the time, Pallas kernels for 0%

profile of v1, /device:TPU:0, one launch (start us, length us, event | category | flops | bytes accessed | tf_op | source)
XLA Modules:
  0.0 96.9 jit_solution(2936118630255563593)
XLA Ops:
  0.8 2.9 %collective-permute-start = (s32[1,128]{1,0:T(1,128)S(1)}, s32[1,128]{1,0:T(1,128)S(1)}, u32[]{:S(2)}, u32[]{:S(2)}) collective-permute-start(s32[1,128]{1,0:T(1,128)S(1)} %bitcast.157), channel_id=1, source_target_pairs={{0,2},{2,0},{4,6},{6,4},{8,10},{10,8},{12,14},{14,12},{16,18},{18,... | collective-permute-start | bytes 1544 | tf_op jit(solution)/shard_map/ppermute | solution.py:124
  3.7 1.5 %collective-permute-start.1 = (s32[1,128]{1,0:T(1,128)S(1)}, s32[1,128]{1,0:T(1,128)S(1)}, u32[]{:S(2)}, u32[]{:S(2)}) collective-permute-start(s32[1,128]{1,0:T(1,128)S(1)} %bitcast.158), channel_id=1, source_target_pairs={{0,16},{2,18},{4,20},{6,22},{8,24},{10,26},{12,28},{14,30},{16,0},... | collective-permute-start | bytes 1544 | tf_op jit(solution)/shard_map/ppermute | solution.py:124
  6.6 2.0 %collective-permute-start.3 = (bf16[128,1024]{1,0:T(8,128)(2,1)S(1)}, bf16[128,1024]{1,0:T(8,128)(2,1)S(1)}, u32[]{:S(2)}, u32[]{:S(2)}) collective-permute-start(bf16[128,1024]{1,0:T(8,128)(2,1)S(1)} %get-tuple-element.10), channel_id=1, source_target_pairs={{0,2},{2,0},{4,6},{6,4},{8,10},{10,8},{12,14},{14,12},{16,18},{18,... | collective-permute-start | bytes 786440 | tf_op jit(solution)/shard_map/ppermute | solution.py:124
  8.6 1.5 %collective-permute-start.4 = (bf16[128,1024]{1,0:T(8,128)(2,1)S(1)}, bf16[128,1024]{1,0:T(8,128)(2,1)S(1)}, u32[]{:S(2)}, u32[]{:S(2)}) collective-permute-start(bf16[128,1024]{1,0:T(8,128)(2,1)S(1)} %get-tuple-element.12), channel_id=1, source_target_pairs={{0,16},{2,18},{4,20},{6,22},{8,24},{10,26},{12,28},{14,30},{16,0},... | collective-permute-start | bytes 786440 | tf_op jit(solution)/shard_map/ppermute | solution.py:124
  10.4 1.9 %collective-permute-start.29 = (bf16[64,512]{1,0:T(8,128)(2,1)S(1)}, bf16[64,512]{1,0:T(8,128)(2,1)S(1)}, u32[]{:S(2)}, u32[]{:S(2)}) collective-permute-start(bf16[64,512]{1,0:T(8,128)(2,1)S(1)} %dynamic-slice_bitcast_fusion.2), channel_id=1, source_target_pairs={{0,2},{2,0},{4,6},{6,4},{8,10},{10,8},{12,14},{14,12},{16,18},{18,... | collective-permute-start | bytes 196616 | tf_op jit(solution)/shard_map/ppermute | solution.py:124
  12.3 8.9 %collective-permute-done.29 = bf16[64,512]{1,0:T(8,128)(2,1)S(1)} collective-permute-done((bf16[64,512]{1,0:T(8,128)(2,1)S(1)}, bf16[64,512]{1,0:T(8,128)(2,1)S(1)}, u32[]{:S(2)}, u32[]{:S(2)}) %collective-permute-start.29) | collective-permute-done | bytes 65568 | tf_op jit(solution)/shard_map/ppermute | solution.py:124
  21.2 1.8 %collective-permute-start.30 = (bf16[128,512]{1,0:T(8,128)(2,1)S(1)}, bf16[128,512]{1,0:T(8,128)(2,1)S(1)}, u32[]{:S(2)}, u32[]{:S(2)}) collective-permute-start(bf16[128,512]{1,0:T(8,128)(2,1)S(1)} %pad_maximum_fusion.1), channel_id=1, source_target_pairs={{0,4},{2,6},{4,0},{6,2},{8,12},{10,14},{12,8},{14,10},{1,5},{3,7},... | collective-permute-start | bytes 393224 | tf_op jit(solution)/shard_map/ppermute | solution.py:140
  23.0 2.7 %collective-permute-start.31 = (bf16[128,512]{1,0:T(8,128)(2,1)S(1)}, bf16[128,512]{1,0:T(8,128)(2,1)S(1)}, u32[]{:S(2)}, u32[]{:S(2)}) collective-permute-start(bf16[128,512]{1,0:T(8,128)(2,1)S(1)} %pad_maximum_fusion.1), channel_id=1, source_target_pairs={{0,8},{2,10},{4,12},{6,14},{8,0},{10,2},{12,4},{14,6},{1,9},{3,11}... | collective-permute-start | bytes 393224 | tf_op jit(solution)/shard_map/ppermute | solution.py:140
  27.1 1.5 %collective-permute-start.6 = (bf16[64,1024]{1,0:T(8,128)(2,1)S(1)}, bf16[64,1024]{1,0:T(8,128)(2,1)S(1)}, u32[]{:S(2)}, u32[]{:S(2)}) collective-permute-start(bf16[64,1024]{1,0:T(8,128)(2,1)S(1)} %get-tuple-element.17), channel_id=1, source_target_pairs={{0,2},{2,0},{4,6},{6,4},{8,10},{10,8},{12,14},{14,12},{16,18},{18,... | collective-permute-start | bytes 393224 | tf_op jit(solution)/shard_map/ppermute | solution.py:124
  28.6 1.9 %collective-permute-done.31 = bf16[128,512]{1,0:T(8,128)(2,1)S(1)} collective-permute-done((bf16[128,512]{1,0:T(8,128)(2,1)S(1)}, bf16[128,512]{1,0:T(8,128)(2,1)S(1)}, u32[]{:S(2)}, u32[]{:S(2)}) %collective-permute-start.31) | collective-permute-done | bytes 131104 | tf_op jit(solution)/shard_map/ppermute | solution.py:140
  30.5 1.5 %collective-permute-done.6 = bf16[64,1024]{1,0:T(8,128)(2,1)S(1)} collective-permute-done((bf16[64,1024]{1,0:T(8,128)(2,1)S(1)}, bf16[64,1024]{1,0:T(8,128)(2,1)S(1)}, u32[]{:S(2)}, u32[]{:S(2)}) %collective-permute-start.6) | collective-permute-done | bytes 131104 | tf_op jit(solution)/shard_map/ppermute | solution.py:124
  32.0 2.0 %collective-permute-start.9 = (bf16[64,1024]{1,0:T(8,128)(2,1)S(1)}, bf16[64,1024]{1,0:T(8,128)(2,1)S(1)}, u32[]{:S(2)}, u32[]{:S(2)}) collective-permute-start(bf16[64,1024]{1,0:T(8,128)(2,1)S(1)} %get-tuple-element.18), channel_id=1, source_target_pairs={{0,8},{2,10},{4,12},{6,14},{8,0},{10,2},{12,4},{14,6},{1,9},{3,11}... | collective-permute-start | bytes 393224 | tf_op jit(solution)/shard_map/ppermute | solution.py:140
  35.3 7.4 %collective-permute-start.8 = (bf16[64,1024]{1,0:T(8,128)(2,1)S(1)}, bf16[64,1024]{1,0:T(8,128)(2,1)S(1)}, u32[]{:S(2)}, u32[]{:S(2)}) collective-permute-start(bf16[64,1024]{1,0:T(8,128)(2,1)S(1)} %collective-permute-done.6), channel_id=1, source_target_pairs={{0,4},{2,6},{4,0},{6,2},{8,12},{10,14},{12,8},{14,10},{1,5},{3,7},... | collective-permute-start | bytes 393224 | tf_op jit(solution)/shard_map/ppermute | solution.py:140
  49.3 2.6 %collective-permute-done.10 = bf16[64,1024]{1,0:T(8,128)(2,1)S(1)} collective-permute-done((bf16[64,1024]{1,0:T(8,128)(2,1)S(1)}, bf16[64,1024]{1,0:T(8,128)(2,1)S(1)}, u32[]{:S(2)}, u32[]{:S(2)}) %collective-permute-start.10) | collective-permute-done | bytes 131104 | tf_op jit(solution)/shard_map/ppermute | solution.py:140
  54.1 4.6 %collective-permute-done.14 = bf16[64,1024]{1,0:T(8,128)(2,1)S(1)} collective-permute-done((bf16[64,1024]{1,0:T(8,128)(2,1)S(1)}, bf16[64,1024]{1,0:T(8,128)(2,1)S(1)}, u32[]{:S(2)}, u32[]{:S(2)}) %collective-permute-start.14) | collective-permute-done | bytes 131104 | tf_op jit(solution)/shard_map/ppermute | solution.py:140
  59.4 2.7 %collective-permute-start.21 = (f32[8,512]{1,0:T(8,128)S(1)}, f32[8,512]{1,0:T(8,128)S(1)}, u32[]{:S(2)}, u32[]{:S(2)}) collective-permute-start(f32[8,512]{1,0:T(8,128)S(1)} %get-tuple-element.20), channel_id=1, source_target_pairs={{0,19},{1,18},{2,17},{3,16},{4,23},{5,22},{6,21},{7,20},{8,27},{9,... | collective-permute-start | bytes 49160 | tf_op jit(solution)/shard_map/ppermute | solution.py:137
  62.1 1.5 %collective-permute-start.20 = (f32[8,512]{1,0:T(8,128)S(1)}, f32[8,512]{1,0:T(8,128)S(1)}, u32[]{:S(2)}, u32[]{:S(2)}) collective-permute-start(f32[8,512]{1,0:T(8,128)S(1)} %get-tuple-element.21), channel_id=1, source_target_pairs={{0,18},{1,19},{2,16},{3,17},{4,22},{5,23},{6,20},{7,21},{8,26},{9,... | collective-permute-start | bytes 49160 | tf_op jit(solution)/shard_map/ppermute | solution.py:137
  65.6 1.7 %collective-permute-done.18 = f32[8,512]{1,0:T(8,128)S(1)} collective-permute-done((f32[8,512]{1,0:T(8,128)S(1)}, f32[8,512]{1,0:T(8,128)S(1)}, u32[]{:S(2)}, u32[]{:S(2)}) %collective-permute-start.18) | collective-permute-done | bytes 16416 | tf_op jit(solution)/shard_map/ppermute | solution.py:137
  72.4 1.7 %collective-permute-start.27 = (bf16[8,512]{1,0:T(8,128)(2,1)S(1)}, bf16[8,512]{1,0:T(8,128)(2,1)S(1)}, u32[]{:S(2)}, u32[]{:S(2)}) collective-permute-start(bf16[8,512]{1,0:T(8,128)(2,1)S(1)} %fusion.33), channel_id=1, source_target_pairs={{0,18},{1,19},{2,16},{3,17},{4,22},{5,23},{6,20},{7,21},{8,26},{9,... | collective-permute-start | bytes 24584 | tf_op jit(solution)/shard_map/ppermute | solution.py:137
  75.0 1.9 %collective-permute-done.27 = bf16[8,512]{1,0:T(8,128)(2,1)S(1)} collective-permute-done((bf16[8,512]{1,0:T(8,128)(2,1)S(1)}, bf16[8,512]{1,0:T(8,128)(2,1)S(1)}, u32[]{:S(2)}, u32[]{:S(2)}) %collective-permute-start.27) | collective-permute-done | bytes 8224 | tf_op jit(solution)/shard_map/ppermute | solution.py:137
  81.9 1.7 %collective-permute-start.36 = (bf16[128,512]{1,0:T(8,128)(2,1)S(1)}, bf16[128,512]{1,0:T(8,128)(2,1)S(1)}, u32[]{:S(2)}, u32[]{:S(2)}) collective-permute-start(bf16[128,512]{1,0:T(8,128)(2,1)S(1)} %get-tuple-element.13), channel_id=1, source_target_pairs={{0,18},{2,16},{4,22},{6,20},{8,26},{10,24},{12,30},{14,28},{16,2},... | collective-permute-start | bytes 393224 | tf_op jit(solution)/shard_map/ppermute | solution.py:124
  83.7 3.0 %collective-permute-done.34.rest_1_ = bf16[128,512]{1,0:T(8,128)(2,1)S(1)} collective-permute-done((bf16[128,512]{1,0:T(8,128)(2,1)}, bf16[128,512]{1,0:T(8,128)(2,1)S(1)}, u32[]{:S(2)}, u32[]{:S(2)}) %collective-permute-start.34) | collective-permute-done | bytes 131104 | tf_op jit(solution)/shard_map/ppermute | solution.py:124
  87.3 2.1 %collective-permute-done.36.rest_3_ = bf16[128,512]{1,0:T(8,128)(2,1)S(1)} collective-permute-done((bf16[128,512]{1,0:T(8,128)(2,1)S(1)}, bf16[128,512]{1,0:T(8,128)(2,1)S(1)}, u32[]{:S(2)}, u32[]{:S(2)}) %collective-permute-start.36) | collective-permute-done | bytes 131104 | tf_op jit(solution)/shard_map/ppermute | solution.py:124
  89.4 7.5 %shard_map.109 = bf16[128,2048]{1,0:T(8,128)(2,1)} custom-call(s32[1]{0:T(128)} %bitcast.me_ref, bf16[128,2048]{1,0:T(8,128)(2,1)S(1)} %copy-done.2, bf16[128,256]{1,0:T(8,128)(2,1)S(1)} %copy-done.3, bf16[128,256]{1,0:T(8,128)(2,1)S(1)} %copy-done.4, bf16[128,16,256]{2,1,0:T(8,128)(2,1)S(1)} %copy-done, bf16[128,16,256]{2,1,0:T(8,128)(2,1)S(1)} %copy-done.1, ...), custom_call_target="tpu_custom_call" | custom-call | flops 268435456 | bytes 3145728 | tf_op jit(solution)/shard_map/pallas_call | solution.py:74
  (124 shorter events, 27.8 us)
Async XLA Ops:
  0.8 9.5 %collective-permute-start = (s32[1,128]{1,0:T(1,128)S(1)}, s32[1,128]{1,0:T(1,128)S(1)}, u32[]{:S(2)}, u32[]{:S(2)}) collective-permute-start(s32[1,128]{1,0:T(1,128)S(1)} %bitcast.157), channel_id=1, source_target_pairs={{0,2},{2,0},{4,6},{6,4},{8,10},{10,8},{12,14},{14,12},{16,18},{18,... | collective-permute-start | bytes 1544 | tf_op jit(solution)/shard_map/ppermute | solution.py:124
  3.7 6.7 %collective-permute-start.1 = (s32[1,128]{1,0:T(1,128)S(1)}, s32[1,128]{1,0:T(1,128)S(1)}, u32[]{:S(2)}, u32[]{:S(2)}) collective-permute-start(s32[1,128]{1,0:T(1,128)S(1)} %bitcast.158), channel_id=1, source_target_pairs={{0,16},{2,18},{4,20},{6,22},{8,24},{10,26},{12,28},{14,30},{16,0},... | collective-permute-start | bytes 1544 | tf_op jit(solution)/shard_map/ppermute | solution.py:124
  5.2 7.1 %collective-permute-start.2 = (s32[1,128]{1,0:T(1,128)S(1)}, s32[1,128]{1,0:T(1,128)S(1)}, u32[]{:S(2)}, u32[]{:S(2)}) collective-permute-start(s32[1,128]{1,0:T(1,128)S(1)} %bitcast.159), channel_id=1, source_target_pairs={{0,18},{2,16},{4,22},{6,20},{8,26},{10,24},{12,30},{14,28},{16,2},... | collective-permute-start | bytes 1544 | tf_op jit(solution)/shard_map/ppermute | solution.py:124
  6.6 27.4 %collective-permute-start.3 = (bf16[128,1024]{1,0:T(8,128)(2,1)S(1)}, bf16[128,1024]{1,0:T(8,128)(2,1)S(1)}, u32[]{:S(2)}, u32[]{:S(2)}) collective-permute-start(bf16[128,1024]{1,0:T(8,128)(2,1)S(1)} %get-tuple-element.10), channel_id=1, source_target_pairs={{0,2},{2,0},{4,6},{6,4},{8,10},{10,8},{12,14},{14,12},{16,18},{18,... | collective-permute-start | bytes 786440 | tf_op jit(solution)/shard_map/ppermute | solution.py:124
  8.6 26.1 %collective-permute-start.4 = (bf16[128,1024]{1,0:T(8,128)(2,1)S(1)}, bf16[128,1024]{1,0:T(8,128)(2,1)S(1)}, u32[]{:S(2)}, u32[]{:S(2)}) collective-permute-start(bf16[128,1024]{1,0:T(8,128)(2,1)S(1)} %get-tuple-element.12), channel_id=1, source_target_pairs={{0,16},{2,18},{4,20},{6,22},{8,24},{10,26},{12,28},{14,30},{16,0},... | collective-permute-start | bytes 786440 | tf_op jit(solution)/shard_map/ppermute | solution.py:124
  10.3 25.1 %collective-permute-start.5 = (bf16[128,1024]{1,0:T(8,128)(2,1)S(1)}, bf16[128,1024]{1,0:T(8,128)(2,1)S(1)}, u32[]{:S(2)}, u32[]{:S(2)}) collective-permute-start(bf16[128,1024]{1,0:T(8,128)(2,1)S(1)} %get-tuple-element.11), channel_id=1, source_target_pairs={{0,18},{2,16},{4,22},{6,20},{8,26},{10,24},{12,30},{14,28},{16,2},... | collective-permute-start | bytes 786440 | tf_op jit(solution)/shard_map/ppermute | solution.py:124
  10.4 10.8 %collective-permute-start.29 = (bf16[64,512]{1,0:T(8,128)(2,1)S(1)}, bf16[64,512]{1,0:T(8,128)(2,1)S(1)}, u32[]{:S(2)}, u32[]{:S(2)}) collective-permute-start(bf16[64,512]{1,0:T(8,128)(2,1)S(1)} %dynamic-slice_bitcast_fusion.2), channel_id=1, source_target_pairs={{0,2},{2,0},{4,6},{6,4},{8,10},{10,8},{12,14},{14,12},{16,18},{18,... | collective-permute-start | bytes 196616 | tf_op jit(solution)/shard_map/ppermute | solution.py:124
  21.2 5.9 %collective-permute-start.30 = (bf16[128,512]{1,0:T(8,128)(2,1)S(1)}, bf16[128,512]{1,0:T(8,128)(2,1)S(1)}, u32[]{:S(2)}, u32[]{:S(2)}) collective-permute-start(bf16[128,512]{1,0:T(8,128)(2,1)S(1)} %pad_maximum_fusion.1), channel_id=1, source_target_pairs={{0,4},{2,6},{4,0},{6,2},{8,12},{10,14},{12,8},{14,10},{1,5},{3,7},... | collective-permute-start | bytes 393224 | tf_op jit(solution)/shard_map/ppermute | solution.py:140
  23.0 7.4 %collective-permute-start.31 = (bf16[128,512]{1,0:T(8,128)(2,1)S(1)}, bf16[128,512]{1,0:T(8,128)(2,1)S(1)}, u32[]{:S(2)}, u32[]{:S(2)}) collective-permute-start(bf16[128,512]{1,0:T(8,128)(2,1)S(1)} %pad_maximum_fusion.1), channel_id=1, source_target_pairs={{0,8},{2,10},{4,12},{6,14},{8,0},{10,2},{12,4},{14,6},{1,9},{3,11}... | collective-permute-start | bytes 393224 | tf_op jit(solution)/shard_map/ppermute | solution.py:140
  30.5 12.8 %collective-permute-start.7 = (bf16[64,1024]{1,0:T(8,128)(2,1)S(1)}, bf16[64,1024]{1,0:T(8,128)(2,1)S(1)}, u32[]{:S(2)}, u32[]{:S(2)}) collective-permute-start(bf16[64,1024]{1,0:T(8,128)(2,1)S(1)} %get-tuple-element.18), channel_id=1, source_target_pairs={{0,4},{2,6},{4,0},{6,2},{8,12},{10,14},{12,8},{14,10},{1,5},{3,7},... | collective-permute-start | bytes 393224 | tf_op jit(solution)/shard_map/ppermute | solution.py:140
  32.0 11.4 %collective-permute-start.9 = (bf16[64,1024]{1,0:T(8,128)(2,1)S(1)}, bf16[64,1024]{1,0:T(8,128)(2,1)S(1)}, u32[]{:S(2)}, u32[]{:S(2)}) collective-permute-start(bf16[64,1024]{1,0:T(8,128)(2,1)S(1)} %get-tuple-element.18), channel_id=1, source_target_pairs={{0,8},{2,10},{4,12},{6,14},{8,0},{10,2},{12,4},{14,6},{1,9},{3,11}... | collective-permute-start | bytes 393224 | tf_op jit(solution)/shard_map/ppermute | solution.py:140
  34.0 14.0 %collective-permute-start.11 = (bf16[64,1024]{1,0:T(8,128)(2,1)S(1)}, bf16[64,1024]{1,0:T(8,128)(2,1)S(1)}, u32[]{:S(2)}, u32[]{:S(2)}) collective-permute-start(bf16[64,1024]{1,0:T(8,128)(2,1)S(1)} %get-tuple-element.18), channel_id=1, source_target_pairs={{4,8},{6,10},{8,4},{10,6},{5,9},{7,11},{9,5},{11,7},{20,24},{22,26... | collective-permute-start | bytes 393224 | tf_op jit(solution)/shard_map/ppermute | solution.py:140
  34.7 24.6 %collective-permute-start.32 = (bf16[128,512]{1,0:T(8,128)(2,1)S(1)}, bf16[128,512]{1,0:T(8,128)(2,1)S(1)}, u32[]{:S(2)}, u32[]{:S(2)}) collective-permute-start(bf16[128,512]{1,0:T(8,128)(2,1)S(1)} %pad_maximum_fusion.1), channel_id=1, source_target_pairs={{4,8},{6,10},{8,4},{10,6},{5,9},{7,11},{9,5},{11,7},{20,24},{22,26... | collective-permute-start | bytes 393224 | tf_op jit(solution)/shard_map/ppermute | solution.py:140
  35.3 11.5 %collective-permute-start.8 = (bf16[64,1024]{1,0:T(8,128)(2,1)S(1)}, bf16[64,1024]{1,0:T(8,128)(2,1)S(1)}, u32[]{:S(2)}, u32[]{:S(2)}) collective-permute-start(bf16[64,1024]{1,0:T(8,128)(2,1)S(1)} %collective-permute-done.6), channel_id=1, source_target_pairs={{0,4},{2,6},{4,0},{6,2},{8,12},{10,14},{12,8},{14,10},{1,5},{3,7},... | collective-permute-start | bytes 393224 | tf_op jit(solution)/shard_map/ppermute | solution.py:140
  43.3 8.6 %collective-permute-start.10 = (bf16[64,1024]{1,0:T(8,128)(2,1)S(1)}, bf16[64,1024]{1,0:T(8,128)(2,1)S(1)}, u32[]{:S(2)}, u32[]{:S(2)}) collective-permute-start(bf16[64,1024]{1,0:T(8,128)(2,1)S(1)} %collective-permute-done.6), channel_id=1, source_target_pairs={{0,8},{2,10},{4,12},{6,14},{8,0},{10,2},{12,4},{14,6},{1,9},{3,11}... | collective-permute-start | bytes 393224 | tf_op jit(solution)/shard_map/ppermute | solution.py:140
  43.4 9.8 %collective-permute-start.12 = (bf16[64,1024]{1,0:T(8,128)(2,1)S(1)}, bf16[64,1024]{1,0:T(8,128)(2,1)S(1)}, u32[]{:S(2)}, u32[]{:S(2)}) collective-permute-start(bf16[64,1024]{1,0:T(8,128)(2,1)S(1)} %collective-permute-done.9), channel_id=1, source_target_pairs={{8,12},{10,14},{4,0},{6,2},{9,13},{11,15},{5,1},{7,3},{24,28},{26,... | collective-permute-start | bytes 393224 | tf_op jit(solution)/shard_map/ppermute | solution.py:140
  46.9 7.2 %collective-permute-start.13 = (bf16[64,1024]{1,0:T(8,128)(2,1)S(1)}, bf16[64,1024]{1,0:T(8,128)(2,1)S(1)}, u32[]{:S(2)}, u32[]{:S(2)}) collective-permute-start(bf16[64,1024]{1,0:T(8,128)(2,1)S(1)} %collective-permute-done.6), channel_id=1, source_target_pairs={{4,8},{6,10},{8,4},{10,6},{5,9},{7,11},{9,5},{11,7},{20,24},{22,26... | collective-permute-start | bytes 393224 | tf_op jit(solution)/shard_map/ppermute | solution.py:140
  48.0 11.3 %collective-permute-start.33 = (bf16[128,512]{1,0:T(8,128)(2,1)S(1)}, bf16[128,512]{1,0:T(8,128)(2,1)S(1)}, u32[]{:S(2)}, u32[]{:S(2)}) collective-permute-start(bf16[128,512]{1,0:T(8,128)(2,1)S(1)} %collective-permute-done.31), channel_id=1, source_target_pairs={{8,12},{10,14},{4,0},{6,2},{9,13},{11,15},{5,1},{7,3},{24,28},{26,... | collective-permute-start | bytes 393224 | tf_op jit(solution)/shard_map/ppermute | solution.py:140
  51.9 6.8 %collective-permute-start.14 = (bf16[64,1024]{1,0:T(8,128)(2,1)S(1)}, bf16[64,1024]{1,0:T(8,128)(2,1)S(1)}, u32[]{:S(2)}, u32[]{:S(2)}) collective-permute-start(bf16[64,1024]{1,0:T(8,128)(2,1)S(1)} %collective-permute-done.10), channel_id=1, source_target_pairs={{8,12},{10,14},{4,0},{6,2},{9,13},{11,15},{5,1},{7,3},{24,28},{26,... | collective-permute-start | bytes 393224 | tf_op jit(solution)/shard_map/ppermute | solution.py:140
  59.4 7.9 %collective-permute-start.21 = (f32[8,512]{1,0:T(8,128)S(1)}, f32[8,512]{1,0:T(8,128)S(1)}, u32[]{:S(2)}, u32[]{:S(2)}) collective-permute-start(f32[8,512]{1,0:T(8,128)S(1)} %get-tuple-element.20), channel_id=1, source_target_pairs={{0,19},{1,18},{2,17},{3,16},{4,23},{5,22},{6,21},{7,20},{8,27},{9,... | collective-permute-start | bytes 49160 | tf_op jit(solution)/shard_map/ppermute | solution.py:137
  68.5 5.6 %collective-permute-start.22 = (bf16[8,512]{1,0:T(8,128)(2,1)S(1)}, bf16[8,512]{1,0:T(8,128)(2,1)S(1)}, u32[]{:S(2)}, u32[]{:S(2)}) collective-permute-start(bf16[8,512]{1,0:T(8,128)(2,1)S(1)} %fusion.33), channel_id=1, source_target_pairs={{0,1},{1,0},{2,3},{3,2},{4,5},{5,4},{6,7},{7,6},{8,9},{9,8},{10,11... | collective-permute-start | bytes 24584 | tf_op jit(solution)/shard_map/ppermute | solution.py:137
  80.1 6.6 %collective-permute-start.34 = (bf16[128,512]{1,0:T(8,128)(2,1)}, bf16[128,512]{1,0:T(8,128)(2,1)S(1)}, u32[]{:S(2)}, u32[]{:S(2)}) collective-permute-start(bf16[128,512]{1,0:T(8,128)(2,1)} %get-tuple-element.15), channel_id=1, source_target_pairs={{0,2},{2,0},{4,6},{6,4},{8,10},{10,8},{12,14},{14,12},{16,18},{18,... | collective-permute-start | bytes 393224 | tf_op jit(solution)/shard_map/ppermute | solution.py:124
  81.1 6.2 %collective-permute-start.35 = (bf16[128,512]{1,0:T(8,128)(2,1)}, bf16[128,512]{1,0:T(8,128)(2,1)S(1)}, u32[]{:S(2)}, u32[]{:S(2)}) collective-permute-start(bf16[128,512]{1,0:T(8,128)(2,1)} %get-tuple-element.14), channel_id=1, source_target_pairs={{0,16},{2,18},{4,20},{6,22},{8,24},{10,26},{12,28},{14,30},{16,0},... | collective-permute-start | bytes 393224 | tf_op jit(solution)/shard_map/ppermute | solution.py:124
  81.9 7.4 %collective-permute-start.36 = (bf16[128,512]{1,0:T(8,128)(2,1)S(1)}, bf16[128,512]{1,0:T(8,128)(2,1)S(1)}, u32[]{:S(2)}, u32[]{:S(2)}) collective-permute-start(bf16[128,512]{1,0:T(8,128)(2,1)S(1)} %get-tuple-element.13), channel_id=1, source_target_pairs={{0,18},{2,16},{4,22},{6,20},{8,26},{10,24},{12,30},{14,28},{16,2},... | collective-permute-start | bytes 393224 | tf_op jit(solution)/shard_map/ppermute | solution.py:124
  (21 other events, 119.8 us)

commit v2 on v0

v2 whole, which is shorter than its diff:
```python
import functools
import math

import jax
import jax.numpy as jnp
from jax import lax
from jax.experimental import pallas as pl
from jax.experimental.pallas import tpu as pltpu
from jax.sharding import Mesh
from jax.sharding import PartitionSpec as P

HEAD = 128
LANES = 128
STEP = 16
HALF = 8
DEAD = -1e30
VMEM = pl.BlockSpec(memory_space=pltpu.VMEM)
PARAMS = pltpu.CompilerParams(vmem_limit_bytes=32 * 1024 * 1024)


def chunk_of(pool):
    return math.gcd(pool, 8)


def owner_mask(owners, start, count, rank):
    lane = lax.broadcasted_iota(jnp.int32, (owners.shape[0], count * rank), 1) // rank + start
    wide = jnp.concatenate([owners] * (count * rank // LANES), axis=1)
    return wide == lane


def shrink_kernel(features, rows_ref, weight_ref, out_ref):
    squares, requests, _ = rows_ref.shape
    count, rank, _ = weight_ref.shape
    step = pl.program_id(0)

    @pl.when(step == 0)
    def _():
        out_ref[...] = jnp.zeros_like(out_ref)

    weight = weight_ref[...].reshape(count * rank, features)
    low = lax.broadcasted_iota(jnp.int32, (requests, LANES), 1) < rank
    folded = []
    for s in range(squares):
        owners = rows_ref[s, :, features:].astype(jnp.float32).astype(jnp.int32)
        sums = lax.dot_general(
            rows_ref[s, :, :features],
            weight,
            (((1,), (1,)), ((), ())),
            preferred_element_type=jnp.float32,
        )
        sums = jnp.where(owner_mask(owners, step * count, count, rank), sums, 0.0)
        total = sums[:, :LANES]
        for k in range(1, count * rank // LANES):
            total = total + sums[:, k * LANES : (k + 1) * LANES]
        folded.append(total + pltpu.roll(total, rank, 1))
    half = squares // 2
    for s in range(half):
        rows = pl.ds(s * requests, requests)
        out_ref[rows, :] += jnp.where(low, folded[s], folded[s + half])


def expand_kernel(features, rows_ref, low_ref, weight_ref, out_ref, total_ref):
    squares, requests, _ = rows_ref.shape
    count, rank, outputs = weight_ref.shape
    step = pl.program_id(0)
    half = squares // 2
    weight = weight_ref[...].reshape(count * rank, outputs)
    low = lax.broadcasted_iota(jnp.int32, (requests, LANES), 1) < rank
    for s in range(squares):
        owners = rows_ref[s, :, features:].astype(jnp.float32).astype(jnp.int32)
        held = low_ref[pl.ds((s % half) * requests, requests), :]
        turned = pltpu.roll(held, rank, 1)
        both = jnp.where(low, held, turned) if s < half else jnp.where(low, turned, held)
        wide = jnp.concatenate([both] * (count * rank // LANES), axis=1)
        wide = jnp.where(owner_mask(owners, step * count, count, rank), wide, 0.0)
        part = jnp.dot(wide.astype(jnp.bfloat16), weight, preferred_element_type=jnp.float32)

        @pl.when(step == 0)
        def _():
            total_ref[s] = part

        @pl.when(step > 0)
        def _():
            total_ref[s] += part

    @pl.when(step == pl.num_programs(0) - 1)
    def _():
        out_ref[...] = total_ref[...].astype(jnp.bfloat16)


def attend_kernel(len_ref, base_ref, nk_ref, nv_ref, ck_ref, cv_ref, delta_ref, out_ref):
    requests, columns = base_ref.shape
    groups = nk_ref.shape[1] // HEAD
    slots = ck_ref.shape[1]
    parts, _, width = delta_ref.shape
    heads = columns // groups // HEAD
    scale = 1.0 / math.sqrt(HEAD)
    keys_in = HALF * slots
    rows = heads * HALF
    col = lax.broadcasted_iota(jnp.int32, (HALF, keys_in), 1)
    row = lax.broadcasted_iota(jnp.int32, (HALF, keys_in), 0)
    same = row == col // slots
    slot = col % slots
    own_col = lax.broadcasted_iota(jnp.int32, (HALF, LANES), 1)
    own_row = lax.broadcasted_iota(jnp.int32, (HALF, LANES), 0)
    own_bias = jnp.where(own_col == own_row, 0.0, DEAD)
    ones = jnp.ones((keys_in + LANES, HEAD), jnp.bfloat16)
    empty = jnp.zeros((LANES - HALF, HEAD), jnp.float32)
    contract = (((1,), (1,)), ((), ()))

    def body(i, _):
        at = pl.ds(pl.multiple_of(i * STEP, STEP), STEP)
        delta = jnp.concatenate([delta_ref[s, at, :] for s in range(parts)], axis=1)
        query = base_ref[at, :].astype(jnp.float32) + delta.astype(jnp.float32)
        fresh_key = nk_ref[at, :].astype(jnp.float32)
        fresh_value = nv_ref[at, :].astype(jnp.float32)
        outs = []
        for h in range(STEP // HALF):
            mine = slice(h * HALF, (h + 1) * HALF)
            lens = len_ref[pl.ds(pl.multiple_of(i * STEP + h * HALF, HALF), HALF), :]
            bias = jnp.where(same & (slot < lens), 0.0, DEAD)
            bias = jnp.concatenate([bias, own_bias], axis=1)
            bias = jnp.concatenate([bias] * heads, axis=0)
            slab = pl.ds(pl.multiple_of(i * STEP + h * HALF, HALF), HALF)
            for g in range(groups):
                lanes = slice(g * HEAD, (g + 1) * HEAD)
                q = jnp.concatenate(
                    [
                        query[mine, (g * heads + k) * HEAD : (g * heads + k + 1) * HEAD]
                        for k in range(heads)
                    ],
                    axis=0,
                ).astype(jnp.bfloat16)
                own_key = jnp.concatenate([fresh_key[mine, lanes], empty], axis=0)
                own_value = jnp.concatenate([fresh_value[mine, lanes], empty], axis=0)
                keys = jnp.concatenate(
                    [ck_ref[slab, :, lanes].reshape(keys_in, HEAD), own_key.astype(jnp.bfloat16)],
                    axis=0,
                )
                values = jnp.concatenate(
                    [cv_ref[slab, :, lanes].reshape(keys_in, HEAD), own_value.astype(jnp.bfloat16)],
                    axis=0,
                )
                scores = lax.dot_general(q, keys, contract, preferred_element_type=jnp.float32)
                scores = scores + bias
                top = jnp.max(scores, axis=1, keepdims=True)
                exps = jnp.exp((scores - top) * scale).astype(jnp.bfloat16)
                mixed = jnp.dot(
                    exps,
                    jnp.concatenate([values, ones], axis=1),
                    preferred_element_type=jnp.float32,
                )
                mixed = mixed[:, :HEAD] / mixed[:, HEAD:]
                outs.append([mixed[k * HALF : (k + 1) * HALF] for k in range(heads)])
        for g in range(groups):
            for k in range(heads):
                both = [outs[h * groups + g][k] for h in range(STEP // HALF)]
                c = (g * heads + k) * HEAD
                out_ref[at, c : c + HEAD] = jnp.concatenate(both, axis=0).astype(jnp.bfloat16)
        return 0

    lax.fori_loop(0, requests // STEP, body, 0)


def attend(base, new_key, new_value, cache_keys, cache_values, lengths, delta):
    requests, columns = base.shape
    kv = new_key.shape[1]
    slots = cache_keys.shape[1]
    return pl.pallas_call(
        attend_kernel,
        out_shape=jax.ShapeDtypeStruct((requests, columns), jnp.bfloat16),
        in_specs=[VMEM] * 7,
        out_specs=VMEM,
        compiler_params=PARAMS,
        cost_estimate=pl.CostEstimate(
            flops=4 * requests * HALF * slots * columns,
            bytes_accessed=4 * requests * (columns + slots * kv),
            transcendentals=requests * slots * columns // 8,
        ),
    )(lengths, base, new_key, new_value, cache_keys, cache_values, delta)


def per_device(
    hidden,
    adapter_ids,
    owner_map,
    shrink_factors,
    expand_factors,
    query_base,
    new_key,
    new_value,
    cache_keys,
    cache_values,
    lengths,
):
    reps, levels, sides, tp = (lax.axis_size(a) for a in ("rep", "level", "side", "tp"))
    pool = levels * sides
    requests, wide = hidden.shape
    rank = shrink_factors.shape[2]
    square = reps * sides
    features = wide // square
    outputs = query_base.shape[1] // square
    chips = ("rep", "side")
    me = lax.axis_index("rep") * sides + lax.axis_index("side")

    shrink = shrink_factors[0].T
    expand = expand_factors[0]
    row_of = lax.axis_index("rep") * sides

    def quarters(a, width):
        mine = lax.dynamic_slice_in_dim(a, row_of * width, sides * width, 1)
        mine = mine.reshape(rank, sides, width).transpose(1, 0, 2)
        return lax.all_to_all(mine, "side", split_axis=0, concat_axis=0, tiled=True)

    shrink = quarters(shrink, features)
    expand = quarters(expand, outputs)
    shrink = lax.all_gather(shrink, "level", axis=0, tiled=True)
    expand = lax.all_gather(expand, "level", axis=0, tiled=True)

    ids = adapter_ids[:, 0]
    adapters = jnp.arange(owner_map.shape[0], dtype=jnp.int32)
    owners = jnp.sum(jnp.where(ids[:, None] == adapters[None, :], owner_map[None, :], 0), axis=1)
    owners = jnp.broadcast_to(owners.astype(jnp.bfloat16)[None, :, None], (square, requests, LANES))
    rows = hidden.reshape(requests, square, features).transpose(1, 0, 2)
    rows = jnp.concatenate([rows, owners], axis=2)
    rows = lax.all_to_all(rows, chips, split_axis=0, concat_axis=0, tiled=True)

    chunk = chunk_of(pool)
    partial = pl.pallas_call(
        functools.partial(shrink_kernel, features),
        out_shape=jax.ShapeDtypeStruct((square // 2 * requests, LANES), jnp.float32),
        grid=(pool // chunk,),
        in_specs=[
            pl.BlockSpec(rows.shape, lambda i: (0, 0, 0)),
            pl.BlockSpec((chunk, rank, features), lambda i: (i, 0, 0)),
        ],
        out_specs=pl.BlockSpec((square // 2 * requests, LANES), lambda i: (0, 0)),
        compiler_params=PARAMS,
    )(rows, shrink)
    low_rank = lax.psum(partial, ("rep", "side", "tp"))
    delta = pl.pallas_call(
        functools.partial(expand_kernel, features),
        out_shape=jax.ShapeDtypeStruct((square, requests, outputs), jnp.bfloat16),
        grid=(pool // chunk,),
        in_specs=[
            pl.BlockSpec(rows.shape, lambda i: (0, 0, 0)),
            pl.BlockSpec(partial.shape, lambda i: (0, 0)),
            pl.BlockSpec((chunk, rank, outputs), lambda i: (i, 0, 0)),
        ],
        out_specs=pl.BlockSpec((square, requests, outputs), lambda i: (0, 0, 0)),
        scratch_shapes=[pltpu.VMEM((square, requests, outputs), jnp.float32)],
        compiler_params=PARAMS,
    )(rows, low_rank, expand)
    delta = lax.all_to_all(delta, chips, split_axis=0, concat_axis=0, tiled=True)
    return attend(
        query_base, new_key, new_value, cache_keys, cache_values, lengths[:, None], delta
    )


def solution(mesh):
    reps, pool, tp = (mesh.shape[a] for a in ("rep", "pool", "tp"))
    finer = Mesh(mesh.devices.reshape(reps, pool // 2, 2, tp), ("rep", "level", "side", "tp"))
    pooled = ("level", "side")
    requests = ("rep", "level", "side")
    in_specs = (
        P(requests, "tp"),
        P(requests, None),
        P(),
        P(pooled, "tp", None),
        P(pooled, None, "tp"),
        P(requests, "tp"),
        P(requests, "tp"),
        P(requests, "tp"),
        P(requests, None, "tp"),
        P(requests, None, "tp"),
        P(requests),
    )
    return jax.shard_map(
        per_device, mesh=finer, in_specs=in_specs, out_specs=P(requests, "tp"), check_vma=False
    )
```

time: 101 us -> 134 us (1.33)
  waiting for transfers between devices: 26.2 us -> 61.7 us
  blocking collectives: 59.2 us -> 25.2 us
  between operations: 0.19 us -> 13.6 us
  Pallas kernels: 0 us -> 13.2 us
  matrix products: 7.84 us -> 0 us
  starting transfers between devices: 3.59 us -> 10.7 us
  local copies, waits for them, and re-layouts: 2.04 us -> 7.58 us
    all_to_all x1, blocking collectives: 55.4 us -> 9.73 us  [quarters(): return lax.all_to_all(mine, 'side', split_axis=0, concat_axis=0, tiled=True)]
    psum x0 -> x1, waiting for transfers between devices: none -> 37 us  [per_device(): low_rank = lax.psum(partial, ('rep', 'side', 'tp'))]
    all_gather x0 -> x1, blocking collectives: none -> 15.5 us  [per_device(): expand = lax.all_gather(expand, 'level', axis=0, tiled=True)]
    pallas_call x0 -> x3, Pallas kernels: none -> 13.2 us  [the longest x1 9.68 us: attend(): pl.pallas_call(attend_kernel, out_shape=jax.ShapeDtypeStruct((requests, c...]
    dot_general x7 -> x0, matrix products: 7.84 us -> none  [the longest x1 2.13 us: attend_requests(): jnp.einsum('rgqj,rjgd->rgqd', cache_probs, cached_values, preferred_eleme...]
    all_to_all x1 -> x3, starting transfers between devices: 3.59 us -> 10.6 us  [the longest x1 3.66 us: per_device(): rows = lax.all_to_all(rows, chips, split_axis=0, concat_axis=0, tiled=True)]
    all_to_all x1 -> x3, waiting for transfers between devices: 26.2 us -> 21.2 us  [the longest x1 13.8 us: per_device(): rows = lax.all_to_all(rows, chips, split_axis=0, concat_axis=0, tiled=True)]
    unnamed x16 -> x25, local copies, waits for them, and re-layouts: 1.31 us -> 5.84 us
  transfers between devices with their start and end apart: 1 -> 5, of which waited for: 1 -> 4; matrix products, arithmetic and copies ran while one was open for 0% -> 3% of each run, Pallas kernels for 0% -> 2%
where the time goes in v2:
time: 134 us; the launch traced here: 133 us
  waiting for transfers between devices  61.7 us (46%)
  blocking collectives  25.2 us (19%)
  between operations  13.6 us (10%)
  Pallas kernels  13.2 us (10%)
  starting transfers between devices  10.7 us (8%)
  local copies, waits for them, and re-layouts  7.58 us (6%)
    psum x1, waiting for transfers between devices, per_device(): low_rank = lax.psum(partial, ('rep', 'side', 'tp'))  37 us
    all_gather x1, blocking collectives, per_device(): expand = lax.all_gather(expand, 'level', axis=0, tiled=True)  15.5 us
    all_to_all x1, waiting for transfers between devices, per_device(): rows = lax.all_to_all(rows, chips, split_axis=0, concat_axis=0, tiled=True)  13.8 us
    all_to_all x1, blocking collectives, quarters(): return lax.all_to_all(mine, 'side', split_axis=0, concat_axis=0, tiled=True)  9.73 us
    pallas_call x1, Pallas kernels, attend(): pl.pallas_call(attend_kernel, out_shape=jax.ShapeDtypeStruct((requests, c...  9.68 us
    all_to_all x1, waiting for transfers between devices, per_device(): lax.all_to_all(delta, chips, split_axis=0, concat_axis=0, tiled=True)  7.36 us
    unnamed x25, local copies, waits for them, and re-layouts  5.84 us
    all_to_all x1, starting transfers between devices, per_device(): rows = lax.all_to_all(rows, chips, split_axis=0, concat_axis=0, tiled=True)  3.66 us
  transfers between devices with their start and end apart: 5, of which 4 were waited for; matrix products, arithmetic and copies ran while one was open for 3% of the time, Pallas kernels for 2%

profile of v2, /device:TPU:0, one launch (start us, length us, event | category | flops | bytes accessed | tf_op | source)
XLA Modules:
  0.0 133.2 jit_solution(9657392045058783430)
XLA Ops:
  6.5 1.0 copy-done
  7.6 0.2 reshape.20
  7.8 9.7 %all_to_all.20 = bf16[2,64,1024]{2,1,0:T(8,128)(2,1)} all-to-all(bf16[2,64,1024]{2,1,0:T(8,128)(2,1)S(1)} %copy.30), channel_id=1, replica_groups=mesh['rep'=2,'level'=4,'side'=2,'tp'=2] {'side'}, dimensions={0} | all-to-all | bytes 524288 | tf_op jit(solution)/shard_map/all_to_all | solution.py:213
  17.6 0.1 select_reduce_fusion
  17.7 1.6 %copy.28 = bf16[128,4096]{0,1:T(8,128)(2,1)S(1)} copy(bf16[128,4096]{1,0:T(8,128)(2,1)} %param.11) | data formatting | bytes 2097152 | tf_op args[0]
  19.3 0.5 copy.29
  19.9 0.1 broadcast_in_dim.26
  20.0 1.2 pad_maximum_fusion
  21.1 3.7 %all-to-all-start = ((bf16[4,128,1152]{2,1,0:T(8,128)(2,1)}), bf16[4,128,1152]{2,1,0:T(8,128)(2,1)S(1)}, u32[]{:S(2)}, u32[]{:S(2)}) async-start(bf16[4,128,1152]{2,1,0:T(8,128)(2,1)} %pad_maximum_fusion), calls=%async_computation | async-start | bytes 2359296 | tf_op jit(solution)/shard_map/all_to_all | solution.py:226
  24.9 0.7 copy.31
  25.6 13.8 %all-to-all-done.rows_ref = bf16[4,128,1152]{2,1,0:T(8,128)(2,1)S(1)} async-done(((bf16[4,128,1152]{2,1,0:T(8,128)(2,1)}), bf16[4,128,1152]{2,1,0:T(8,128)(2,1)S(1)}, u32[]{:S(2)}, u32[]{:S(2)}) %all-to-all-start) | async-done | bytes 1179680 | tf_op jit(solution)/shard_map/all_to_all | solution.py:226
  39.4 3.4 %all-to-all-start.2 = ((bf16[2,64,512]{2,1,0:T(8,128)(2,1)}), bf16[2,64,512]{2,1,0:T(8,128)(2,1)S(1)}, u32[]{:S(2)}, u32[]{:S(2)}) async-start(bf16[2,64,512]{2,1,0:T(8,128)(2,1)} %copy.31), calls=%async_computation.2 | async-start | bytes 262144 | tf_op jit(solution)/shard_map/all_to_all | solution.py:213
  42.9 3.4 %all-gather.2.cloned.1.call-done.weight_ref = bf16[8,64,1024]{2,1,0:T(8,128)(2,1)} async-done(((bf16[2,64,1024]{2,1,0:T(8,128)(2,1)}), bf16[8,64,1024]{2,1,0:T(8,128)(2,1)}) %all-gather.2.cloned.1.call-update) | async-done | bytes 1048592 | tf_op jit(solution)/shard_map/all_gather | solution.py:217
  46.3 1.2 copy-done.1
  47.5 2.2 %shard_map.109 = f32[256,128]{1,0:T(8,128)} custom-call(bf16[4,128,1152]{2,1,0:T(8,128)(2,1)S(1)} %all-to-all-done.rows_ref, bf16[8,64,1024]{2,1,0:T(8,128)(2,1)S(1)} %copy-done.1), custom_call_target="tpu_custom_call" | custom-call | tf_op jit(solution)/shard_map/pallas_call | solution.py:229
  49.7 15.5 %all_gather.7.weight_ref = bf16[8,64,512]{2,1,0:T(8,128)(2,1)S(1)} all-gather(bf16[2,64,512]{2,1,0:T(8,128)(2,1)S(1)} %all-to-all-done.2), channel_id=1, replica_groups=mesh['rep'=2,'level'=4,'side'=2,'tp'=2] {'level'}, dimensions={0}, use_global_device_ids=true | all-gather | bytes 655360 | tf_op jit(solution)/shard_map/all_gather | solution.py:218
  65.2 37.0 %all-reduce.2.cloned.1.call-done.low_ref = f32[256,128]{1,0:T(8,128)} async-done(((f32[256,128]{1,0:T(8,128)}), f32[256,128]{1,0:T(8,128)}) %all-reduce.2.cloned.1.call-update) | async-done | bytes 131088 | tf_op jit(solution)/shard_map/psum | solution.py:240
  102.3 0.9 copy-done.5
  103.2 1.3 shard_map.110
  104.5 3.6 %all-to-all-start.3 = ((bf16[4,128,512]{2,1,0:T(8,128)(2,1)}), bf16[4,128,512]{2,1,0:T(8,128)(2,1)S(1)}, u32[]{:S(2)}, u32[]{:S(2)}) async-start(bf16[4,128,512]{2,1,0:T(8,128)(2,1)} %shard_map.110), calls=%async_computation.3 | async-start | bytes 1048576 | tf_op jit(solution)/shard_map/all_to_all | solution.py:254
  108.1 0.1 copy.32.len_ref
  108.2 7.4 %all-to-all-done.3.delta_ref = bf16[4,128,512]{2,1,0:T(8,128)(2,1)S(1)} async-done(((bf16[4,128,512]{2,1,0:T(8,128)(2,1)}), bf16[4,128,512]{2,1,0:T(8,128)(2,1)S(1)}, u32[]{:S(2)}, u32[]{:S(2)}) %all-to-all-start.3) | async-done | bytes 524320 | tf_op jit(solution)/shard_map/all_to_all | solution.py:254
  115.6 1.0 copy-done.4
  116.6 9.7 %shard_map.111 = bf16[128,2048]{1,0:T(8,128)(2,1)} custom-call(s32[128,1]{1,0:T(8,128)S(1)} %copy.32.len_ref, bf16[128,2048]{1,0:T(8,128)(2,1)S(1)} %copy-done.4, bf16[128,256]{1,0:T(8,128)(2,1)S(1)} %copy-done.6, bf16[128,256]{1,0:T(8,128)(2,1)S(1)} %copy-done.7, bf16[128,16,256]{2,1,0:T(8,128)(2,1)S(1)} %copy-done.2, bf16[128,16,256]{2,1,0:T(8,128)(2,1)S(1)} %copy-done.3, ...), custom_call_target="tpu_custom_call" | custom-call | flops 134217728 | bytes 3145728 | tf_op jit(solution)/shard_map/pallas_call | solution.py:169
  (30 shorter events, 0.3 us)
Async XLA Ops:
  6.5 1.0 copy-start
  6.5 39.7 %all-gather.2.cloned.1.call-start = ((), (), s32[]{:S(2)}) async-start(), calls=%async_computation.4 | async-start | bytes 1310720 | tf_op jit(solution)/shard_map/all_gather | solution.py:217
  7.6 10.0 %copy-start.10 = (s32[8]{0:T(128)S(1)}, s32[8]{0:T(128)}, u32[]{:S(2)}) copy-start(s32[8]{0:T(128)} %param.13) | copy-start | bytes 100
  7.6 10.0 %copy-start.11 = (s32[128,1]{0,1:T(1,128)S(1)}, s32[128,1]{0,1:T(1,128)}, u32[]{:S(2)}) copy-start(s32[128,1]{0,1:T(1,128)} %param.12) | copy-start | bytes 1540
  21.1 3.7 %copy-start.8 = (bf16[1,64,2048]{2,1,0:T(8,128)(2,1)S(1)}, bf16[1,64,2048]{2,1,0:T(8,128)(2,1)}, u32[]{:S(2)}) copy-start(bf16[1,64,2048]{2,1,0:T(8,128)(2,1)} %param.15) | copy-start | bytes 786436
  21.1 18.3 %all-to-all-start = ((bf16[4,128,1152]{2,1,0:T(8,128)(2,1)}), bf16[4,128,1152]{2,1,0:T(8,128)(2,1)S(1)}, u32[]{:S(2)}, u32[]{:S(2)}) async-start(bf16[4,128,1152]{2,1,0:T(8,128)(2,1)} %pad_maximum_fusion), calls=%async_computation | async-start | bytes 2359296 | tf_op jit(solution)/shard_map/all_to_all | solution.py:226
  39.4 10.3 %all-to-all-start.2 = ((bf16[2,64,512]{2,1,0:T(8,128)(2,1)}), bf16[2,64,512]{2,1,0:T(8,128)(2,1)S(1)}, u32[]{:S(2)}, u32[]{:S(2)}) async-start(bf16[2,64,512]{2,1,0:T(8,128)(2,1)} %copy.31), calls=%async_computation.2 | async-start | bytes 262144 | tf_op jit(solution)/shard_map/all_to_all | solution.py:213
  42.8 59.5 %all-reduce.2.cloned.1.call-start = ((), (), s32[]{:S(2)}) async-start(), calls=%async_computation.5 | async-start | bytes 262144 | tf_op jit(solution)/shard_map/psum | solution.py:240
  46.3 1.2 copy-start.1
  65.2 50.3 %copy-start.2 = (bf16[128,16,256]{2,1,0:T(8,128)(2,1)S(1)}, bf16[128,16,256]{2,1,0:T(8,128)(2,1)}, u32[]{:S(2)}) copy-start(bf16[128,16,256]{2,1,0:T(8,128)(2,1)} %ck_ref.1) | copy-start | bytes 3145732
  102.3 0.9 copy-start.5
  103.2 4.9 %copy-start.9 = (s32[128]{0:T(128)S(1)}, s32[128]{0:T(128)}, u32[]{:S(2)}) copy-start(s32[128]{0:T(128)} %param.21) | copy-start | bytes 1540
  103.2 12.4 %copy-start.6 = (bf16[128,256]{1,0:T(8,128)(2,1)S(1)}, bf16[128,256]{1,0:T(8,128)(2,1)}, u32[]{:S(2)}) copy-start(bf16[128,256]{1,0:T(8,128)(2,1)} %nk_ref.1) | copy-start | bytes 196612
  103.2 12.4 %copy-start.7 = (bf16[128,256]{1,0:T(8,128)(2,1)S(1)}, bf16[128,256]{1,0:T(8,128)(2,1)}, u32[]{:S(2)}) copy-start(bf16[128,256]{1,0:T(8,128)(2,1)} %nv_ref.1) | copy-start | bytes 196612
  104.5 11.1 %copy-start.3 = (bf16[128,16,256]{2,1,0:T(8,128)(2,1)S(1)}, bf16[128,16,256]{2,1,0:T(8,128)(2,1)}, u32[]{:S(2)}) copy-start(bf16[128,16,256]{2,1,0:T(8,128)(2,1)} %cv_ref.1) | copy-start | bytes 3145732
  104.5 11.1 %all-to-all-start.3 = ((bf16[4,128,512]{2,1,0:T(8,128)(2,1)}), bf16[4,128,512]{2,1,0:T(8,128)(2,1)S(1)}, u32[]{:S(2)}, u32[]{:S(2)}) async-start(bf16[4,128,512]{2,1,0:T(8,128)(2,1)} %shard_map.110), calls=%async_computation.3 | async-start | bytes 1048576 | tf_op jit(solution)/shard_map/all_to_all | solution.py:254
  115.6 1.0 copy-start.4
Sparse Core Ops, SparseCore 0:
  17.7 28.4 all-gather.1
  49.8 52.4 all-reduce.1

commit v3 on v0

v3 whole, which is shorter than its diff:
```python
import functools
import math

import jax
import jax.numpy as jnp
from jax import lax
from jax.experimental import pallas as pl
from jax.experimental.pallas import tpu as pltpu
from jax.sharding import Mesh
from jax.sharding import PartitionSpec as P

HEAD = 128
LANES = 128
STEP = 16
HALF = 8
BATCH = 4
DEAD = -1e30
VMEM = pl.BlockSpec(memory_space=pltpu.VMEM)
SMEM = pl.BlockSpec(memory_space=pltpu.SMEM)
PARAMS = pltpu.CompilerParams(vmem_limit_bytes=32 * 1024 * 1024)
NT = (((1,), (1,)), ((), ()))
TN = (((0,), (0,)), ((), ()))


def pack_kernel(parts, me_ref, map_ref, ids_ref, hidden_ref, *out_refs):
    requests, wide = hidden_ref.shape
    features = wide // parts
    me = me_ref[0]
    ids = ids_ref[...]

    def look(k, found):
        return jnp.where(ids == k, map_ref[k], found)

    owners = lax.fori_loop(0, map_ref.shape[0], look, jnp.zeros_like(ids))
    owners = jnp.broadcast_to(owners.astype(jnp.float32), (requests, LANES)).astype(jnp.bfloat16)
    for s in range(parts):
        at = pl.ds(pl.multiple_of((me ^ s) * features, features), features)
        out_refs[s][:, :features] = hidden_ref[:, at]
        out_refs[s][:, features:] = owners


def owner_mask(owners, ids, rank):
    lane = lax.broadcasted_iota(jnp.int32, (1, len(ids) * rank), 1) // rank
    named = jnp.full_like(lane, -1)
    for k, owner in enumerate(ids):
        named = jnp.where(lane == k, owner, named)
    wide = jnp.concatenate([owners] * (len(ids) * rank // LANES), axis=1)
    return wide == named


def row_owners(ref, features):
    return ref[:, features:].astype(jnp.float32).astype(jnp.int32)


def stacked(refs):
    blocks = [r[k] for r in refs for k in range(r.shape[0])]
    return jnp.concatenate(blocks, axis=0)


def shrink_kernel(parts, blocks, gridded, ids_ref, *refs):
    row_refs, weight_refs, base_ref, out_ref = (
        refs[:parts],
        refs[parts : parts + blocks],
        refs[parts + blocks],
        refs[-1],
    )
    rank, features = weight_refs[0].shape[1:]
    requests = row_refs[0].shape[0]
    count = sum(r.shape[0] for r in weight_refs)
    step = pl.program_id(0) if gridded else 0
    ids = [ids_ref[step * count + k] for k in range(count)]
    weight = stacked(weight_refs)
    low = lax.broadcasted_iota(jnp.int32, (requests, LANES), 1) < rank
    folded = []
    for ref in row_refs:
        sums = lax.dot_general(
            ref[:, :features], weight, NT, preferred_element_type=jnp.float32
        )
        sums = jnp.where(owner_mask(row_owners(ref, features), ids, rank), sums, 0.0)
        total = sums[:, :LANES]
        for k in range(1, count * rank // LANES):
            total = total + sums[:, k * LANES : (k + 1) * LANES]
        folded.append(total + pltpu.roll(total, rank, 1))
    if gridded:

        @pl.when(step == 0)
        def _():
            out_ref[...] = base_ref[...]

    else:
        out_ref[...] = base_ref[...]
    half = parts // 2
    for s in range(half):
        rows = pl.ds(s * requests, requests)
        out_ref[rows, :] += jnp.where(low, folded[s], folded[s + half])


def expand_kernel(parts, blocks, cores, gridded, ids_ref, me_ref, *refs):
    row_refs, low_ref, weight_refs, out_refs, total_ref = (
        refs[:parts],
        refs[parts],
        refs[parts + 1 : parts + 1 + blocks],
        refs[-parts - 1 : -1],
        refs[-1],
    )
    rank, outputs = weight_refs[0].shape[1:]
    features = row_refs[0].shape[1] - LANES
    requests = row_refs[0].shape[0]
    count = sum(r.shape[0] for r in weight_refs)
    step = pl.program_id(0) if gridded else 0
    last = pl.num_programs(0) - 1 if gridded else 0
    ids = [ids_ref[step * count + k] for k in range(count)]
    weight = stacked(weight_refs)
    half = parts // 2
    low = lax.broadcasted_iota(jnp.int32, (requests, LANES), 1) < rank
    me = me_ref[0]
    held = [[0.0] * half for _ in range(2)]
    for t in range(parts):
        for core in range(cores):
            sums = low_ref[(me ^ t) * cores + core].astype(jnp.float32)
            for s in range(half):
                at = (s ^ t) % half
                piece = sums[at * requests : (at + 1) * requests]
                held[t // half][s] = held[t // half][s] + piece
    for s in range(half):
        straight = held[0][s] + pltpu.roll(held[1][s], rank, 1)
        turned = pltpu.roll(straight, rank, 1)
        for part in (s, s + half):
            first = straight if part < half else turned
            other = turned if part < half else straight
            both = jnp.where(low, first, other)
            wide = jnp.concatenate([both] * (count * rank // LANES), axis=1)
            mask = owner_mask(row_owners(row_refs[part], features), ids, rank)
            wide = jnp.where(mask, wide, 0.0).astype(jnp.bfloat16)
            product = jnp.dot(wide, weight, preferred_element_type=jnp.float32)
            if not gridded:
                out_refs[part][...] = product.astype(jnp.bfloat16)
            else:

                @pl.when(step == 0)
                def _():
                    total_ref[part] = product

                @pl.when(step > 0)
                def _():
                    total_ref[part] += product

                @pl.when(step == last)
                def _():
                    out_refs[part][...] = total_ref[part].astype(jnp.bfloat16)


def attend_kernel(
    parts, me_ref, len_ref, base_ref, nk_ref, nv_ref, ck_ref, cv_ref, *refs
):
    delta_refs, out_ref = refs[:parts], refs[parts]
    me = me_ref[0]
    requests, columns = base_ref.shape
    width = columns // parts
    groups = nk_ref.shape[1] // HEAD
    slots = ck_ref.shape[1]
    heads = columns // HEAD
    per_part = width // HEAD
    span = heads * HALF
    part_span = per_part * HALF
    keys_in = HALF * slots + STEP
    row = lax.broadcasted_iota(jnp.int32, (keys_in, span), 0)
    lane_req = lax.broadcasted_iota(jnp.int32, (keys_in, span), 1) % HALF
    own = row - HALF * slots
    slot_of = []
    for h in range(STEP // HALF):
        cached = jnp.where(row // slots == lane_req, row % slots, slots)
        fresh = jnp.where(own == lane_req + h * HALF, -1, slots)
        slot_of.append(jnp.where(own >= 0, fresh, cached))
    part_at = [me ^ s for s in range(parts)]
    group_at = [p // (parts // groups) for p in part_at]
    lane_part = lax.broadcasted_iota(jnp.int32, (1, span), 1) // part_span
    lane_group = jnp.zeros_like(lane_part)
    for s in range(parts):
        lane_group = jnp.where(lane_part == s, group_at[s], lane_group)
    scale = 1.0 / math.sqrt(HEAD)
    ones = jnp.ones((keys_in, HEAD), jnp.bfloat16)

    def body(step, _):
        units = []
        for j in range(BATCH):
            start = pl.multiple_of((step * BATCH + j) * STEP, STEP)
            at = pl.ds(start, STEP)
            pieces = []
            for s in range(parts):
                lanes = pl.ds(pl.multiple_of(part_at[s] * width, width), width)
                q = base_ref[at, lanes].astype(jnp.float32)
                q = q + delta_refs[s][at, :].astype(jnp.float32)
                pieces += [q[:, k * HEAD : (k + 1) * HEAD] for k in range(per_part)]
            for h in range(STEP // HALF):
                slab = pl.ds(pl.multiple_of(start + h * HALF, HALF), HALF)
                q = jnp.concatenate([p[h * HALF : (h + 1) * HALF] for p in pieces], axis=0)
                units.append((step * BATCH + j, at, h, slab, q.astype(jnp.bfloat16)))
        scores = []
        for _, at, h, slab, q in units:
            both = []
            for g in range(groups):
                lanes = slice(g * HEAD, (g + 1) * HEAD)
                keys = ck_ref[slab, :, lanes].reshape(HALF * slots, HEAD)
                keys = jnp.concatenate([keys, nk_ref[at, lanes]], axis=0)
                both.append(lax.dot_general(keys, q, NT, preferred_element_type=jnp.float32))
            score = both[0]
            for g in range(1, groups):
                score = jnp.where(lane_group == g, both[g], score)
            scores.append(score)
        probs = []
        for (i, at, h, slab, q), score in zip(units, scores):
            lens = len_ref[pl.ds(i * (STEP // HALF) + h, 1), :]
            score = jnp.where(slot_of[h] < lens, score, DEAD)
            top = jnp.max(score, axis=0, keepdims=True)
            exps = jnp.exp((score - top) * scale)
            total = jnp.sum(exps, axis=0, keepdims=True)
            probs.append((exps * (1.0 / total)).astype(jnp.bfloat16))
        mixed = []
        for (i, at, h, slab, q), prob in zip(units, probs):
            whole = []
            for g in range(groups):
                lanes = slice(g * HEAD, (g + 1) * HEAD)
                values = cv_ref[slab, :, lanes].reshape(HALF * slots, HEAD)
                values = jnp.concatenate([values, nv_ref[at, lanes]], axis=0)
                whole.append(
                    lax.dot_general(prob, values, TN, preferred_element_type=jnp.float32)
                )
            mixed.append(whole)
        for j in range(BATCH):
            at = units[2 * j][1]
            for s in range(parts):
                rows = slice(s * part_span, (s + 1) * part_span)
                halves = []
                for h in range(STEP // HALF):
                    whole = mixed[2 * j + h]
                    part = whole[0][rows]
                    for g in range(1, groups):
                        part = jnp.where(group_at[s] == g, whole[g][rows], part)
                    halves.append(part)
                out = [
                    jnp.concatenate([p[k * HALF : (k + 1) * HALF] for p in halves], axis=0)
                    for k in range(per_part)
                ]
                lanes = pl.ds(pl.multiple_of(part_at[s] * width, width), width)
                out_ref[at, lanes] = jnp.concatenate(out, axis=1).astype(jnp.bfloat16)
        return 0

    lax.fori_loop(0, requests // (STEP * BATCH), body, 0)


def attend(me, base, new_key, new_value, cache_keys, cache_values, lengths, deltas):
    requests, columns = base.shape
    kv = new_key.shape[1]
    slots = cache_keys.shape[1]
    lengths = jnp.tile(lengths.reshape(requests // HALF, HALF), (1, columns // HEAD))
    return pl.pallas_call(
        functools.partial(attend_kernel, len(deltas)),
        out_shape=jax.ShapeDtypeStruct((requests, columns), jnp.bfloat16),
        in_specs=[SMEM] + [VMEM] * (6 + len(deltas)),
        out_specs=VMEM,
        compiler_params=PARAMS,
        cost_estimate=pl.CostEstimate(
            flops=4 * requests * HALF * slots * columns,
            bytes_accessed=4 * requests * (columns + slots * kv),
            transcendentals=requests * slots * columns // 16,
        ),
    )(me, lengths, base, new_key, new_value, cache_keys, cache_values, *deltas)


def shrink_rows(ids, rows, weights, base, chunk):
    parts = len(rows)
    gridded = chunk is not None
    rank, features = weights[0].shape[1:]
    specs = [SMEM] + [VMEM] * (parts + len(weights) + 1)
    grid = ()
    if gridded:
        grid = (weights[0].shape[0] // chunk,)
        specs[1 + parts] = pl.BlockSpec((chunk, rank, features), lambda i: (i, 0, 0))
    return pl.pallas_call(
        functools.partial(shrink_kernel, parts, len(weights), gridded),
        out_shape=jax.ShapeDtypeStruct(base.shape, jnp.float32),
        grid=grid,
        in_specs=specs,
        out_specs=VMEM,
        compiler_params=PARAMS,
        cost_estimate=pl.CostEstimate(
            flops=2 * parts * rows[0].shape[0] * features * rank * sum(w.shape[0] for w in weights),
            bytes_accessed=4 * parts * rows[0].size,
            transcendentals=0,
        ),
    )(ids, *rows, *weights, base)


def expand_rows(ids, me, rows, low, weights, chunk, cores):
    parts = len(rows)
    gridded = chunk is not None
    rank, outputs = weights[0].shape[1:]
    requests = rows[0].shape[0]
    specs = [SMEM, SMEM] + [VMEM] * (parts + 1 + len(weights))
    grid = ()
    if gridded:
        grid = (weights[0].shape[0] // chunk,)
        specs[3 + parts] = pl.BlockSpec((chunk, rank, outputs), lambda i: (i, 0, 0))
    held = (parts, requests, outputs) if gridded else (1, 8, LANES)
    return pl.pallas_call(
        functools.partial(expand_kernel, parts, len(weights), cores, gridded),
        out_shape=[jax.ShapeDtypeStruct((requests, outputs), jnp.bfloat16)] * parts,
        grid=grid,
        in_specs=specs,
        out_specs=[VMEM] * parts,
        scratch_shapes=[pltpu.VMEM(held, jnp.float32)],
        compiler_params=PARAMS,
    )(ids, me, *rows, low, *weights)


def per_device(
    hidden,
    adapter_ids,
    owner_map,
    shrink_factors,
    expand_factors,
    query_base,
    new_key,
    new_value,
    cache_keys,
    cache_values,
    lengths,
):
    reps, levels, sides, tp = (lax.axis_size(a) for a in ("rep", "level", "side", "tp"))
    requests, wide = hidden.shape
    rank = shrink_factors.shape[2]
    square = reps * sides
    features = wide // square
    outputs = query_base.shape[1] // square
    level, side = lax.axis_index("level"), lax.axis_index("side")
    me = lax.axis_index("rep") * sides + side

    def swap(a, s):
        pairs = [(c, c ^ s) for c in range(square)]
        return lax.ppermute(a, ("rep", "side"), pairs)

    def tied(a, *others):
        return lax.optimization_barrier((a, *others))[0]

    def cut(a, width, at):
        return lax.dynamic_slice_in_dim(a, at * width, width, 2)

    shrink = shrink_factors.swapaxes(1, 2)
    shrink_own = cut(shrink, features, me)
    shrink_next = swap(cut(shrink, features, me ^ 1), 1)
    rows = pl.pallas_call(
        functools.partial(pack_kernel, square),
        out_shape=[jax.ShapeDtypeStruct((requests, features + LANES), jnp.bfloat16)] * square,
        in_specs=[SMEM, SMEM, VMEM, VMEM],
        out_specs=[VMEM] * square,
        compiler_params=PARAMS,
    )(me[None], owner_map, adapter_ids, hidden)
    rows = [rows[0]] + [swap(rows[s], s) for s in range(1, square)]

    empty = jnp.zeros((square // 2 * requests, LANES), jnp.float32)
    order = jnp.arange(levels, dtype=jnp.int32)
    if levels == 4:
        near_pairs = [(i, i ^ 1) for i in range(levels)]
        far_pairs = [(i, i ^ 2) for i in range(levels)]

        def gather(a):
            far = lax.ppermute(a, "level", far_pairs)
            near = lax.ppermute(a, "level", near_pairs)
            inner = lax.ppermute(a, "level", [(1, 2), (2, 1)])
            outer = lax.ppermute(far, "level", [(2, 3), (1, 0)])
            return [a, near, far, jnp.where((level == 1) | (level == 2), inner, outer)]

        own_ids = (level ^ order) * sides + side
        next_ids = (level ^ order) * sides + (side ^ 1)
        own_blocks = gather(shrink_own)
        next_blocks = gather(shrink_next)
        partial = shrink_rows(own_ids, rows, own_blocks, empty, None)
        partial = shrink_rows(next_ids, rows, next_blocks, partial, None)
        expand = tied(expand_factors, own_blocks[1], own_blocks[2])
        expand_own = cut(expand, outputs, me)
        expand_next = swap(cut(expand, outputs, me ^ 1), 1)
        expand = gather(jnp.concatenate([expand_own, expand_next], axis=0))
        expand_ids = jnp.stack([own_ids, next_ids], axis=1).reshape(-1)
        chunk = None
    else:
        expand_own = cut(expand_factors, outputs, me)
        expand_next = swap(cut(expand_factors, outputs, me ^ 1), 1)
        pair = jnp.stack([side, side ^ 1])
        expand_ids = (order[:, None] * sides + pair[None, :]).reshape(-1)
        chunk = 4

        def gather(own, other):
            both = jnp.concatenate([own, other], axis=0)
            return lax.all_gather(both, "level", axis=0, tiled=True)

        expand = [gather(expand_own, expand_next)]
        weights = [gather(shrink_own, shrink_next)]
        partial = shrink_rows(expand_ids, rows, weights, empty, chunk)

    partial = partial.astype(jnp.bfloat16)
    partial = jnp.broadcast_to(partial[None], (square * tp,) + partial.shape)
    sums = lax.all_to_all(partial, ("rep", "side", "tp"), split_axis=0, concat_axis=0, tiled=True)
    deltas = expand_rows(expand_ids, me[None], rows, sums, expand, chunk, tp)
    deltas = [deltas[0]] + [swap(deltas[s], s) for s in range(1, square)]
    return attend(
        me[None],
        query_base,
        new_key,
        new_value,
        cache_keys,
        cache_values,
        lengths,
        deltas,
    )


def solution(mesh):
    reps, pool, tp = (mesh.shape[a] for a in ("rep", "pool", "tp"))
    finer = Mesh(mesh.devices.reshape(reps, pool // 2, 2, tp), ("rep", "level", "side", "tp"))
    pooled = ("level", "side")
    requests = ("rep", "level", "side")
    in_specs = (
        P(requests, "tp"),
        P(requests, None),
        P(),
        P(pooled, "tp", None),
        P(pooled, None, "tp"),
        P(requests, "tp"),
        P(requests, "tp"),
        P(requests, "tp"),
        P(requests, None, "tp"),
        P(requests, None, "tp"),
        P(requests),
    )
    return jax.shard_map(
        per_device, mesh=finer, in_specs=in_specs, out_specs=P(requests, "tp"), check_vma=False
    )
```

time: 101 us -> 74.7 us (0.74)
  blocking collectives: 59.2 us -> 0 us
  starting transfers between devices: 3.59 us -> 37.4 us
  local copies, waits for them, and re-layouts: 2.04 us -> 11.4 us
  waiting for transfers between devices: 26.2 us -> 17.2 us
  matrix products: 7.84 us -> 0 us
  Pallas kernels: 0 us -> 7.65 us
  other arithmetic: 1.9 us -> 0.16 us
    all_to_all x1 -> x0, blocking collectives: 55.4 us -> none  [per_device(): lax.all_to_all(outgoing, 'pool', split_axis=0, concat_axis=0, tiled=True)]
    ppermute x0 -> x20, starting transfers between devices: none -> 33.9 us  [the longest x8 10.1 us: swap(): return lax.ppermute(a, ('rep', 'side'), pairs)]
    all_to_all x1, waiting for transfers between devices: 26.2 us -> 0.01 us  [per_device(): lax.all_to_all(partial, ('rep', 'side', 'tp'), split_axis=0, concat_axis=...]
    ppermute x0 -> x20, waiting for transfers between devices: none -> 17.2 us  [the longest x8 10.6 us: swap(): return lax.ppermute(a, ('rep', 'side'), pairs)]
    unnamed x16 -> x33, local copies, waits for them, and re-layouts: 1.31 us -> 9.23 us
    dot_general x7 -> x0, matrix products: 7.84 us -> none  [the longest x1 2.13 us: attend_requests(): jnp.einsum('rgqj,rjgd->rgqd', cache_probs, cached_values, preferred_eleme...]
    pallas_call x0 -> x5, Pallas kernels: none -> 7.65 us  [the longest x2 2.84 us: shrink_rows(): pl.pallas_call(functools.partial(shrink_kernel, parts, len(weights), grid...]
    psum x1 -> x0, blocking collectives: 3.75 us -> none  [per_device(): rank_total = lax.psum(partial_sum, 'tp')]
  transfers between devices with their start and end apart: 1 -> 21, of which waited for: 1 -> 7; matrix products, arithmetic and copies ran while one was open for 0% -> 2% of each run, Pallas kernels for 0% -> 5%
where the time goes in v3:
time: 74.7 us; the launch traced here: 74.2 us
  starting transfers between devices  37.4 us (50%)
  waiting for transfers between devices  17.2 us (23%)
  local copies, waits for them, and re-layouts  11.4 us (15%)
  Pallas kernels  7.65 us (10%)
    ppermute x8, waiting for transfers between devices, swap(): return lax.ppermute(a, ('rep', 'side'), pairs)  10.6 us
    ppermute x8, starting transfers between devices, swap(): return lax.ppermute(a, ('rep', 'side'), pairs)  10.1 us
    ppermute x3, starting transfers between devices, gather(): near = lax.ppermute(a, 'level', near_pairs)  9.35 us
    unnamed x33, local copies, waits for them, and re-layouts  9.23 us
    ppermute x3, starting transfers between devices, gather(): far = lax.ppermute(a, 'level', far_pairs)  8.61 us
    ppermute x3, starting transfers between devices, gather(): outer = lax.ppermute(far, 'level', [(2, 3), (1, 0)])  3.85 us
    all_to_all x1, starting transfers between devices, per_device(): lax.all_to_all(partial, ('rep', 'side', 'tp'), split_axis=0, concat_axis=...  3.49 us
    pallas_call x2, Pallas kernels, shrink_rows(): pl.pallas_call(functools.partial(shrink_kernel, parts, len(weights), grid...  2.84 us
  transfers between devices with their start and end apart: 21, of which 7 were waited for; matrix products, arithmetic and copies ran while one was open for 2% of the time, Pallas kernels for 5%

profile of v3, /device:TPU:0, one launch (start us, length us, event | category | flops | bytes accessed | tf_op | source)
XLA Modules:
  0.0 74.2 jit_solution(18443852919871238550)
XLA Ops:
  1.0 4.1 %collective-permute-start.9 = (bf16[1,64,1024]{2,1,0:T(8,128)(2,1)S(1)}, bf16[1,64,1024]{2,1,0:T(8,128)(2,1)S(1)}, u32[]{:S(2)}, u32[]{:S(2)}) collective-permute-start(bf16[1,64,1024]{2,1,0:T(8,128)(2,1)S(1)} %get-tuple-element.23.refs_4_), channel_id=1, source_target_pairs={{0,8},{4,12},{8,0},{12,4},{1,9},{5,13},{9,1},{13,5},{2,10},{6,14},... | collective-permute-start | bytes 393224 | tf_op jit(solution)/shard_map/ppermute | solution.py:368
  5.1 1.6 %collective-permute-start.8 = (bf16[1,64,1024]{2,1,0:T(8,128)(2,1)S(1)}, bf16[1,64,1024]{2,1,0:T(8,128)(2,1)S(1)}, u32[]{:S(2)}, u32[]{:S(2)}) collective-permute-start(bf16[1,64,1024]{2,1,0:T(8,128)(2,1)S(1)} %get-tuple-element.23.refs_4_), channel_id=1, source_target_pairs={{0,4},{4,0},{8,12},{12,8},{1,5},{5,1},{9,13},{13,9},{2,6},{6,2},{1... | collective-permute-start | bytes 393224 | tf_op jit(solution)/shard_map/ppermute | solution.py:369
  6.7 1.5 %collective-permute-start.3 = (bf16[1,64,1024]{2,1,0:T(8,128)(2,1)S(1)}, bf16[1,64,1024]{2,1,0:T(8,128)(2,1)S(1)}, u32[]{:S(2)}, u32[]{:S(2)}) collective-permute-start(bf16[1,64,1024]{2,1,0:T(8,128)(2,1)S(1)} %get-tuple-element.24), channel_id=1, source_target_pairs={{0,2},{2,0},{16,18},{18,16},{1,3},{3,1},{17,19},{19,17},{4,6},{6,4... | collective-permute-start | bytes 393224 | tf_op jit(solution)/shard_map/ppermute | solution.py:341
  12.2 1.6 %collective-permute-start.12 = (bf16[1,64,512]{2,1,0:T(8,128)(2,1)S(1)}, bf16[1,64,512]{2,1,0:T(8,128)(2,1)S(1)}, u32[]{:S(2)}, u32[]{:S(2)}) collective-permute-start(bf16[1,64,512]{2,1,0:T(8,128)(2,1)S(1)} %get-tuple-element.26), channel_id=1, source_target_pairs={{0,2},{2,0},{16,18},{18,16},{1,3},{3,1},{17,19},{19,17},{4,6},{6,4... | collective-permute-start | bytes 196616 | tf_op jit(solution)/shard_map/ppermute | solution.py:341
  15.0 4.1 %collective-permute-start.5 = (bf16[1,64,1024]{2,1,0:T(8,128)(2,1)S(1)}, bf16[1,64,1024]{2,1,0:T(8,128)(2,1)S(1)}, u32[]{:S(2)}, u32[]{:S(2)}) collective-permute-start(bf16[1,64,1024]{2,1,0:T(8,128)(2,1)S(1)} %collective-permute-done.3.refs_4_), channel_id=1, source_target_pairs={{0,8},{4,12},{8,0},{12,4},{1,9},{5,13},{9,1},{13,5},{2,10},{6,14},... | collective-permute-start | bytes 393224 | tf_op jit(solution)/shard_map/ppermute | solution.py:368
  19.2 1.5 %collective-permute-start.1 = (bf16[128,1152]{1,0:T(8,128)(2,1)S(1)}, bf16[128,1152]{1,0:T(8,128)(2,1)S(1)}, u32[]{:S(2)}, u32[]{:S(2)}) collective-permute-start(bf16[128,1152]{1,0:T(8,128)(2,1)S(1)} %get-tuple-element.16), channel_id=1, source_target_pairs={{0,16},{2,18},{16,0},{18,2},{1,17},{3,19},{17,1},{19,3},{4,20},{6,... | collective-permute-start | bytes 884744 | tf_op jit(solution)/shard_map/ppermute | solution.py:341
  20.9 1.5 %collective-permute-start.2 = (bf16[128,1152]{1,0:T(8,128)(2,1)S(1)}, bf16[128,1152]{1,0:T(8,128)(2,1)S(1)}, u32[]{:S(2)}, u32[]{:S(2)}) collective-permute-start(bf16[128,1152]{1,0:T(8,128)(2,1)S(1)} %get-tuple-element.17), channel_id=1, source_target_pairs={{0,18},{2,16},{16,2},{18,0},{1,19},{3,17},{17,3},{19,1},{4,22},{6,... | collective-permute-start | bytes 884744 | tf_op jit(solution)/shard_map/ppermute | solution.py:341
  23.1 1.4 %collective-permute-done.5.refs_6_ = bf16[1,64,1024]{2,1,0:T(8,128)(2,1)S(1)} collective-permute-done((bf16[1,64,1024]{2,1,0:T(8,128)(2,1)S(1)}, bf16[1,64,1024]{2,1,0:T(8,128)(2,1)S(1)}, u32[]{:S(2)}, u32[]{:S(2)}) %collective-permute-start.5) | collective-permute-done | bytes 131104 | tf_op jit(solution)/shard_map/ppermute | solution.py:368
  24.5 1.3 %collective-permute-start.7 = (bf16[1,64,1024]{2,1,0:T(8,128)(2,1)S(1)}, bf16[1,64,1024]{2,1,0:T(8,128)(2,1)S(1)}, u32[]{:S(2)}, u32[]{:S(2)}) collective-permute-start(bf16[1,64,1024]{2,1,0:T(8,128)(2,1)S(1)} %collective-permute-done.5.refs_6_), channel_id=1, source_target_pairs={{8,12},{4,0},{9,13},{5,1},{10,14},{6,2},{11,15},{7,3},{24,28},{20,... | collective-permute-start | bytes 393224 | tf_op jit(solution)/shard_map/ppermute | solution.py:371
  25.8 3.4 %collective-permute-start.4 = (bf16[1,64,1024]{2,1,0:T(8,128)(2,1)S(1)}, bf16[1,64,1024]{2,1,0:T(8,128)(2,1)S(1)}, u32[]{:S(2)}, u32[]{:S(2)}) collective-permute-start(bf16[1,64,1024]{2,1,0:T(8,128)(2,1)S(1)} %collective-permute-done.3.refs_4_), channel_id=1, source_target_pairs={{0,4},{4,0},{8,12},{12,8},{1,5},{5,1},{9,13},{13,9},{2,6},{6,2},{1... | collective-permute-start | bytes 393224 | tf_op jit(solution)/shard_map/ppermute | solution.py:369
  29.2 4.3 %collective-permute-done.1.refs_2_ = bf16[128,1152]{1,0:T(8,128)(2,1)S(1)} collective-permute-done((bf16[128,1152]{1,0:T(8,128)(2,1)S(1)}, bf16[128,1152]{1,0:T(8,128)(2,1)S(1)}, u32[]{:S(2)}, u32[]{:S(2)}) %collective-permute-start.1) | collective-permute-done | bytes 294944 | tf_op jit(solution)/shard_map/ppermute | solution.py:341
  34.6 1.4 %shard_map.110.refs_8_ = f32[256,128]{1,0:T(8,128)S(1)} custom-call(s32[4]{0:T(128)S(1)} %get-tuple-element.29.ids_ref, bf16[128,1152]{1,0:T(8,128)(2,1)S(1)} %get-tuple-element.14.refs_0_, bf16[128,1152]{1,0:T(8,128)(2,1)S(1)} %collective-permute-done.refs_1_, bf16[128,1152]{1,0:T(8,128)(2,1)S(1)} %collective-permute-done.1.refs_2_, ...), custom_call_target="tpu_custom_call" | custom-call | flops 268435456 | bytes 2359296 | tf_op jit(solution)/shard_map/pallas_call | solution.py:280
  36.1 1.4 %shard_map.111 = f32[256,128]{1,0:T(8,128)S(1)} custom-call(s32[4]{0:T(128)S(1)} %get-tuple-element.30.ids_ref, bf16[128,1152]{1,0:T(8,128)(2,1)S(1)} %get-tuple-element.14.refs_0_, bf16[128,1152]{1,0:T(8,128)(2,1)S(1)} %collective-permute-done.refs_1_, bf16[128,1152]{1,0:T(8,128)(2,1)S(1)} %collective-permute-done.1.refs_2_, ...), custom_call_target="tpu_custom_call" | custom-call | flops 268435456 | bytes 2359296 | tf_op jit(solution)/shard_map/pallas_call | solution.py:280
  38.4 3.5 %all-to-all-start = ((bf16[8,256,128]{2,1,0:T(8,128)(2,1)}), bf16[8,256,128]{2,1,0:T(8,128)(2,1)S(1)}, u32[]{:S(2)}, u32[]{:S(2)}) async-start(bf16[8,256,128]{2,1,0:T(8,128)(2,1)} %broadcast_in_dim.16), calls=%async_computation | async-start | bytes 1048576 | tf_op jit(solution)/shard_map/all_to_all | solution.py:403
  41.9 1.3 %collective-permute-start.16 = (bf16[2,64,512]{2,1,0:T(8,128)(2,1)S(1)}, bf16[2,64,512]{2,1,0:T(8,128)(2,1)S(1)}, u32[]{:S(2)}, u32[]{:S(2)}) collective-permute-start(bf16[2,64,512]{2,1,0:T(8,128)(2,1)S(1)} %collective-permute-done.14.refs_7_), channel_id=1, source_target_pairs={{8,12},{4,0},{9,13},{5,1},{10,14},{6,2},{11,15},{7,3},{24,28},{20,... | collective-permute-start | bytes 393224 | tf_op jit(solution)/shard_map/ppermute | solution.py:371
  44.7 4.4 %collective-permute-start.13 = (bf16[2,64,512]{2,1,0:T(8,128)(2,1)S(1)}, bf16[2,64,512]{2,1,0:T(8,128)(2,1)S(1)}, u32[]{:S(2)}, u32[]{:S(2)}) collective-permute-start(bf16[2,64,512]{2,1,0:T(8,128)(2,1)S(1)} %pad_maximum_fusion.refs_5_), channel_id=1, source_target_pairs={{0,4},{4,0},{8,12},{12,8},{1,5},{5,1},{9,13},{13,9},{2,6},{6,2},{1... | collective-permute-start | bytes 393224 | tf_op jit(solution)/shard_map/ppermute | solution.py:369
  49.1 2.7 %collective-permute-done.16 = bf16[2,64,512]{2,1,0:T(8,128)(2,1)S(1)} collective-permute-done((bf16[2,64,512]{2,1,0:T(8,128)(2,1)S(1)}, bf16[2,64,512]{2,1,0:T(8,128)(2,1)S(1)}, u32[]{:S(2)}, u32[]{:S(2)}) %collective-permute-start.16) | collective-permute-done | bytes 131104 | tf_op jit(solution)/shard_map/ppermute | solution.py:371
  51.9 2.5 %collective-permute-done.13.refs_6_ = bf16[2,64,512]{2,1,0:T(8,128)(2,1)S(1)} collective-permute-done((bf16[2,64,512]{2,1,0:T(8,128)(2,1)S(1)}, bf16[2,64,512]{2,1,0:T(8,128)(2,1)S(1)}, u32[]{:S(2)}, u32[]{:S(2)}) %collective-permute-start.13) | collective-permute-done | bytes 131104 | tf_op jit(solution)/shard_map/ppermute | solution.py:369
  56.8 1.8 %shard_map.112 = (bf16[128,512]{1,0:T(8,128)(2,1)S(1)}, bf16[128,512]{1,0:T(8,128)(2,1)}, bf16[128,512]{1,0:T(8,128)(2,1)}, bf16[128,512]{1,0:T(8,128)(2,1)}) custom-call(s32[8]{0:T(128)S(1)} %reshape.25.ids_ref, s32[1]{0:T(128)} %bitcast.me_ref, bf16[128,1152]{1,0:T(8,128)(2,1)S(1)} %get-tuple-element.14.refs_0_, ...), custom_call_target="tpu_custom_call" | custom-call | tf_op jit(solution)/shard_map/pallas_call | solution.py:306
  59.2 1.7 %collective-permute-start.17 = (bf16[128,512]{1,0:T(8,128)(2,1)}, bf16[128,512]{1,0:T(8,128)(2,1)S(1)}, u32[]{:S(2)}, u32[]{:S(2)}) collective-permute-start(bf16[128,512]{1,0:T(8,128)(2,1)} %get-tuple-element.20), channel_id=1, source_target_pairs={{0,2},{2,0},{16,18},{18,16},{1,3},{3,1},{17,19},{19,17},{4,6},{6,4... | collective-permute-start | bytes 393224 | tf_op jit(solution)/shard_map/ppermute | solution.py:341
  60.9 1.5 %collective-permute-start.18 = (bf16[128,512]{1,0:T(8,128)(2,1)}, bf16[128,512]{1,0:T(8,128)(2,1)S(1)}, u32[]{:S(2)}, u32[]{:S(2)}) collective-permute-start(bf16[128,512]{1,0:T(8,128)(2,1)} %get-tuple-element.21), channel_id=1, source_target_pairs={{0,16},{2,18},{16,0},{18,2},{1,17},{3,19},{17,1},{19,3},{4,20},{6,... | collective-permute-start | bytes 393224 | tf_op jit(solution)/shard_map/ppermute | solution.py:341
  62.8 2.4 %collective-permute-done.17.refs_1_ = bf16[128,512]{1,0:T(8,128)(2,1)S(1)} collective-permute-done((bf16[128,512]{1,0:T(8,128)(2,1)}, bf16[128,512]{1,0:T(8,128)(2,1)S(1)}, u32[]{:S(2)}, u32[]{:S(2)}) %collective-permute-start.17) | collective-permute-done | bytes 131104 | tf_op jit(solution)/shard_map/ppermute | solution.py:341
  65.1 3.7 %collective-permute-done.18.refs_2_ = bf16[128,512]{1,0:T(8,128)(2,1)S(1)} collective-permute-done((bf16[128,512]{1,0:T(8,128)(2,1)}, bf16[128,512]{1,0:T(8,128)(2,1)S(1)}, u32[]{:S(2)}, u32[]{:S(2)}) %collective-permute-start.18) | collective-permute-done | bytes 131104 | tf_op jit(solution)/shard_map/ppermute | solution.py:341
  71.8 2.3 %shard_map.113 = bf16[128,2048]{1,0:T(8,128)(2,1)} custom-call(s32[1]{0:T(128)} %bitcast.me_ref, s32[16,128]{1,0:T(8,128)S(1)} %copy.15.len_ref, bf16[128,2048]{1,0:T(8,128)(2,1)S(1)} %copy-done.3, bf16[128,256]{1,0:T(8,128)(2,1)S(1)} %copy-done.10, bf16[128,256]{1,0:T(8,128)(2,1)S(1)} %copy-done.11, bf16[128,16,256]{2,1,0:T(8,128)(2,1)S(1)} %copy-done.1, ...), custom_call_target="tpu_custom_call" | custom-call | flops 134217728 | bytes 3145728 | tf_op jit(solution)/shard_map/pallas_call | solution.py:257
  (73 shorter events, 17.1 us)
Async XLA Ops:
  1.0 11.1 %collective-permute-start.9 = (bf16[1,64,1024]{2,1,0:T(8,128)(2,1)S(1)}, bf16[1,64,1024]{2,1,0:T(8,128)(2,1)S(1)}, u32[]{:S(2)}, u32[]{:S(2)}) collective-permute-start(bf16[1,64,1024]{2,1,0:T(8,128)(2,1)S(1)} %get-tuple-element.23.refs_4_), channel_id=1, source_target_pairs={{0,8},{4,12},{8,0},{12,4},{1,9},{5,13},{9,1},{13,5},{2,10},{6,14},... | collective-permute-start | bytes 393224 | tf_op jit(solution)/shard_map/ppermute | solution.py:368
  5.1 7.0 %collective-permute-start.8 = (bf16[1,64,1024]{2,1,0:T(8,128)(2,1)S(1)}, bf16[1,64,1024]{2,1,0:T(8,128)(2,1)S(1)}, u32[]{:S(2)}, u32[]{:S(2)}) collective-permute-start(bf16[1,64,1024]{2,1,0:T(8,128)(2,1)S(1)} %get-tuple-element.23.refs_4_), channel_id=1, source_target_pairs={{0,4},{4,0},{8,12},{12,8},{1,5},{5,1},{9,13},{13,9},{2,6},{6,2},{1... | collective-permute-start | bytes 393224 | tf_op jit(solution)/shard_map/ppermute | solution.py:369
  6.7 8.4 %collective-permute-start.3 = (bf16[1,64,1024]{2,1,0:T(8,128)(2,1)S(1)}, bf16[1,64,1024]{2,1,0:T(8,128)(2,1)S(1)}, u32[]{:S(2)}, u32[]{:S(2)}) collective-permute-start(bf16[1,64,1024]{2,1,0:T(8,128)(2,1)S(1)} %get-tuple-element.24), channel_id=1, source_target_pairs={{0,2},{2,0},{16,18},{18,16},{1,3},{3,1},{17,19},{19,17},{4,6},{6,4... | collective-permute-start | bytes 393224 | tf_op jit(solution)/shard_map/ppermute | solution.py:341
  8.2 11.0 %collective-permute-start.10 = (bf16[1,64,1024]{2,1,0:T(8,128)(2,1)S(1)}, bf16[1,64,1024]{2,1,0:T(8,128)(2,1)S(1)}, u32[]{:S(2)}, u32[]{:S(2)}) collective-permute-start(bf16[1,64,1024]{2,1,0:T(8,128)(2,1)S(1)} %get-tuple-element.23.refs_4_), channel_id=1, source_target_pairs={{4,8},{8,4},{5,9},{9,5},{6,10},{10,6},{7,11},{11,7},{20,24},{24,20... | collective-permute-start | bytes 393224 | tf_op jit(solution)/shard_map/ppermute | solution.py:370
  11.5 14.3 %collective-permute-start = (bf16[128,1152]{1,0:T(8,128)(2,1)S(1)}, bf16[128,1152]{1,0:T(8,128)(2,1)S(1)}, u32[]{:S(2)}, u32[]{:S(2)}) collective-permute-start(bf16[128,1152]{1,0:T(8,128)(2,1)S(1)} %get-tuple-element.15), channel_id=1, source_target_pairs={{0,2},{2,0},{16,18},{18,16},{1,3},{3,1},{17,19},{19,17},{4,6},{6,4... | collective-permute-start | bytes 884744 | tf_op jit(solution)/shard_map/ppermute | solution.py:341
  12.2 8.7 %collective-permute-start.12 = (bf16[1,64,512]{2,1,0:T(8,128)(2,1)S(1)}, bf16[1,64,512]{2,1,0:T(8,128)(2,1)S(1)}, u32[]{:S(2)}, u32[]{:S(2)}) collective-permute-start(bf16[1,64,512]{2,1,0:T(8,128)(2,1)S(1)} %get-tuple-element.26), channel_id=1, source_target_pairs={{0,2},{2,0},{16,18},{18,16},{1,3},{3,1},{17,19},{19,17},{4,6},{6,4... | collective-permute-start | bytes 196616 | tf_op jit(solution)/shard_map/ppermute | solution.py:341
  13.7 8.7 %collective-permute-start.11 = (bf16[1,64,1024]{2,1,0:T(8,128)(2,1)S(1)}, bf16[1,64,1024]{2,1,0:T(8,128)(2,1)S(1)}, u32[]{:S(2)}, u32[]{:S(2)}) collective-permute-start(bf16[1,64,1024]{2,1,0:T(8,128)(2,1)S(1)} %collective-permute-done.9.refs_6_), channel_id=1, source_target_pairs={{8,12},{4,0},{9,13},{5,1},{10,14},{6,2},{11,15},{7,3},{24,28},{20,... | collective-permute-start | bytes 393224 | tf_op jit(solution)/shard_map/ppermute | solution.py:371
  15.0 9.5 %collective-permute-start.5 = (bf16[1,64,1024]{2,1,0:T(8,128)(2,1)S(1)}, bf16[1,64,1024]{2,1,0:T(8,128)(2,1)S(1)}, u32[]{:S(2)}, u32[]{:S(2)}) collective-permute-start(bf16[1,64,1024]{2,1,0:T(8,128)(2,1)S(1)} %collective-permute-done.3.refs_4_), channel_id=1, source_target_pairs={{0,8},{4,12},{8,0},{12,4},{1,9},{5,13},{9,1},{13,5},{2,10},{6,14},... | collective-permute-start | bytes 393224 | tf_op jit(solution)/shard_map/ppermute | solution.py:368
  19.2 14.3 %collective-permute-start.1 = (bf16[128,1152]{1,0:T(8,128)(2,1)S(1)}, bf16[128,1152]{1,0:T(8,128)(2,1)S(1)}, u32[]{:S(2)}, u32[]{:S(2)}) collective-permute-start(bf16[128,1152]{1,0:T(8,128)(2,1)S(1)} %get-tuple-element.16), channel_id=1, source_target_pairs={{0,16},{2,18},{16,0},{18,2},{1,17},{3,19},{17,1},{19,3},{4,20},{6,... | collective-permute-start | bytes 884744 | tf_op jit(solution)/shard_map/ppermute | solution.py:341
  20.9 13.0 %collective-permute-start.2 = (bf16[128,1152]{1,0:T(8,128)(2,1)S(1)}, bf16[128,1152]{1,0:T(8,128)(2,1)S(1)}, u32[]{:S(2)}, u32[]{:S(2)}) collective-permute-start(bf16[128,1152]{1,0:T(8,128)(2,1)S(1)} %get-tuple-element.17), channel_id=1, source_target_pairs={{0,18},{2,16},{16,2},{18,0},{1,19},{3,17},{17,3},{19,1},{4,22},{6,... | collective-permute-start | bytes 884744 | tf_op jit(solution)/shard_map/ppermute | solution.py:341
  22.4 13.6 %collective-permute-start.6 = (bf16[1,64,1024]{2,1,0:T(8,128)(2,1)S(1)}, bf16[1,64,1024]{2,1,0:T(8,128)(2,1)S(1)}, u32[]{:S(2)}, u32[]{:S(2)}) collective-permute-start(bf16[1,64,1024]{2,1,0:T(8,128)(2,1)S(1)} %collective-permute-done.3.refs_4_), channel_id=1, source_target_pairs={{4,8},{8,4},{5,9},{9,5},{6,10},{10,6},{7,11},{11,7},{20,24},{24,20... | collective-permute-start | bytes 393224 | tf_op jit(solution)/shard_map/ppermute | solution.py:370
  24.5 11.5 %collective-permute-start.7 = (bf16[1,64,1024]{2,1,0:T(8,128)(2,1)S(1)}, bf16[1,64,1024]{2,1,0:T(8,128)(2,1)S(1)}, u32[]{:S(2)}, u32[]{:S(2)}) collective-permute-start(bf16[1,64,1024]{2,1,0:T(8,128)(2,1)S(1)} %collective-permute-done.5.refs_6_), channel_id=1, source_target_pairs={{8,12},{4,0},{9,13},{5,1},{10,14},{6,2},{11,15},{7,3},{24,28},{20,... | collective-permute-start | bytes 393224 | tf_op jit(solution)/shard_map/ppermute | solution.py:371
  25.8 10.2 %collective-permute-start.4 = (bf16[1,64,1024]{2,1,0:T(8,128)(2,1)S(1)}, bf16[1,64,1024]{2,1,0:T(8,128)(2,1)S(1)}, u32[]{:S(2)}, u32[]{:S(2)}) collective-permute-start(bf16[1,64,1024]{2,1,0:T(8,128)(2,1)S(1)} %collective-permute-done.3.refs_4_), channel_id=1, source_target_pairs={{0,4},{4,0},{8,12},{12,8},{1,5},{5,1},{9,13},{13,9},{2,6},{6,2},{1... | collective-permute-start | bytes 393224 | tf_op jit(solution)/shard_map/ppermute | solution.py:369
  33.5 8.4 %collective-permute-start.14 = (bf16[2,64,512]{2,1,0:T(8,128)(2,1)S(1)}, bf16[2,64,512]{2,1,0:T(8,128)(2,1)S(1)}, u32[]{:S(2)}, u32[]{:S(2)}) collective-permute-start(bf16[2,64,512]{2,1,0:T(8,128)(2,1)S(1)} %pad_maximum_fusion.refs_5_), channel_id=1, source_target_pairs={{0,8},{4,12},{8,0},{12,4},{1,9},{5,13},{9,1},{13,5},{2,10},{6,14},... | collective-permute-start | bytes 393224 | tf_op jit(solution)/shard_map/ppermute | solution.py:368
  33.9 15.2 %collective-permute-start.15 = (bf16[2,64,512]{2,1,0:T(8,128)(2,1)S(1)}, bf16[2,64,512]{2,1,0:T(8,128)(2,1)S(1)}, u32[]{:S(2)}, u32[]{:S(2)}) collective-permute-start(bf16[2,64,512]{2,1,0:T(8,128)(2,1)S(1)} %pad_maximum_fusion.refs_5_), channel_id=1, source_target_pairs={{4,8},{8,4},{5,9},{9,5},{6,10},{10,6},{7,11},{11,7},{20,24},{24,20... | collective-permute-start | bytes 393224 | tf_op jit(solution)/shard_map/ppermute | solution.py:370
  38.4 16.6 %all-to-all-start = ((bf16[8,256,128]{2,1,0:T(8,128)(2,1)}), bf16[8,256,128]{2,1,0:T(8,128)(2,1)S(1)}, u32[]{:S(2)}, u32[]{:S(2)}) async-start(bf16[8,256,128]{2,1,0:T(8,128)(2,1)} %broadcast_in_dim.16), calls=%async_computation | async-start | bytes 1048576 | tf_op jit(solution)/shard_map/all_to_all | solution.py:403
  41.9 10.0 %collective-permute-start.16 = (bf16[2,64,512]{2,1,0:T(8,128)(2,1)S(1)}, bf16[2,64,512]{2,1,0:T(8,128)(2,1)S(1)}, u32[]{:S(2)}, u32[]{:S(2)}) collective-permute-start(bf16[2,64,512]{2,1,0:T(8,128)(2,1)S(1)} %collective-permute-done.14.refs_7_), channel_id=1, source_target_pairs={{8,12},{4,0},{9,13},{5,1},{10,14},{6,2},{11,15},{7,3},{24,28},{20,... | collective-permute-start | bytes 393224 | tf_op jit(solution)/shard_map/ppermute | solution.py:371
  44.7 9.6 %collective-permute-start.13 = (bf16[2,64,512]{2,1,0:T(8,128)(2,1)S(1)}, bf16[2,64,512]{2,1,0:T(8,128)(2,1)S(1)}, u32[]{:S(2)}, u32[]{:S(2)}) collective-permute-start(bf16[2,64,512]{2,1,0:T(8,128)(2,1)S(1)} %pad_maximum_fusion.refs_5_), channel_id=1, source_target_pairs={{0,4},{4,0},{8,12},{12,8},{1,5},{5,1},{9,13},{13,9},{2,6},{6,2},{1... | collective-permute-start | bytes 393224 | tf_op jit(solution)/shard_map/ppermute | solution.py:369
  51.9 17.0 %copy-start.1 = (bf16[128,16,256]{2,1,0:T(8,128)(2,1)S(1)}, bf16[128,16,256]{2,1,0:T(8,128)(2,1)}, u32[]{:S(2)}) copy-start(bf16[128,16,256]{2,1,0:T(8,128)(2,1)} %ck_ref.1) | copy-start | bytes 3145732
  51.9 17.0 %copy-start.3 = (bf16[128,2048]{1,0:T(8,128)(2,1)S(1)}, bf16[128,2048]{1,0:T(8,128)(2,1)}, u32[]{:S(2)}) copy-start(bf16[128,2048]{1,0:T(8,128)(2,1)} %base_ref.1) | copy-start | bytes 1572868
  59.2 9.7 %copy-start.7 = (bf16[128,512]{1,0:T(8,128)(2,1)S(1)}, bf16[128,512]{1,0:T(8,128)(2,1)}, u32[]{:S(2)}) copy-start(bf16[128,512]{1,0:T(8,128)(2,1)} %copy-done.6) | copy-start | bytes 393220
  59.2 5.9 %collective-permute-start.17 = (bf16[128,512]{1,0:T(8,128)(2,1)}, bf16[128,512]{1,0:T(8,128)(2,1)S(1)}, u32[]{:S(2)}, u32[]{:S(2)}) collective-permute-start(bf16[128,512]{1,0:T(8,128)(2,1)} %get-tuple-element.20), channel_id=1, source_target_pairs={{0,2},{2,0},{16,18},{18,16},{1,3},{3,1},{17,19},{19,17},{4,6},{6,4... | collective-permute-start | bytes 393224 | tf_op jit(solution)/shard_map/ppermute | solution.py:341
  60.9 8.0 %collective-permute-start.18 = (bf16[128,512]{1,0:T(8,128)(2,1)}, bf16[128,512]{1,0:T(8,128)(2,1)S(1)}, u32[]{:S(2)}, u32[]{:S(2)}) collective-permute-start(bf16[128,512]{1,0:T(8,128)(2,1)} %get-tuple-element.21), channel_id=1, source_target_pairs={{0,16},{2,18},{16,0},{18,2},{1,17},{3,19},{17,1},{19,3},{4,20},{6,... | collective-permute-start | bytes 393224 | tf_op jit(solution)/shard_map/ppermute | solution.py:341
  62.4 6.5 %collective-permute-start.19 = (bf16[128,512]{1,0:T(8,128)(2,1)}, bf16[128,512]{1,0:T(8,128)(2,1)S(1)}, u32[]{:S(2)}, u32[]{:S(2)}) collective-permute-start(bf16[128,512]{1,0:T(8,128)(2,1)} %get-tuple-element.22), channel_id=1, source_target_pairs={{0,18},{2,16},{16,2},{18,0},{1,19},{3,17},{17,3},{19,1},{4,22},{6,... | collective-permute-start | bytes 393224 | tf_op jit(solution)/shard_map/ppermute | solution.py:341
  (13 other events, 18.4 us)

commit v4 on v3

--- a/solution.py
+++ b/solution.py
@@ -17,26 +17,44 @@
 DEAD = -1e30
 VMEM = pl.BlockSpec(memory_space=pltpu.VMEM)
 SMEM = pl.BlockSpec(memory_space=pltpu.SMEM)
-PARAMS = pltpu.CompilerParams(vmem_limit_bytes=32 * 1024 * 1024)
+HBM = pl.BlockSpec(memory_space=pltpu.HBM)
+PARAMS = pltpu.CompilerParams(vmem_limit_bytes=12 * 1024 * 1024)
 NT = (((1,), (1,)), ((), ()))
 TN = (((0,), (0,)), ((), ()))
 
 
-def pack_kernel(parts, me_ref, map_ref, ids_ref, hidden_ref, *out_refs):
+def pack_kernel(parts, me_ref, map_ref, ids_ref, hidden_ref, shrink_ref, expand_ref, *refs):
+    rows_ref, own_ref, next_ref, expand_own_ref, sems = refs
     requests, wide = hidden_ref.shape
-    features = wide // parts
+    features, outputs = wide // parts, expand_ref.shape[2] // parts
     me = me_ref[0]
+
+    def columns(at, width):
+        return pl.ds(pl.multiple_of(at * width, width), width)
+
+    moves = [
+        (shrink_ref.at[:, :, columns(me, features)], own_ref),
+        (shrink_ref.at[:, :, columns(me ^ 1, features)], next_ref.at[:, :, :features]),
+        (expand_ref.at[:, :, columns(me ^ 1, outputs)], next_ref.at[:, :, features:]),
+        (expand_ref.at[:, :, columns(me, outputs)], expand_own_ref),
+    ]
+    for s in range(parts):
+        at = slice(s * features, (s + 1) * features)
+        moves.append((hidden_ref.at[:, at], rows_ref.at[s, :, :features]))
+    copies = [pltpu.make_async_copy(src, dst, sems.at[k]) for k, (src, dst) in enumerate(moves)]
+    for copy in copies:
+        copy.start()
     ids = ids_ref[...]
 
     def look(k, found):
         return jnp.where(ids == k, map_ref[k], found)
 
     owners = lax.fori_loop(0, map_ref.shape[0], look, jnp.zeros_like(ids))
-    owners = jnp.broadcast_to(owners.astype(jnp.float32), (requests, LANES)).astype(jnp.bfloat16)
+    owners = jnp.broadcast_to(owners.astype(jnp.float32), (LANES, requests)).T
     for s in range(parts):
-        at = pl.ds(pl.multiple_of((me ^ s) * features, features), features)
-        out_refs[s][:, :features] = hidden_ref[:, at]
-        out_refs[s][:, features:] = owners
+        rows_ref[s, :, features:] = owners.astype(jnp.bfloat16)
+    for copy in copies:
+        copy.wait()
 
 
 def owner_mask(owners, ids, rank):
@@ -58,12 +76,8 @@
 
 
 def shrink_kernel(parts, blocks, gridded, ids_ref, *refs):
-    row_refs, weight_refs, base_ref, out_ref = (
-        refs[:parts],
-        refs[parts : parts + blocks],
-        refs[parts + blocks],
-        refs[-1],
-    )
+    rows_ref, weight_refs, base_ref, out_ref = refs[0], refs[1 : 1 + blocks], refs[1 + blocks], refs[-1]
+    row_refs = [rows_ref.at[s] for s in range(parts)]
     rank, features = weight_refs[0].shape[1:]
     requests = row_refs[0].shape[0]
     count = sum(r.shape[0] for r in weight_refs)
@@ -95,17 +109,16 @@
         out_ref[rows, :] += jnp.where(low, folded[s], folded[s + half])
 
 
-def expand_kernel(parts, blocks, cores, gridded, ids_ref, me_ref, *refs):
-    row_refs, low_ref, weight_refs, out_refs, total_ref = (
+def expand_kernel(parts, blocks, gridded, ids_ref, me_ref, rows_ref, *refs):
+    low_refs, weight_refs, out_refs, (held_ref, total_ref) = (
         refs[:parts],
-        refs[parts],
-        refs[parts + 1 : parts + 1 + blocks],
-        refs[-parts - 1 : -1],
-        refs[-1],
+        refs[parts : parts + blocks],
+        refs[parts + blocks : 2 * parts + blocks],
+        refs[-2:],
     )
+    me = me_ref[0]
     rank, outputs = weight_refs[0].shape[1:]
-    features = row_refs[0].shape[1] - LANES
-    requests = row_refs[0].shape[0]
+    requests, features = rows_ref.shape[1], rows_ref.shape[2] - LANES
     count = sum(r.shape[0] for r in weight_refs)
     step = pl.program_id(0) if gridded else 0
     last = pl.num_programs(0) - 1 if gridded else 0
@@ -113,41 +126,35 @@
     weight = stacked(weight_refs)
     half = parts // 2
     low = lax.broadcasted_iota(jnp.int32, (requests, LANES), 1) < rank
-    me = me_ref[0]
-    held = [[0.0] * half for _ in range(2)]
-    for t in range(parts):
-        for core in range(cores):
-            sums = low_ref[(me ^ t) * cores + core].astype(jnp.float32)
-            for s in range(half):
-                at = (s ^ t) % half
-                piece = sums[at * requests : (at + 1) * requests]
-                held[t // half][s] = held[t // half][s] + piece
+    low_sum = low_refs[0][...].astype(jnp.float32)
+    for ref in low_refs[1:]:
+        low_sum = low_sum + ref[...].astype(jnp.float32)
     for s in range(half):
-        straight = held[0][s] + pltpu.roll(held[1][s], rank, 1)
+        straight = low_sum[s * requests : (s + 1) * requests]
         turned = pltpu.roll(straight, rank, 1)
-        for part in (s, s + half):
-            first = straight if part < half else turned
-            other = turned if part < half else straight
-            both = jnp.where(low, first, other)
-            wide = jnp.concatenate([both] * (count * rank // LANES), axis=1)
-            mask = owner_mask(row_owners(row_refs[part], features), ids, rank)
-            wide = jnp.where(mask, wide, 0.0).astype(jnp.bfloat16)
-            product = jnp.dot(wide, weight, preferred_element_type=jnp.float32)
-            if not gridded:
-                out_refs[part][...] = product.astype(jnp.bfloat16)
-            else:
-
-                @pl.when(step == 0)
-                def _():
-                    total_ref[part] = product
-
-                @pl.when(step > 0)
-                def _():
-                    total_ref[part] += product
-
-                @pl.when(step == last)
-                def _():
-                    out_refs[part][...] = total_ref[part].astype(jnp.bfloat16)
+        held_ref[s] = jnp.where(low, straight, turned)
+        held_ref[s + half] = jnp.where(low, turned, straight)
+    for s in range(parts):
+        both = held_ref[me ^ s]
+        wide = jnp.concatenate([both] * (count * rank // LANES), axis=1)
+        mask = owner_mask(row_owners(rows_ref.at[me ^ s], features), ids, rank)
+        wide = jnp.where(mask, wide, 0.0).astype(jnp.bfloat16)
+        product = jnp.dot(wide, weight, preferred_element_type=jnp.float32)
+        if not gridded:
+            out_refs[s][...] = product.astype(jnp.bfloat16)
+        else:
+
+            @pl.when(step == 0)
+            def _():
+                total_ref[s] = product
+
+            @pl.when(step > 0)
+            def _():
+                total_ref[s] += product
+
+            @pl.when(step == last)
+            def _():
+                out_refs[s][...] = total_ref[s].astype(jnp.bfloat16)
 
 
 def attend_kernel(
@@ -269,14 +276,14 @@
 
 
 def shrink_rows(ids, rows, weights, base, chunk):
-    parts = len(rows)
+    parts = rows.shape[0]
     gridded = chunk is not None
     rank, features = weights[0].shape[1:]
-    specs = [SMEM] + [VMEM] * (parts + len(weights) + 1)
+    specs = [SMEM] + [VMEM] * (len(weights) + 2)
     grid = ()
     if gridded:
         grid = (weights[0].shape[0] // chunk,)
-        specs[1 + parts] = pl.BlockSpec((chunk, rank, features), lambda i: (i, 0, 0))
+        specs[2] = pl.BlockSpec((chunk, rank, features), lambda i: (i, 0, 0))
     return pl.pallas_call(
         functools.partial(shrink_kernel, parts, len(weights), gridded),
         out_shape=jax.ShapeDtypeStruct(base.shape, jnp.float32),
@@ -285,33 +292,35 @@
         out_specs=VMEM,
         compiler_params=PARAMS,
         cost_estimate=pl.CostEstimate(
-            flops=2 * parts * rows[0].shape[0] * features * rank * sum(w.shape[0] for w in weights),
-            bytes_accessed=4 * parts * rows[0].size,
+            flops=2 * parts * rows.shape[1] * features * rank * sum(w.shape[0] for w in weights),
+            bytes_accessed=4 * rows.size,
             transcendentals=0,
         ),
-    )(ids, *rows, *weights, base)
-
-
-def expand_rows(ids, me, rows, low, weights, chunk, cores):
-    parts = len(rows)
+    )(ids, rows, *weights, base)
+
+
+def expand_rows(ids, me, rows, lows, weights, chunk):
+    parts, requests, _ = rows.shape
     gridded = chunk is not None
     rank, outputs = weights[0].shape[1:]
-    requests = rows[0].shape[0]
-    specs = [SMEM, SMEM] + [VMEM] * (parts + 1 + len(weights))
+    specs = [SMEM, SMEM] + [VMEM] * (1 + parts + len(weights))
     grid = ()
     if gridded:
         grid = (weights[0].shape[0] // chunk,)
         specs[3 + parts] = pl.BlockSpec((chunk, rank, outputs), lambda i: (i, 0, 0))
     held = (parts, requests, outputs) if gridded else (1, 8, LANES)
     return pl.pallas_call(
-        functools.partial(expand_kernel, parts, len(weights), cores, gridded),
+        functools.partial(expand_kernel, parts, len(weights), gridded),
         out_shape=[jax.ShapeDtypeStruct((requests, outputs), jnp.bfloat16)] * parts,
         grid=grid,
         in_specs=specs,
         out_specs=[VMEM] * parts,
-        scratch_shapes=[pltpu.VMEM(held, jnp.float32)],
+        scratch_shapes=[
+            pltpu.VMEM((parts, requests, LANES), jnp.float32),
+            pltpu.VMEM(held, jnp.float32),
+        ],
         compiler_params=PARAMS,
-    )(ids, me, *rows, low, *weights)
+    )(ids, me, rows, *lows, *weights)
 
 
 def per_device(
@@ -343,65 +352,58 @@
     def tied(a, *others):
         return lax.optimization_barrier((a, *others))[0]
 
-    def cut(a, width, at):
-        return lax.dynamic_slice_in_dim(a, at * width, width, 2)
-
     shrink = shrink_factors.swapaxes(1, 2)
-    shrink_own = cut(shrink, features, me)
-    shrink_next = swap(cut(shrink, features, me ^ 1), 1)
-    rows = pl.pallas_call(
+    rows, shrink_own, both_next, expand_own = pl.pallas_call(
         functools.partial(pack_kernel, square),
-        out_shape=[jax.ShapeDtypeStruct((requests, features + LANES), jnp.bfloat16)] * square,
-        in_specs=[SMEM, SMEM, VMEM, VMEM],
-        out_specs=[VMEM] * square,
-        compiler_params=PARAMS,
-    )(me[None], owner_map, adapter_ids, hidden)
-    rows = [rows[0]] + [swap(rows[s], s) for s in range(1, square)]
+        out_shape=[jax.ShapeDtypeStruct((square, requests, features + LANES), jnp.bfloat16)]
+        + [jax.ShapeDtypeStruct((1, rank, w), jnp.bfloat16) for w in (features, features + outputs, outputs)],
+        in_specs=[SMEM, SMEM, VMEM, HBM, HBM, HBM],
+        out_specs=[VMEM] * 4,
+        scratch_shapes=[pltpu.SemaphoreType.DMA((square + 4,))],
+        compiler_params=pltpu.CompilerParams(vmem_limit_bytes=48 * 1024 * 1024),
+    )(me[None], owner_map, adapter_ids.T, hidden, shrink, expand_factors)
+    both_next = swap(both_next, 1)
+    rows = lax.all_to_all(rows, ("rep", "side"), split_axis=0, concat_axis=0, tiled=True)
+    shrink_next, expand_next = both_next[:, :, :features], both_next[:, :, features:]
 
     empty = jnp.zeros((square // 2 * requests, LANES), jnp.float32)
     order = jnp.arange(levels, dtype=jnp.int32)
+    both_sides = jnp.stack([side, side ^ 1])[None, :]
+
+    def gather_pairs(own, other):
+        both = jnp.concatenate([own, other], axis=0)
+        return lax.all_gather(both, "level", axis=0, tiled=True)
+
     if levels == 4:
-        near_pairs = [(i, i ^ 1) for i in range(levels)]
-        far_pairs = [(i, i ^ 2) for i in range(levels)]
 
         def gather(a):
-            far = lax.ppermute(a, "level", far_pairs)
-            near = lax.ppermute(a, "level", near_pairs)
-            inner = lax.ppermute(a, "level", [(1, 2), (2, 1)])
-            outer = lax.ppermute(far, "level", [(2, 3), (1, 0)])
-            return [a, near, far, jnp.where((level == 1) | (level == 2), inner, outer)]
-
-        own_ids = (level ^ order) * sides + side
-        next_ids = (level ^ order) * sides + (side ^ 1)
+            return [a] + [
+                lax.ppermute(a, "level", [(i, i ^ k) for i in range(levels)])
+                for k in range(1, levels)
+            ]
+
         own_blocks = gather(shrink_own)
         next_blocks = gather(shrink_next)
-        partial = shrink_rows(own_ids, rows, own_blocks, empty, None)
-        partial = shrink_rows(next_ids, rows, next_blocks, partial, None)
-        expand = tied(expand_factors, own_blocks[1], own_blocks[2])
-        expand_own = cut(expand, outputs, me)
-        expand_next = swap(cut(expand, outputs, me ^ 1), 1)
-        expand = gather(jnp.concatenate([expand_own, expand_next], axis=0))
-        expand_ids = jnp.stack([own_ids, next_ids], axis=1).reshape(-1)
+        partial = shrink_rows((level ^ order) * sides + side, rows, own_blocks, empty, None)
+        partial = shrink_rows((level ^ order) * sides + (side ^ 1), rows, next_blocks, partial, None)
+        pair = jnp.concatenate([expand_own, expand_next], axis=0)
+        pair = tied(pair, own_blocks[1], own_blocks[2])
+        expand = gather(pair)
+        level_ids = (level ^ order)[:, None] * sides
         chunk = None
     else:
-        expand_own = cut(expand_factors, outputs, me)
-        expand_next = swap(cut(expand_factors, outputs, me ^ 1), 1)
-        pair = jnp.stack([side, side ^ 1])
-        expand_ids = (order[:, None] * sides + pair[None, :]).reshape(-1)
         chunk = 4
-
-        def gather(own, other):
-            both = jnp.concatenate([own, other], axis=0)
-            return lax.all_gather(both, "level", axis=0, tiled=True)
-
-        expand = [gather(expand_own, expand_next)]
-        weights = [gather(shrink_own, shrink_next)]
-        partial = shrink_rows(expand_ids, rows, weights, empty, chunk)
-
+        level_ids = order[:, None] * sides
+        weights = [gather_pairs(shrink_own, shrink_next)]
+        partial = shrink_rows((level_ids + both_sides).reshape(-1), rows, weights, empty, chunk)
+        expand = [gather_pairs(expand_own, expand_next)]
+
+    for c in range(1, tp):
+        partial = partial + lax.ppermute(partial, "tp", [(t, t ^ c) for t in range(tp)])
     partial = partial.astype(jnp.bfloat16)
-    partial = jnp.broadcast_to(partial[None], (square * tp,) + partial.shape)
-    sums = lax.all_to_all(partial, ("rep", "side", "tp"), split_axis=0, concat_axis=0, tiled=True)
-    deltas = expand_rows(expand_ids, me[None], rows, sums, expand, chunk, tp)
+    lows = [partial] + [swap(partial, s) for s in range(1, square)]
+    expand_ids = (level_ids + both_sides).reshape(-1)
+    deltas = expand_rows(expand_ids, me[None], rows, lows, expand, chunk)
     deltas = [deltas[0]] + [swap(deltas[s], s) for s in range(1, square)]
     return attend(
         me[None],

time: 74.7 us -> 78.9 us (1.056)
  waiting for transfers between devices: 17.2 us -> 31.3 us
  starting transfers between devices: 37.4 us -> 27.4 us
  Pallas kernels: 7.65 us -> 9.42 us
  local copies, waits for them, and re-layouts: 11.4 us -> 9.84 us
    ppermute x12 -> x10, starting transfers between devices: 23.8 us -> 13.4 us  [the longest x9 13.3 us: gather(): lax.ppermute(a, 'level', [(i, i ^ k) for i in range(levels)])]
    ppermute x12 -> x10, waiting for transfers between devices: 6.6 us -> 13.8 us  [the longest x9 13.8 us: gather(): lax.ppermute(a, 'level', [(i, i ^ k) for i in range(levels)])]
    ppermute x8 -> x7, waiting for transfers between devices: 10.6 us -> 17.4 us  [swap(): return lax.ppermute(a, ('rep', 'side'), pairs)]
    all_to_all x1, starting transfers between devices: 3.49 us -> 5.18 us  [per_device(): lax.all_to_all(rows, ('rep', 'side'), split_axis=0, concat_axis=0, tiled=...]
    ppermute x8 -> x7, starting transfers between devices: 10.1 us -> 8.86 us  [swap(): return lax.ppermute(a, ('rep', 'side'), pairs)]
    pallas_call x1, Pallas kernels: 0.7 us -> 1.94 us  [per_device(): pl.pallas_call(functools.partial(pack_kernel, square), out_shape=[jax.Sha...]
    dynamic_slice x2 -> x0, local copies, waits for them, and re-layouts: 1 us -> none  [cut(): return lax.dynamic_slice_in_dim(a, at * width, width, 2)]
    broadcast_in_dim x1 -> x0, local copies, waits for them, and re-layouts: 0.86 us -> none  [per_device(): partial = jnp.broadcast_to(partial[None], (square * tp,) + partial.shape)]
  transfers between devices with their start and end apart: 21 -> 18, of which waited for: 7 -> 8; matrix products, arithmetic and copies ran while one was open for 2% -> 1% of each run, Pallas kernels for 5% -> 2%
where the time goes in v4:
time: 78.9 us; the launch traced here: 78.3 us
  waiting for transfers between devices  31.3 us (40%)
  starting transfers between devices  27.4 us (35%)
  local copies, waits for them, and re-layouts  9.84 us (12%)
  Pallas kernels  9.42 us (12%)
    ppermute x7, waiting for transfers between devices, swap(): return lax.ppermute(a, ('rep', 'side'), pairs)  17.4 us
    ppermute x9, waiting for transfers between devices, gather(): lax.ppermute(a, 'level', [(i, i ^ k) for i in range(levels)])  13.8 us
    ppermute x9, starting transfers between devices, gather(): lax.ppermute(a, 'level', [(i, i ^ k) for i in range(levels)])  13.3 us
    unnamed x30, local copies, waits for them, and re-layouts  9.53 us
    ppermute x7, starting transfers between devices, swap(): return lax.ppermute(a, ('rep', 'side'), pairs)  8.86 us
    all_to_all x1, starting transfers between devices, per_device(): lax.all_to_all(rows, ('rep', 'side'), split_axis=0, concat_axis=0, tiled=...  5.18 us
    pallas_call x2, Pallas kernels, shrink_rows(): pl.pallas_call(functools.partial(shrink_kernel, parts, len(weights), grid...  2.84 us
    pallas_call x1, Pallas kernels, attend(): pl.pallas_call(functools.partial(attend_kernel, len(deltas)), out_shape=j...  2.38 us
  transfers between devices with their start and end apart: 18, of which 8 were waited for; matrix products, arithmetic and copies ran while one was open for 1% of the time, Pallas kernels for 2%

profile of v4, /device:TPU:0, one launch (start us, length us, event | category | flops | bytes accessed | tf_op | source)
XLA Modules:
  0.0 78.3 jit_solution(4730974071440466650)
XLA Ops:
  0.0 1.2 %copy-done = bf16[128,4096]{1,0:T(8,128)(2,1)S(1)} copy-done((bf16[128,4096]{1,0:T(8,128)(2,1)S(1)}, bf16[128,4096]{1,0:T(8,128)(2,1)}, u32[]{:S(2)}) %copy-start) | copy-done | bytes 1048600
  4.5 1.9 %shard_map.109 = (bf16[4,128,1152]{2,1,0:T(8,128)(2,1)}, bf16[1,64,1024]{2,1,0:T(8,128)(2,1)S(1)}, bf16[1,64,1536]{2,1,0:T(8,128)(2,1)S(1)}, bf16[1,64,512]{2,1,0:T(8,128)(2,1)S(1)}) custom-call(s32[1]{0:T(128)} %bitcast.me_ref, s32[8]{0:T(128)S(1)} %copy-done.12, s32[1,128]{1,0:T(1,128)S(1)} %bitcast.8, bf16[128,4096]{1,0:T(8,128)(2,1)S(1)} %copy-done, ...), custom_call_target="tpu_custom_call" | custom-call | tf_op jit(solution)/shard_map/pallas_call | solution.py:356
  6.5 5.2 %all-to-all-start = ((bf16[4,128,1152]{2,1,0:T(8,128)(2,1)}), bf16[4,128,1152]{2,1,0:T(8,128)(2,1)S(1)}, u32[]{:S(2)}, u32[]{:S(2)}) async-start(bf16[4,128,1152]{2,1,0:T(8,128)(2,1)} %get-tuple-element.14), calls=%async_computation | async-start | bytes 2359296 | tf_op jit(solution)/shard_map/all_to_all | solution.py:366
  11.7 2.0 %collective-permute-start = (bf16[1,64,1536]{2,1,0:T(8,128)(2,1)S(1)}, bf16[1,64,1536]{2,1,0:T(8,128)(2,1)S(1)}, u32[]{:S(2)}, u32[]{:S(2)}) collective-permute-start(bf16[1,64,1536]{2,1,0:T(8,128)(2,1)S(1)} %get-tuple-element.15), channel_id=1, source_target_pairs={{0,2},{2,0},{16,18},{18,16},{1,3},{3,1},{17,19},{19,17},{4,6},{6,4... | collective-permute-start | bytes 589832 | tf_op jit(solution)/shard_map/ppermute | solution.py:350
  13.7 1.6 %collective-permute-start.4 = (bf16[1,64,1024]{2,1,0:T(8,128)(2,1)S(1)}, bf16[1,64,1024]{2,1,0:T(8,128)(2,1)S(1)}, u32[]{:S(2)}, u32[]{:S(2)}) collective-permute-start(bf16[1,64,1024]{2,1,0:T(8,128)(2,1)S(1)} %get-tuple-element.16.refs_1_), channel_id=1, source_target_pairs={{0,4},{4,0},{8,12},{12,8},{1,5},{5,1},{9,13},{13,9},{2,6},{6,2},{1... | collective-permute-start | bytes 393224 | tf_op jit(solution)/shard_map/ppermute | solution.py:381
  15.3 2.6 %collective-permute-start.5 = (bf16[1,64,1024]{2,1,0:T(8,128)(2,1)S(1)}, bf16[1,64,1024]{2,1,0:T(8,128)(2,1)S(1)}, u32[]{:S(2)}, u32[]{:S(2)}) collective-permute-start(bf16[1,64,1024]{2,1,0:T(8,128)(2,1)S(1)} %get-tuple-element.16.refs_1_), channel_id=1, source_target_pairs={{0,8},{4,12},{8,0},{12,4},{1,9},{5,13},{9,1},{13,5},{2,10},{6,14},... | collective-permute-start | bytes 393224 | tf_op jit(solution)/shard_map/ppermute | solution.py:381
  18.1 12.8 %collective-permute-done = bf16[1,64,1536]{2,1,0:T(8,128)(2,1)S(1)} collective-permute-done((bf16[1,64,1536]{2,1,0:T(8,128)(2,1)S(1)}, bf16[1,64,1536]{2,1,0:T(8,128)(2,1)S(1)}, u32[]{:S(2)}, u32[]{:S(2)}) %collective-permute-start) | collective-permute-done | bytes 196640 | tf_op jit(solution)/shard_map/ppermute | solution.py:350
  30.9 1.7 %collective-permute-start.1 = (bf16[1,64,1024]{2,1,0:T(8,128)(2,1)S(1)}, bf16[1,64,1024]{2,1,0:T(8,128)(2,1)S(1)}, u32[]{:S(2)}, u32[]{:S(2)}) collective-permute-start(bf16[1,64,1024]{2,1,0:T(8,128)(2,1)S(1)} %slice.8.refs_1_), channel_id=1, source_target_pairs={{0,4},{4,0},{8,12},{12,8},{1,5},{5,1},{9,13},{13,9},{2,6},{6,2},{1... | collective-permute-start | bytes 393224 | tf_op jit(solution)/shard_map/ppermute | solution.py:381
  32.6 2.6 %collective-permute-start.2 = (bf16[1,64,1024]{2,1,0:T(8,128)(2,1)S(1)}, bf16[1,64,1024]{2,1,0:T(8,128)(2,1)S(1)}, u32[]{:S(2)}, u32[]{:S(2)}) collective-permute-start(bf16[1,64,1024]{2,1,0:T(8,128)(2,1)S(1)} %slice.8.refs_1_), channel_id=1, source_target_pairs={{0,8},{4,12},{8,0},{12,4},{1,9},{5,13},{9,1},{13,5},{2,10},{6,14},... | collective-permute-start | bytes 393224 | tf_op jit(solution)/shard_map/ppermute | solution.py:381
  35.4 1.4 %shard_map.110.refs_5_ = f32[256,128]{1,0:T(8,128)S(1)} custom-call(s32[4]{0:T(128)S(1)} %get-tuple-element.23.ids_ref, bf16[4,128,1152]{2,1,0:T(8,128)(2,1)S(1)} %all-to-all-done.refs_0_.rows_ref, bf16[1,64,1024]{2,1,0:T(8,128)(2,1)S(1)} %get-tuple-element.16.refs_1_, bf16[1,64,1024]{2,1,0:T(8,128)(2,1)S(1)} %collective-permute-done.4.refs_2_, ...), custom_call_target="tpu_custom_call" | custom-call | flops 268435456 | bytes 2359296 | tf_op jit(solution)/shard_map/pallas_call | solution.py:287
  37.4 7.1 %collective-permute-done.2.refs_3_ = bf16[1,64,1024]{2,1,0:T(8,128)(2,1)S(1)} collective-permute-done((bf16[1,64,1024]{2,1,0:T(8,128)(2,1)S(1)}, bf16[1,64,1024]{2,1,0:T(8,128)(2,1)S(1)}, u32[]{:S(2)}, u32[]{:S(2)}) %collective-permute-start.2) | collective-permute-done | bytes 131104 | tf_op jit(solution)/shard_map/ppermute | solution.py:381
  44.5 1.4 %shard_map.111 = f32[256,128]{1,0:T(8,128)S(1)} custom-call(s32[4]{0:T(128)S(1)} %get-tuple-element.24.ids_ref, bf16[4,128,1152]{2,1,0:T(8,128)(2,1)S(1)} %all-to-all-done.refs_0_.rows_ref, bf16[1,64,1024]{2,1,0:T(8,128)(2,1)S(1)} %slice.8.refs_1_, bf16[1,64,1024]{2,1,0:T(8,128)(2,1)S(1)} %collective-permute-done.1.refs_2_, ...), custom_call_target="tpu_custom_call" | custom-call | flops 268435456 | bytes 2359296 | tf_op jit(solution)/shard_map/pallas_call | solution.py:287
  46.1 2.0 %collective-permute-start.11 = (bf16[2,64,512]{2,1,0:T(8,128)(2,1)S(1)}, bf16[2,64,512]{2,1,0:T(8,128)(2,1)S(1)}, u32[]{:S(2)}, u32[]{:S(2)}) collective-permute-start(bf16[2,64,512]{2,1,0:T(8,128)(2,1)S(1)} %pad_maximum_fusion.refs_4_), channel_id=1, source_target_pairs={{0,4},{4,0},{8,12},{12,8},{1,5},{5,1},{9,13},{13,9},{2,6},{6,2},{1... | collective-permute-start | bytes 393224 | tf_op jit(solution)/shard_map/ppermute | solution.py:381
  49.2 1.4 %collective-permute-start.13 = (bf16[2,64,512]{2,1,0:T(8,128)(2,1)S(1)}, bf16[2,64,512]{2,1,0:T(8,128)(2,1)}, u32[]{:S(2)}, u32[]{:S(2)}) collective-permute-start(bf16[2,64,512]{2,1,0:T(8,128)(2,1)S(1)} %pad_maximum_fusion.refs_4_), channel_id=1, source_target_pairs={{0,12},{4,8},{8,4},{12,0},{1,13},{5,9},{9,5},{13,1},{2,14},{6,10},... | collective-permute-start | bytes 393224 | tf_op jit(solution)/shard_map/ppermute | solution.py:381
  51.3 1.3 %collective-permute-start.9 = (bf16[256,128]{1,0:T(8,128)(2,1)S(1)}, bf16[256,128]{1,0:T(8,128)(2,1)}, u32[]{:S(2)}, u32[]{:S(2)}) collective-permute-start(bf16[256,128]{1,0:T(8,128)(2,1)S(1)} %add_convert_fusion.refs_0_), channel_id=1, source_target_pairs={{0,16},{2,18},{16,0},{18,2},{1,17},{3,19},{17,1},{19,3},{4,20},{6,... | collective-permute-start | bytes 196616 | tf_op jit(solution)/shard_map/ppermute | solution.py:350
  52.6 1.9 %collective-permute-done.11.refs_5_ = bf16[2,64,512]{2,1,0:T(8,128)(2,1)S(1)} collective-permute-done((bf16[2,64,512]{2,1,0:T(8,128)(2,1)S(1)}, bf16[2,64,512]{2,1,0:T(8,128)(2,1)S(1)}, u32[]{:S(2)}, u32[]{:S(2)}) %collective-permute-start.11) | collective-permute-done | bytes 131104 | tf_op jit(solution)/shard_map/ppermute | solution.py:381
  55.2 1.3 %collective-permute-start.10 = (bf16[256,128]{1,0:T(8,128)(2,1)S(1)}, bf16[256,128]{1,0:T(8,128)(2,1)}, u32[]{:S(2)}, u32[]{:S(2)}) collective-permute-start(bf16[256,128]{1,0:T(8,128)(2,1)S(1)} %add_convert_fusion.refs_0_), channel_id=1, source_target_pairs={{0,18},{2,16},{16,2},{18,0},{1,19},{3,17},{17,3},{19,1},{4,22},{6,... | collective-permute-start | bytes 196616 | tf_op jit(solution)/shard_map/ppermute | solution.py:350
  56.9 4.3 %collective-permute-done.12.refs_6_ = bf16[2,64,512]{2,1,0:T(8,128)(2,1)} collective-permute-done((bf16[2,64,512]{2,1,0:T(8,128)(2,1)S(1)}, bf16[2,64,512]{2,1,0:T(8,128)(2,1)}, u32[]{:S(2)}, u32[]{:S(2)}) %collective-permute-start.12) | collective-permute-done | bytes 131104 | tf_op jit(solution)/shard_map/ppermute | solution.py:381
  62.1 2.3 %shard_map.112 = (bf16[128,512]{1,0:T(8,128)(2,1)S(1)}, bf16[128,512]{1,0:T(8,128)(2,1)}, bf16[128,512]{1,0:T(8,128)(2,1)}, bf16[128,512]{1,0:T(8,128)(2,1)}) custom-call(s32[8]{0:T(128)S(1)} %add.39.ids_ref, s32[1]{0:T(128)} %bitcast.me_ref, bf16[4,128,1152]{2,1,0:T(8,128)(2,1)S(1)} %all-to-all-done.refs_0_.rows_ref, ...), custom_call_target="tpu_custom_call" | custom-call | tf_op jit(solution)/shard_map/pallas_call | solution.py:312
  65.6 1.3 %collective-permute-start.15 = (bf16[128,512]{1,0:T(8,128)(2,1)}, bf16[128,512]{1,0:T(8,128)(2,1)S(1)}, u32[]{:S(2)}, u32[]{:S(2)}) collective-permute-start(bf16[128,512]{1,0:T(8,128)(2,1)} %get-tuple-element.21), channel_id=1, source_target_pairs={{0,16},{2,18},{16,0},{18,2},{1,17},{3,19},{17,1},{19,3},{4,20},{6,... | collective-permute-start | bytes 393224 | tf_op jit(solution)/shard_map/ppermute | solution.py:350
  66.9 1.6 %collective-permute-start.16 = (bf16[128,512]{1,0:T(8,128)(2,1)}, bf16[128,512]{1,0:T(8,128)(2,1)S(1)}, u32[]{:S(2)}, u32[]{:S(2)}) collective-permute-start(bf16[128,512]{1,0:T(8,128)(2,1)} %get-tuple-element.22), channel_id=1, source_target_pairs={{0,18},{2,16},{16,2},{18,0},{1,19},{3,17},{17,3},{19,1},{4,22},{6,... | collective-permute-start | bytes 393224 | tf_op jit(solution)/shard_map/ppermute | solution.py:350
  68.5 2.4 %collective-permute-done.14.refs_1_ = bf16[128,512]{1,0:T(8,128)(2,1)S(1)} collective-permute-done((bf16[128,512]{1,0:T(8,128)(2,1)}, bf16[128,512]{1,0:T(8,128)(2,1)S(1)}, u32[]{:S(2)}, u32[]{:S(2)}) %collective-permute-start.14) | collective-permute-done | bytes 131104 | tf_op jit(solution)/shard_map/ppermute | solution.py:350
  71.7 1.4 %collective-permute-done.16.refs_3_ = bf16[128,512]{1,0:T(8,128)(2,1)S(1)} collective-permute-done((bf16[128,512]{1,0:T(8,128)(2,1)}, bf16[128,512]{1,0:T(8,128)(2,1)S(1)}, u32[]{:S(2)}, u32[]{:S(2)}) %collective-permute-start.16) | collective-permute-done | bytes 131104 | tf_op jit(solution)/shard_map/ppermute | solution.py:350
  75.9 2.4 %shard_map.113 = bf16[128,2048]{1,0:T(8,128)(2,1)} custom-call(s32[1]{0:T(128)} %bitcast.me_ref, s32[16,128]{1,0:T(8,128)S(1)} %copy.13.len_ref, bf16[128,2048]{1,0:T(8,128)(2,1)S(1)} %copy-done.4, bf16[128,256]{1,0:T(8,128)(2,1)S(1)} %copy-done.10, bf16[128,256]{1,0:T(8,128)(2,1)S(1)} %copy-done.11, bf16[128,16,256]{2,1,0:T(8,128)(2,1)S(1)} %copy-done.1, ...), custom_call_target="tpu_custom_call" | custom-call | flops 134217728 | bytes 3145728 | tf_op jit(solution)/shard_map/pallas_call | solution.py:264
  (61 shorter events, 13.0 us)
Async XLA Ops:
  0.0 1.2 %copy-start = (bf16[128,4096]{1,0:T(8,128)(2,1)S(1)}, bf16[128,4096]{1,0:T(8,128)(2,1)}, u32[]{:S(2)}) copy-start(bf16[128,4096]{1,0:T(8,128)(2,1)} %hidden_ref.1) | copy-start | bytes 3145732
  6.5 28.9 %all-to-all-start = ((bf16[4,128,1152]{2,1,0:T(8,128)(2,1)}), bf16[4,128,1152]{2,1,0:T(8,128)(2,1)S(1)}, u32[]{:S(2)}, u32[]{:S(2)}) async-start(bf16[4,128,1152]{2,1,0:T(8,128)(2,1)} %get-tuple-element.14), calls=%async_computation | async-start | bytes 2359296 | tf_op jit(solution)/shard_map/all_to_all | solution.py:366
  11.7 19.3 %collective-permute-start = (bf16[1,64,1536]{2,1,0:T(8,128)(2,1)S(1)}, bf16[1,64,1536]{2,1,0:T(8,128)(2,1)S(1)}, u32[]{:S(2)}, u32[]{:S(2)}) collective-permute-start(bf16[1,64,1536]{2,1,0:T(8,128)(2,1)S(1)} %get-tuple-element.15), channel_id=1, source_target_pairs={{0,2},{2,0},{16,18},{18,16},{1,3},{3,1},{17,19},{19,17},{4,6},{6,4... | collective-permute-start | bytes 589832 | tf_op jit(solution)/shard_map/ppermute | solution.py:350
  13.7 21.5 %collective-permute-start.4 = (bf16[1,64,1024]{2,1,0:T(8,128)(2,1)S(1)}, bf16[1,64,1024]{2,1,0:T(8,128)(2,1)S(1)}, u32[]{:S(2)}, u32[]{:S(2)}) collective-permute-start(bf16[1,64,1024]{2,1,0:T(8,128)(2,1)S(1)} %get-tuple-element.16.refs_1_), channel_id=1, source_target_pairs={{0,4},{4,0},{8,12},{12,8},{1,5},{5,1},{9,13},{13,9},{2,6},{6,2},{1... | collective-permute-start | bytes 393224 | tf_op jit(solution)/shard_map/ppermute | solution.py:381
  15.3 20.1 %collective-permute-start.5 = (bf16[1,64,1024]{2,1,0:T(8,128)(2,1)S(1)}, bf16[1,64,1024]{2,1,0:T(8,128)(2,1)S(1)}, u32[]{:S(2)}, u32[]{:S(2)}) collective-permute-start(bf16[1,64,1024]{2,1,0:T(8,128)(2,1)S(1)} %get-tuple-element.16.refs_1_), channel_id=1, source_target_pairs={{0,8},{4,12},{8,0},{12,4},{1,9},{5,13},{9,1},{13,5},{2,10},{6,14},... | collective-permute-start | bytes 393224 | tf_op jit(solution)/shard_map/ppermute | solution.py:381
  17.8 17.5 %collective-permute-start.6 = (bf16[1,64,1024]{2,1,0:T(8,128)(2,1)S(1)}, bf16[1,64,1024]{2,1,0:T(8,128)(2,1)S(1)}, u32[]{:S(2)}, u32[]{:S(2)}) collective-permute-start(bf16[1,64,1024]{2,1,0:T(8,128)(2,1)S(1)} %get-tuple-element.16.refs_1_), channel_id=1, source_target_pairs={{0,12},{4,8},{8,4},{12,0},{1,13},{5,9},{9,5},{13,1},{2,14},{6,10},... | collective-permute-start | bytes 393224 | tf_op jit(solution)/shard_map/ppermute | solution.py:381
  30.9 6.5 %collective-permute-start.1 = (bf16[1,64,1024]{2,1,0:T(8,128)(2,1)S(1)}, bf16[1,64,1024]{2,1,0:T(8,128)(2,1)S(1)}, u32[]{:S(2)}, u32[]{:S(2)}) collective-permute-start(bf16[1,64,1024]{2,1,0:T(8,128)(2,1)S(1)} %slice.8.refs_1_), channel_id=1, source_target_pairs={{0,4},{4,0},{8,12},{12,8},{1,5},{5,1},{9,13},{13,9},{2,6},{6,2},{1... | collective-permute-start | bytes 393224 | tf_op jit(solution)/shard_map/ppermute | solution.py:381
  32.6 11.8 %collective-permute-start.2 = (bf16[1,64,1024]{2,1,0:T(8,128)(2,1)S(1)}, bf16[1,64,1024]{2,1,0:T(8,128)(2,1)S(1)}, u32[]{:S(2)}, u32[]{:S(2)}) collective-permute-start(bf16[1,64,1024]{2,1,0:T(8,128)(2,1)S(1)} %slice.8.refs_1_), channel_id=1, source_target_pairs={{0,8},{4,12},{8,0},{12,4},{1,9},{5,13},{9,1},{13,5},{2,10},{6,14},... | collective-permute-start | bytes 393224 | tf_op jit(solution)/shard_map/ppermute | solution.py:381
  35.2 9.3 %collective-permute-start.3 = (bf16[1,64,1024]{2,1,0:T(8,128)(2,1)S(1)}, bf16[1,64,1024]{2,1,0:T(8,128)(2,1)S(1)}, u32[]{:S(2)}, u32[]{:S(2)}) collective-permute-start(bf16[1,64,1024]{2,1,0:T(8,128)(2,1)S(1)} %slice.8.refs_1_), channel_id=1, source_target_pairs={{0,12},{4,8},{8,4},{12,0},{1,13},{5,9},{9,5},{13,1},{2,14},{6,10},... | collective-permute-start | bytes 393224 | tf_op jit(solution)/shard_map/ppermute | solution.py:381
  44.5 12.1 %copy-start.14 = (s32[128]{0:T(128)S(1)}, s32[128]{0:T(128)}, u32[]{:S(2)}) copy-start(s32[128]{0:T(128)} %param.21) | copy-start | bytes 1540
  45.9 4.7 %collective-permute-start.7 = (f32[256,128]{1,0:T(8,128)S(1)}, f32[256,128]{1,0:T(8,128)S(1)}, u32[]{:S(2)}, u32[]{:S(2)}) collective-permute-start(f32[256,128]{1,0:T(8,128)S(1)} %shard_map.111), channel_id=1, source_target_pairs={{0,1},{1,0},{2,3},{3,2},{4,5},{5,4},{6,7},{7,6},{8,9},{9,8},{10,11... | collective-permute-start | bytes 393224 | tf_op jit(solution)/shard_map/ppermute | solution.py:402
  46.1 27.1 %copy-start.10 = (bf16[128,256]{1,0:T(8,128)(2,1)S(1)}, bf16[128,256]{1,0:T(8,128)(2,1)}, u32[]{:S(2)}) copy-start(bf16[128,256]{1,0:T(8,128)(2,1)} %nk_ref.1) | copy-start | bytes 196612
  46.1 27.0 %copy-start.1 = (bf16[128,16,256]{2,1,0:T(8,128)(2,1)S(1)}, bf16[128,16,256]{2,1,0:T(8,128)(2,1)}, u32[]{:S(2)}) copy-start(bf16[128,16,256]{2,1,0:T(8,128)(2,1)} %ck_ref.1) | copy-start | bytes 3145732
  46.1 27.0 %copy-start.2 = (bf16[128,16,256]{2,1,0:T(8,128)(2,1)S(1)}, bf16[128,16,256]{2,1,0:T(8,128)(2,1)}, u32[]{:S(2)}) copy-start(bf16[128,16,256]{2,1,0:T(8,128)(2,1)} %cv_ref.1) | copy-start | bytes 3145732
  46.1 8.4 %collective-permute-start.11 = (bf16[2,64,512]{2,1,0:T(8,128)(2,1)S(1)}, bf16[2,64,512]{2,1,0:T(8,128)(2,1)S(1)}, u32[]{:S(2)}, u32[]{:S(2)}) collective-permute-start(bf16[2,64,512]{2,1,0:T(8,128)(2,1)S(1)} %pad_maximum_fusion.refs_4_), channel_id=1, source_target_pairs={{0,4},{4,0},{8,12},{12,8},{1,5},{5,1},{9,13},{13,9},{2,6},{6,2},{1... | collective-permute-start | bytes 393224 | tf_op jit(solution)/shard_map/ppermute | solution.py:381
  48.1 13.0 %collective-permute-start.12 = (bf16[2,64,512]{2,1,0:T(8,128)(2,1)S(1)}, bf16[2,64,512]{2,1,0:T(8,128)(2,1)}, u32[]{:S(2)}, u32[]{:S(2)}) collective-permute-start(bf16[2,64,512]{2,1,0:T(8,128)(2,1)S(1)} %pad_maximum_fusion.refs_4_), channel_id=1, source_target_pairs={{0,8},{4,12},{8,0},{12,4},{1,9},{5,13},{9,1},{13,5},{2,10},{6,14},... | collective-permute-start | bytes 393224 | tf_op jit(solution)/shard_map/ppermute | solution.py:381
  49.2 11.9 %collective-permute-start.13 = (bf16[2,64,512]{2,1,0:T(8,128)(2,1)S(1)}, bf16[2,64,512]{2,1,0:T(8,128)(2,1)}, u32[]{:S(2)}, u32[]{:S(2)}) collective-permute-start(bf16[2,64,512]{2,1,0:T(8,128)(2,1)S(1)} %pad_maximum_fusion.refs_4_), channel_id=1, source_target_pairs={{0,12},{4,8},{8,4},{12,0},{1,13},{5,9},{9,5},{13,1},{2,14},{6,10},... | collective-permute-start | bytes 393224 | tf_op jit(solution)/shard_map/ppermute | solution.py:381
  50.6 10.5 %collective-permute-start.8 = (bf16[256,128]{1,0:T(8,128)(2,1)S(1)}, bf16[256,128]{1,0:T(8,128)(2,1)}, u32[]{:S(2)}, u32[]{:S(2)}) collective-permute-start(bf16[256,128]{1,0:T(8,128)(2,1)S(1)} %add_convert_fusion.refs_0_), channel_id=1, source_target_pairs={{0,2},{2,0},{16,18},{18,16},{1,3},{3,1},{17,19},{19,17},{4,6},{6,4... | collective-permute-start | bytes 196616 | tf_op jit(solution)/shard_map/ppermute | solution.py:350
  51.3 9.9 %collective-permute-start.9 = (bf16[256,128]{1,0:T(8,128)(2,1)S(1)}, bf16[256,128]{1,0:T(8,128)(2,1)}, u32[]{:S(2)}, u32[]{:S(2)}) collective-permute-start(bf16[256,128]{1,0:T(8,128)(2,1)S(1)} %add_convert_fusion.refs_0_), channel_id=1, source_target_pairs={{0,16},{2,18},{16,0},{18,2},{1,17},{3,19},{17,1},{19,3},{4,20},{6,... | collective-permute-start | bytes 196616 | tf_op jit(solution)/shard_map/ppermute | solution.py:350
  55.2 6.0 %collective-permute-start.10 = (bf16[256,128]{1,0:T(8,128)(2,1)S(1)}, bf16[256,128]{1,0:T(8,128)(2,1)}, u32[]{:S(2)}, u32[]{:S(2)}) collective-permute-start(bf16[256,128]{1,0:T(8,128)(2,1)S(1)} %add_convert_fusion.refs_0_), channel_id=1, source_target_pairs={{0,18},{2,16},{16,2},{18,0},{1,19},{3,17},{17,3},{19,1},{4,22},{6,... | collective-permute-start | bytes 196616 | tf_op jit(solution)/shard_map/ppermute | solution.py:350
  65.0 5.9 %collective-permute-start.14 = (bf16[128,512]{1,0:T(8,128)(2,1)}, bf16[128,512]{1,0:T(8,128)(2,1)S(1)}, u32[]{:S(2)}, u32[]{:S(2)}) collective-permute-start(bf16[128,512]{1,0:T(8,128)(2,1)} %get-tuple-element.20), channel_id=1, source_target_pairs={{0,2},{2,0},{16,18},{18,16},{1,3},{3,1},{17,19},{19,17},{4,6},{6,4... | collective-permute-start | bytes 393224 | tf_op jit(solution)/shard_map/ppermute | solution.py:350
  65.6 6.1 %collective-permute-start.15 = (bf16[128,512]{1,0:T(8,128)(2,1)}, bf16[128,512]{1,0:T(8,128)(2,1)S(1)}, u32[]{:S(2)}, u32[]{:S(2)}) collective-permute-start(bf16[128,512]{1,0:T(8,128)(2,1)} %get-tuple-element.21), channel_id=1, source_target_pairs={{0,16},{2,18},{16,0},{18,2},{1,17},{3,19},{17,1},{19,3},{4,20},{6,... | collective-permute-start | bytes 393224 | tf_op jit(solution)/shard_map/ppermute | solution.py:350
  66.9 6.2 %collective-permute-start.16 = (bf16[128,512]{1,0:T(8,128)(2,1)}, bf16[128,512]{1,0:T(8,128)(2,1)S(1)}, u32[]{:S(2)}, u32[]{:S(2)}) collective-permute-start(bf16[128,512]{1,0:T(8,128)(2,1)} %get-tuple-element.22), channel_id=1, source_target_pairs={{0,18},{2,16},{16,2},{18,0},{1,19},{3,17},{17,3},{19,1},{4,22},{6,... | collective-permute-start | bytes 393224 | tf_op jit(solution)/shard_map/ppermute | solution.py:350
  73.1 1.0 %copy-start.4 = (bf16[128,2048]{1,0:T(8,128)(2,1)S(1)}, bf16[128,2048]{1,0:T(8,128)(2,1)}, u32[]{:S(2)}) copy-start(bf16[128,2048]{1,0:T(8,128)(2,1)} %base_ref.1) | copy-start | bytes 1572868
  (9 other events, 7.3 us)

commit v5 on v4

--- a/solution.py
+++ b/solution.py
@@ -13,7 +13,7 @@
 LANES = 128
 STEP = 16
 HALF = 8
-BATCH = 4
+BATCH = 2
 DEAD = -1e30
 VMEM = pl.BlockSpec(memory_space=pltpu.VMEM)
 SMEM = pl.BlockSpec(memory_space=pltpu.SMEM)
@@ -23,25 +23,34 @@
 TN = (((0,), (0,)), ((), ()))
 
 
-def pack_kernel(parts, me_ref, map_ref, ids_ref, hidden_ref, shrink_ref, expand_ref, *refs):
-    rows_ref, own_ref, next_ref, expand_own_ref, sems = refs
+def columns(at, width):
+    return pl.ds(pl.multiple_of(at * width, width), width)
+
+
+def factor_kernel(parts, me_ref, shrink_ref, expand_ref, own_ref, next_ref, sems):
+    features, outputs = shrink_ref.shape[2] // parts, expand_ref.shape[2] // parts
+    copies = []
+    for k, (at, ref) in enumerate(((me_ref[0] ^ 1, next_ref), (me_ref[0], own_ref))):
+        shrink = shrink_ref.at[:, :, columns(at, features)]
+        expand = expand_ref.at[:, :, columns(at, outputs)]
+        copies += [
+            pltpu.make_async_copy(shrink, ref.at[:, :, :features], sems.at[2 * k]),
+            pltpu.make_async_copy(expand, ref.at[:, :, features:], sems.at[2 * k + 1]),
+        ]
+    for copy in copies:
+        copy.start()
+    for copy in copies:
+        copy.wait()
+
+
+def row_kernel(parts, map_ref, ids_ref, hidden_ref, rows_ref, sems):
     requests, wide = hidden_ref.shape
-    features, outputs = wide // parts, expand_ref.shape[2] // parts
-    me = me_ref[0]
-
-    def columns(at, width):
-        return pl.ds(pl.multiple_of(at * width, width), width)
-
-    moves = [
-        (shrink_ref.at[:, :, columns(me, features)], own_ref),
-        (shrink_ref.at[:, :, columns(me ^ 1, features)], next_ref.at[:, :, :features]),
-        (expand_ref.at[:, :, columns(me ^ 1, outputs)], next_ref.at[:, :, features:]),
-        (expand_ref.at[:, :, columns(me, outputs)], expand_own_ref),
-    ]
+    features = wide // parts
+    copies = []
     for s in range(parts):
         at = slice(s * features, (s + 1) * features)
-        moves.append((hidden_ref.at[:, at], rows_ref.at[s, :, :features]))
-    copies = [pltpu.make_async_copy(src, dst, sems.at[k]) for k, (src, dst) in enumerate(moves)]
+        dst = rows_ref.at[s, :, :features]
+        copies.append(pltpu.make_async_copy(hidden_ref.at[:, at], dst, sems.at[s]))
     for copy in copies:
         copy.start()
     ids = ids_ref[...]
@@ -70,20 +79,20 @@
     return ref[:, features:].astype(jnp.float32).astype(jnp.int32)
 
 
-def stacked(refs):
-    blocks = [r[k] for r in refs for k in range(r.shape[0])]
+def stacked(refs, lanes):
+    blocks = [r[k, :, lanes] for r in refs for k in range(r.shape[0])]
     return jnp.concatenate(blocks, axis=0)
 
 
 def shrink_kernel(parts, blocks, gridded, ids_ref, *refs):
     rows_ref, weight_refs, base_ref, out_ref = refs[0], refs[1 : 1 + blocks], refs[1 + blocks], refs[-1]
     row_refs = [rows_ref.at[s] for s in range(parts)]
-    rank, features = weight_refs[0].shape[1:]
-    requests = row_refs[0].shape[0]
+    rank = weight_refs[0].shape[1]
+    requests, features = rows_ref.shape[1], rows_ref.shape[2] - LANES
     count = sum(r.shape[0] for r in weight_refs)
     step = pl.program_id(0) if gridded else 0
     ids = [ids_ref[step * count + k] for k in range(count)]
-    weight = stacked(weight_refs)
+    weight = stacked(weight_refs, slice(0, features))
     low = lax.broadcasted_iota(jnp.int32, (requests, LANES), 1) < rank
     folded = []
     for ref in row_refs:
@@ -117,13 +126,13 @@
         refs[-2:],
     )
     me = me_ref[0]
-    rank, outputs = weight_refs[0].shape[1:]
+    rank, outputs = weight_refs[0].shape[1], out_refs[0].shape[1]
     requests, features = rows_ref.shape[1], rows_ref.shape[2] - LANES
     count = sum(r.shape[0] for r in weight_refs)
     step = pl.program_id(0) if gridded else 0
     last = pl.num_programs(0) - 1 if gridded else 0
     ids = [ids_ref[step * count + k] for k in range(count)]
-    weight = stacked(weight_refs)
+    weight = stacked(weight_refs, slice(features, features + outputs))
     half = parts // 2
     low = lax.broadcasted_iota(jnp.int32, (requests, LANES), 1) < rank
     low_sum = low_refs[0][...].astype(jnp.float32)
@@ -188,10 +197,11 @@
     scale = 1.0 / math.sqrt(HEAD)
     ones = jnp.ones((keys_in, HEAD), jnp.bfloat16)
 
-    def body(step, _):
+    if True:
+        step = pl.program_id(0)
         units = []
         for j in range(BATCH):
-            start = pl.multiple_of((step * BATCH + j) * STEP, STEP)
+            start = j * STEP
             at = pl.ds(start, STEP)
             pieces = []
             for s in range(parts):
@@ -200,7 +210,7 @@
                 q = q + delta_refs[s][at, :].astype(jnp.float32)
                 pieces += [q[:, k * HEAD : (k + 1) * HEAD] for k in range(per_part)]
             for h in range(STEP // HALF):
-                slab = pl.ds(pl.multiple_of(start + h * HALF, HALF), HALF)
+                slab = pl.ds(start + h * HALF, HALF)
                 q = jnp.concatenate([p[h * HALF : (h + 1) * HALF] for p in pieces], axis=0)
                 units.append((step * BATCH + j, at, h, slab, q.astype(jnp.bfloat16)))
         scores = []
@@ -251,9 +261,6 @@
                 ]
                 lanes = pl.ds(pl.multiple_of(part_at[s] * width, width), width)
                 out_ref[at, lanes] = jnp.concatenate(out, axis=1).astype(jnp.bfloat16)
-        return 0
-
-    lax.fori_loop(0, requests // (STEP * BATCH), body, 0)
 
 
 def attend(me, base, new_key, new_value, cache_keys, cache_values, lengths, deltas):
@@ -261,11 +268,16 @@
     kv = new_key.shape[1]
     slots = cache_keys.shape[1]
     lengths = jnp.tile(lengths.reshape(requests // HALF, HALF), (1, columns // HEAD))
+    block = STEP * BATCH
+    rows2 = lambda w: pl.BlockSpec((block, w), lambda i: (i, 0))
+    rows3 = pl.BlockSpec((block, slots, kv), lambda i: (i, 0, 0))
     return pl.pallas_call(
         functools.partial(attend_kernel, len(deltas)),
         out_shape=jax.ShapeDtypeStruct((requests, columns), jnp.bfloat16),
-        in_specs=[SMEM] + [VMEM] * (6 + len(deltas)),
-        out_specs=VMEM,
+        grid=(requests // block,),
+        in_specs=[SMEM, whole(lengths), rows2(columns), rows2(kv), rows2(kv), rows3, rows3]
+        + [rows2(d.shape[1]) for d in deltas],
+        out_specs=rows2(columns),
         compiler_params=PARAMS,
         cost_estimate=pl.CostEstimate(
             flops=4 * requests * HALF * slots * columns,
@@ -275,46 +287,43 @@
     )(me, lengths, base, new_key, new_value, cache_keys, cache_values, *deltas)
 
 
+def whole(array):
+    return pl.BlockSpec(array.shape, lambda *_: (0,) * len(array.shape))
+
+
+def factor_specs(weights, chunk):
+    if chunk is None:
+        return (1,), [whole(w) for w in weights]
+    (weight,) = weights
+    return (weight.shape[0] // chunk,), [
+        pl.BlockSpec((chunk,) + weight.shape[1:], lambda i: (i, 0, 0))
+    ]
+
+
 def shrink_rows(ids, rows, weights, base, chunk):
     parts = rows.shape[0]
-    gridded = chunk is not None
-    rank, features = weights[0].shape[1:]
-    specs = [SMEM] + [VMEM] * (len(weights) + 2)
-    grid = ()
-    if gridded:
-        grid = (weights[0].shape[0] // chunk,)
-        specs[2] = pl.BlockSpec((chunk, rank, features), lambda i: (i, 0, 0))
+    grid, specs = factor_specs(weights, chunk)
     return pl.pallas_call(
-        functools.partial(shrink_kernel, parts, len(weights), gridded),
+        functools.partial(shrink_kernel, parts, len(weights), chunk is not None),
         out_shape=jax.ShapeDtypeStruct(base.shape, jnp.float32),
         grid=grid,
-        in_specs=specs,
-        out_specs=VMEM,
+        in_specs=[SMEM, whole(rows), *specs, whole(base)],
+        out_specs=whole(base),
         compiler_params=PARAMS,
-        cost_estimate=pl.CostEstimate(
-            flops=2 * parts * rows.shape[1] * features * rank * sum(w.shape[0] for w in weights),
-            bytes_accessed=4 * rows.size,
-            transcendentals=0,
-        ),
     )(ids, rows, *weights, base)
 
 
-def expand_rows(ids, me, rows, lows, weights, chunk):
+def expand_rows(ids, me, rows, lows, weights, chunk, outputs):
     parts, requests, _ = rows.shape
-    gridded = chunk is not None
-    rank, outputs = weights[0].shape[1:]
-    specs = [SMEM, SMEM] + [VMEM] * (1 + parts + len(weights))
-    grid = ()
-    if gridded:
-        grid = (weights[0].shape[0] // chunk,)
-        specs[3 + parts] = pl.BlockSpec((chunk, rank, outputs), lambda i: (i, 0, 0))
-    held = (parts, requests, outputs) if gridded else (1, 8, LANES)
+    grid, specs = factor_specs(weights, chunk)
+    out = jax.ShapeDtypeStruct((requests, outputs), jnp.bfloat16)
+    held = (1, 8, LANES) if chunk is None else (parts, requests, outputs)
     return pl.pallas_call(
-        functools.partial(expand_kernel, parts, len(weights), gridded),
-        out_shape=[jax.ShapeDtypeStruct((requests, outputs), jnp.bfloat16)] * parts,
+        functools.partial(expand_kernel, parts, len(weights), chunk is not None),
+        out_shape=[out] * parts,
         grid=grid,
-        in_specs=specs,
-        out_specs=[VMEM] * parts,
+        in_specs=[SMEM, SMEM, whole(rows), *map(whole, lows), *specs],
+        out_specs=[whole(out)] * parts,
         scratch_shapes=[
             pltpu.VMEM((parts, requests, LANES), jnp.float32),
             pltpu.VMEM(held, jnp.float32),
@@ -353,57 +362,56 @@
         return lax.optimization_barrier((a, *others))[0]
 
     shrink = shrink_factors.swapaxes(1, 2)
-    rows, shrink_own, both_next, expand_own = pl.pallas_call(
-        functools.partial(pack_kernel, square),
-        out_shape=[jax.ShapeDtypeStruct((square, requests, features + LANES), jnp.bfloat16)]
-        + [jax.ShapeDtypeStruct((1, rank, w), jnp.bfloat16) for w in (features, features + outputs, outputs)],
-        in_specs=[SMEM, SMEM, VMEM, HBM, HBM, HBM],
-        out_specs=[VMEM] * 4,
-        scratch_shapes=[pltpu.SemaphoreType.DMA((square + 4,))],
-        compiler_params=pltpu.CompilerParams(vmem_limit_bytes=48 * 1024 * 1024),
-    )(me[None], owner_map, adapter_ids.T, hidden, shrink, expand_factors)
-    both_next = swap(both_next, 1)
+    block = jax.ShapeDtypeStruct((1, rank, features + outputs), jnp.bfloat16)
+    own, other = pl.pallas_call(
+        functools.partial(factor_kernel, square),
+        out_shape=[block, block],
+        in_specs=[SMEM, HBM, HBM],
+        out_specs=[VMEM, VMEM],
+        scratch_shapes=[pltpu.SemaphoreType.DMA((4,))],
+    )(me[None], shrink, expand_factors)
+    other = swap(other, 1)
+    rows = pl.pallas_call(
+        functools.partial(row_kernel, square),
+        out_shape=jax.ShapeDtypeStruct((square, requests, features + LANES), jnp.bfloat16),
+        in_specs=[SMEM, VMEM, HBM],
+        out_specs=VMEM,
+        scratch_shapes=[pltpu.SemaphoreType.DMA((square,))],
+    )(owner_map, adapter_ids.T, hidden)
+    rows = tied(rows, other)
     rows = lax.all_to_all(rows, ("rep", "side"), split_axis=0, concat_axis=0, tiled=True)
-    shrink_next, expand_next = both_next[:, :, :features], both_next[:, :, features:]
 
     empty = jnp.zeros((square // 2 * requests, LANES), jnp.float32)
     order = jnp.arange(levels, dtype=jnp.int32)
-    both_sides = jnp.stack([side, side ^ 1])[None, :]
-
-    def gather_pairs(own, other):
+    if levels == 4:
+        near_pairs = [(i, i ^ 1) for i in range(levels)]
+        far_pairs = [(i, i ^ 2) for i in range(levels)]
+
+        def gather(a):
+            far = lax.ppermute(a, "level", far_pairs)
+            near = lax.ppermute(a, "level", near_pairs)
+            inner = lax.ppermute(a, "level", [(1, 2), (2, 1)])
+            outer = lax.ppermute(far, "level", [(2, 3), (1, 0)])
+            return [a, near, far, jnp.where((level == 1) | (level == 2), inner, outer)]
+
+        own_ids = (level ^ order) * sides + side
+        next_ids = (level ^ order) * sides + (side ^ 1)
+        own, other = gather(own), gather(other)
+        partial = shrink_rows(own_ids, rows, own, empty, None)
+        partial = shrink_rows(next_ids, rows, other, partial, None)
+        factors, ids, chunk = own + other, jnp.concatenate([own_ids, next_ids]), None
+    else:
         both = jnp.concatenate([own, other], axis=0)
-        return lax.all_gather(both, "level", axis=0, tiled=True)
-
-    if levels == 4:
-
-        def gather(a):
-            return [a] + [
-                lax.ppermute(a, "level", [(i, i ^ k) for i in range(levels)])
-                for k in range(1, levels)
-            ]
-
-        own_blocks = gather(shrink_own)
-        next_blocks = gather(shrink_next)
-        partial = shrink_rows((level ^ order) * sides + side, rows, own_blocks, empty, None)
-        partial = shrink_rows((level ^ order) * sides + (side ^ 1), rows, next_blocks, partial, None)
-        pair = jnp.concatenate([expand_own, expand_next], axis=0)
-        pair = tied(pair, own_blocks[1], own_blocks[2])
-        expand = gather(pair)
-        level_ids = (level ^ order)[:, None] * sides
-        chunk = None
-    else:
+        factors = [lax.all_gather(both, "level", axis=0, tiled=True)]
+        ids = (order[:, None] * sides + jnp.stack([side, side ^ 1])[None, :]).reshape(-1)
         chunk = 4
-        level_ids = order[:, None] * sides
-        weights = [gather_pairs(shrink_own, shrink_next)]
-        partial = shrink_rows((level_ids + both_sides).reshape(-1), rows, weights, empty, chunk)
-        expand = [gather_pairs(expand_own, expand_next)]
+        partial = shrink_rows(ids, rows, factors, empty, chunk)
 
     for c in range(1, tp):
         partial = partial + lax.ppermute(partial, "tp", [(t, t ^ c) for t in range(tp)])
     partial = partial.astype(jnp.bfloat16)
     lows = [partial] + [swap(partial, s) for s in range(1, square)]
-    expand_ids = (level_ids + both_sides).reshape(-1)
-    deltas = expand_rows(expand_ids, me[None], rows, lows, expand, chunk)
+    deltas = expand_rows(ids, me[None], rows, lows, factors, chunk, outputs)
     deltas = [deltas[0]] + [swap(deltas[s], s) for s in range(1, square)]
     return attend(
         me[None],

time: 78.9 us -> 76.2 us (0.966)
  local copies, waits for them, and re-layouts: 9.84 us -> 6.04 us
  waiting for transfers between devices: 31.3 us -> 28.2 us
  Pallas kernels: 9.42 us -> 12.5 us
  starting transfers between devices: 27.4 us -> 28.7 us
    ppermute x7, waiting for transfers between devices: 17.4 us -> 10.2 us  [swap(): return lax.ppermute(a, ('rep', 'side'), pairs)]
    unnamed x30 -> x22, local copies, waits for them, and re-layouts: 9.53 us -> 5.82 us
    ppermute x9 -> x8, waiting for transfers between devices: 13.8 us -> 16.8 us  [the longest x2 9.11 us: gather(): far = lax.ppermute(a, 'level', far_pairs)]
    pallas_call x4 -> x5, Pallas kernels: 7.04 us -> 9.2 us  [the longest x1 2.91 us: per_device(): pl.pallas_call(functools.partial(row_kernel, square), out_shape=jax.Shape...]
    ppermute x9 -> x8, starting transfers between devices: 13.3 us -> 15 us  [the longest x2 5.56 us: gather(): near = lax.ppermute(a, 'level', near_pairs)]
    all_to_all x1, starting transfers between devices: 5.18 us -> 3.54 us  [per_device(): lax.all_to_all(rows, ('rep', 'side'), split_axis=0, concat_axis=0, tiled=...]
    ppermute x7, starting transfers between devices: 8.86 us -> 10 us  [swap(): return lax.ppermute(a, ('rep', 'side'), pairs)]
    ppermute x1, waiting for transfers between devices: 0.01 us -> 1.17 us  [per_device(): lax.ppermute(partial, 'tp', [(t, t ^ c) for t in range(tp)])]
  transfers between devices with their start and end apart: 18 -> 17, of which waited for: 8 -> 9; matrix products, arithmetic and copies ran while one was open for 1% -> 0% of each run, Pallas kernels for 2% -> 6%
where the time goes in v5:
time: 76.2 us; the launch traced here: 75.7 us
  starting transfers between devices  28.7 us (38%)
  waiting for transfers between devices  28.2 us (37%)
  Pallas kernels  12.5 us (16%)
  local copies, waits for them, and re-layouts  6.04 us (8%)
    ppermute x7, waiting for transfers between devices, swap(): return lax.ppermute(a, ('rep', 'side'), pairs)  10.2 us
    ppermute x7, starting transfers between devices, swap(): return lax.ppermute(a, ('rep', 'side'), pairs)  10 us
    ppermute x2, waiting for transfers between devices, gather(): far = lax.ppermute(a, 'level', far_pairs)  9.11 us
    ppermute x2, waiting for transfers between devices, gather(): outer = lax.ppermute(far, 'level', [(2, 3), (1, 0)])  7.63 us
    unnamed x22, local copies, waits for them, and re-layouts  5.82 us
    ppermute x2, starting transfers between devices, gather(): near = lax.ppermute(a, 'level', near_pairs)  5.56 us
    ppermute x2, starting transfers between devices, gather(): far = lax.ppermute(a, 'level', far_pairs)  5.43 us
    all_to_all x1, starting transfers between devices, per_device(): lax.all_to_all(rows, ('rep', 'side'), split_axis=0, concat_axis=0, tiled=...  3.54 us
  transfers between devices with their start and end apart: 17, of which 9 were waited for; matrix products, arithmetic and copies ran while one was open for 0% of the time, Pallas kernels for 6%

profile of v5, /device:TPU:0, one launch (start us, length us, event | category | flops | bytes accessed | tf_op | source)
XLA Modules:
  0.0 75.7 jit_solution(11921654340647745546)
XLA Ops:
  0.0 1.8 %shard_map.110 = (bf16[1,64,1536]{2,1,0:T(8,128)(2,1)}, bf16[1,64,1536]{2,1,0:T(8,128)(2,1)}) custom-call(s32[1]{0:T(128)} %bitcast.me_ref, bf16[1,64,4096]{2,1,0:T(8,128)(2,1)} %bitcast.5, bf16[1,64,2048]{2,1,0:T(8,128)(2,1)} %expand_ref.1), custom_call_target="tpu_custom_call" | custom-call | tf_op jit(solution)/shard_map/pallas_call | solution.py:366
  1.8 3.0 %collective-permute-start = (bf16[1,64,1536]{2,1,0:T(8,128)(2,1)}, bf16[1,64,1536]{2,1,0:T(8,128)(2,1)S(1)}, u32[]{:S(2)}, u32[]{:S(2)}) collective-permute-start(bf16[1,64,1536]{2,1,0:T(8,128)(2,1)} %get-tuple-element.12), channel_id=1, source_target_pairs={{0,2},{2,0},{16,18},{18,16},{1,3},{3,1},{17,19},{19,17},{4,6},{6,4... | collective-permute-start | bytes 589832 | tf_op jit(solution)/shard_map/ppermute | solution.py:359
  4.8 2.6 %collective-permute-start.6 = (bf16[1,64,1536]{2,1,0:T(8,128)(2,1)}, bf16[1,64,1536]{2,1,0:T(8,128)(2,1)S(1)}, u32[]{:S(2)}, u32[]{:S(2)}) collective-permute-start(bf16[1,64,1536]{2,1,0:T(8,128)(2,1)} %get-tuple-element.14.refs_1_.refs_4_), channel_id=1, source_target_pairs={{0,8},{4,12},{8,0},{12,4},{1,9},{5,13},{9,1},{13,5},{2,10},{6,14},... | collective-permute-start | bytes 589832 | tf_op jit(solution)/shard_map/ppermute | solution.py:391
  8.0 1.9 %collective-permute-done.refs_1_.refs_8_ = bf16[1,64,1536]{2,1,0:T(8,128)(2,1)S(1)} collective-permute-done((bf16[1,64,1536]{2,1,0:T(8,128)(2,1)}, bf16[1,64,1536]{2,1,0:T(8,128)(2,1)S(1)}, u32[]{:S(2)}, u32[]{:S(2)}) %collective-permute-start) | collective-permute-done | bytes 196640 | tf_op jit(solution)/shard_map/ppermute | solution.py:359
  9.9 2.8 %collective-permute-start.2 = (bf16[1,64,1536]{2,1,0:T(8,128)(2,1)S(1)}, bf16[1,64,1536]{2,1,0:T(8,128)(2,1)S(1)}, u32[]{:S(2)}, u32[]{:S(2)}) collective-permute-start(bf16[1,64,1536]{2,1,0:T(8,128)(2,1)S(1)} %collective-permute-done.refs_1_.refs_8_), channel_id=1, source_target_pairs={{0,8},{4,12},{8,0},{12,4},{1,9},{5,13},{9,1},{13,5},{2,10},{6,14},... | collective-permute-start | bytes 589832 | tf_op jit(solution)/shard_map/ppermute | solution.py:391
  12.7 9.1 %collective-permute-done.6.refs_3_.refs_6_ = bf16[1,64,1536]{2,1,0:T(8,128)(2,1)S(1)} collective-permute-done((bf16[1,64,1536]{2,1,0:T(8,128)(2,1)}, bf16[1,64,1536]{2,1,0:T(8,128)(2,1)S(1)}, u32[]{:S(2)}, u32[]{:S(2)}) %collective-permute-start.6) | collective-permute-done | bytes 196640 | tf_op jit(solution)/shard_map/ppermute | solution.py:391
  21.8 1.3 %collective-permute-start.8 = (bf16[1,64,1536]{2,1,0:T(8,128)(2,1)S(1)}, bf16[1,64,1536]{2,1,0:T(8,128)(2,1)S(1)}, u32[]{:S(2)}, u32[]{:S(2)}) collective-permute-start(bf16[1,64,1536]{2,1,0:T(8,128)(2,1)S(1)} %collective-permute-done.6.refs_3_.refs_6_), channel_id=1, source_target_pairs={{8,12},{4,0},{9,13},{5,1},{10,14},{6,2},{11,15},{7,3},{24,28},{20,... | collective-permute-start | bytes 589832 | tf_op jit(solution)/shard_map/ppermute | solution.py:394
  23.1 2.7 %collective-permute-start.5 = (bf16[1,64,1536]{2,1,0:T(8,128)(2,1)}, bf16[1,64,1536]{2,1,0:T(8,128)(2,1)S(1)}, u32[]{:S(2)}, u32[]{:S(2)}) collective-permute-start(bf16[1,64,1536]{2,1,0:T(8,128)(2,1)} %get-tuple-element.14.refs_1_.refs_4_), channel_id=1, source_target_pairs={{0,4},{4,0},{8,12},{12,8},{1,5},{5,1},{9,13},{13,9},{2,6},{6,2},{1... | collective-permute-start | bytes 589832 | tf_op jit(solution)/shard_map/ppermute | solution.py:392
  25.9 2.9 %shard_map.109 = bf16[4,128,1152]{2,1,0:T(8,128)(2,1)} custom-call(s32[8]{0:T(128)} %map_ref.1, s32[1,128]{1,0:T(1,128)} %bitcast.6, bf16[128,4096]{1,0:T(8,128)(2,1)} %hidden_ref.1), custom_call_target="tpu_custom_call" | custom-call | tf_op jit(solution)/shard_map/pallas_call | solution.py:374
  28.8 3.5 %all-to-all-start = ((bf16[4,128,1152]{2,1,0:T(8,128)(2,1)}), bf16[4,128,1152]{2,1,0:T(8,128)(2,1)S(1)}, u32[]{:S(2)}, u32[]{:S(2)}) async-start(bf16[4,128,1152]{2,1,0:T(8,128)(2,1)} %shard_map.109), calls=%async_computation | async-start | bytes 2359296 | tf_op jit(solution)/shard_map/all_to_all | solution.py:382
  33.2 2.8 %collective-permute-start.1 = (bf16[1,64,1536]{2,1,0:T(8,128)(2,1)S(1)}, bf16[1,64,1536]{2,1,0:T(8,128)(2,1)S(1)}, u32[]{:S(2)}, u32[]{:S(2)}) collective-permute-start(bf16[1,64,1536]{2,1,0:T(8,128)(2,1)S(1)} %collective-permute-done.refs_1_.refs_8_), channel_id=1, source_target_pairs={{0,4},{4,0},{8,12},{12,8},{1,5},{5,1},{9,13},{13,9},{2,6},{6,2},{1... | collective-permute-start | bytes 589832 | tf_op jit(solution)/shard_map/ppermute | solution.py:392
  36.0 1.3 %collective-permute-start.4 = (bf16[1,64,1536]{2,1,0:T(8,128)(2,1)S(1)}, bf16[1,64,1536]{2,1,0:T(8,128)(2,1)S(1)}, u32[]{:S(2)}, u32[]{:S(2)}) collective-permute-start(bf16[1,64,1536]{2,1,0:T(8,128)(2,1)S(1)} %collective-permute-done.2.refs_3_.refs_10_), channel_id=1, source_target_pairs={{8,12},{4,0},{9,13},{5,1},{10,14},{6,2},{11,15},{7,3},{24,28},{20,... | collective-permute-start | bytes 589832 | tf_op jit(solution)/shard_map/ppermute | solution.py:394
  37.4 7.6 %collective-permute-done.4 = bf16[1,64,1536]{2,1,0:T(8,128)(2,1)S(1)} collective-permute-done((bf16[1,64,1536]{2,1,0:T(8,128)(2,1)S(1)}, bf16[1,64,1536]{2,1,0:T(8,128)(2,1)S(1)}, u32[]{:S(2)}, u32[]{:S(2)}) %collective-permute-start.4) | collective-permute-done | bytes 196640 | tf_op jit(solution)/shard_map/ppermute | solution.py:394
  45.1 1.4 %shard_map.111.refs_5_ = f32[256,128]{1,0:T(8,128)S(1)} custom-call(s32[4]{0:T(128)S(1)} %get-tuple-element.20.ids_ref, bf16[4,128,1152]{2,1,0:T(8,128)(2,1)S(1)} %all-to-all-done.refs_0_.rows_ref, bf16[1,64,1536]{2,1,0:T(8,128)(2,1)S(1)} %copy-done.2, bf16[1,64,1536]{2,1,0:T(8,128)(2,1)S(1)} %collective-permute-done.5.refs_2_.refs_5_, ...), custom_call_target="tpu_custom_call" | custom-call | tf_op jit(solution)/shard_map/pallas_call | solution.py:306
  46.5 1.4 %shard_map.112 = f32[256,128]{1,0:T(8,128)S(1)} custom-call(s32[4]{0:T(128)S(1)} %get-tuple-element.19.ids_ref, bf16[4,128,1152]{2,1,0:T(8,128)(2,1)S(1)} %all-to-all-done.refs_0_.rows_ref, bf16[1,64,1536]{2,1,0:T(8,128)(2,1)S(1)} %collective-permute-done.refs_1_.refs_8_, bf16[1,64,1536]{2,1,0:T(8,128)(2,1)S(1)} %collective-permute-done.1.refs_2_.refs_9_, ...), custom_call_target="tpu_custom_call" | custom-call | tf_op jit(solution)/shard_map/pallas_call | solution.py:306
  49.4 1.4 %collective-permute-start.10 = (bf16[256,128]{1,0:T(8,128)(2,1)S(1)}, bf16[256,128]{1,0:T(8,128)(2,1)S(1)}, u32[]{:S(2)}, u32[]{:S(2)}) collective-permute-start(bf16[256,128]{1,0:T(8,128)(2,1)S(1)} %add_convert_fusion.refs_0_), channel_id=1, source_target_pairs={{0,2},{2,0},{16,18},{18,16},{1,3},{3,1},{17,19},{19,17},{4,6},{6,4... | collective-permute-start | bytes 196616 | tf_op jit(solution)/shard_map/ppermute | solution.py:359
  50.8 1.4 %collective-permute-start.11 = (bf16[256,128]{1,0:T(8,128)(2,1)S(1)}, bf16[256,128]{1,0:T(8,128)(2,1)S(1)}, u32[]{:S(2)}, u32[]{:S(2)}) collective-permute-start(bf16[256,128]{1,0:T(8,128)(2,1)S(1)} %add_convert_fusion.refs_0_), channel_id=1, source_target_pairs={{0,16},{2,18},{16,0},{18,2},{1,17},{3,19},{17,1},{19,3},{4,20},{6,... | collective-permute-start | bytes 196616 | tf_op jit(solution)/shard_map/ppermute | solution.py:359
  53.7 1.4 %collective-permute-done.11.refs_2_ = bf16[256,128]{1,0:T(8,128)(2,1)S(1)} collective-permute-done((bf16[256,128]{1,0:T(8,128)(2,1)S(1)}, bf16[256,128]{1,0:T(8,128)(2,1)S(1)}, u32[]{:S(2)}, u32[]{:S(2)}) %collective-permute-start.11) | collective-permute-done | bytes 65568 | tf_op jit(solution)/shard_map/ppermute | solution.py:359
  55.1 2.3 %collective-permute-done.12.refs_3_ = bf16[256,128]{1,0:T(8,128)(2,1)S(1)} collective-permute-done((bf16[256,128]{1,0:T(8,128)(2,1)S(1)}, bf16[256,128]{1,0:T(8,128)(2,1)S(1)}, u32[]{:S(2)}, u32[]{:S(2)}) %collective-permute-start.12) | collective-permute-done | bytes 65568 | tf_op jit(solution)/shard_map/ppermute | solution.py:359
  59.3 1.7 %shard_map.113 = (bf16[128,512]{1,0:T(8,128)(2,1)S(1)}, bf16[128,512]{1,0:T(8,128)(2,1)}, bf16[128,512]{1,0:T(8,128)(2,1)}, bf16[128,512]{1,0:T(8,128)(2,1)}) custom-call(s32[8]{0:T(128)S(1)} %pad_add_fusion.ids_ref, s32[1]{0:T(128)} %bitcast.me_ref, bf16[4,128,1152]{2,1,0:T(8,128)(2,1)S(1)} %all-to-all-done.refs_0_.rows_ref, ...), custom_call_target="tpu_custom_call" | custom-call | tf_op jit(solution)/shard_map/pallas_call | solution.py:321
  62.2 2.3 %collective-permute-start.15 = (bf16[128,512]{1,0:T(8,128)(2,1)}, bf16[128,512]{1,0:T(8,128)(2,1)S(1)}, u32[]{:S(2)}, u32[]{:S(2)}) collective-permute-start(bf16[128,512]{1,0:T(8,128)(2,1)} %get-tuple-element.18), channel_id=1, source_target_pairs={{0,18},{2,16},{16,2},{18,0},{1,19},{3,17},{17,3},{19,1},{4,22},{6,... | collective-permute-start | bytes 393224 | tf_op jit(solution)/shard_map/ppermute | solution.py:359
  64.6 2.1 %collective-permute-done.13.refs_1_ = bf16[128,512]{1,0:T(8,128)(2,1)S(1)} collective-permute-done((bf16[128,512]{1,0:T(8,128)(2,1)}, bf16[128,512]{1,0:T(8,128)(2,1)S(1)}, u32[]{:S(2)}, u32[]{:S(2)}) %collective-permute-start.13) | collective-permute-done | bytes 131104 | tf_op jit(solution)/shard_map/ppermute | solution.py:359
  66.7 1.8 %collective-permute-done.14.refs_2_ = bf16[128,512]{1,0:T(8,128)(2,1)S(1)} collective-permute-done((bf16[128,512]{1,0:T(8,128)(2,1)}, bf16[128,512]{1,0:T(8,128)(2,1)S(1)}, u32[]{:S(2)}, u32[]{:S(2)}) %collective-permute-start.14) | collective-permute-done | bytes 131104 | tf_op jit(solution)/shard_map/ppermute | solution.py:359
  72.5 3.3 %shard_map.114 = bf16[128,2048]{1,0:T(8,128)(2,1)} custom-call(s32[1]{0:T(128)} %bitcast.me_ref, s32[16,128]{1,0:T(8,128)S(1)} %copy.13.len_ref, bf16[128,2048]{1,0:T(8,128)(2,1)S(1)} %copy-done.7, bf16[128,256]{1,0:T(8,128)(2,1)S(1)} %copy-done.8, bf16[128,256]{1,0:T(8,128)(2,1)S(1)} %copy-done.9, bf16[128,16,256]{2,1,0:T(8,128)(2,1)S(1)} %copy-done, ...), custom_call_target="tpu_custom_call" | custom-call | flops 134217728 | bytes 3145728 | tf_op jit(solution)/shard_map/pallas_call | solution.py:274
  (48 shorter events, 11.5 us)
Async XLA Ops:
  1.8 8.1 %collective-permute-start = (bf16[1,64,1536]{2,1,0:T(8,128)(2,1)}, bf16[1,64,1536]{2,1,0:T(8,128)(2,1)S(1)}, u32[]{:S(2)}, u32[]{:S(2)}) collective-permute-start(bf16[1,64,1536]{2,1,0:T(8,128)(2,1)} %get-tuple-element.12), channel_id=1, source_target_pairs={{0,2},{2,0},{16,18},{18,16},{1,3},{3,1},{17,19},{19,17},{4,6},{6,4... | collective-permute-start | bytes 589832 | tf_op jit(solution)/shard_map/ppermute | solution.py:359
  4.8 17.1 %collective-permute-start.6 = (bf16[1,64,1536]{2,1,0:T(8,128)(2,1)}, bf16[1,64,1536]{2,1,0:T(8,128)(2,1)S(1)}, u32[]{:S(2)}, u32[]{:S(2)}) collective-permute-start(bf16[1,64,1536]{2,1,0:T(8,128)(2,1)} %get-tuple-element.14.refs_1_.refs_4_), channel_id=1, source_target_pairs={{0,8},{4,12},{8,0},{12,4},{1,9},{5,13},{9,1},{13,5},{2,10},{6,14},... | collective-permute-start | bytes 589832 | tf_op jit(solution)/shard_map/ppermute | solution.py:391
  7.4 25.8 %collective-permute-start.7 = (bf16[1,64,1536]{2,1,0:T(8,128)(2,1)}, bf16[1,64,1536]{2,1,0:T(8,128)(2,1)S(1)}, u32[]{:S(2)}, u32[]{:S(2)}) collective-permute-start(bf16[1,64,1536]{2,1,0:T(8,128)(2,1)} %get-tuple-element.14.refs_1_.refs_4_), channel_id=1, source_target_pairs={{4,8},{8,4},{5,9},{9,5},{6,10},{10,6},{7,11},{11,7},{20,24},{24,20... | collective-permute-start | bytes 589832 | tf_op jit(solution)/shard_map/ppermute | solution.py:393
  9.9 26.1 %collective-permute-start.2 = (bf16[1,64,1536]{2,1,0:T(8,128)(2,1)S(1)}, bf16[1,64,1536]{2,1,0:T(8,128)(2,1)S(1)}, u32[]{:S(2)}, u32[]{:S(2)}) collective-permute-start(bf16[1,64,1536]{2,1,0:T(8,128)(2,1)S(1)} %collective-permute-done.refs_1_.refs_8_), channel_id=1, source_target_pairs={{0,8},{4,12},{8,0},{12,4},{1,9},{5,13},{9,1},{13,5},{2,10},{6,14},... | collective-permute-start | bytes 589832 | tf_op jit(solution)/shard_map/ppermute | solution.py:391
  21.8 15.5 %collective-permute-start.8 = (bf16[1,64,1536]{2,1,0:T(8,128)(2,1)S(1)}, bf16[1,64,1536]{2,1,0:T(8,128)(2,1)S(1)}, u32[]{:S(2)}, u32[]{:S(2)}) collective-permute-start(bf16[1,64,1536]{2,1,0:T(8,128)(2,1)S(1)} %collective-permute-done.6.refs_3_.refs_6_), channel_id=1, source_target_pairs={{8,12},{4,0},{9,13},{5,1},{10,14},{6,2},{11,15},{7,3},{24,28},{20,... | collective-permute-start | bytes 589832 | tf_op jit(solution)/shard_map/ppermute | solution.py:394
  23.1 21.9 %collective-permute-start.5 = (bf16[1,64,1536]{2,1,0:T(8,128)(2,1)}, bf16[1,64,1536]{2,1,0:T(8,128)(2,1)S(1)}, u32[]{:S(2)}, u32[]{:S(2)}) collective-permute-start(bf16[1,64,1536]{2,1,0:T(8,128)(2,1)} %get-tuple-element.14.refs_1_.refs_4_), channel_id=1, source_target_pairs={{0,4},{4,0},{8,12},{12,8},{1,5},{5,1},{9,13},{13,9},{2,6},{6,2},{1... | collective-permute-start | bytes 589832 | tf_op jit(solution)/shard_map/ppermute | solution.py:392
  28.8 16.3 %all-to-all-start = ((bf16[4,128,1152]{2,1,0:T(8,128)(2,1)}), bf16[4,128,1152]{2,1,0:T(8,128)(2,1)S(1)}, u32[]{:S(2)}, u32[]{:S(2)}) async-start(bf16[4,128,1152]{2,1,0:T(8,128)(2,1)} %shard_map.109), calls=%async_computation | async-start | bytes 2359296 | tf_op jit(solution)/shard_map/all_to_all | solution.py:382
  32.3 12.7 %copy-start.2 = (bf16[1,64,1536]{2,1,0:T(8,128)(2,1)S(1)}, bf16[1,64,1536]{2,1,0:T(8,128)(2,1)}, u32[]{:S(2)}) copy-start(bf16[1,64,1536]{2,1,0:T(8,128)(2,1)} %get-tuple-element.14.refs_1_.refs_4_) | copy-start | bytes 589828
  32.3 5.0 %collective-permute-start.3 = (bf16[1,64,1536]{2,1,0:T(8,128)(2,1)S(1)}, bf16[1,64,1536]{2,1,0:T(8,128)(2,1)S(1)}, u32[]{:S(2)}, u32[]{:S(2)}) collective-permute-start(bf16[1,64,1536]{2,1,0:T(8,128)(2,1)S(1)} %collective-permute-done.refs_1_.refs_8_), channel_id=1, source_target_pairs={{4,8},{8,4},{5,9},{9,5},{6,10},{10,6},{7,11},{11,7},{20,24},{24,20... | collective-permute-start | bytes 589832 | tf_op jit(solution)/shard_map/ppermute | solution.py:393
  33.2 13.3 %collective-permute-start.1 = (bf16[1,64,1536]{2,1,0:T(8,128)(2,1)S(1)}, bf16[1,64,1536]{2,1,0:T(8,128)(2,1)S(1)}, u32[]{:S(2)}, u32[]{:S(2)}) collective-permute-start(bf16[1,64,1536]{2,1,0:T(8,128)(2,1)S(1)} %collective-permute-done.refs_1_.refs_8_), channel_id=1, source_target_pairs={{0,4},{4,0},{8,12},{12,8},{1,5},{5,1},{9,13},{13,9},{2,6},{6,2},{1... | collective-permute-start | bytes 589832 | tf_op jit(solution)/shard_map/ppermute | solution.py:392
  36.0 9.0 %collective-permute-start.4 = (bf16[1,64,1536]{2,1,0:T(8,128)(2,1)S(1)}, bf16[1,64,1536]{2,1,0:T(8,128)(2,1)S(1)}, u32[]{:S(2)}, u32[]{:S(2)}) collective-permute-start(bf16[1,64,1536]{2,1,0:T(8,128)(2,1)S(1)} %collective-permute-done.2.refs_3_.refs_10_), channel_id=1, source_target_pairs={{8,12},{4,0},{9,13},{5,1},{10,14},{6,2},{11,15},{7,3},{24,28},{20,... | collective-permute-start | bytes 589832 | tf_op jit(solution)/shard_map/ppermute | solution.py:394
  45.0 1.5 %copy-start.3 = (bf16[1,64,1536]{2,1,0:T(8,128)(2,1)}, bf16[1,64,1536]{2,1,0:T(8,128)(2,1)S(1)}, u32[]{:S(2)}) copy-start(bf16[1,64,1536]{2,1,0:T(8,128)(2,1)S(1)} %collective-permute-done.5.refs_2_.refs_5_) | copy-start | bytes 589828
  46.5 1.5 %copy-start.10 = (s32[128]{0:T(128)S(1)}, s32[128]{0:T(128)}, u32[]{:S(2)}) copy-start(s32[128]{0:T(128)} %param.21) | copy-start | bytes 1540
  46.5 2.9 %copy-start.5 = (bf16[1,64,1536]{2,1,0:T(8,128)(2,1)}, bf16[1,64,1536]{2,1,0:T(8,128)(2,1)S(1)}, u32[]{:S(2)}) copy-start(bf16[1,64,1536]{2,1,0:T(8,128)(2,1)S(1)} %collective-permute-done.1.refs_2_.refs_9_) | copy-start | bytes 589828
  47.9 1.4 %collective-permute-start.9 = (f32[256,128]{1,0:T(8,128)S(1)}, f32[256,128]{1,0:T(8,128)S(1)}, u32[]{:S(2)}, u32[]{:S(2)}) collective-permute-start(f32[256,128]{1,0:T(8,128)S(1)} %shard_map.112), channel_id=1, source_target_pairs={{0,1},{1,0},{2,3},{3,2},{4,5},{5,4},{6,7},{7,6},{8,9},{9,8},{10,11... | collective-permute-start | bytes 393224 | tf_op jit(solution)/shard_map/ppermute | solution.py:411
  49.4 4.3 %collective-permute-start.10 = (bf16[256,128]{1,0:T(8,128)(2,1)S(1)}, bf16[256,128]{1,0:T(8,128)(2,1)S(1)}, u32[]{:S(2)}, u32[]{:S(2)}) collective-permute-start(bf16[256,128]{1,0:T(8,128)(2,1)S(1)} %add_convert_fusion.refs_0_), channel_id=1, source_target_pairs={{0,2},{2,0},{16,18},{18,16},{1,3},{3,1},{17,19},{19,17},{4,6},{6,4... | collective-permute-start | bytes 196616 | tf_op jit(solution)/shard_map/ppermute | solution.py:359
  50.8 4.3 %collective-permute-start.11 = (bf16[256,128]{1,0:T(8,128)(2,1)S(1)}, bf16[256,128]{1,0:T(8,128)(2,1)S(1)}, u32[]{:S(2)}, u32[]{:S(2)}) collective-permute-start(bf16[256,128]{1,0:T(8,128)(2,1)S(1)} %add_convert_fusion.refs_0_), channel_id=1, source_target_pairs={{0,16},{2,18},{16,0},{18,2},{1,17},{3,19},{17,1},{19,3},{4,20},{6,... | collective-permute-start | bytes 196616 | tf_op jit(solution)/shard_map/ppermute | solution.py:359
  52.3 5.2 %collective-permute-start.12 = (bf16[256,128]{1,0:T(8,128)(2,1)S(1)}, bf16[256,128]{1,0:T(8,128)(2,1)S(1)}, u32[]{:S(2)}, u32[]{:S(2)}) collective-permute-start(bf16[256,128]{1,0:T(8,128)(2,1)S(1)} %add_convert_fusion.refs_0_), channel_id=1, source_target_pairs={{0,18},{2,16},{16,2},{18,0},{1,19},{3,17},{17,3},{19,1},{4,22},{6,... | collective-permute-start | bytes 196616 | tf_op jit(solution)/shard_map/ppermute | solution.py:359
  53.0 15.5 %copy-start = (bf16[128,16,256]{2,1,0:T(8,128)(2,1)S(1)}, bf16[128,16,256]{2,1,0:T(8,128)(2,1)}, u32[]{:S(2)}) copy-start(bf16[128,16,256]{2,1,0:T(8,128)(2,1)} %ck_ref.1) | copy-start | bytes 3145732
  61.0 5.7 %collective-permute-start.13 = (bf16[128,512]{1,0:T(8,128)(2,1)}, bf16[128,512]{1,0:T(8,128)(2,1)S(1)}, u32[]{:S(2)}, u32[]{:S(2)}) collective-permute-start(bf16[128,512]{1,0:T(8,128)(2,1)} %get-tuple-element.16), channel_id=1, source_target_pairs={{0,2},{2,0},{16,18},{18,16},{1,3},{3,1},{17,19},{19,17},{4,6},{6,4... | collective-permute-start | bytes 393224 | tf_op jit(solution)/shard_map/ppermute | solution.py:359
  61.7 6.8 %collective-permute-start.14 = (bf16[128,512]{1,0:T(8,128)(2,1)}, bf16[128,512]{1,0:T(8,128)(2,1)S(1)}, u32[]{:S(2)}, u32[]{:S(2)}) collective-permute-start(bf16[128,512]{1,0:T(8,128)(2,1)} %get-tuple-element.17), channel_id=1, source_target_pairs={{0,16},{2,18},{16,0},{18,2},{1,17},{3,19},{17,1},{19,3},{4,20},{6,... | collective-permute-start | bytes 393224 | tf_op jit(solution)/shard_map/ppermute | solution.py:359
  62.2 6.3 %collective-permute-start.15 = (bf16[128,512]{1,0:T(8,128)(2,1)}, bf16[128,512]{1,0:T(8,128)(2,1)S(1)}, u32[]{:S(2)}, u32[]{:S(2)}) collective-permute-start(bf16[128,512]{1,0:T(8,128)(2,1)} %get-tuple-element.18), channel_id=1, source_target_pairs={{0,18},{2,16},{16,2},{18,0},{1,19},{3,17},{17,3},{19,1},{4,22},{6,... | collective-permute-start | bytes 393224 | tf_op jit(solution)/shard_map/ppermute | solution.py:359
  68.5 1.2 %copy-start.1 = (bf16[128,16,256]{2,1,0:T(8,128)(2,1)S(1)}, bf16[128,16,256]{2,1,0:T(8,128)(2,1)}, u32[]{:S(2)}) copy-start(bf16[128,16,256]{2,1,0:T(8,128)(2,1)} %cv_ref.1) | copy-start | bytes 3145732
  69.7 1.0 %copy-start.7 = (bf16[128,2048]{1,0:T(8,128)(2,1)S(1)}, bf16[128,2048]{1,0:T(8,128)(2,1)}, u32[]{:S(2)}) copy-start(bf16[128,2048]{1,0:T(8,128)(2,1)} %base_ref.1) | copy-start | bytes 1572868
  (4 other events, 3.5 us)

commit v6 on v5

--- a/solution.py
+++ b/solution.py
@@ -27,16 +27,16 @@
     return pl.ds(pl.multiple_of(at * width, width), width)
 
 
-def factor_kernel(parts, me_ref, shrink_ref, expand_ref, own_ref, next_ref, sems):
+def factor_kernel(parts, me_ref, shrink_ref, expand_ref, own_ref, expand_own_ref, next_ref, sems):
     features, outputs = shrink_ref.shape[2] // parts, expand_ref.shape[2] // parts
-    copies = []
-    for k, (at, ref) in enumerate(((me_ref[0] ^ 1, next_ref), (me_ref[0], own_ref))):
-        shrink = shrink_ref.at[:, :, columns(at, features)]
-        expand = expand_ref.at[:, :, columns(at, outputs)]
-        copies += [
-            pltpu.make_async_copy(shrink, ref.at[:, :, :features], sems.at[2 * k]),
-            pltpu.make_async_copy(expand, ref.at[:, :, features:], sems.at[2 * k + 1]),
-        ]
+    me = me_ref[0]
+    moves = [
+        (shrink_ref.at[:, :, columns(me ^ 1, features)], next_ref.at[:, :, :features]),
+        (expand_ref.at[:, :, columns(me ^ 1, outputs)], next_ref.at[:, :, features:]),
+        (shrink_ref.at[:, :, columns(me, features)], own_ref),
+        (expand_ref.at[:, :, columns(me, outputs)], expand_own_ref),
+    ]
+    copies = [pltpu.make_async_copy(src, dst, sems.at[k]) for k, (src, dst) in enumerate(moves)]
     for copy in copies:
         copy.start()
     for copy in copies:
@@ -79,8 +79,8 @@
     return ref[:, features:].astype(jnp.float32).astype(jnp.int32)
 
 
-def stacked(refs, lanes):
-    blocks = [r[k, :, lanes] for r in refs for k in range(r.shape[0])]
+def stacked(refs):
+    blocks = [r[k] for r in refs for k in range(r.shape[0])]
     return jnp.concatenate(blocks, axis=0)
 
 
@@ -92,7 +92,7 @@
     count = sum(r.shape[0] for r in weight_refs)
     step = pl.program_id(0) if gridded else 0
     ids = [ids_ref[step * count + k] for k in range(count)]
-    weight = stacked(weight_refs, slice(0, features))
+    weight = stacked(weight_refs)
     low = lax.broadcasted_iota(jnp.int32, (requests, LANES), 1) < rank
     folded = []
     for ref in row_refs:
@@ -132,7 +132,7 @@
     step = pl.program_id(0) if gridded else 0
     last = pl.num_programs(0) - 1 if gridded else 0
     ids = [ids_ref[step * count + k] for k in range(count)]
-    weight = stacked(weight_refs, slice(features, features + outputs))
+    weight = stacked(weight_refs)
     half = parts // 2
     low = lax.broadcasted_iota(jnp.int32, (requests, LANES), 1) < rank
     low_sum = low_refs[0][...].astype(jnp.float32)
@@ -278,7 +278,6 @@
         in_specs=[SMEM, whole(lengths), rows2(columns), rows2(kv), rows2(kv), rows3, rows3]
         + [rows2(d.shape[1]) for d in deltas],
         out_specs=rows2(columns),
-        compiler_params=PARAMS,
         cost_estimate=pl.CostEstimate(
             flops=4 * requests * HALF * slots * columns,
             bytes_accessed=4 * requests * (columns + slots * kv),
@@ -362,12 +361,14 @@
         return lax.optimization_barrier((a, *others))[0]
 
     shrink = shrink_factors.swapaxes(1, 2)
-    block = jax.ShapeDtypeStruct((1, rank, features + outputs), jnp.bfloat16)
-    own, other = pl.pallas_call(
+    own, expand_own, other = pl.pallas_call(
         functools.partial(factor_kernel, square),
-        out_shape=[block, block],
+        out_shape=[
+            jax.ShapeDtypeStruct((1, rank, w), jnp.bfloat16)
+            for w in (features, outputs, features + outputs)
+        ],
         in_specs=[SMEM, HBM, HBM],
-        out_specs=[VMEM, VMEM],
+        out_specs=[VMEM] * 3,
         scratch_shapes=[pltpu.SemaphoreType.DMA((4,))],
     )(me[None], shrink, expand_factors)
     other = swap(other, 1)
@@ -383,35 +384,38 @@
 
     empty = jnp.zeros((square // 2 * requests, LANES), jnp.float32)
     order = jnp.arange(levels, dtype=jnp.int32)
+    ids = (order[:, None] * sides + jnp.stack([side, side ^ 1])[None, :]).reshape(-1)
+    other, expand_next = other[:, :, :features], other[:, :, features:]
+
+    def gather_pairs(own, other):
+        both = jnp.concatenate([own, other], axis=0)
+        return lax.all_gather(both, "level", axis=0, tiled=True)
+
+    expand = gather_pairs(expand_own, expand_next)
     if levels == 4:
-        near_pairs = [(i, i ^ 1) for i in range(levels)]
-        far_pairs = [(i, i ^ 2) for i in range(levels)]
 
         def gather(a):
-            far = lax.ppermute(a, "level", far_pairs)
-            near = lax.ppermute(a, "level", near_pairs)
-            inner = lax.ppermute(a, "level", [(1, 2), (2, 1)])
-            outer = lax.ppermute(far, "level", [(2, 3), (1, 0)])
-            return [a, near, far, jnp.where((level == 1) | (level == 2), inner, outer)]
+            return [a] + [
+                lax.ppermute(a, "level", [(i, i ^ k) for i in range(levels)])
+                for k in range(1, levels)
+            ]
 
         own_ids = (level ^ order) * sides + side
         next_ids = (level ^ order) * sides + (side ^ 1)
         own, other = gather(own), gather(other)
         partial = shrink_rows(own_ids, rows, own, empty, None)
+        partial, expand = lax.optimization_barrier((partial, expand))
         partial = shrink_rows(next_ids, rows, other, partial, None)
-        factors, ids, chunk = own + other, jnp.concatenate([own_ids, next_ids]), None
+        chunk = None
     else:
-        both = jnp.concatenate([own, other], axis=0)
-        factors = [lax.all_gather(both, "level", axis=0, tiled=True)]
-        ids = (order[:, None] * sides + jnp.stack([side, side ^ 1])[None, :]).reshape(-1)
         chunk = 4
-        partial = shrink_rows(ids, rows, factors, empty, chunk)
+        partial = shrink_rows(ids, rows, [gather_pairs(own, other)], empty, chunk)
 
     for c in range(1, tp):
         partial = partial + lax.ppermute(partial, "tp", [(t, t ^ c) for t in range(tp)])
     partial = partial.astype(jnp.bfloat16)
     lows = [partial] + [swap(partial, s) for s in range(1, square)]
-    deltas = expand_rows(ids, me[None], rows, lows, factors, chunk, outputs)
+    deltas = expand_rows(ids, me[None], rows, lows, [expand], chunk, outputs)
     deltas = [deltas[0]] + [swap(deltas[s], s) for s in range(1, square)]
     return attend(
         me[None],

time: 76.2 us -> 80.6 us (1.058)
  blocking collectives: 0 us -> 28.1 us
  waiting for transfers between devices: 28.2 us -> 12.3 us
  starting transfers between devices: 28.7 us -> 23.6 us
  local copies, waits for them, and re-layouts: 6.04 us -> 2.28 us
  Pallas kernels: 12.5 us -> 13.7 us
    all_gather x0 -> x1, blocking collectives: none -> 28.1 us  [gather_pairs(): return lax.all_gather(both, 'level', axis=0, tiled=True)]
    ppermute x8 -> x6, waiting for transfers between devices: 16.8 us -> 0.5 us  [gather(): lax.ppermute(a, 'level', [(i, i ^ k) for i in range(levels)])]
    ppermute x8 -> x6, starting transfers between devices: 15 us -> 9.51 us  [gather(): lax.ppermute(a, 'level', [(i, i ^ k) for i in range(levels)])]
    unnamed x22 -> x14, local copies, waits for them, and re-layouts: 5.82 us -> 1.35 us
    pallas_call x1, Pallas kernels: 3.27 us -> 5.08 us  [attend(): pl.pallas_call(functools.partial(attend_kernel, len(deltas)), out_shape=j...]
  transfers between devices with their start and end apart: 17 -> 15, of which waited for: 9 -> 8; matrix products, arithmetic and copies ran while one was open for 0% -> 1% of each run, Pallas kernels for 6% -> 5%
where the time goes in v6:
time: 80.6 us; the launch traced here: 80.3 us
  blocking collectives  28.1 us (35%)
  starting transfers between devices  23.6 us (29%)
  Pallas kernels  13.7 us (17%)
  waiting for transfers between devices  12.3 us (15%)
  local copies, waits for them, and re-layouts  2.28 us (3%)
    all_gather x1, blocking collectives, gather_pairs(): return lax.all_gather(both, 'level', axis=0, tiled=True)  28.1 us
    ppermute x7, waiting for transfers between devices, swap(): return lax.ppermute(a, ('rep', 'side'), pairs)  10.5 us
    ppermute x7, starting transfers between devices, swap(): return lax.ppermute(a, ('rep', 'side'), pairs)  10 us
    ppermute x6, starting transfers between devices, gather(): lax.ppermute(a, 'level', [(i, i ^ k) for i in range(levels)])  9.51 us
    pallas_call x1, Pallas kernels, attend(): pl.pallas_call(functools.partial(attend_kernel, len(deltas)), out_shape=j...  5.08 us
    all_to_all x1, starting transfers between devices, per_device(): lax.all_to_all(rows, ('rep', 'side'), split_axis=0, concat_axis=0, tiled=...  3.97 us
    pallas_call x1, Pallas kernels, per_device(): pl.pallas_call(functools.partial(row_kernel, square), out_shape=jax.Shape...  2.91 us
    pallas_call x2, Pallas kernels, shrink_rows(): pl.pallas_call(functools.partial(shrink_kernel, parts, len(weights), chun...  2.85 us
  transfers between devices with their start and end apart: 15, of which 8 were waited for; matrix products, arithmetic and copies ran while one was open for 1% of the time, Pallas kernels for 5%

profile of v6, /device:TPU:0, one launch (start us, length us, event | category | flops | bytes accessed | tf_op | source)
XLA Modules:
  0.0 80.3 jit_solution(8998348332980227211)
XLA Ops:
  0.0 1.8 %shard_map.110 = (bf16[1,64,1024]{2,1,0:T(8,128)(2,1)}, bf16[1,64,512]{2,1,0:T(8,128)(2,1)}, bf16[1,64,1536]{2,1,0:T(8,128)(2,1)}) custom-call(s32[1]{0:T(128)} %bitcast.me_ref, bf16[1,64,4096]{2,1,0:T(8,128)(2,1)} %bitcast.7, bf16[1,64,2048]{2,1,0:T(8,128)(2,1)} %expand_ref.1), custom_call_target="tpu_custom_call" | custom-call | tf_op jit(solution)/shard_map/pallas_call | solution.py:364
  1.8 3.0 %collective-permute-start = (bf16[1,64,1536]{2,1,0:T(8,128)(2,1)}, bf16[1,64,1536]{2,1,0:T(8,128)(2,1)S(1)}, u32[]{:S(2)}, u32[]{:S(2)}) collective-permute-start(bf16[1,64,1536]{2,1,0:T(8,128)(2,1)} %get-tuple-element.15), channel_id=1, source_target_pairs={{0,2},{2,0},{16,18},{18,16},{1,3},{3,1},{17,19},{19,17},{4,6},{6,4... | collective-permute-start | bytes 589832 | tf_op jit(solution)/shard_map/ppermute | solution.py:358
  4.8 2.9 %shard_map.109 = bf16[4,128,1152]{2,1,0:T(8,128)(2,1)} custom-call(s32[8]{0:T(128)} %map_ref.1, s32[1,128]{1,0:T(1,128)} %bitcast.8, bf16[128,4096]{1,0:T(8,128)(2,1)} %hidden_ref.1), custom_call_target="tpu_custom_call" | custom-call | tf_op jit(solution)/shard_map/pallas_call | solution.py:375
  7.7 2.2 %collective-permute-done = bf16[1,64,1536]{2,1,0:T(8,128)(2,1)S(1)} collective-permute-done((bf16[1,64,1536]{2,1,0:T(8,128)(2,1)}, bf16[1,64,1536]{2,1,0:T(8,128)(2,1)S(1)}, u32[]{:S(2)}, u32[]{:S(2)}) %collective-permute-start) | collective-permute-done | bytes 196640 | tf_op jit(solution)/shard_map/ppermute | solution.py:358
  9.9 4.0 %all-to-all-start = ((bf16[4,128,1152]{2,1,0:T(8,128)(2,1)}), bf16[4,128,1152]{2,1,0:T(8,128)(2,1)S(1)}, u32[]{:S(2)}, u32[]{:S(2)}) async-start(bf16[4,128,1152]{2,1,0:T(8,128)(2,1)} %shard_map.109), calls=%async_computation | async-start | bytes 2359296 | tf_op jit(solution)/shard_map/all_to_all | solution.py:383
  13.9 1.6 %collective-permute-start.4 = (bf16[1,64,1024]{2,1,0:T(8,128)(2,1)S(1)}, bf16[1,64,1024]{2,1,0:T(8,128)(2,1)S(1)}, u32[]{:S(2)}, u32[]{:S(2)}) collective-permute-start(bf16[1,64,1024]{2,1,0:T(8,128)(2,1)S(1)} %copy-done), channel_id=1, source_target_pairs={{0,4},{4,0},{8,12},{12,8},{1,5},{5,1},{9,13},{13,9},{2,6},{6,2},{1... | collective-permute-start | bytes 393224 | tf_op jit(solution)/shard_map/ppermute | solution.py:399
  15.4 2.6 %collective-permute-start.5 = (bf16[1,64,1024]{2,1,0:T(8,128)(2,1)S(1)}, bf16[1,64,1024]{2,1,0:T(8,128)(2,1)S(1)}, u32[]{:S(2)}, u32[]{:S(2)}) collective-permute-start(bf16[1,64,1024]{2,1,0:T(8,128)(2,1)S(1)} %copy-done), channel_id=1, source_target_pairs={{0,8},{4,12},{8,0},{12,4},{1,9},{5,13},{9,1},{13,5},{2,10},{6,14},... | collective-permute-start | bytes 393224 | tf_op jit(solution)/shard_map/ppermute | solution.py:399
  18.3 0.7 collective-permute-start.1
  19.0 3.5 %collective-permute-start.2 = (bf16[1,64,1024]{2,1,0:T(8,128)(2,1)S(1)}, bf16[1,64,1024]{2,1,0:T(8,128)(2,1)S(1)}, u32[]{:S(2)}, u32[]{:S(2)}) collective-permute-start(bf16[1,64,1024]{2,1,0:T(8,128)(2,1)S(1)} %slice.8.refs_1_), channel_id=1, source_target_pairs={{0,8},{4,12},{8,0},{12,4},{1,9},{5,13},{9,1},{13,5},{2,10},{6,14},... | collective-permute-start | bytes 393224 | tf_op jit(solution)/shard_map/ppermute | solution.py:399
  23.0 0.9 %collective-permute-start.3 = (bf16[1,64,1024]{2,1,0:T(8,128)(2,1)S(1)}, bf16[1,64,1024]{2,1,0:T(8,128)(2,1)S(1)}, u32[]{:S(2)}, u32[]{:S(2)}) collective-permute-start(bf16[1,64,1024]{2,1,0:T(8,128)(2,1)S(1)} %slice.8.refs_1_), channel_id=1, source_target_pairs={{0,12},{4,8},{8,4},{12,0},{1,13},{5,9},{9,5},{13,1},{2,14},{6,10},... | collective-permute-start | bytes 393224 | tf_op jit(solution)/shard_map/ppermute | solution.py:399
  23.9 28.1 %all_gather.3.refs_4_ = bf16[8,64,512]{2,1,0:T(8,128)(2,1)S(1)} all-gather(bf16[2,64,512]{2,1,0:T(8,128)(2,1)S(1)} %pad_maximum_fusion), channel_id=1, replica_groups=mesh['rep'=2,'level'=4,'side'=2,'tp'=2] {'level'}, dimensions={0}, use_global_device_ids=true | all-gather | bytes 655360 | tf_op jit(solution)/shard_map/all_gather | solution.py:392
  52.0 1.4 %shard_map.111.refs_5_ = f32[256,128]{1,0:T(8,128)S(1)} custom-call(s32[4]{0:T(128)S(1)} %fusion.ids_ref, bf16[4,128,1152]{2,1,0:T(8,128)(2,1)S(1)} %all-to-all-done.refs_0_.rows_ref, bf16[1,64,1024]{2,1,0:T(8,128)(2,1)S(1)} %copy-done, bf16[1,64,1024]{2,1,0:T(8,128)(2,1)S(1)} %collective-permute-done.4.refs_2_, ...), custom_call_target="tpu_custom_call" | custom-call | tf_op jit(solution)/shard_map/pallas_call | solution.py:305
  53.5 1.4 %shard_map.112 = f32[256,128]{1,0:T(8,128)S(1)} custom-call(s32[4]{0:T(128)S(1)} %fusion.1.ids_ref, bf16[4,128,1152]{2,1,0:T(8,128)(2,1)S(1)} %all-to-all-done.refs_0_.rows_ref, bf16[1,64,1024]{2,1,0:T(8,128)(2,1)S(1)} %slice.8.refs_1_, bf16[1,64,1024]{2,1,0:T(8,128)(2,1)S(1)} %collective-permute-done.1.refs_2_, ...), custom_call_target="tpu_custom_call" | custom-call | tf_op jit(solution)/shard_map/pallas_call | solution.py:305
  55.1 1.2 %collective-permute-done.7 = f32[256,128]{1,0:T(8,128)S(1)} collective-permute-done((f32[256,128]{1,0:T(8,128)S(1)}, f32[256,128]{1,0:T(8,128)S(1)}, u32[]{:S(2)}, u32[]{:S(2)}) %collective-permute-start.7) | collective-permute-done | bytes 131104 | tf_op jit(solution)/shard_map/ppermute | solution.py:415
  56.4 2.6 %collective-permute-start.10 = (bf16[256,128]{1,0:T(8,128)(2,1)S(1)}, bf16[256,128]{1,0:T(8,128)(2,1)S(1)}, u32[]{:S(2)}, u32[]{:S(2)}) collective-permute-start(bf16[256,128]{1,0:T(8,128)(2,1)S(1)} %add_convert_fusion.refs_0_), channel_id=1, source_target_pairs={{0,18},{2,16},{16,2},{18,0},{1,19},{3,17},{17,3},{19,1},{4,22},{6,... | collective-permute-start | bytes 196616 | tf_op jit(solution)/shard_map/ppermute | solution.py:358
  60.2 1.6 %collective-permute-done.10.refs_3_ = bf16[256,128]{1,0:T(8,128)(2,1)S(1)} collective-permute-done((bf16[256,128]{1,0:T(8,128)(2,1)S(1)}, bf16[256,128]{1,0:T(8,128)(2,1)S(1)}, u32[]{:S(2)}, u32[]{:S(2)}) %collective-permute-start.10) | collective-permute-done | bytes 65568 | tf_op jit(solution)/shard_map/ppermute | solution.py:358
  61.8 1.5 %collective-permute-done.8.refs_1_ = bf16[256,128]{1,0:T(8,128)(2,1)S(1)} collective-permute-done((bf16[256,128]{1,0:T(8,128)(2,1)S(1)}, bf16[256,128]{1,0:T(8,128)(2,1)S(1)}, u32[]{:S(2)}, u32[]{:S(2)}) %collective-permute-start.8) | collective-permute-done | bytes 65568 | tf_op jit(solution)/shard_map/ppermute | solution.py:358
  63.8 1.1 %shard_map.113 = (bf16[128,512]{1,0:T(8,128)(2,1)S(1)}, bf16[128,512]{1,0:T(8,128)(2,1)S(1)}, bf16[128,512]{1,0:T(8,128)(2,1)S(1)}, bf16[128,512]{1,0:T(8,128)(2,1)S(1)}) custom-call(s32[8]{0:T(128)S(1)} %add.39.ids_ref, s32[1]{0:T(128)} %bitcast.me_ref, bf16[4,128,1152]{2,1,0:T(8,128)(2,1)S(1)} %all-to-all-done.refs_0_.rows_ref, ...), custom_call_target="tpu_custom_call" | custom-call | tf_op jit(solution)/shard_map/pallas_call | solution.py:320
  65.6 1.5 %collective-permute-start.11 = (bf16[128,512]{1,0:T(8,128)(2,1)S(1)}, bf16[128,512]{1,0:T(8,128)(2,1)S(1)}, u32[]{:S(2)}, u32[]{:S(2)}) collective-permute-start(bf16[128,512]{1,0:T(8,128)(2,1)S(1)} %get-tuple-element.22), channel_id=1, source_target_pairs={{0,2},{2,0},{16,18},{18,16},{1,3},{3,1},{17,19},{19,17},{4,6},{6,4... | collective-permute-start | bytes 393224 | tf_op jit(solution)/shard_map/ppermute | solution.py:358
  67.0 0.7 collective-permute-start.12
  67.7 1.3 %collective-permute-start.13 = (bf16[128,512]{1,0:T(8,128)(2,1)S(1)}, bf16[128,512]{1,0:T(8,128)(2,1)S(1)}, u32[]{:S(2)}, u32[]{:S(2)}) collective-permute-start(bf16[128,512]{1,0:T(8,128)(2,1)S(1)} %get-tuple-element.24), channel_id=1, source_target_pairs={{0,18},{2,16},{16,2},{18,0},{1,19},{3,17},{17,3},{19,1},{4,22},{6,... | collective-permute-start | bytes 393224 | tf_op jit(solution)/shard_map/ppermute | solution.py:358
  69.7 1.8 %collective-permute-done.11.refs_1_ = bf16[128,512]{1,0:T(8,128)(2,1)S(1)} collective-permute-done((bf16[128,512]{1,0:T(8,128)(2,1)S(1)}, bf16[128,512]{1,0:T(8,128)(2,1)S(1)}, u32[]{:S(2)}, u32[]{:S(2)}) %collective-permute-start.11) | collective-permute-done | bytes 131104 | tf_op jit(solution)/shard_map/ppermute | solution.py:358
  71.5 3.0 %collective-permute-done.12.refs_2_ = bf16[128,512]{1,0:T(8,128)(2,1)S(1)} collective-permute-done((bf16[128,512]{1,0:T(8,128)(2,1)S(1)}, bf16[128,512]{1,0:T(8,128)(2,1)S(1)}, u32[]{:S(2)}, u32[]{:S(2)}) %collective-permute-start.12) | collective-permute-done | bytes 131104 | tf_op jit(solution)/shard_map/ppermute | solution.py:358
  75.2 5.1 %shard_map.114 = bf16[128,2048]{1,0:T(8,128)(2,1)} custom-call(s32[1]{0:T(128)} %bitcast.me_ref, s32[16,128]{1,0:T(8,128)} %copy.15.len_ref, bf16[128,2048]{1,0:T(8,128)(2,1)} %base_ref.1, bf16[128,256]{1,0:T(8,128)(2,1)} %nk_ref.1, bf16[128,256]{1,0:T(8,128)(2,1)} %nv_ref.1, bf16[128,16,256]{2,1,0:T(8,128)(2,1)} %ck_ref.1, bf16[128,16,256]{2,1,0:T(8,128)(2,1)} %cv_ref.1, ...), custom_call_target="tpu_custom_call" | custom-call | flops 134217728 | bytes 3145728 | tf_op jit(solution)/shard_map/pallas_call | solution.py:274
  (42 shorter events, 4.8 us)
Async XLA Ops:
  1.8 8.1 %collective-permute-start = (bf16[1,64,1536]{2,1,0:T(8,128)(2,1)}, bf16[1,64,1536]{2,1,0:T(8,128)(2,1)S(1)}, u32[]{:S(2)}, u32[]{:S(2)}) collective-permute-start(bf16[1,64,1536]{2,1,0:T(8,128)(2,1)} %get-tuple-element.15), channel_id=1, source_target_pairs={{0,2},{2,0},{16,18},{18,16},{1,3},{3,1},{17,19},{19,17},{4,6},{6,4... | collective-permute-start | bytes 589832 | tf_op jit(solution)/shard_map/ppermute | solution.py:358
  7.7 6.2 %copy-start = (bf16[1,64,1024]{2,1,0:T(8,128)(2,1)S(1)}, bf16[1,64,1024]{2,1,0:T(8,128)(2,1)}, u32[]{:S(2)}) copy-start(bf16[1,64,1024]{2,1,0:T(8,128)(2,1)} %get-tuple-element.17.refs_1_) | copy-start | bytes 393220
  7.7 14.8 %copy-start.5 = (bf16[1,64,512]{2,1,0:T(8,128)(2,1)S(1)}, bf16[1,64,512]{2,1,0:T(8,128)(2,1)}, u32[]{:S(2)}) copy-start(bf16[1,64,512]{2,1,0:T(8,128)(2,1)} %get-tuple-element.18) | copy-start | bytes 196612
  9.9 42.1 %all-to-all-start = ((bf16[4,128,1152]{2,1,0:T(8,128)(2,1)}), bf16[4,128,1152]{2,1,0:T(8,128)(2,1)S(1)}, u32[]{:S(2)}, u32[]{:S(2)}) async-start(bf16[4,128,1152]{2,1,0:T(8,128)(2,1)} %shard_map.109), calls=%async_computation | async-start | bytes 2359296 | tf_op jit(solution)/shard_map/all_to_all | solution.py:383
  13.9 9.2 %collective-permute-start.4 = (bf16[1,64,1024]{2,1,0:T(8,128)(2,1)S(1)}, bf16[1,64,1024]{2,1,0:T(8,128)(2,1)S(1)}, u32[]{:S(2)}, u32[]{:S(2)}) collective-permute-start(bf16[1,64,1024]{2,1,0:T(8,128)(2,1)S(1)} %copy-done), channel_id=1, source_target_pairs={{0,4},{4,0},{8,12},{12,8},{1,5},{5,1},{9,13},{13,9},{2,6},{6,2},{1... | collective-permute-start | bytes 393224 | tf_op jit(solution)/shard_map/ppermute | solution.py:399
  15.4 36.5 %collective-permute-start.5 = (bf16[1,64,1024]{2,1,0:T(8,128)(2,1)S(1)}, bf16[1,64,1024]{2,1,0:T(8,128)(2,1)S(1)}, u32[]{:S(2)}, u32[]{:S(2)}) collective-permute-start(bf16[1,64,1024]{2,1,0:T(8,128)(2,1)S(1)} %copy-done), channel_id=1, source_target_pairs={{0,8},{4,12},{8,0},{12,4},{1,9},{5,13},{9,1},{13,5},{2,10},{6,14},... | collective-permute-start | bytes 393224 | tf_op jit(solution)/shard_map/ppermute | solution.py:399
  18.0 34.0 %collective-permute-start.6 = (bf16[1,64,1024]{2,1,0:T(8,128)(2,1)S(1)}, bf16[1,64,1024]{2,1,0:T(8,128)(2,1)S(1)}, u32[]{:S(2)}, u32[]{:S(2)}) collective-permute-start(bf16[1,64,1024]{2,1,0:T(8,128)(2,1)S(1)} %copy-done), channel_id=1, source_target_pairs={{0,12},{4,8},{8,4},{12,0},{1,13},{5,9},{9,5},{13,1},{2,14},{6,10},... | collective-permute-start | bytes 393224 | tf_op jit(solution)/shard_map/ppermute | solution.py:399
  18.3 35.2 %collective-permute-start.1 = (bf16[1,64,1024]{2,1,0:T(8,128)(2,1)S(1)}, bf16[1,64,1024]{2,1,0:T(8,128)(2,1)S(1)}, u32[]{:S(2)}, u32[]{:S(2)}) collective-permute-start(bf16[1,64,1024]{2,1,0:T(8,128)(2,1)S(1)} %slice.8.refs_1_), channel_id=1, source_target_pairs={{0,4},{4,0},{8,12},{12,8},{1,5},{5,1},{9,13},{13,9},{2,6},{6,2},{1... | collective-permute-start | bytes 393224 | tf_op jit(solution)/shard_map/ppermute | solution.py:399
  19.0 34.4 %collective-permute-start.2 = (bf16[1,64,1024]{2,1,0:T(8,128)(2,1)S(1)}, bf16[1,64,1024]{2,1,0:T(8,128)(2,1)S(1)}, u32[]{:S(2)}, u32[]{:S(2)}) collective-permute-start(bf16[1,64,1024]{2,1,0:T(8,128)(2,1)S(1)} %slice.8.refs_1_), channel_id=1, source_target_pairs={{0,8},{4,12},{8,0},{12,4},{1,9},{5,13},{9,1},{13,5},{2,10},{6,14},... | collective-permute-start | bytes 393224 | tf_op jit(solution)/shard_map/ppermute | solution.py:399
  23.0 30.4 %collective-permute-start.3 = (bf16[1,64,1024]{2,1,0:T(8,128)(2,1)S(1)}, bf16[1,64,1024]{2,1,0:T(8,128)(2,1)S(1)}, u32[]{:S(2)}, u32[]{:S(2)}) collective-permute-start(bf16[1,64,1024]{2,1,0:T(8,128)(2,1)S(1)} %slice.8.refs_1_), channel_id=1, source_target_pairs={{0,12},{4,8},{8,4},{12,0},{1,13},{5,9},{9,5},{13,1},{2,14},{6,10},... | collective-permute-start | bytes 393224 | tf_op jit(solution)/shard_map/ppermute | solution.py:399
  53.5 6.6 %copy-start.6 = (s32[128]{0:T(128)S(1)}, s32[128]{0:T(128)}, u32[]{:S(2)}) copy-start(s32[128]{0:T(128)} %param.21) | copy-start | bytes 1540
  54.9 1.4 %collective-permute-start.7 = (f32[256,128]{1,0:T(8,128)S(1)}, f32[256,128]{1,0:T(8,128)S(1)}, u32[]{:S(2)}, u32[]{:S(2)}) collective-permute-start(f32[256,128]{1,0:T(8,128)S(1)} %shard_map.112), channel_id=1, source_target_pairs={{0,1},{1,0},{2,3},{3,2},{4,5},{5,4},{6,7},{7,6},{8,9},{9,8},{10,11... | collective-permute-start | bytes 393224 | tf_op jit(solution)/shard_map/ppermute | solution.py:415
  56.4 5.4 %collective-permute-start.10 = (bf16[256,128]{1,0:T(8,128)(2,1)S(1)}, bf16[256,128]{1,0:T(8,128)(2,1)S(1)}, u32[]{:S(2)}, u32[]{:S(2)}) collective-permute-start(bf16[256,128]{1,0:T(8,128)(2,1)S(1)} %add_convert_fusion.refs_0_), channel_id=1, source_target_pairs={{0,18},{2,16},{16,2},{18,0},{1,19},{3,17},{17,3},{19,1},{4,22},{6,... | collective-permute-start | bytes 196616 | tf_op jit(solution)/shard_map/ppermute | solution.py:358
  59.0 4.3 %collective-permute-start.8 = (bf16[256,128]{1,0:T(8,128)(2,1)S(1)}, bf16[256,128]{1,0:T(8,128)(2,1)S(1)}, u32[]{:S(2)}, u32[]{:S(2)}) collective-permute-start(bf16[256,128]{1,0:T(8,128)(2,1)S(1)} %add_convert_fusion.refs_0_), channel_id=1, source_target_pairs={{0,2},{2,0},{16,18},{18,16},{1,3},{3,1},{17,19},{19,17},{4,6},{6,4... | collective-permute-start | bytes 196616 | tf_op jit(solution)/shard_map/ppermute | solution.py:358
  59.6 4.3 %collective-permute-start.9 = (bf16[256,128]{1,0:T(8,128)(2,1)S(1)}, bf16[256,128]{1,0:T(8,128)(2,1)S(1)}, u32[]{:S(2)}, u32[]{:S(2)}) collective-permute-start(bf16[256,128]{1,0:T(8,128)(2,1)S(1)} %add_convert_fusion.refs_0_), channel_id=1, source_target_pairs={{0,16},{2,18},{16,0},{18,2},{1,17},{3,19},{17,1},{19,3},{4,20},{6,... | collective-permute-start | bytes 196616 | tf_op jit(solution)/shard_map/ppermute | solution.py:358
  64.9 0.6 copy-start.1
  65.6 6.0 %collective-permute-start.11 = (bf16[128,512]{1,0:T(8,128)(2,1)S(1)}, bf16[128,512]{1,0:T(8,128)(2,1)S(1)}, u32[]{:S(2)}, u32[]{:S(2)}) collective-permute-start(bf16[128,512]{1,0:T(8,128)(2,1)S(1)} %get-tuple-element.22), channel_id=1, source_target_pairs={{0,2},{2,0},{16,18},{18,16},{1,3},{3,1},{17,19},{19,17},{4,6},{6,4... | collective-permute-start | bytes 393224 | tf_op jit(solution)/shard_map/ppermute | solution.py:358
  67.0 7.5 %collective-permute-start.12 = (bf16[128,512]{1,0:T(8,128)(2,1)S(1)}, bf16[128,512]{1,0:T(8,128)(2,1)S(1)}, u32[]{:S(2)}, u32[]{:S(2)}) collective-permute-start(bf16[128,512]{1,0:T(8,128)(2,1)S(1)} %get-tuple-element.23), channel_id=1, source_target_pairs={{0,16},{2,18},{16,0},{18,2},{1,17},{3,19},{17,1},{19,3},{4,20},{6,... | collective-permute-start | bytes 393224 | tf_op jit(solution)/shard_map/ppermute | solution.py:358
  67.7 6.7 %collective-permute-start.13 = (bf16[128,512]{1,0:T(8,128)(2,1)S(1)}, bf16[128,512]{1,0:T(8,128)(2,1)S(1)}, u32[]{:S(2)}, u32[]{:S(2)}) collective-permute-start(bf16[128,512]{1,0:T(8,128)(2,1)S(1)} %get-tuple-element.24), channel_id=1, source_target_pairs={{0,18},{2,16},{16,2},{18,0},{1,19},{3,17},{17,3},{19,1},{4,22},{6,... | collective-permute-start | bytes 393224 | tf_op jit(solution)/shard_map/ppermute | solution.py:358
  71.5 3.0 %copy-start.2 = (bf16[128,512]{1,0:T(8,128)(2,1)}, bf16[128,512]{1,0:T(8,128)(2,1)S(1)}, u32[]{:S(2)}) copy-start(bf16[128,512]{1,0:T(8,128)(2,1)S(1)} %collective-permute-done.11.refs_1_) | copy-start | bytes 393220
  74.5 0.7 copy-start.3
  74.5 0.7 copy-start.4

commit v7 on v5

--- a/solution.py
+++ b/solution.py
@@ -17,6 +17,7 @@
 DEAD = -1e30
 VMEM = pl.BlockSpec(memory_space=pltpu.VMEM)
 SMEM = pl.BlockSpec(memory_space=pltpu.SMEM)
+ANY = pl.BlockSpec(memory_space=pl.ANY)
 HBM = pl.BlockSpec(memory_space=pltpu.HBM)
 PARAMS = pltpu.CompilerParams(vmem_limit_bytes=12 * 1024 * 1024)
 NT = (((1,), (1,)), ((), ()))
@@ -27,30 +28,19 @@
     return pl.ds(pl.multiple_of(at * width, width), width)
 
 
-def factor_kernel(parts, me_ref, shrink_ref, expand_ref, own_ref, next_ref, sems):
-    features, outputs = shrink_ref.shape[2] // parts, expand_ref.shape[2] // parts
-    copies = []
-    for k, (at, ref) in enumerate(((me_ref[0] ^ 1, next_ref), (me_ref[0], own_ref))):
-        shrink = shrink_ref.at[:, :, columns(at, features)]
-        expand = expand_ref.at[:, :, columns(at, outputs)]
-        copies += [
-            pltpu.make_async_copy(shrink, ref.at[:, :, :features], sems.at[2 * k]),
-            pltpu.make_async_copy(expand, ref.at[:, :, features:], sems.at[2 * k + 1]),
-        ]
-    for copy in copies:
-        copy.start()
-    for copy in copies:
-        copy.wait()
-
-
-def row_kernel(parts, map_ref, ids_ref, hidden_ref, rows_ref, sems):
+def cut_kernel(parts, me_ref, map_ref, ids_ref, hidden_ref, shrink_ref, expand_ref, *refs):
+    own_ref, next_ref, rows_ref, sems = refs
     requests, wide = hidden_ref.shape
-    features = wide // parts
-    copies = []
+    features, outputs = wide // parts, expand_ref.shape[2] // parts
+    me = me_ref[0]
+    moves = []
+    for at, ref in ((me ^ 1, next_ref), (me, own_ref)):
+        moves.append((shrink_ref.at[:, :, columns(at, features)], ref.at[:, :, :features]))
+        moves.append((expand_ref.at[:, :, columns(at, outputs)], ref.at[:, :, features:]))
     for s in range(parts):
         at = slice(s * features, (s + 1) * features)
-        dst = rows_ref.at[s, :, :features]
-        copies.append(pltpu.make_async_copy(hidden_ref.at[:, at], dst, sems.at[s]))
+        moves.append((hidden_ref.at[:, at], rows_ref.at[s, :, :features]))
+    copies = [pltpu.make_async_copy(src, dst, sems.at[k]) for k, (src, dst) in enumerate(moves)]
     for copy in copies:
         copy.start()
     ids = ids_ref[...]
@@ -166,11 +156,25 @@
                 out_refs[s][...] = total_ref[s].astype(jnp.bfloat16)
 
 
-def attend_kernel(
-    parts, me_ref, len_ref, base_ref, nk_ref, nv_ref, ck_ref, cv_ref, *refs
-):
-    delta_refs, out_ref = refs[:parts], refs[parts]
+def attend_kernel(parts, me_ref, len_ref, *refs):
+    inputs = 5 + parts
+    sources, out_hbm = refs[:inputs], refs[inputs]
+    held, (out_ref, sems, out_sems) = refs[inputs + 1 : 2 * inputs + 1], refs[2 * inputs + 1 :]
+    base_ref, nk_ref, nv_ref, ck_ref, cv_ref, *delta_refs = held
     me = me_ref[0]
+    block = STEP * BATCH
+    steps = base_ref.shape[0] // block
+    arrivals = []
+    for step in range(steps):
+        at = pl.ds(step * block, block)
+        arrivals.append(
+            [
+                pltpu.make_async_copy(src.at[at], dst.at[at], sems.at[step, k])
+                for k, (src, dst) in enumerate(zip(sources, held))
+            ]
+        )
+        for copy in arrivals[-1]:
+            copy.start()
     requests, columns = base_ref.shape
     width = columns // parts
     groups = nk_ref.shape[1] // HEAD
@@ -197,11 +201,13 @@
     scale = 1.0 / math.sqrt(HEAD)
     ones = jnp.ones((keys_in, HEAD), jnp.bfloat16)
 
-    if True:
-        step = pl.program_id(0)
+    departures = []
+    for step in range(steps):
+        for copy in arrivals[step]:
+            copy.wait()
         units = []
         for j in range(BATCH):
-            start = j * STEP
+            start = step * block + j * STEP
             at = pl.ds(start, STEP)
             pieces = []
             for s in range(parts):
@@ -261,6 +267,12 @@
                 ]
                 lanes = pl.ds(pl.multiple_of(part_at[s] * width, width), width)
                 out_ref[at, lanes] = jnp.concatenate(out, axis=1).astype(jnp.bfloat16)
+        at = pl.ds(step * block, block)
+        copy = pltpu.make_async_copy(out_ref.at[at], out_hbm.at[at], out_sems.at[step])
+        copy.start()
+        departures.append(copy)
+    for copy in departures:
+        copy.wait()
 
 
 def attend(me, base, new_key, new_value, cache_keys, cache_values, lengths, deltas):
@@ -268,23 +280,25 @@
     kv = new_key.shape[1]
     slots = cache_keys.shape[1]
     lengths = jnp.tile(lengths.reshape(requests // HALF, HALF), (1, columns // HEAD))
-    block = STEP * BATCH
-    rows2 = lambda w: pl.BlockSpec((block, w), lambda i: (i, 0))
-    rows3 = pl.BlockSpec((block, slots, kv), lambda i: (i, 0, 0))
+    steps = requests // (STEP * BATCH)
+    arrays = [base, new_key, new_value, cache_keys, cache_values, *deltas]
     return pl.pallas_call(
         functools.partial(attend_kernel, len(deltas)),
         out_shape=jax.ShapeDtypeStruct((requests, columns), jnp.bfloat16),
-        grid=(requests // block,),
-        in_specs=[SMEM, whole(lengths), rows2(columns), rows2(kv), rows2(kv), rows3, rows3]
-        + [rows2(d.shape[1]) for d in deltas],
-        out_specs=rows2(columns),
-        compiler_params=PARAMS,
+        in_specs=[SMEM, VMEM] + [ANY] * len(arrays),
+        out_specs=ANY,
+        scratch_shapes=[pltpu.VMEM(a.shape, jnp.bfloat16) for a in arrays]
+        + [
+            pltpu.VMEM((requests, columns), jnp.bfloat16),
+            pltpu.SemaphoreType.DMA((steps, len(arrays))),
+            pltpu.SemaphoreType.DMA((steps,)),
+        ],
         cost_estimate=pl.CostEstimate(
             flops=4 * requests * HALF * slots * columns,
             bytes_accessed=4 * requests * (columns + slots * kv),
             transcendentals=requests * slots * columns // 16,
         ),
-    )(me, lengths, base, new_key, new_value, cache_keys, cache_values, *deltas)
+    )(me, lengths, *arrays)
 
 
 def whole(array):
@@ -363,49 +377,41 @@
 
     shrink = shrink_factors.swapaxes(1, 2)
     block = jax.ShapeDtypeStruct((1, rank, features + outputs), jnp.bfloat16)
-    own, other = pl.pallas_call(
-        functools.partial(factor_kernel, square),
-        out_shape=[block, block],
-        in_specs=[SMEM, HBM, HBM],
-        out_specs=[VMEM, VMEM],
-        scratch_shapes=[pltpu.SemaphoreType.DMA((4,))],
-    )(me[None], shrink, expand_factors)
+    own, other, rows = pl.pallas_call(
+        functools.partial(cut_kernel, square),
+        out_shape=[
+            block,
+            block,
+            jax.ShapeDtypeStruct((square, requests, features + LANES), jnp.bfloat16),
+        ],
+        in_specs=[SMEM, SMEM, VMEM, HBM, HBM, HBM],
+        out_specs=[VMEM] * 3,
+        scratch_shapes=[pltpu.SemaphoreType.DMA((square + 4,))],
+    )(me[None], owner_map, adapter_ids.T, hidden, shrink, expand_factors)
+    own = lax.all_gather(own, "level", axis=0, tiled=True)
     other = swap(other, 1)
-    rows = pl.pallas_call(
-        functools.partial(row_kernel, square),
-        out_shape=jax.ShapeDtypeStruct((square, requests, features + LANES), jnp.bfloat16),
-        in_specs=[SMEM, VMEM, HBM],
-        out_specs=VMEM,
-        scratch_shapes=[pltpu.SemaphoreType.DMA((square,))],
-    )(owner_map, adapter_ids.T, hidden)
     rows = tied(rows, other)
     rows = lax.all_to_all(rows, ("rep", "side"), split_axis=0, concat_axis=0, tiled=True)
 
-    empty = jnp.zeros((square // 2 * requests, LANES), jnp.float32)
     order = jnp.arange(levels, dtype=jnp.int32)
+    own_ids = order * sides + side
+    partial = jnp.zeros((square // 2 * requests, LANES), jnp.float32)
     if levels == 4:
-        near_pairs = [(i, i ^ 1) for i in range(levels)]
-        far_pairs = [(i, i ^ 2) for i in range(levels)]
-
-        def gather(a):
-            far = lax.ppermute(a, "level", far_pairs)
-            near = lax.ppermute(a, "level", near_pairs)
-            inner = lax.ppermute(a, "level", [(1, 2), (2, 1)])
-            outer = lax.ppermute(far, "level", [(2, 3), (1, 0)])
-            return [a, near, far, jnp.where((level == 1) | (level == 2), inner, outer)]
-
-        own_ids = (level ^ order) * sides + side
-        next_ids = (level ^ order) * sides + (side ^ 1)
-        own, other = gather(own), gather(other)
-        partial = shrink_rows(own_ids, rows, own, empty, None)
-        partial = shrink_rows(next_ids, rows, other, partial, None)
-        factors, ids, chunk = own + other, jnp.concatenate([own_ids, next_ids]), None
+        other = [other] + [
+            lax.ppermute(other, "level", [(i, i ^ k) for i in range(levels)])
+            for k in range(1, levels)
+        ]
+        other_ids = (level ^ order) * sides + (side ^ 1)
+        chunk = None
+        partial = shrink_rows(own_ids, rows, [own], partial, chunk)
+        partial = shrink_rows(other_ids, rows, other, partial, chunk)
+        factors, ids = [own] + other, jnp.concatenate([own_ids, other_ids])
     else:
-        both = jnp.concatenate([own, other], axis=0)
-        factors = [lax.all_gather(both, "level", axis=0, tiled=True)]
-        ids = (order[:, None] * sides + jnp.stack([side, side ^ 1])[None, :]).reshape(-1)
+        other = lax.all_gather(other, "level", axis=0, tiled=True)
+        factors = [jnp.concatenate([own, other], axis=0)]
+        ids = jnp.concatenate([own_ids, order * sides + (side ^ 1)])
         chunk = 4
-        partial = shrink_rows(ids, rows, factors, empty, chunk)
+        partial = shrink_rows(ids, rows, factors, partial, chunk)
 
     for c in range(1, tp):
         partial = partial + lax.ppermute(partial, "tp", [(t, t ^ c) for t in range(tp)])

time: 76.2 us -> 80.2 us (1.052)
  blocking collectives: 0 us -> 31.9 us
  waiting for transfers between devices: 28.2 us -> 14.5 us
  starting transfers between devices: 28.7 us -> 18.6 us
  local copies, waits for them, and re-layouts: 6.04 us -> 2.12 us
    all_gather x0 -> x1, blocking collectives: none -> 31.9 us  [per_device(): own = lax.all_gather(own, 'level', axis=0, tiled=True)]
    ppermute x8 -> x3, waiting for transfers between devices: 16.8 us -> 0.01 us  [per_device(): lax.ppermute(other, 'level', [(i, i ^ k) for i in range(levels)])]
    ppermute x8 -> x3, starting transfers between devices: 15 us -> 4.39 us  [per_device(): lax.ppermute(other, 'level', [(i, i ^ k) for i in range(levels)])]
    unnamed x22 -> x12, local copies, waits for them, and re-layouts: 5.82 us -> 1.29 us
    ppermute x7, waiting for transfers between devices: 10.2 us -> 13.3 us  [swap(): return lax.ppermute(a, ('rep', 'side'), pairs)]
    pallas_call x1, Pallas kernels: 3.27 us -> 5.46 us  [attend(): pl.pallas_call(functools.partial(attend_kernel, len(deltas)), out_shape=j...]
    pallas_call x2 -> x1, Pallas kernels: 4.68 us -> 3.3 us  [per_device(): pl.pallas_call(functools.partial(cut_kernel, square), out_shape=[block, b...]
  transfers between devices with their start and end apart: 17 -> 12, of which waited for: 9 -> 8; matrix products, arithmetic and copies ran while one was open for 0% -> 1% of each run, Pallas kernels for 6% -> 2%
where the time goes in v7:
time: 80.2 us; the launch traced here: 79.9 us
  blocking collectives  31.9 us (40%)
  starting transfers between devices  18.6 us (23%)
  waiting for transfers between devices  14.5 us (18%)
  Pallas kernels  12.6 us (16%)
  local copies, waits for them, and re-layouts  2.12 us (3%)
    all_gather x1, blocking collectives, per_device(): own = lax.all_gather(own, 'level', axis=0, tiled=True)  31.9 us
    ppermute x7, waiting for transfers between devices, swap(): return lax.ppermute(a, ('rep', 'side'), pairs)  13.3 us
    ppermute x7, starting transfers between devices, swap(): return lax.ppermute(a, ('rep', 'side'), pairs)  10 us
    pallas_call x1, Pallas kernels, attend(): pl.pallas_call(functools.partial(attend_kernel, len(deltas)), out_shape=j...  5.46 us
    ppermute x3, starting transfers between devices, per_device(): lax.ppermute(other, 'level', [(i, i ^ k) for i in range(levels)])  4.39 us
    all_to_all x1, starting transfers between devices, per_device(): lax.all_to_all(rows, ('rep', 'side'), split_axis=0, concat_axis=0, tiled=...  4.1 us
    pallas_call x1, Pallas kernels, per_device(): pl.pallas_call(functools.partial(cut_kernel, square), out_shape=[block, b...  3.3 us
    pallas_call x2, Pallas kernels, shrink_rows(): pl.pallas_call(functools.partial(shrink_kernel, parts, len(weights), chun...  2.81 us
  transfers between devices with their start and end apart: 12, of which 8 were waited for; matrix products, arithmetic and copies ran while one was open for 1% of the time, Pallas kernels for 2%

profile of v7, /device:TPU:0, one launch (start us, length us, event | category | flops | bytes accessed | tf_op | source)
XLA Modules:
  0.0 79.9 jit_solution(16346507601577649506)
XLA Ops:
  0.0 3.3 %shard_map.109 = (bf16[1,64,1536]{2,1,0:T(8,128)(2,1)}, bf16[1,64,1536]{2,1,0:T(8,128)(2,1)}, bf16[4,128,1152]{2,1,0:T(8,128)(2,1)}) custom-call(s32[1]{0:T(128)} %bitcast.me_ref, s32[8]{0:T(128)} %map_ref.1, s32[1,128]{1,0:T(1,128)} %bitcast.6, bf16[128,4096]{1,0:T(8,128)(2,1)} %hidden_ref.1, bf16[1,64,4096]{2,1,0:T(8,128)(2,1)} %bitcast.5, ...), custom_call_target="tpu_custom_call" | custom-call | tf_op jit(solution)/shard_map/pallas_call | solution.py:380
  3.3 3.0 %collective-permute-start = (bf16[1,64,1536]{2,1,0:T(8,128)(2,1)}, bf16[1,64,1536]{2,1,0:T(8,128)(2,1)S(1)}, u32[]{:S(2)}, u32[]{:S(2)}) collective-permute-start(bf16[1,64,1536]{2,1,0:T(8,128)(2,1)} %get-tuple-element.14), channel_id=1, source_target_pairs={{0,2},{2,0},{16,18},{18,16},{1,3},{3,1},{17,19},{19,17},{4,6},{6,4... | collective-permute-start | bytes 589832 | tf_op jit(solution)/shard_map/ppermute | solution.py:373
  6.3 5.1 %collective-permute-done.refs_1_.refs_5_ = bf16[1,64,1536]{2,1,0:T(8,128)(2,1)S(1)} collective-permute-done((bf16[1,64,1536]{2,1,0:T(8,128)(2,1)}, bf16[1,64,1536]{2,1,0:T(8,128)(2,1)S(1)}, u32[]{:S(2)}, u32[]{:S(2)}) %collective-permute-start) | collective-permute-done | bytes 196640 | tf_op jit(solution)/shard_map/ppermute | solution.py:373
  11.4 4.1 %all-to-all-start = ((bf16[4,128,1152]{2,1,0:T(8,128)(2,1)}), bf16[4,128,1152]{2,1,0:T(8,128)(2,1)S(1)}, u32[]{:S(2)}, u32[]{:S(2)}) async-start(bf16[4,128,1152]{2,1,0:T(8,128)(2,1)} %get-tuple-element.15), calls=%async_computation | async-start | bytes 2359296 | tf_op jit(solution)/shard_map/all_to_all | solution.py:394
  15.5 1.6 %collective-permute-start.1 = (bf16[1,64,1536]{2,1,0:T(8,128)(2,1)S(1)}, bf16[1,64,1536]{2,1,0:T(8,128)(2,1)S(1)}, u32[]{:S(2)}, u32[]{:S(2)}) collective-permute-start(bf16[1,64,1536]{2,1,0:T(8,128)(2,1)S(1)} %collective-permute-done.refs_1_.refs_5_), channel_id=1, source_target_pairs={{0,4},{4,0},{8,12},{12,8},{1,5},{5,1},{9,13},{13,9},{2,6},{6,2},{1... | collective-permute-start | bytes 589832 | tf_op jit(solution)/shard_map/ppermute | solution.py:401
  17.1 2.6 %collective-permute-start.2 = (bf16[1,64,1536]{2,1,0:T(8,128)(2,1)S(1)}, bf16[1,64,1536]{2,1,0:T(8,128)(2,1)S(1)}, u32[]{:S(2)}, u32[]{:S(2)}) collective-permute-start(bf16[1,64,1536]{2,1,0:T(8,128)(2,1)S(1)} %collective-permute-done.refs_1_.refs_5_), channel_id=1, source_target_pairs={{0,8},{4,12},{8,0},{12,4},{1,9},{5,13},{9,1},{13,5},{2,10},{6,14},... | collective-permute-start | bytes 589832 | tf_op jit(solution)/shard_map/ppermute | solution.py:401
  19.9 31.9 %all_gather.3.refs_1_.refs_4_ = bf16[4,64,1536]{2,1,0:T(8,128)(2,1)S(1)} all-gather(bf16[1,64,1536]{2,1,0:T(8,128)(2,1)S(1)} %copy-done.1), channel_id=1, replica_groups=mesh['rep'=2,'level'=4,'side'=2,'tp'=2] {'level'}, dimensions={0}, use_global_device_ids=true | all-gather | bytes 983040 | tf_op jit(solution)/shard_map/all_gather | solution.py:391
  51.8 1.4 %shard_map.110.refs_5_ = f32[256,128]{1,0:T(8,128)S(1)} custom-call(s32[4]{0:T(128)S(1)} %get-tuple-element.22.ids_ref, bf16[4,128,1152]{2,1,0:T(8,128)(2,1)S(1)} %all-to-all-done.refs_0_.rows_ref, bf16[4,64,1536]{2,1,0:T(8,128)(2,1)S(1)} %all_gather.3.refs_1_.refs_4_, f32[256,128]{1,0:T(8,128)S(1)} %broadcast_in_dim.9.refs_2_), custom_call_target="tpu_custom_call" | custom-call | tf_op jit(solution)/shard_map/pallas_call | solution.py:320
  53.3 1.4 %shard_map.111 = f32[256,128]{1,0:T(8,128)S(1)} custom-call(s32[4]{0:T(128)S(1)} %get-tuple-element.21.ids_ref, bf16[4,128,1152]{2,1,0:T(8,128)(2,1)S(1)} %all-to-all-done.refs_0_.rows_ref, bf16[1,64,1536]{2,1,0:T(8,128)(2,1)S(1)} %collective-permute-done.refs_1_.refs_5_, bf16[1,64,1536]{2,1,0:T(8,128)(2,1)S(1)} %collective-permute-done.1.refs_2_.refs_6_, ...), custom_call_target="tpu_custom_call" | custom-call | tf_op jit(solution)/shard_map/pallas_call | solution.py:320
  54.9 1.2 %collective-permute-done.4 = f32[256,128]{1,0:T(8,128)S(1)} collective-permute-done((f32[256,128]{1,0:T(8,128)S(1)}, f32[256,128]{1,0:T(8,128)S(1)}, u32[]{:S(2)}, u32[]{:S(2)}) %collective-permute-start.4) | collective-permute-done | bytes 131104 | tf_op jit(solution)/shard_map/ppermute | solution.py:417
  56.1 1.8 %collective-permute-start.5 = (bf16[256,128]{1,0:T(8,128)(2,1)S(1)}, bf16[256,128]{1,0:T(8,128)(2,1)S(1)}, u32[]{:S(2)}, u32[]{:S(2)}) collective-permute-start(bf16[256,128]{1,0:T(8,128)(2,1)S(1)} %add_convert_fusion.refs_0_), channel_id=1, source_target_pairs={{0,2},{2,0},{16,18},{18,16},{1,3},{3,1},{17,19},{19,17},{4,6},{6,4... | collective-permute-start | bytes 196616 | tf_op jit(solution)/shard_map/ppermute | solution.py:373
  57.9 1.5 %collective-permute-start.6 = (bf16[256,128]{1,0:T(8,128)(2,1)S(1)}, bf16[256,128]{1,0:T(8,128)(2,1)S(1)}, u32[]{:S(2)}, u32[]{:S(2)}) collective-permute-start(bf16[256,128]{1,0:T(8,128)(2,1)S(1)} %add_convert_fusion.refs_0_), channel_id=1, source_target_pairs={{0,16},{2,18},{16,0},{18,2},{1,17},{3,19},{17,1},{19,3},{4,20},{6,... | collective-permute-start | bytes 196616 | tf_op jit(solution)/shard_map/ppermute | solution.py:373
  59.8 0.7 collective-permute-done.5.refs_1_
  60.5 1.7 %collective-permute-done.6.refs_2_ = bf16[256,128]{1,0:T(8,128)(2,1)S(1)} collective-permute-done((bf16[256,128]{1,0:T(8,128)(2,1)S(1)}, bf16[256,128]{1,0:T(8,128)(2,1)S(1)}, u32[]{:S(2)}, u32[]{:S(2)}) %collective-permute-start.6) | collective-permute-done | bytes 65568 | tf_op jit(solution)/shard_map/ppermute | solution.py:373
  62.2 2.4 %collective-permute-done.7.refs_3_ = bf16[256,128]{1,0:T(8,128)(2,1)S(1)} collective-permute-done((bf16[256,128]{1,0:T(8,128)(2,1)S(1)}, bf16[256,128]{1,0:T(8,128)(2,1)S(1)}, u32[]{:S(2)}, u32[]{:S(2)}) %collective-permute-start.7) | collective-permute-done | bytes 65568 | tf_op jit(solution)/shard_map/ppermute | solution.py:373
  64.6 1.1 %shard_map.112 = (bf16[128,512]{1,0:T(8,128)(2,1)S(1)}, bf16[128,512]{1,0:T(8,128)(2,1)S(1)}, bf16[128,512]{1,0:T(8,128)(2,1)S(1)}, bf16[128,512]{1,0:T(8,128)(2,1)S(1)}) custom-call(s32[8]{0:T(128)S(1)} %pad_add_fusion.ids_ref, s32[1]{0:T(128)} %bitcast.me_ref, bf16[4,128,1152]{2,1,0:T(8,128)(2,1)S(1)} %all-to-all-done.refs_0_.rows_ref, ...), custom_call_target="tpu_custom_call" | custom-call | tf_op jit(solution)/shard_map/pallas_call | solution.py:335
  65.6 0.6 copy-done
  66.7 1.6 %collective-permute-start.8 = (bf16[128,512]{1,0:T(8,128)(2,1)S(1)}, bf16[128,512]{1,0:T(8,128)(2,1)S(1)}, u32[]{:S(2)}, u32[]{:S(2)}) collective-permute-start(bf16[128,512]{1,0:T(8,128)(2,1)S(1)} %get-tuple-element.18), channel_id=1, source_target_pairs={{0,2},{2,0},{16,18},{18,16},{1,3},{3,1},{17,19},{19,17},{4,6},{6,4... | collective-permute-start | bytes 393224 | tf_op jit(solution)/shard_map/ppermute | solution.py:373
  68.3 1.5 %collective-permute-start.9 = (bf16[128,512]{1,0:T(8,128)(2,1)S(1)}, bf16[128,512]{1,0:T(8,128)(2,1)S(1)}, u32[]{:S(2)}, u32[]{:S(2)}) collective-permute-start(bf16[128,512]{1,0:T(8,128)(2,1)S(1)} %get-tuple-element.19), channel_id=1, source_target_pairs={{0,16},{2,18},{16,0},{18,2},{1,17},{3,19},{17,1},{19,3},{4,20},{6,... | collective-permute-start | bytes 393224 | tf_op jit(solution)/shard_map/ppermute | solution.py:373
  69.8 0.7 copy.15.len_ref
  70.4 2.0 %collective-permute-done.10.refs_8_ = bf16[128,512]{1,0:T(8,128)(2,1)S(1)} collective-permute-done((bf16[128,512]{1,0:T(8,128)(2,1)S(1)}, bf16[128,512]{1,0:T(8,128)(2,1)S(1)}, u32[]{:S(2)}, u32[]{:S(2)}) %collective-permute-start.10) | collective-permute-done | bytes 131104 | tf_op jit(solution)/shard_map/ppermute | solution.py:373
  73.0 0.8 collective-permute-done.9.refs_7_
  73.8 0.6 copy-done.4
  74.5 5.5 %shard_map.113 = bf16[128,2048]{1,0:T(8,128)(2,1)} custom-call(s32[1]{0:T(128)} %bitcast.me_ref, s32[16,128]{1,0:T(8,128)} %copy.15.len_ref, bf16[128,2048]{1,0:T(8,128)(2,1)} %refs_0_.1, bf16[128,256]{1,0:T(8,128)(2,1)} %refs_1_.1, bf16[128,256]{1,0:T(8,128)(2,1)} %refs_2_.1, bf16[128,16,256]{2,1,0:T(8,128)(2,1)} %refs_3_.1, bf16[128,16,256]{2,1,0:T(8,128)(2,1)} %refs_4_.1, ...), custom_call_target="tpu_custom_call" | custom-call | flops 134217728 | bytes 3145728 | tf_op jit(solution)/shard_map/pallas_call | solution.py:285
  (26 shorter events, 1.8 us)
Async XLA Ops:
  3.3 8.1 %collective-permute-start = (bf16[1,64,1536]{2,1,0:T(8,128)(2,1)}, bf16[1,64,1536]{2,1,0:T(8,128)(2,1)S(1)}, u32[]{:S(2)}, u32[]{:S(2)}) collective-permute-start(bf16[1,64,1536]{2,1,0:T(8,128)(2,1)} %get-tuple-element.14), channel_id=1, source_target_pairs={{0,2},{2,0},{16,18},{18,16},{1,3},{3,1},{17,19},{19,17},{4,6},{6,4... | collective-permute-start | bytes 589832 | tf_op jit(solution)/shard_map/ppermute | solution.py:373
  11.4 8.5 %copy-start.1 = (bf16[1,64,1536]{2,1,0:T(8,128)(2,1)S(1)}, bf16[1,64,1536]{2,1,0:T(8,128)(2,1)}, u32[]{:S(2)}) copy-start(bf16[1,64,1536]{2,1,0:T(8,128)(2,1)} %get-tuple-element.16) | copy-start | bytes 589828
  11.4 40.4 %all-to-all-start = ((bf16[4,128,1152]{2,1,0:T(8,128)(2,1)}), bf16[4,128,1152]{2,1,0:T(8,128)(2,1)S(1)}, u32[]{:S(2)}, u32[]{:S(2)}) async-start(bf16[4,128,1152]{2,1,0:T(8,128)(2,1)} %get-tuple-element.15), calls=%async_computation | async-start | bytes 2359296 | tf_op jit(solution)/shard_map/all_to_all | solution.py:394
  15.5 37.7 %collective-permute-start.1 = (bf16[1,64,1536]{2,1,0:T(8,128)(2,1)S(1)}, bf16[1,64,1536]{2,1,0:T(8,128)(2,1)S(1)}, u32[]{:S(2)}, u32[]{:S(2)}) collective-permute-start(bf16[1,64,1536]{2,1,0:T(8,128)(2,1)S(1)} %collective-permute-done.refs_1_.refs_5_), channel_id=1, source_target_pairs={{0,4},{4,0},{8,12},{12,8},{1,5},{5,1},{9,13},{13,9},{2,6},{6,2},{1... | collective-permute-start | bytes 589832 | tf_op jit(solution)/shard_map/ppermute | solution.py:401
  17.1 36.2 %collective-permute-start.2 = (bf16[1,64,1536]{2,1,0:T(8,128)(2,1)S(1)}, bf16[1,64,1536]{2,1,0:T(8,128)(2,1)S(1)}, u32[]{:S(2)}, u32[]{:S(2)}) collective-permute-start(bf16[1,64,1536]{2,1,0:T(8,128)(2,1)S(1)} %collective-permute-done.refs_1_.refs_5_), channel_id=1, source_target_pairs={{0,8},{4,12},{8,0},{12,4},{1,9},{5,13},{9,1},{13,5},{2,10},{6,14},... | collective-permute-start | bytes 589832 | tf_op jit(solution)/shard_map/ppermute | solution.py:401
  19.7 33.6 %collective-permute-start.3 = (bf16[1,64,1536]{2,1,0:T(8,128)(2,1)S(1)}, bf16[1,64,1536]{2,1,0:T(8,128)(2,1)S(1)}, u32[]{:S(2)}, u32[]{:S(2)}) collective-permute-start(bf16[1,64,1536]{2,1,0:T(8,128)(2,1)S(1)} %collective-permute-done.refs_1_.refs_5_), channel_id=1, source_target_pairs={{0,12},{4,8},{8,4},{12,0},{1,13},{5,9},{9,5},{13,1},{2,14},{6,10},... | collective-permute-start | bytes 589832 | tf_op jit(solution)/shard_map/ppermute | solution.py:401
  53.2 1.5 %copy-start.5 = (s32[128]{0:T(128)S(1)}, s32[128]{0:T(128)}, u32[]{:S(2)}) copy-start(s32[128]{0:T(128)} %param.21) | copy-start | bytes 1540
  54.7 1.4 %collective-permute-start.4 = (f32[256,128]{1,0:T(8,128)S(1)}, f32[256,128]{1,0:T(8,128)S(1)}, u32[]{:S(2)}, u32[]{:S(2)}) collective-permute-start(f32[256,128]{1,0:T(8,128)S(1)} %shard_map.111), channel_id=1, source_target_pairs={{0,1},{1,0},{2,3},{3,2},{4,5},{5,4},{6,7},{7,6},{8,9},{9,8},{10,11... | collective-permute-start | bytes 393224 | tf_op jit(solution)/shard_map/ppermute | solution.py:417
  56.1 4.3 %collective-permute-start.5 = (bf16[256,128]{1,0:T(8,128)(2,1)S(1)}, bf16[256,128]{1,0:T(8,128)(2,1)S(1)}, u32[]{:S(2)}, u32[]{:S(2)}) collective-permute-start(bf16[256,128]{1,0:T(8,128)(2,1)S(1)} %add_convert_fusion.refs_0_), channel_id=1, source_target_pairs={{0,2},{2,0},{16,18},{18,16},{1,3},{3,1},{17,19},{19,17},{4,6},{6,4... | collective-permute-start | bytes 196616 | tf_op jit(solution)/shard_map/ppermute | solution.py:373
  57.9 4.3 %collective-permute-start.6 = (bf16[256,128]{1,0:T(8,128)(2,1)S(1)}, bf16[256,128]{1,0:T(8,128)(2,1)S(1)}, u32[]{:S(2)}, u32[]{:S(2)}) collective-permute-start(bf16[256,128]{1,0:T(8,128)(2,1)S(1)} %add_convert_fusion.refs_0_), channel_id=1, source_target_pairs={{0,16},{2,18},{16,0},{18,2},{1,17},{3,19},{17,1},{19,3},{4,20},{6,... | collective-permute-start | bytes 196616 | tf_op jit(solution)/shard_map/ppermute | solution.py:373
  59.4 5.2 %collective-permute-start.7 = (bf16[256,128]{1,0:T(8,128)(2,1)S(1)}, bf16[256,128]{1,0:T(8,128)(2,1)S(1)}, u32[]{:S(2)}, u32[]{:S(2)}) collective-permute-start(bf16[256,128]{1,0:T(8,128)(2,1)S(1)} %add_convert_fusion.refs_0_), channel_id=1, source_target_pairs={{0,18},{2,16},{16,2},{18,0},{1,19},{3,17},{17,3},{19,1},{4,22},{6,... | collective-permute-start | bytes 196616 | tf_op jit(solution)/shard_map/ppermute | solution.py:373
  65.6 0.6 copy-start
  66.3 6.2 %collective-permute-start.10 = (bf16[128,512]{1,0:T(8,128)(2,1)S(1)}, bf16[128,512]{1,0:T(8,128)(2,1)S(1)}, u32[]{:S(2)}, u32[]{:S(2)}) collective-permute-start(bf16[128,512]{1,0:T(8,128)(2,1)S(1)} %get-tuple-element.20), channel_id=1, source_target_pairs={{0,18},{2,16},{16,2},{18,0},{1,19},{3,17},{17,3},{19,1},{4,22},{6,... | collective-permute-start | bytes 393224 | tf_op jit(solution)/shard_map/ppermute | solution.py:373
  66.7 6.3 %collective-permute-start.8 = (bf16[128,512]{1,0:T(8,128)(2,1)S(1)}, bf16[128,512]{1,0:T(8,128)(2,1)S(1)}, u32[]{:S(2)}, u32[]{:S(2)}) collective-permute-start(bf16[128,512]{1,0:T(8,128)(2,1)S(1)} %get-tuple-element.18), channel_id=1, source_target_pairs={{0,2},{2,0},{16,18},{18,16},{1,3},{3,1},{17,19},{19,17},{4,6},{6,4... | collective-permute-start | bytes 393224 | tf_op jit(solution)/shard_map/ppermute | solution.py:373
  68.3 5.5 %collective-permute-start.9 = (bf16[128,512]{1,0:T(8,128)(2,1)S(1)}, bf16[128,512]{1,0:T(8,128)(2,1)S(1)}, u32[]{:S(2)}, u32[]{:S(2)}) collective-permute-start(bf16[128,512]{1,0:T(8,128)(2,1)S(1)} %get-tuple-element.19), channel_id=1, source_target_pairs={{0,16},{2,18},{16,0},{18,2},{1,17},{3,19},{17,1},{19,3},{4,20},{6,... | collective-permute-start | bytes 393224 | tf_op jit(solution)/shard_map/ppermute | solution.py:373
  72.5 1.3 %copy-start.2 = (bf16[128,512]{1,0:T(8,128)(2,1)}, bf16[128,512]{1,0:T(8,128)(2,1)S(1)}, u32[]{:S(2)}) copy-start(bf16[128,512]{1,0:T(8,128)(2,1)S(1)} %collective-permute-done.10.refs_8_) | copy-start | bytes 393220
  73.0 0.8 %copy-start.3 = (bf16[128,512]{1,0:T(8,128)(2,1)}, bf16[128,512]{1,0:T(8,128)(2,1)S(1)}, u32[]{:S(2)}) copy-start(bf16[128,512]{1,0:T(8,128)(2,1)S(1)} %collective-permute-done.8.refs_6_) | copy-start | bytes 393220
  73.8 0.6 copy-start.4

commit v8 on v5

--- a/solution.py
+++ b/solution.py
@@ -23,20 +23,22 @@
 TN = (((0,), (0,)), ((), ()))
 
 
+def beside(us):
+    return pl.CostEstimate(flops=0, bytes_accessed=us * 3_690_000, transcendentals=0)
+
+
 def columns(at, width):
     return pl.ds(pl.multiple_of(at * width, width), width)
 
 
 def factor_kernel(parts, me_ref, shrink_ref, expand_ref, own_ref, next_ref, sems):
     features, outputs = shrink_ref.shape[2] // parts, expand_ref.shape[2] // parts
-    copies = []
-    for k, (at, ref) in enumerate(((me_ref[0] ^ 1, next_ref), (me_ref[0], own_ref))):
-        shrink = shrink_ref.at[:, :, columns(at, features)]
-        expand = expand_ref.at[:, :, columns(at, outputs)]
-        copies += [
-            pltpu.make_async_copy(shrink, ref.at[:, :, :features], sems.at[2 * k]),
-            pltpu.make_async_copy(expand, ref.at[:, :, features:], sems.at[2 * k + 1]),
-        ]
+    me = me_ref[0]
+    moves = []
+    for at, ref in ((me ^ 1, next_ref), (me, own_ref)):
+        moves.append((shrink_ref.at[:, :, columns(at, features)], ref.at[:, :, :features]))
+        moves.append((expand_ref.at[:, :, columns(at, outputs)], ref.at[:, :, features:]))
+    copies = [pltpu.make_async_copy(src, dst, sems.at[k]) for k, (src, dst) in enumerate(moves)]
     for copy in copies:
         copy.start()
     for copy in copies:
@@ -166,11 +168,11 @@
                 out_refs[s][...] = total_ref[s].astype(jnp.bfloat16)
 
 
-def attend_kernel(
-    parts, me_ref, len_ref, base_ref, nk_ref, nv_ref, ck_ref, cv_ref, *refs
-):
-    delta_refs, out_ref = refs[:parts], refs[parts]
+def attend_kernel(parts, me_ref, len_ref, *refs):
+    base_ref, nk_ref, nv_ref, ck_ref, cv_ref, *delta_refs, out_ref = refs
     me = me_ref[0]
+    block = STEP * BATCH
+    steps = base_ref.shape[0] // block
     requests, columns = base_ref.shape
     width = columns // parts
     groups = nk_ref.shape[1] // HEAD
@@ -197,11 +199,10 @@
     scale = 1.0 / math.sqrt(HEAD)
     ones = jnp.ones((keys_in, HEAD), jnp.bfloat16)
 
-    if True:
-        step = pl.program_id(0)
+    for step in range(steps):
         units = []
         for j in range(BATCH):
-            start = j * STEP
+            start = step * block + j * STEP
             at = pl.ds(start, STEP)
             pieces = []
             for s in range(parts):
@@ -268,23 +269,19 @@
     kv = new_key.shape[1]
     slots = cache_keys.shape[1]
     lengths = jnp.tile(lengths.reshape(requests // HALF, HALF), (1, columns // HEAD))
-    block = STEP * BATCH
-    rows2 = lambda w: pl.BlockSpec((block, w), lambda i: (i, 0))
-    rows3 = pl.BlockSpec((block, slots, kv), lambda i: (i, 0, 0))
+    arrays = [base, new_key, new_value, cache_keys, cache_values, *deltas]
     return pl.pallas_call(
         functools.partial(attend_kernel, len(deltas)),
         out_shape=jax.ShapeDtypeStruct((requests, columns), jnp.bfloat16),
-        grid=(requests // block,),
-        in_specs=[SMEM, whole(lengths), rows2(columns), rows2(kv), rows2(kv), rows3, rows3]
-        + [rows2(d.shape[1]) for d in deltas],
-        out_specs=rows2(columns),
+        in_specs=[SMEM] + [VMEM] * (1 + len(arrays)),
+        out_specs=VMEM,
         compiler_params=PARAMS,
         cost_estimate=pl.CostEstimate(
             flops=4 * requests * HALF * slots * columns,
             bytes_accessed=4 * requests * (columns + slots * kv),
             transcendentals=requests * slots * columns // 16,
         ),
-    )(me, lengths, base, new_key, new_value, cache_keys, cache_values, *deltas)
+    )(me, lengths, *arrays)
 
 
 def whole(array):
@@ -310,6 +307,7 @@
         in_specs=[SMEM, whole(rows), *specs, whole(base)],
         out_specs=whole(base),
         compiler_params=PARAMS,
+        cost_estimate=beside(10),
     )(ids, rows, *weights, base)
 
 
@@ -329,6 +327,7 @@
             pltpu.VMEM(held, jnp.float32),
         ],
         compiler_params=PARAMS,
+        cost_estimate=beside(20),
     )(ids, me, rows, *lows, *weights)
 
 
@@ -367,45 +366,41 @@
         functools.partial(factor_kernel, square),
         out_shape=[block, block],
         in_specs=[SMEM, HBM, HBM],
-        out_specs=[VMEM, VMEM],
+        out_specs=[VMEM] * 2,
         scratch_shapes=[pltpu.SemaphoreType.DMA((4,))],
     )(me[None], shrink, expand_factors)
-    other = swap(other, 1)
+    own = lax.all_gather(own, "level", axis=0, tiled=True)
     rows = pl.pallas_call(
         functools.partial(row_kernel, square),
         out_shape=jax.ShapeDtypeStruct((square, requests, features + LANES), jnp.bfloat16),
         in_specs=[SMEM, VMEM, HBM],
         out_specs=VMEM,
         scratch_shapes=[pltpu.SemaphoreType.DMA((square,))],
+        cost_estimate=beside(100),
     )(owner_map, adapter_ids.T, hidden)
+    other = swap(other, 1)
     rows = tied(rows, other)
     rows = lax.all_to_all(rows, ("rep", "side"), split_axis=0, concat_axis=0, tiled=True)
 
-    empty = jnp.zeros((square // 2 * requests, LANES), jnp.float32)
     order = jnp.arange(levels, dtype=jnp.int32)
+    own_ids = order * sides + side
+    partial = jnp.zeros((square // 2 * requests, LANES), jnp.float32)
     if levels == 4:
-        near_pairs = [(i, i ^ 1) for i in range(levels)]
-        far_pairs = [(i, i ^ 2) for i in range(levels)]
-
-        def gather(a):
-            far = lax.ppermute(a, "level", far_pairs)
-            near = lax.ppermute(a, "level", near_pairs)
-            inner = lax.ppermute(a, "level", [(1, 2), (2, 1)])
-            outer = lax.ppermute(far, "level", [(2, 3), (1, 0)])
-            return [a, near, far, jnp.where((level == 1) | (level == 2), inner, outer)]
-
-        own_ids = (level ^ order) * sides + side
-        next_ids = (level ^ order) * sides + (side ^ 1)
-        own, other = gather(own), gather(other)
-        partial = shrink_rows(own_ids, rows, own, empty, None)
-        partial = shrink_rows(next_ids, rows, other, partial, None)
-        factors, ids, chunk = own + other, jnp.concatenate([own_ids, next_ids]), None
+        other = [other] + [
+            lax.ppermute(other, "level", [(i, i ^ k) for i in range(levels)])
+            for k in range(1, levels)
+        ]
+        other_ids = (level ^ order) * sides + (side ^ 1)
+        chunk = None
+        partial = shrink_rows(own_ids, rows, [own], partial, chunk)
+        partial = shrink_rows(other_ids, rows, other, partial, chunk)
+        factors, ids = [own] + other, jnp.concatenate([own_ids, other_ids])
     else:
-        both = jnp.concatenate([own, other], axis=0)
-        factors = [lax.all_gather(both, "level", axis=0, tiled=True)]
-        ids = (order[:, None] * sides + jnp.stack([side, side ^ 1])[None, :]).reshape(-1)
+        other = lax.all_gather(other, "level", axis=0, tiled=True)
+        factors = [jnp.concatenate([own, other], axis=0)]
+        ids = jnp.concatenate([own_ids, order * sides + (side ^ 1)])
         chunk = 4
-        partial = shrink_rows(ids, rows, factors, empty, chunk)
+        partial = shrink_rows(ids, rows, factors, partial, chunk)
 
     for c in range(1, tp):
         partial = partial + lax.ppermute(partial, "tp", [(t, t ^ c) for t in range(tp)])

time: 76.2 us -> 81.6 us (1.071)
  blocking collectives: 0 us -> 31.9 us
  waiting for transfers between devices: 28.2 us -> 12.3 us
  starting transfers between devices: 28.7 us -> 18.5 us
    all_gather x0 -> x1, blocking collectives: none -> 31.9 us  [per_device(): own = lax.all_gather(own, 'level', axis=0, tiled=True)]
    ppermute x8 -> x3, waiting for transfers between devices: 16.8 us -> 0.01 us  [per_device(): lax.ppermute(other, 'level', [(i, i ^ k) for i in range(levels)])]
    ppermute x8 -> x3, starting transfers between devices: 15 us -> 4.39 us  [per_device(): lax.ppermute(other, 'level', [(i, i ^ k) for i in range(levels)])]
    ppermute x7, waiting for transfers between devices: 10.2 us -> 11.2 us  [swap(): return lax.ppermute(a, ('rep', 'side'), pairs)]
  transfers between devices with their start and end apart: 17 -> 12, of which waited for: 9 -> 8; matrix products, arithmetic and copies ran while one was open for 0% -> 0% of each run, Pallas kernels for 6% -> 5%
where the time goes in v8:
time: 81.6 us; the launch traced here: 81.1 us
  blocking collectives  31.9 us (39%)
  starting transfers between devices  18.5 us (23%)
  waiting for transfers between devices  12.3 us (15%)
  Pallas kernels  12.1 us (15%)
  local copies, waits for them, and re-layouts  6.04 us (7%)
    all_gather x1, blocking collectives, per_device(): own = lax.all_gather(own, 'level', axis=0, tiled=True)  31.9 us
    ppermute x7, waiting for transfers between devices, swap(): return lax.ppermute(a, ('rep', 'side'), pairs)  11.2 us
    ppermute x7, starting transfers between devices, swap(): return lax.ppermute(a, ('rep', 'side'), pairs)  10 us
    unnamed x22, local copies, waits for them, and re-layouts  5.82 us
    ppermute x3, starting transfers between devices, per_device(): lax.ppermute(other, 'level', [(i, i ^ k) for i in range(levels)])  4.39 us
    all_to_all x1, starting transfers between devices, per_device(): lax.all_to_all(rows, ('rep', 'side'), split_axis=0, concat_axis=0, tiled=...  3.97 us
    pallas_call x1, Pallas kernels, per_device(): pl.pallas_call(functools.partial(row_kernel, square), out_shape=jax.Shape...  2.94 us
    pallas_call x1, Pallas kernels, attend(): pl.pallas_call(functools.partial(attend_kernel, len(deltas)), out_shape=j...  2.86 us
  transfers between devices with their start and end apart: 12, of which 8 were waited for; matrix products, arithmetic and copies ran while one was open for 0% of the time, Pallas kernels for 5%

profile of v8, /device:TPU:0, one launch (start us, length us, event | category | flops | bytes accessed | tf_op | source)
XLA Modules:
  0.0 81.1 jit_solution(13589643180332419466)
XLA Ops:
  0.0 1.8 %shard_map.110 = (bf16[1,64,1536]{2,1,0:T(8,128)(2,1)}, bf16[1,64,1536]{2,1,0:T(8,128)(2,1)}) custom-call(s32[1]{0:T(128)} %bitcast.me_ref, bf16[1,64,4096]{2,1,0:T(8,128)(2,1)} %bitcast.5, bf16[1,64,2048]{2,1,0:T(8,128)(2,1)} %expand_ref.1), custom_call_target="tpu_custom_call" | custom-call | tf_op jit(solution)/shard_map/pallas_call | solution.py:365
  1.8 3.0 %collective-permute-start = (bf16[1,64,1536]{2,1,0:T(8,128)(2,1)}, bf16[1,64,1536]{2,1,0:T(8,128)(2,1)S(1)}, u32[]{:S(2)}, u32[]{:S(2)}) collective-permute-start(bf16[1,64,1536]{2,1,0:T(8,128)(2,1)} %get-tuple-element.12), channel_id=1, source_target_pairs={{0,2},{2,0},{16,18},{18,16},{1,3},{3,1},{17,19},{19,17},{4,6},{6,4... | collective-permute-start | bytes 589832 | tf_op jit(solution)/shard_map/ppermute | solution.py:358
  4.8 2.9 %shard_map.109 = bf16[4,128,1152]{2,1,0:T(8,128)(2,1)} custom-call(s32[8]{0:T(128)} %map_ref.1, s32[1,128]{1,0:T(1,128)} %bitcast.6, bf16[128,4096]{1,0:T(8,128)(2,1)} %hidden_ref.1), custom_call_target="tpu_custom_call" | custom-call | bytes 369000000 | tf_op jit(solution)/shard_map/pallas_call | solution.py:373
  7.8 2.1 %collective-permute-done.refs_1_.refs_5_ = bf16[1,64,1536]{2,1,0:T(8,128)(2,1)S(1)} collective-permute-done((bf16[1,64,1536]{2,1,0:T(8,128)(2,1)}, bf16[1,64,1536]{2,1,0:T(8,128)(2,1)S(1)}, u32[]{:S(2)}, u32[]{:S(2)}) %collective-permute-start) | collective-permute-done | bytes 196640 | tf_op jit(solution)/shard_map/ppermute | solution.py:358
  9.9 4.0 %all-to-all-start = ((bf16[4,128,1152]{2,1,0:T(8,128)(2,1)}), bf16[4,128,1152]{2,1,0:T(8,128)(2,1)S(1)}, u32[]{:S(2)}, u32[]{:S(2)}) async-start(bf16[4,128,1152]{2,1,0:T(8,128)(2,1)} %shard_map.109), calls=%async_computation | async-start | bytes 2359296 | tf_op jit(solution)/shard_map/all_to_all | solution.py:383
  13.9 1.6 %collective-permute-start.1 = (bf16[1,64,1536]{2,1,0:T(8,128)(2,1)S(1)}, bf16[1,64,1536]{2,1,0:T(8,128)(2,1)S(1)}, u32[]{:S(2)}, u32[]{:S(2)}) collective-permute-start(bf16[1,64,1536]{2,1,0:T(8,128)(2,1)S(1)} %collective-permute-done.refs_1_.refs_5_), channel_id=1, source_target_pairs={{0,4},{4,0},{8,12},{12,8},{1,5},{5,1},{9,13},{13,9},{2,6},{6,2},{1... | collective-permute-start | bytes 589832 | tf_op jit(solution)/shard_map/ppermute | solution.py:390
  15.5 2.6 %collective-permute-start.2 = (bf16[1,64,1536]{2,1,0:T(8,128)(2,1)S(1)}, bf16[1,64,1536]{2,1,0:T(8,128)(2,1)S(1)}, u32[]{:S(2)}, u32[]{:S(2)}) collective-permute-start(bf16[1,64,1536]{2,1,0:T(8,128)(2,1)S(1)} %collective-permute-done.refs_1_.refs_5_), channel_id=1, source_target_pairs={{0,8},{4,12},{8,0},{12,4},{1,9},{5,13},{9,1},{13,5},{2,10},{6,14},... | collective-permute-start | bytes 589832 | tf_op jit(solution)/shard_map/ppermute | solution.py:390
  18.3 31.9 %all_gather.3.refs_1_.refs_4_ = bf16[4,64,1536]{2,1,0:T(8,128)(2,1)S(1)} all-gather(bf16[1,64,1536]{2,1,0:T(8,128)(2,1)S(1)} %copy-done.9), channel_id=1, replica_groups=mesh['rep'=2,'level'=4,'side'=2,'tp'=2] {'level'}, dimensions={0}, use_global_device_ids=true | all-gather | bytes 983040 | tf_op jit(solution)/shard_map/all_gather | solution.py:372
  50.2 1.4 %shard_map.111.refs_5_ = f32[256,128]{1,0:T(8,128)S(1)} custom-call(s32[4]{0:T(128)S(1)} %get-tuple-element.20.ids_ref, bf16[4,128,1152]{2,1,0:T(8,128)(2,1)S(1)} %all-to-all-done.refs_0_.rows_ref, bf16[4,64,1536]{2,1,0:T(8,128)(2,1)S(1)} %all_gather.3.refs_1_.refs_4_, f32[256,128]{1,0:T(8,128)S(1)} %broadcast_in_dim.9.refs_2_), custom_call_target="tpu_custom_call" | custom-call | bytes 36900000 | tf_op jit(solution)/shard_map/pallas_call | solution.py:303
  51.7 1.4 %shard_map.112 = f32[256,128]{1,0:T(8,128)S(1)} custom-call(s32[4]{0:T(128)S(1)} %get-tuple-element.19.ids_ref, bf16[4,128,1152]{2,1,0:T(8,128)(2,1)S(1)} %all-to-all-done.refs_0_.rows_ref, bf16[1,64,1536]{2,1,0:T(8,128)(2,1)S(1)} %collective-permute-done.refs_1_.refs_5_, bf16[1,64,1536]{2,1,0:T(8,128)(2,1)S(1)} %collective-permute-done.1.refs_2_.refs_6_, ...), custom_call_target="tpu_custom_call" | custom-call | bytes 36900000 | tf_op jit(solution)/shard_map/pallas_call | solution.py:303
  53.3 1.2 %collective-permute-done.4 = f32[256,128]{1,0:T(8,128)S(1)} collective-permute-done((f32[256,128]{1,0:T(8,128)S(1)}, f32[256,128]{1,0:T(8,128)S(1)}, u32[]{:S(2)}, u32[]{:S(2)}) %collective-permute-start.4) | collective-permute-done | bytes 131104 | tf_op jit(solution)/shard_map/ppermute | solution.py:406
  54.5 1.8 %collective-permute-start.5 = (bf16[256,128]{1,0:T(8,128)(2,1)S(1)}, bf16[256,128]{1,0:T(8,128)(2,1)S(1)}, u32[]{:S(2)}, u32[]{:S(2)}) collective-permute-start(bf16[256,128]{1,0:T(8,128)(2,1)S(1)} %add_convert_fusion.refs_0_), channel_id=1, source_target_pairs={{0,2},{2,0},{16,18},{18,16},{1,3},{3,1},{17,19},{19,17},{4,6},{6,4... | collective-permute-start | bytes 196616 | tf_op jit(solution)/shard_map/ppermute | solution.py:358
  56.3 1.5 %collective-permute-start.6 = (bf16[256,128]{1,0:T(8,128)(2,1)S(1)}, bf16[256,128]{1,0:T(8,128)(2,1)S(1)}, u32[]{:S(2)}, u32[]{:S(2)}) collective-permute-start(bf16[256,128]{1,0:T(8,128)(2,1)S(1)} %add_convert_fusion.refs_0_), channel_id=1, source_target_pairs={{0,16},{2,18},{16,0},{18,2},{1,17},{3,19},{17,1},{19,3},{4,20},{6,... | collective-permute-start | bytes 196616 | tf_op jit(solution)/shard_map/ppermute | solution.py:358
  58.9 1.7 %collective-permute-done.6.refs_2_ = bf16[256,128]{1,0:T(8,128)(2,1)S(1)} collective-permute-done((bf16[256,128]{1,0:T(8,128)(2,1)S(1)}, bf16[256,128]{1,0:T(8,128)(2,1)S(1)}, u32[]{:S(2)}, u32[]{:S(2)}) %collective-permute-start.6) | collective-permute-done | bytes 65568 | tf_op jit(solution)/shard_map/ppermute | solution.py:358
  60.6 2.4 %collective-permute-done.7.refs_3_ = bf16[256,128]{1,0:T(8,128)(2,1)S(1)} collective-permute-done((bf16[256,128]{1,0:T(8,128)(2,1)S(1)}, bf16[256,128]{1,0:T(8,128)(2,1)S(1)}, u32[]{:S(2)}, u32[]{:S(2)}) %collective-permute-start.7) | collective-permute-done | bytes 65568 | tf_op jit(solution)/shard_map/ppermute | solution.py:358
  63.0 0.9 %copy-done.3 = bf16[1,64,1536]{2,1,0:T(8,128)(2,1)S(1)} copy-done((bf16[1,64,1536]{2,1,0:T(8,128)(2,1)S(1)}, bf16[1,64,1536]{2,1,0:T(8,128)(2,1)}, u32[]{:S(2)}) %copy-start.3) | copy-done | bytes 196632
  63.9 0.9 %copy-done.5 = bf16[1,64,1536]{2,1,0:T(8,128)(2,1)S(1)} copy-done((bf16[1,64,1536]{2,1,0:T(8,128)(2,1)S(1)}, bf16[1,64,1536]{2,1,0:T(8,128)(2,1)}, u32[]{:S(2)}) %copy-start.5) | copy-done | bytes 196632
  64.8 1.7 %shard_map.113 = (bf16[128,512]{1,0:T(8,128)(2,1)S(1)}, bf16[128,512]{1,0:T(8,128)(2,1)}, bf16[128,512]{1,0:T(8,128)(2,1)}, bf16[128,512]{1,0:T(8,128)(2,1)}) custom-call(s32[8]{0:T(128)S(1)} %pad_add_fusion.ids_ref, s32[1]{0:T(128)} %bitcast.me_ref, bf16[4,128,1152]{2,1,0:T(8,128)(2,1)S(1)} %all-to-all-done.refs_0_.rows_ref, ...), custom_call_target="tpu_custom_call" | custom-call | bytes 73800000 | tf_op jit(solution)/shard_map/pallas_call | solution.py:319
  66.9 1.6 %collective-permute-start.8 = (bf16[128,512]{1,0:T(8,128)(2,1)}, bf16[128,512]{1,0:T(8,128)(2,1)S(1)}, u32[]{:S(2)}, u32[]{:S(2)}) collective-permute-start(bf16[128,512]{1,0:T(8,128)(2,1)} %get-tuple-element.16), channel_id=1, source_target_pairs={{0,2},{2,0},{16,18},{18,16},{1,3},{3,1},{17,19},{19,17},{4,6},{6,4... | collective-permute-start | bytes 393224 | tf_op jit(solution)/shard_map/ppermute | solution.py:358
  68.6 1.5 %collective-permute-start.9 = (bf16[128,512]{1,0:T(8,128)(2,1)}, bf16[128,512]{1,0:T(8,128)(2,1)S(1)}, u32[]{:S(2)}, u32[]{:S(2)}) collective-permute-start(bf16[128,512]{1,0:T(8,128)(2,1)} %get-tuple-element.17), channel_id=1, source_target_pairs={{0,16},{2,18},{16,0},{18,2},{1,17},{3,19},{17,1},{19,3},{4,20},{6,... | collective-permute-start | bytes 393224 | tf_op jit(solution)/shard_map/ppermute | solution.py:358
  70.1 2.9 %collective-permute-done.10.refs_8_ = bf16[128,512]{1,0:T(8,128)(2,1)S(1)} collective-permute-done((bf16[128,512]{1,0:T(8,128)(2,1)}, bf16[128,512]{1,0:T(8,128)(2,1)S(1)}, u32[]{:S(2)}, u32[]{:S(2)}) %collective-permute-start.10) | collective-permute-done | bytes 131104 | tf_op jit(solution)/shard_map/ppermute | solution.py:358
  74.3 1.2 %copy-done.1 = bf16[128,16,256]{2,1,0:T(8,128)(2,1)S(1)} copy-done((bf16[128,16,256]{2,1,0:T(8,128)(2,1)S(1)}, bf16[128,16,256]{2,1,0:T(8,128)(2,1)}, u32[]{:S(2)}) %copy-start.1) | copy-done | bytes 1048600
  75.5 1.0 %copy-done.6 = bf16[128,2048]{1,0:T(8,128)(2,1)S(1)} copy-done((bf16[128,2048]{1,0:T(8,128)(2,1)S(1)}, bf16[128,2048]{1,0:T(8,128)(2,1)}, u32[]{:S(2)}) %copy-start.6) | copy-done | bytes 524312
  78.2 2.9 %shard_map.114 = bf16[128,2048]{1,0:T(8,128)(2,1)} custom-call(s32[1]{0:T(128)} %bitcast.me_ref, s32[16,128]{1,0:T(8,128)S(1)} %copy.15.len_ref, bf16[128,2048]{1,0:T(8,128)(2,1)S(1)} %copy-done.6, bf16[128,256]{1,0:T(8,128)(2,1)S(1)} %copy-done.7, bf16[128,256]{1,0:T(8,128)(2,1)S(1)} %copy-done.8, bf16[128,16,256]{2,1,0:T(8,128)(2,1)S(1)} %copy-done, ...), custom_call_target="tpu_custom_call" | custom-call | flops 134217728 | bytes 3145728 | tf_op jit(solution)/shard_map/pallas_call | solution.py:273
  (37 shorter events, 5.1 us)
Async XLA Ops:
  1.8 8.1 %collective-permute-start = (bf16[1,64,1536]{2,1,0:T(8,128)(2,1)}, bf16[1,64,1536]{2,1,0:T(8,128)(2,1)S(1)}, u32[]{:S(2)}, u32[]{:S(2)}) collective-permute-start(bf16[1,64,1536]{2,1,0:T(8,128)(2,1)} %get-tuple-element.12), channel_id=1, source_target_pairs={{0,2},{2,0},{16,18},{18,16},{1,3},{3,1},{17,19},{19,17},{4,6},{6,4... | collective-permute-start | bytes 589832 | tf_op jit(solution)/shard_map/ppermute | solution.py:358
  7.8 10.5 %copy-start.9 = (bf16[1,64,1536]{2,1,0:T(8,128)(2,1)S(1)}, bf16[1,64,1536]{2,1,0:T(8,128)(2,1)}, u32[]{:S(2)}) copy-start(bf16[1,64,1536]{2,1,0:T(8,128)(2,1)} %get-tuple-element.14) | copy-start | bytes 589828
  9.9 40.3 %all-to-all-start = ((bf16[4,128,1152]{2,1,0:T(8,128)(2,1)}), bf16[4,128,1152]{2,1,0:T(8,128)(2,1)S(1)}, u32[]{:S(2)}, u32[]{:S(2)}) async-start(bf16[4,128,1152]{2,1,0:T(8,128)(2,1)} %shard_map.109), calls=%async_computation | async-start | bytes 2359296 | tf_op jit(solution)/shard_map/all_to_all | solution.py:383
  13.9 37.7 %collective-permute-start.1 = (bf16[1,64,1536]{2,1,0:T(8,128)(2,1)S(1)}, bf16[1,64,1536]{2,1,0:T(8,128)(2,1)S(1)}, u32[]{:S(2)}, u32[]{:S(2)}) collective-permute-start(bf16[1,64,1536]{2,1,0:T(8,128)(2,1)S(1)} %collective-permute-done.refs_1_.refs_5_), channel_id=1, source_target_pairs={{0,4},{4,0},{8,12},{12,8},{1,5},{5,1},{9,13},{13,9},{2,6},{6,2},{1... | collective-permute-start | bytes 589832 | tf_op jit(solution)/shard_map/ppermute | solution.py:390
  15.5 36.2 %collective-permute-start.2 = (bf16[1,64,1536]{2,1,0:T(8,128)(2,1)S(1)}, bf16[1,64,1536]{2,1,0:T(8,128)(2,1)S(1)}, u32[]{:S(2)}, u32[]{:S(2)}) collective-permute-start(bf16[1,64,1536]{2,1,0:T(8,128)(2,1)S(1)} %collective-permute-done.refs_1_.refs_5_), channel_id=1, source_target_pairs={{0,8},{4,12},{8,0},{12,4},{1,9},{5,13},{9,1},{13,5},{2,10},{6,14},... | collective-permute-start | bytes 589832 | tf_op jit(solution)/shard_map/ppermute | solution.py:390
  18.0 33.6 %collective-permute-start.3 = (bf16[1,64,1536]{2,1,0:T(8,128)(2,1)S(1)}, bf16[1,64,1536]{2,1,0:T(8,128)(2,1)S(1)}, u32[]{:S(2)}, u32[]{:S(2)}) collective-permute-start(bf16[1,64,1536]{2,1,0:T(8,128)(2,1)S(1)} %collective-permute-done.refs_1_.refs_5_), channel_id=1, source_target_pairs={{0,12},{4,8},{8,4},{12,0},{1,13},{5,9},{9,5},{13,1},{2,14},{6,10},... | collective-permute-start | bytes 589832 | tf_op jit(solution)/shard_map/ppermute | solution.py:390
  51.6 1.6 %copy-start.10 = (s32[128]{0:T(128)S(1)}, s32[128]{0:T(128)}, u32[]{:S(2)}) copy-start(s32[128]{0:T(128)} %param.21) | copy-start | bytes 1540
  51.6 2.9 %copy-start.2 = (bf16[1,64,1536]{2,1,0:T(8,128)(2,1)}, bf16[1,64,1536]{2,1,0:T(8,128)(2,1)S(1)}, u32[]{:S(2)}) copy-start(bf16[1,64,1536]{2,1,0:T(8,128)(2,1)S(1)} %collective-permute-done.2.refs_3_.refs_7_) | copy-start | bytes 589828
  51.7 2.9 %copy-start.4 = (bf16[1,64,1536]{2,1,0:T(8,128)(2,1)}, bf16[1,64,1536]{2,1,0:T(8,128)(2,1)S(1)}, u32[]{:S(2)}) copy-start(bf16[1,64,1536]{2,1,0:T(8,128)(2,1)S(1)} %collective-permute-done.3.refs_4_.refs_8_) | copy-start | bytes 589828
  53.1 1.4 %collective-permute-start.4 = (f32[256,128]{1,0:T(8,128)S(1)}, f32[256,128]{1,0:T(8,128)S(1)}, u32[]{:S(2)}, u32[]{:S(2)}) collective-permute-start(f32[256,128]{1,0:T(8,128)S(1)} %shard_map.112), channel_id=1, source_target_pairs={{0,1},{1,0},{2,3},{3,2},{4,5},{5,4},{6,7},{7,6},{8,9},{9,8},{10,11... | collective-permute-start | bytes 393224 | tf_op jit(solution)/shard_map/ppermute | solution.py:406
  54.5 4.3 %collective-permute-start.5 = (bf16[256,128]{1,0:T(8,128)(2,1)S(1)}, bf16[256,128]{1,0:T(8,128)(2,1)S(1)}, u32[]{:S(2)}, u32[]{:S(2)}) collective-permute-start(bf16[256,128]{1,0:T(8,128)(2,1)S(1)} %add_convert_fusion.refs_0_), channel_id=1, source_target_pairs={{0,2},{2,0},{16,18},{18,16},{1,3},{3,1},{17,19},{19,17},{4,6},{6,4... | collective-permute-start | bytes 196616 | tf_op jit(solution)/shard_map/ppermute | solution.py:358
  56.3 4.3 %collective-permute-start.6 = (bf16[256,128]{1,0:T(8,128)(2,1)S(1)}, bf16[256,128]{1,0:T(8,128)(2,1)S(1)}, u32[]{:S(2)}, u32[]{:S(2)}) collective-permute-start(bf16[256,128]{1,0:T(8,128)(2,1)S(1)} %add_convert_fusion.refs_0_), channel_id=1, source_target_pairs={{0,16},{2,18},{16,0},{18,2},{1,17},{3,19},{17,1},{19,3},{4,20},{6,... | collective-permute-start | bytes 196616 | tf_op jit(solution)/shard_map/ppermute | solution.py:358
  57.8 5.2 %collective-permute-start.7 = (bf16[256,128]{1,0:T(8,128)(2,1)S(1)}, bf16[256,128]{1,0:T(8,128)(2,1)S(1)}, u32[]{:S(2)}, u32[]{:S(2)}) collective-permute-start(bf16[256,128]{1,0:T(8,128)(2,1)S(1)} %add_convert_fusion.refs_0_), channel_id=1, source_target_pairs={{0,18},{2,16},{16,2},{18,0},{1,19},{3,17},{17,3},{19,1},{4,22},{6,... | collective-permute-start | bytes 196616 | tf_op jit(solution)/shard_map/ppermute | solution.py:358
  58.2 16.1 %copy-start = (bf16[128,16,256]{2,1,0:T(8,128)(2,1)S(1)}, bf16[128,16,256]{2,1,0:T(8,128)(2,1)}, u32[]{:S(2)}) copy-start(bf16[128,16,256]{2,1,0:T(8,128)(2,1)} %refs_3_.1) | copy-start | bytes 3145732
  63.0 0.9 %copy-start.3 = (bf16[1,64,1536]{2,1,0:T(8,128)(2,1)S(1)}, bf16[1,64,1536]{2,1,0:T(8,128)(2,1)}, u32[]{:S(2)}) copy-start(bf16[1,64,1536]{2,1,0:T(8,128)(2,1)} %copy-done.2) | copy-start | bytes 589828
  63.9 0.9 %copy-start.5 = (bf16[1,64,1536]{2,1,0:T(8,128)(2,1)S(1)}, bf16[1,64,1536]{2,1,0:T(8,128)(2,1)}, u32[]{:S(2)}) copy-start(bf16[1,64,1536]{2,1,0:T(8,128)(2,1)} %copy-done.4) | copy-start | bytes 589828
  66.5 6.4 %collective-permute-start.10 = (bf16[128,512]{1,0:T(8,128)(2,1)}, bf16[128,512]{1,0:T(8,128)(2,1)S(1)}, u32[]{:S(2)}, u32[]{:S(2)}) collective-permute-start(bf16[128,512]{1,0:T(8,128)(2,1)} %get-tuple-element.18), channel_id=1, source_target_pairs={{0,18},{2,16},{16,2},{18,0},{1,19},{3,17},{17,3},{19,1},{4,22},{6,... | collective-permute-start | bytes 393224 | tf_op jit(solution)/shard_map/ppermute | solution.py:358
  66.9 6.6 %collective-permute-start.8 = (bf16[128,512]{1,0:T(8,128)(2,1)}, bf16[128,512]{1,0:T(8,128)(2,1)S(1)}, u32[]{:S(2)}, u32[]{:S(2)}) collective-permute-start(bf16[128,512]{1,0:T(8,128)(2,1)} %get-tuple-element.16), channel_id=1, source_target_pairs={{0,2},{2,0},{16,18},{18,16},{1,3},{3,1},{17,19},{19,17},{4,6},{6,4... | collective-permute-start | bytes 393224 | tf_op jit(solution)/shard_map/ppermute | solution.py:358
  68.6 5.7 %collective-permute-start.9 = (bf16[128,512]{1,0:T(8,128)(2,1)}, bf16[128,512]{1,0:T(8,128)(2,1)S(1)}, u32[]{:S(2)}, u32[]{:S(2)}) collective-permute-start(bf16[128,512]{1,0:T(8,128)(2,1)} %get-tuple-element.17), channel_id=1, source_target_pairs={{0,16},{2,18},{16,0},{18,2},{1,17},{3,19},{17,1},{19,3},{4,20},{6,... | collective-permute-start | bytes 393224 | tf_op jit(solution)/shard_map/ppermute | solution.py:358
  74.3 1.2 %copy-start.1 = (bf16[128,16,256]{2,1,0:T(8,128)(2,1)S(1)}, bf16[128,16,256]{2,1,0:T(8,128)(2,1)}, u32[]{:S(2)}) copy-start(bf16[128,16,256]{2,1,0:T(8,128)(2,1)} %refs_4_.1) | copy-start | bytes 3145732
  75.5 1.0 %copy-start.6 = (bf16[128,2048]{1,0:T(8,128)(2,1)S(1)}, bf16[128,2048]{1,0:T(8,128)(2,1)}, u32[]{:S(2)}) copy-start(bf16[128,2048]{1,0:T(8,128)(2,1)} %refs_0_.1) | copy-start | bytes 1572868
  76.6 0.8 %copy-start.7 = (bf16[128,256]{1,0:T(8,128)(2,1)S(1)}, bf16[128,256]{1,0:T(8,128)(2,1)}, u32[]{:S(2)}) copy-start(bf16[128,256]{1,0:T(8,128)(2,1)} %refs_1_.1) | copy-start | bytes 196612
  77.4 0.8 %copy-start.8 = (bf16[128,256]{1,0:T(8,128)(2,1)S(1)}, bf16[128,256]{1,0:T(8,128)(2,1)}, u32[]{:S(2)}) copy-start(bf16[128,256]{1,0:T(8,128)(2,1)} %refs_2_.1) | copy-start | bytes 196612

commit v9 on v8

v9 whole, which is shorter than its diff:
```python
import functools
import math

import jax
import jax.numpy as jnp
from jax import lax
from jax.experimental import pallas as pl
from jax.experimental.pallas import tpu as pltpu
from jax.sharding import Mesh
from jax.sharding import PartitionSpec as P

HEAD = 128
LANES = 128
STEP = 16
HALF = 8
BATCH = 2
DEAD = -1e30
VMEM = pl.BlockSpec(memory_space=pltpu.VMEM)
SMEM = pl.BlockSpec(memory_space=pltpu.SMEM)
HBM = pl.BlockSpec(memory_space=pltpu.HBM)
PARAMS = pltpu.CompilerParams(vmem_limit_bytes=12 * 1024 * 1024)
NT = (((1,), (1,)), ((), ()))
TN = (((0,), (0,)), ((), ()))


def columns(at, width):
    return pl.ds(pl.multiple_of(at * width, width), width)


def run_copies(moves, sems, meanwhile=None):
    copies = [pltpu.make_async_copy(src, dst, sems.at[k]) for k, (src, dst) in enumerate(moves)]
    for copy in copies:
        copy.start()
    if meanwhile is not None:
        meanwhile()
    for copy in copies:
        copy.wait()


def factor_kernel(sides, levels, rep_ref, factor_ref, send_ref, sems):
    width = send_ref.shape[2]
    moves = []
    for side in range(sides):
        share = factor_ref.at[0, :, columns(rep_ref[0] * sides + side, width)]
        moves += [(share, send_ref.at[level * sides + side]) for level in range(levels)]
    run_copies(moves, sems)


def load_kernel(count, *refs):
    run_copies(list(zip(refs[:count], refs[count : 2 * count])), refs[-1])


def row_kernel(parts, me_ref, map_ref, ids_ref, hidden_ref, *refs):
    out_refs, sems = refs[:parts], refs[parts]
    requests, wide = hidden_ref.shape
    features = wide // parts
    moves = [
        (hidden_ref.at[:, columns(me_ref[0] ^ s, features)], out_refs[s].at[:, :features])
        for s in range(parts)
    ]

    def owners():
        ids = ids_ref[...]

        def look(k, found):
            return jnp.where(ids == k, map_ref[k], found)

        found = lax.fori_loop(0, map_ref.shape[0], look, jnp.zeros_like(ids))
        found = jnp.broadcast_to(found.astype(jnp.float32), (LANES, requests)).T
        for s in range(parts):
            out_refs[s][:, features:] = found.astype(jnp.bfloat16)

    run_copies(moves, sems, owners)


def owner_mask(rows_ref, first, count, rank):
    features = rows_ref.shape[1] - LANES
    owners = rows_ref[:, features:].astype(jnp.float32).astype(jnp.int32)
    wide = jnp.concatenate([owners] * (count * rank // LANES), axis=1)
    return wide == lax.broadcasted_iota(jnp.int32, (1, count * rank), 1) // rank + first


def shrink_kernel(parts, *refs):
    row_refs, weight_ref, out_ref = refs[:parts], refs[parts], refs[parts + 1]
    count, rank, features = weight_ref.shape
    requests = row_refs[0].shape[0]
    step = pl.program_id(0)
    weight = weight_ref[...].reshape(count * rank, features)
    low = lax.broadcasted_iota(jnp.int32, (requests, LANES), 1) < rank
    folded = []
    for ref in row_refs:
        sums = lax.dot_general(
            ref[:, :features], weight, NT, preferred_element_type=jnp.float32
        )
        sums = jnp.where(owner_mask(ref, step * count, count, rank), sums, 0.0)
        total = sums[:, :LANES]
        for k in range(1, count * rank // LANES):
            total = total + sums[:, k * LANES : (k + 1) * LANES]
        folded.append(total + pltpu.roll(total, rank, 1))

    @pl.when(step == 0)
    def _():
        out_ref[...] = jnp.zeros_like(out_ref)

    half = parts // 2
    for s in range(half):
        rows = pl.ds(s * requests, requests)
        out_ref[rows, :] += jnp.where(low, folded[s], folded[s + half])


def expand_kernel(parts, *refs):
    row_refs, low_refs, weight_ref = refs[:parts], refs[parts : 2 * parts], refs[2 * parts]
    out_refs, total_ref = refs[2 * parts + 1 : 3 * parts + 1], refs[3 * parts + 1]
    count, rank, outputs = weight_ref.shape
    requests = row_refs[0].shape[0]
    step, last = pl.program_id(0), pl.num_programs(0) - 1
    weight = weight_ref[...].reshape(count * rank, outputs)
    half = parts // 2
    low = lax.broadcasted_iota(jnp.int32, (requests, LANES), 1) < rank
    held = [[0.0] * half for _ in range(2)]
    for t in range(parts):
        sums = low_refs[t][...].astype(jnp.float32)
        for s in range(half):
            at = (s ^ t) % half
            piece = sums[at * requests : (at + 1) * requests]
            held[t // half][s] = held[t // half][s] + piece
    for s in range(half):
        straight = held[0][s] + pltpu.roll(held[1][s], rank, 1)
        turned = pltpu.roll(straight, rank, 1)
        for part in (s, s + half):
            first, other = (straight, turned) if part < half else (turned, straight)
            wide = jnp.concatenate([jnp.where(low, first, other)] * (count * rank // LANES), axis=1)
            wide = jnp.where(owner_mask(row_refs[part], step * count, count, rank), wide, 0.0)
            product = jnp.dot(
                wide.astype(jnp.bfloat16), weight, preferred_element_type=jnp.float32
            )

            @pl.when(step == 0)
            def _():
                total_ref[part] = product

            @pl.when(step > 0)
            def _():
                total_ref[part] += product

            @pl.when(step == last)
            def _():
                out_refs[part][...] = total_ref[part].astype(jnp.bfloat16)


def attend_kernel(parts, me_ref, len_ref, *refs):
    base_ref, nk_ref, nv_ref, ck_ref, cv_ref, *delta_refs, out_ref = refs
    me = me_ref[0]
    block = STEP * BATCH
    steps = base_ref.shape[0] // block
    requests, columns = base_ref.shape
    width = columns // parts
    groups = nk_ref.shape[1] // HEAD
    slots = ck_ref.shape[1]
    heads = columns // HEAD
    per_part = width // HEAD
    span = heads * HALF
    part_span = per_part * HALF
    keys_in = HALF * slots + STEP
    row = lax.broadcasted_iota(jnp.int32, (keys_in, span), 0)
    lane_req = lax.broadcasted_iota(jnp.int32, (keys_in, span), 1) % HALF
    own = row - HALF * slots
    slot_of = []
    for h in range(STEP // HALF):
        cached = jnp.where(row // slots == lane_req, row % slots, slots)
        fresh = jnp.where(own == lane_req + h * HALF, -1, slots)
        slot_of.append(jnp.where(own >= 0, fresh, cached))
    part_at = [me ^ s for s in range(parts)]
    group_at = [p // (parts // groups) for p in part_at]
    lane_part = lax.broadcasted_iota(jnp.int32, (1, span), 1) // part_span
    lane_group = jnp.zeros_like(lane_part)
    for s in range(parts):
        lane_group = jnp.where(lane_part == s, group_at[s], lane_group)
    scale = 1.0 / math.sqrt(HEAD)
    ones = jnp.ones((keys_in, HEAD), jnp.bfloat16)

    for step in range(steps):
        units = []
        for j in range(BATCH):
            start = step * block + j * STEP
            at = pl.ds(start, STEP)
            pieces = []
            for s in range(parts):
                lanes = pl.ds(pl.multiple_of(part_at[s] * width, width), width)
                q = base_ref[at, lanes].astype(jnp.float32)
                q = q + delta_refs[s][at, :].astype(jnp.float32)
                pieces += [q[:, k * HEAD : (k + 1) * HEAD] for k in range(per_part)]
            for h in range(STEP // HALF):
                slab = pl.ds(start + h * HALF, HALF)
                q = jnp.concatenate([p[h * HALF : (h + 1) * HALF] for p in pieces], axis=0)
                units.append((step * BATCH + j, at, h, slab, q.astype(jnp.bfloat16)))
        scores = []
        for _, at, h, slab, q in units:
            both = []
            for g in range(groups):
                lanes = slice(g * HEAD, (g + 1) * HEAD)
                keys = ck_ref[slab, :, lanes].reshape(HALF * slots, HEAD)
                keys = jnp.concatenate([keys, nk_ref[at, lanes]], axis=0)
                both.append(lax.dot_general(keys, q, NT, preferred_element_type=jnp.float32))
            score = both[0]
            for g in range(1, groups):
                score = jnp.where(lane_group == g, both[g], score)
            scores.append(score)
        probs = []
        for (i, at, h, slab, q), score in zip(units, scores):
            lens = len_ref[pl.ds(i * (STEP // HALF) + h, 1), :]
            score = jnp.where(slot_of[h] < lens, score, DEAD)
            top = jnp.max(score, axis=0, keepdims=True)
            exps = jnp.exp((score - top) * scale)
            total = jnp.sum(exps, axis=0, keepdims=True)
            probs.append((exps * (1.0 / total)).astype(jnp.bfloat16))
        mixed = []
        for (i, at, h, slab, q), prob in zip(units, probs):
            whole = []
            for g in range(groups):
                lanes = slice(g * HEAD, (g + 1) * HEAD)
                values = cv_ref[slab, :, lanes].reshape(HALF * slots, HEAD)
                values = jnp.concatenate([values, nv_ref[at, lanes]], axis=0)
                whole.append(
                    lax.dot_general(prob, values, TN, preferred_element_type=jnp.float32)
                )
            mixed.append(whole)
        for j in range(BATCH):
            at = units[2 * j][1]
            for s in range(parts):
                rows = slice(s * part_span, (s + 1) * part_span)
                halves = []
                for h in range(STEP // HALF):
                    whole = mixed[2 * j + h]
                    part = whole[0][rows]
                    for g in range(1, groups):
                        part = jnp.where(group_at[s] == g, whole[g][rows], part)
                    halves.append(part)
                out = [
                    jnp.concatenate([p[k * HALF : (k + 1) * HALF] for p in halves], axis=0)
                    for k in range(per_part)
                ]
                lanes = pl.ds(pl.multiple_of(part_at[s] * width, width), width)
                out_ref[at, lanes] = jnp.concatenate(out, axis=1).astype(jnp.bfloat16)


def attend(me, base, new_key, new_value, cache_keys, cache_values, lengths, deltas):
    requests, columns = base.shape
    kv = new_key.shape[1]
    slots = cache_keys.shape[1]
    lengths = jnp.tile(lengths.reshape(requests // HALF, HALF), (1, columns // HEAD))
    arrays = [base, new_key, new_value, cache_keys, cache_values, *deltas]
    return pl.pallas_call(
        functools.partial(attend_kernel, len(deltas)),
        out_shape=jax.ShapeDtypeStruct((requests, columns), jnp.bfloat16),
        in_specs=[SMEM] + [VMEM] * (1 + len(arrays)),
        out_specs=VMEM,
        compiler_params=PARAMS,
        cost_estimate=pl.CostEstimate(
            flops=4 * requests * HALF * slots * columns,
            bytes_accessed=4 * requests * (columns + slots * kv),
            transcendentals=requests * slots * columns // 16,
        ),
    )(me, lengths, *arrays)


def whole(array):
    return pl.BlockSpec(array.shape, lambda *_: (0,) * len(array.shape))


def in_chunks(weight):
    chunk = math.gcd(weight.shape[0], 8)
    return weight.shape[0] // chunk, pl.BlockSpec((chunk,) + weight.shape[1:], lambda i: (i, 0, 0))


def shrink_rows(rows, weight):
    parts, requests = len(rows), rows[0].shape[0]
    steps, spec = in_chunks(weight)
    out = jax.ShapeDtypeStruct((parts // 2 * requests, LANES), jnp.float32)
    return pl.pallas_call(
        functools.partial(shrink_kernel, parts),
        out_shape=out,
        grid=(steps,),
        in_specs=[*map(whole, rows), spec],
        out_specs=whole(out),
        compiler_params=PARAMS,
    )(*rows, weight)


def expand_rows(rows, lows, weight):
    parts, requests, outputs = len(rows), rows[0].shape[0], weight.shape[2]
    steps, spec = in_chunks(weight)
    out = jax.ShapeDtypeStruct((requests, outputs), jnp.bfloat16)
    return pl.pallas_call(
        functools.partial(expand_kernel, parts),
        out_shape=[out] * parts,
        grid=(steps,),
        in_specs=[*map(whole, rows), *map(whole, lows), spec],
        out_specs=[whole(out)] * parts,
        scratch_shapes=[pltpu.VMEM((parts, requests, outputs), jnp.float32)],
        compiler_params=PARAMS,
    )(*rows, *lows, weight)


def per_device(
    hidden,
    adapter_ids,
    owner_map,
    shrink_factors,
    expand_factors,
    query_base,
    new_key,
    new_value,
    cache_keys,
    cache_values,
    lengths,
):
    reps, levels, sides, tp = (lax.axis_size(a) for a in ("rep", "level", "side", "tp"))
    pool = levels * sides
    requests, wide = hidden.shape
    rank = shrink_factors.shape[2]
    square = reps * sides
    rep = lax.axis_index("rep")
    me = rep * sides + lax.axis_index("side")

    def swap(a, s):
        pairs = [(c, c ^ s) for c in range(square)]
        return lax.ppermute(a, ("rep", "side"), pairs)

    def to_pool(factor, after=None):
        width = factor.shape[2] // square
        send = pl.pallas_call(
            functools.partial(factor_kernel, sides, levels),
            out_shape=jax.ShapeDtypeStruct((pool, rank, width), jnp.bfloat16),
            in_specs=[SMEM, HBM],
            out_specs=VMEM,
            scratch_shapes=[pltpu.SemaphoreType.DMA((pool,))],
        )(rep[None], factor)
        if after is not None:
            send, after = lax.optimization_barrier((send, after))
        got = lax.all_to_all(send, ("level", "side"), split_axis=0, concat_axis=0, tiled=True)
        return got, after

    shrink, _ = to_pool(shrink_factors.swapaxes(1, 2))
    rows = pl.pallas_call(
        functools.partial(row_kernel, square),
        out_shape=[jax.ShapeDtypeStruct((requests, wide // square + LANES), jnp.bfloat16)] * square,
        in_specs=[SMEM, SMEM, VMEM, HBM],
        out_specs=[VMEM] * square,
        scratch_shapes=[pltpu.SemaphoreType.DMA((square,))],
    )(me[None], owner_map, adapter_ids.T, hidden)
    rows = [rows[0]] + [swap(rows[s], s) for s in range(1, square)]
    arrays = [query_base, new_key, new_value, cache_keys, cache_values]
    arrays = pl.pallas_call(
        functools.partial(load_kernel, len(arrays)),
        out_shape=[jax.ShapeDtypeStruct(a.shape, a.dtype) for a in arrays],
        in_specs=[HBM] * len(arrays),
        out_specs=[VMEM] * len(arrays),
        scratch_shapes=[pltpu.SemaphoreType.DMA((len(arrays),))],
    )(*arrays)
    rows[0], *arrays = lax.optimization_barrier((rows[0], *arrays))

    expand, shrink = to_pool(expand_factors, shrink)
    partial = shrink_rows(rows, shrink)
    for c in range(1, tp):
        partial = partial + lax.ppermute(partial, "tp", [(t, t ^ c) for t in range(tp)])
    partial = partial.astype(jnp.bfloat16)
    lows = [partial] + [swap(partial, s) for s in range(1, square)]
    deltas = expand_rows(rows, lows, expand)
    deltas = [deltas[0]] + [swap(deltas[s], s) for s in range(1, square)]
    return attend(me[None], *arrays, lengths, deltas)


def solution(mesh):
    reps, pool, tp = (mesh.shape[a] for a in ("rep", "pool", "tp"))
    finer = Mesh(mesh.devices.reshape(reps, pool // 2, 2, tp), ("rep", "level", "side", "tp"))
    pooled = ("level", "side")
    requests = ("rep", "level", "side")
    in_specs = (
        P(requests, "tp"),
        P(requests, None),
        P(),
        P(pooled, "tp", None),
        P(pooled, None, "tp"),
        P(requests, "tp"),
        P(requests, "tp"),
        P(requests, "tp"),
        P(requests, None, "tp"),
        P(requests, None, "tp"),
        P(requests),
    )
    return jax.shard_map(
        per_device, mesh=finer, in_specs=in_specs, out_specs=P(requests, "tp"), check_vma=False
    )
```

time: 81.6 us -> 88.5 us (1.085)
  waiting for transfers between devices: 12.3 us -> 45.2 us
  blocking collectives: 31.9 us -> 0 us
  Pallas kernels: 12.1 us -> 16.5 us
  starting transfers between devices: 18.5 us -> 21.8 us
  local copies, waits for them, and re-layouts: 6.04 us -> 4.36 us
    all_gather x1 -> x0, blocking collectives: 31.9 us -> none  [per_device(): own = lax.all_gather(own, 'level', axis=0, tiled=True)]
    all_to_all x1 -> x2, waiting for transfers between devices: 0.01 us -> 23.6 us  [to_pool(): lax.all_to_all(send, ('level', 'side'), split_axis=0, concat_axis=0, tile...]
    ppermute x7 -> x9, waiting for transfers between devices: 11.2 us -> 20.3 us  [swap(): return lax.ppermute(a, ('rep', 'side'), pairs)]
    all_to_all x1 -> x2, starting transfers between devices: 3.97 us -> 10.9 us  [to_pool(): lax.all_to_all(send, ('level', 'side'), split_axis=0, concat_axis=0, tile...]
    ppermute x3 -> x0, starting transfers between devices: 4.39 us -> none  [per_device(): lax.ppermute(other, 'level', [(i, i ^ k) for i in range(levels)])]
    pallas_call x5 -> x6, Pallas kernels: 9.26 us -> 13.6 us  [the longest x2 4.59 us: to_pool(): pl.pallas_call(functools.partial(factor_kernel, sides, levels), out_shape...]
    unnamed x22, local copies, waits for them, and re-layouts: 5.82 us -> 4.16 us
    ppermute x7 -> x9, starting transfers between devices: 10 us -> 10.8 us  [swap(): return lax.ppermute(a, ('rep', 'side'), pairs)]
  transfers between devices with their start and end apart: 12 -> 12, of which waited for: 8 -> 8; matrix products, arithmetic and copies ran while one was open for 0% -> 0% of each run, Pallas kernels for 5% -> 11%
where the time goes in v9:
time: 88.5 us; the launch traced here: 87.9 us
  waiting for transfers between devices  45.2 us (51%)
  starting transfers between devices  21.8 us (25%)
  Pallas kernels  16.5 us (19%)
  local copies, waits for them, and re-layouts  4.36 us (5%)
    all_to_all x2, waiting for transfers between devices, to_pool(): lax.all_to_all(send, ('level', 'side'), split_axis=0, concat_axis=0, tile...  23.6 us
    ppermute x9, waiting for transfers between devices, swap(): return lax.ppermute(a, ('rep', 'side'), pairs)  20.3 us
    all_to_all x2, starting transfers between devices, to_pool(): lax.all_to_all(send, ('level', 'side'), split_axis=0, concat_axis=0, tile...  10.9 us
    ppermute x9, starting transfers between devices, swap(): return lax.ppermute(a, ('rep', 'side'), pairs)  10.8 us
    pallas_call x2, Pallas kernels, to_pool(): pl.pallas_call(functools.partial(factor_kernel, sides, levels), out_shape...  4.59 us
    unnamed x22, local copies, waits for them, and re-layouts  4.16 us
    pallas_call x1, Pallas kernels, per_device(): pl.pallas_call(functools.partial(load_kernel, len(arrays)), out_shape=[ja...  3.33 us
    pallas_call x1, Pallas kernels, per_device(): pl.pallas_call(functools.partial(row_kernel, square), out_shape=[jax.Shap...  2.95 us
  transfers between devices with their start and end apart: 12, of which 8 were waited for; matrix products, arithmetic and copies ran while one was open for 0% of the time, Pallas kernels for 11%

profile of v9, /device:TPU:0, one launch (start us, length us, event | category | flops | bytes accessed | tf_op | source)
XLA Modules:
  0.0 87.9 jit_solution(11198735389560241928)
XLA Ops:
  0.0 2.4 %shard_map.112 = bf16[8,64,1024]{2,1,0:T(8,128)(2,1)} custom-call(s32[1]{0:T(128)} %bitcast.3.rep_ref, bf16[1,64,4096]{2,1,0:T(8,128)(2,1)} %bitcast.6), custom_call_target="tpu_custom_call" | custom-call | tf_op jit(solution)/shard_map/pallas_call | solution.py:332
  2.4 7.3 %all-to-all-start = ((bf16[8,64,1024]{2,1,0:T(8,128)(2,1)}), bf16[8,64,1024]{2,1,0:T(8,128)(2,1)S(1)}, u32[]{:S(2)}, u32[]{:S(2)}) async-start(bf16[8,64,1024]{2,1,0:T(8,128)(2,1)} %shard_map.112), calls=%async_computation | async-start | bytes 2097152 | tf_op jit(solution)/shard_map/all_to_all | solution.py:341
  9.7 2.2 %shard_map.111 = bf16[8,64,512]{2,1,0:T(8,128)(2,1)} custom-call(s32[1]{0:T(128)} %bitcast.3.rep_ref, bf16[1,64,2048]{2,1,0:T(8,128)(2,1)} %factor_ref.1), custom_call_target="tpu_custom_call" | custom-call | tf_op jit(solution)/shard_map/pallas_call | solution.py:332
  11.9 23.6 %all-to-all-done.refs_4_ = bf16[8,64,1024]{2,1,0:T(8,128)(2,1)S(1)} async-done(((bf16[8,64,1024]{2,1,0:T(8,128)(2,1)}), bf16[8,64,1024]{2,1,0:T(8,128)(2,1)S(1)}, u32[]{:S(2)}, u32[]{:S(2)}) %all-to-all-start) | async-done | bytes 1048608 | tf_op jit(solution)/shard_map/all_to_all | solution.py:341
  35.5 3.6 %all-to-all-start.1 = ((bf16[8,64,512]{2,1,0:T(8,128)(2,1)}), bf16[8,64,512]{2,1,0:T(8,128)(2,1)S(1)}, u32[]{:S(2)}, u32[]{:S(2)}) async-start(bf16[8,64,512]{2,1,0:T(8,128)(2,1)} %shard_map.111), calls=%async_computation.1 | async-start | bytes 1048576 | tf_op jit(solution)/shard_map/all_to_all | solution.py:341
  39.0 3.0 %shard_map.109 = (bf16[128,1152]{1,0:T(8,128)(2,1)}, bf16[128,1152]{1,0:T(8,128)(2,1)}, bf16[128,1152]{1,0:T(8,128)(2,1)}, bf16[128,1152]{1,0:T(8,128)(2,1)}) custom-call(s32[1]{0:T(128)} %bitcast.me_ref, s32[8]{0:T(128)} %map_ref.1, s32[1,128]{1,0:T(1,128)} %bitcast.7, bf16[128,4096]{1,0:T(8,128)(2,1)} %hidden_ref.1), custom_call_target="tpu_custom_call" | custom-call | tf_op jit(solution)/shard_map/pallas_call | solution.py:345
  42.0 2.1 %collective-permute-start = (bf16[128,1152]{1,0:T(8,128)(2,1)}, bf16[128,1152]{1,0:T(8,128)(2,1)S(1)}, u32[]{:S(2)}, u32[]{:S(2)}) collective-permute-start(bf16[128,1152]{1,0:T(8,128)(2,1)} %get-tuple-element.38), channel_id=1, source_target_pairs={{0,2},{2,0},{16,18},{18,16},{1,3},{3,1},{17,19},{19,17},{4,6},{6,4... | collective-permute-start | bytes 884744 | tf_op jit(solution)/shard_map/ppermute | solution.py:328
  44.1 1.7 %collective-permute-start.1 = (bf16[128,1152]{1,0:T(8,128)(2,1)}, bf16[128,1152]{1,0:T(8,128)(2,1)S(1)}, u32[]{:S(2)}, u32[]{:S(2)}) collective-permute-start(bf16[128,1152]{1,0:T(8,128)(2,1)} %get-tuple-element.39), channel_id=1, source_target_pairs={{0,16},{2,18},{16,0},{18,2},{1,17},{3,19},{17,1},{19,3},{4,20},{6,... | collective-permute-start | bytes 884744 | tf_op jit(solution)/shard_map/ppermute | solution.py:328
  45.8 3.3 %shard_map.110 = (bf16[128,2048]{1,0:T(8,128)(2,1)}, bf16[128,256]{1,0:T(8,128)(2,1)}, bf16[128,256]{1,0:T(8,128)(2,1)}, bf16[128,16,256]{2,1,0:T(8,128)(2,1)}, bf16[128,16,256]{2,1,0:T(8,128)(2,1)}) custom-call(bf16[128,2048]{1,0:T(8,128)(2,1)} %refs_0_.1, bf16[128,256]{1,0:T(8,128)(2,1)} %refs_1_.1, bf16[128,256]{1,0:T(8,128)(2,1)} %refs_2_.1, ...), custom_call_target="tpu_custom_call" | custom-call | tf_op jit(solution)/shard_map/pallas_call | solution.py:354
  49.1 5.4 %collective-permute-done.refs_1_ = bf16[128,1152]{1,0:T(8,128)(2,1)S(1)} collective-permute-done((bf16[128,1152]{1,0:T(8,128)(2,1)}, bf16[128,1152]{1,0:T(8,128)(2,1)S(1)}, u32[]{:S(2)}, u32[]{:S(2)}) %collective-permute-start) | collective-permute-done | bytes 294944 | tf_op jit(solution)/shard_map/ppermute | solution.py:328
  54.5 7.0 %collective-permute-done.2.refs_3_ = bf16[128,1152]{1,0:T(8,128)(2,1)S(1)} collective-permute-done((bf16[128,1152]{1,0:T(8,128)(2,1)}, bf16[128,1152]{1,0:T(8,128)(2,1)S(1)}, u32[]{:S(2)}, u32[]{:S(2)}) %collective-permute-start.2) | collective-permute-done | bytes 294944 | tf_op jit(solution)/shard_map/ppermute | solution.py:328
  61.5 1.5 %shard_map.113 = f32[256,128]{1,0:T(8,128)S(1)} custom-call(bf16[128,1152]{1,0:T(8,128)(2,1)S(1)} %copy-done, bf16[128,1152]{1,0:T(8,128)(2,1)S(1)} %collective-permute-done.refs_1_, bf16[128,1152]{1,0:T(8,128)(2,1)S(1)} %collective-permute-done.1.refs_2_, bf16[128,1152]{1,0:T(8,128)(2,1)S(1)} %collective-permute-done.2.refs_3_, ...), custom_call_target="tpu_custom_call" | custom-call | tf_op jit(solution)/shard_map/pallas_call | solution.py:280
  63.1 1.3 %collective-permute-done.3 = f32[256,128]{1,0:T(8,128)S(1)} collective-permute-done((f32[256,128]{1,0:T(8,128)S(1)}, f32[256,128]{1,0:T(8,128)S(1)}, u32[]{:S(2)}, u32[]{:S(2)}) %collective-permute-start.3) | collective-permute-done | bytes 131104 | tf_op jit(solution)/shard_map/ppermute | solution.py:366
  65.0 1.7 %collective-permute-start.5 = (bf16[256,128]{1,0:T(8,128)(2,1)S(1)}, bf16[256,128]{1,0:T(8,128)(2,1)S(1)}, u32[]{:S(2)}, u32[]{:S(2)}) collective-permute-start(bf16[256,128]{1,0:T(8,128)(2,1)S(1)} %add_convert_fusion.refs_4_), channel_id=1, source_target_pairs={{0,16},{2,18},{16,0},{18,2},{1,17},{3,19},{17,1},{19,3},{4,20},{6,... | collective-permute-start | bytes 196616 | tf_op jit(solution)/shard_map/ppermute | solution.py:328
  66.7 1.3 %collective-permute-start.4 = (bf16[256,128]{1,0:T(8,128)(2,1)S(1)}, bf16[256,128]{1,0:T(8,128)(2,1)S(1)}, u32[]{:S(2)}, u32[]{:S(2)}) collective-permute-start(bf16[256,128]{1,0:T(8,128)(2,1)S(1)} %add_convert_fusion.refs_4_), channel_id=1, source_target_pairs={{0,2},{2,0},{16,18},{18,16},{1,3},{3,1},{17,19},{19,17},{4,6},{6,4... | collective-permute-start | bytes 196616 | tf_op jit(solution)/shard_map/ppermute | solution.py:328
  68.2 2.1 %collective-permute-done.6.refs_7_ = bf16[256,128]{1,0:T(8,128)(2,1)S(1)} collective-permute-done((bf16[256,128]{1,0:T(8,128)(2,1)S(1)}, bf16[256,128]{1,0:T(8,128)(2,1)S(1)}, u32[]{:S(2)}, u32[]{:S(2)}) %collective-permute-start.6) | collective-permute-done | bytes 65568 | tf_op jit(solution)/shard_map/ppermute | solution.py:328
  71.6 0.8 copy-done.7
  73.3 1.2 %shard_map.114 = (bf16[128,512]{1,0:T(8,128)(2,1)S(1)}, bf16[128,512]{1,0:T(8,128)(2,1)}, bf16[128,512]{1,0:T(8,128)(2,1)}, bf16[128,512]{1,0:T(8,128)(2,1)}) custom-call(bf16[128,1152]{1,0:T(8,128)(2,1)S(1)} %copy-done, bf16[128,1152]{1,0:T(8,128)(2,1)S(1)} %collective-permute-done.refs_1_, bf16[128,1152]{1,0:T(8,128)(2,1)S(1)} %collective-permute-done.1.refs_2_, ...), custom_call_target="tpu_custom_call" | custom-call | tf_op jit(solution)/shard_map/pallas_call | solution.py:294
  74.5 1.3 %collective-permute-start.7 = (bf16[128,512]{1,0:T(8,128)(2,1)}, bf16[128,512]{1,0:T(8,128)(2,1)S(1)}, u32[]{:S(2)}, u32[]{:S(2)}) collective-permute-start(bf16[128,512]{1,0:T(8,128)(2,1)} %get-tuple-element.44), channel_id=1, source_target_pairs={{0,2},{2,0},{16,18},{18,16},{1,3},{3,1},{17,19},{19,17},{4,6},{6,4... | collective-permute-start | bytes 393224 | tf_op jit(solution)/shard_map/ppermute | solution.py:328
  76.5 1.5 %collective-permute-start.9 = (bf16[128,512]{1,0:T(8,128)(2,1)}, bf16[128,512]{1,0:T(8,128)(2,1)S(1)}, u32[]{:S(2)}, u32[]{:S(2)}) collective-permute-start(bf16[128,512]{1,0:T(8,128)(2,1)} %get-tuple-element.46), channel_id=1, source_target_pairs={{0,18},{2,16},{16,2},{18,0},{1,19},{3,17},{17,3},{19,1},{4,22},{6,... | collective-permute-start | bytes 393224 | tf_op jit(solution)/shard_map/ppermute | solution.py:328
  78.1 2.0 %collective-permute-done.7.refs_6_ = bf16[128,512]{1,0:T(8,128)(2,1)S(1)} collective-permute-done((bf16[128,512]{1,0:T(8,128)(2,1)}, bf16[128,512]{1,0:T(8,128)(2,1)S(1)}, u32[]{:S(2)}, u32[]{:S(2)}) %collective-permute-start.7) | collective-permute-done | bytes 131104 | tf_op jit(solution)/shard_map/ppermute | solution.py:328
  80.1 3.7 %collective-permute-done.8.refs_7_ = bf16[128,512]{1,0:T(8,128)(2,1)S(1)} collective-permute-done((bf16[128,512]{1,0:T(8,128)(2,1)}, bf16[128,512]{1,0:T(8,128)(2,1)S(1)}, u32[]{:S(2)}, u32[]{:S(2)}) %collective-permute-start.8) | collective-permute-done | bytes 131104 | tf_op jit(solution)/shard_map/ppermute | solution.py:328
  83.8 1.2 %copy-done.2 = bf16[128,16,256]{2,1,0:T(8,128)(2,1)S(1)} copy-done((bf16[128,16,256]{2,1,0:T(8,128)(2,1)S(1)}, bf16[128,16,256]{2,1,0:T(8,128)(2,1)}, u32[]{:S(2)}) %copy-start.2) | copy-done | bytes 1048600
  85.1 2.9 %shard_map.115 = bf16[128,2048]{1,0:T(8,128)(2,1)} custom-call(s32[1]{0:T(128)} %bitcast.me_ref, s32[16,128]{1,0:T(8,128)S(1)} %copy.13.len_ref, bf16[128,2048]{1,0:T(8,128)(2,1)S(1)} %copy-done.3, bf16[128,256]{1,0:T(8,128)(2,1)S(1)} %copy-done.4, bf16[128,256]{1,0:T(8,128)(2,1)S(1)} %copy-done.5, bf16[128,16,256]{2,1,0:T(8,128)(2,1)S(1)} %copy-done.1, ...), custom_call_target="tpu_custom_call" | custom-call | flops 134217728 | bytes 3145728 | tf_op jit(solution)/shard_map/pallas_call | solution.py:253
  (34 shorter events, 3.6 us)
Async XLA Ops:
  2.4 33.0 %all-to-all-start = ((bf16[8,64,1024]{2,1,0:T(8,128)(2,1)}), bf16[8,64,1024]{2,1,0:T(8,128)(2,1)S(1)}, u32[]{:S(2)}, u32[]{:S(2)}) async-start(bf16[8,64,1024]{2,1,0:T(8,128)(2,1)} %shard_map.112), calls=%async_computation | async-start | bytes 2097152 | tf_op jit(solution)/shard_map/all_to_all | solution.py:341
  35.5 36.2 %all-to-all-start.1 = ((bf16[8,64,512]{2,1,0:T(8,128)(2,1)}), bf16[8,64,512]{2,1,0:T(8,128)(2,1)S(1)}, u32[]{:S(2)}, u32[]{:S(2)}) async-start(bf16[8,64,512]{2,1,0:T(8,128)(2,1)} %shard_map.111), calls=%async_computation.1 | async-start | bytes 1048576 | tf_op jit(solution)/shard_map/all_to_all | solution.py:341
  42.0 12.5 %collective-permute-start = (bf16[128,1152]{1,0:T(8,128)(2,1)}, bf16[128,1152]{1,0:T(8,128)(2,1)S(1)}, u32[]{:S(2)}, u32[]{:S(2)}) collective-permute-start(bf16[128,1152]{1,0:T(8,128)(2,1)} %get-tuple-element.38), channel_id=1, source_target_pairs={{0,2},{2,0},{16,18},{18,16},{1,3},{3,1},{17,19},{19,17},{4,6},{6,4... | collective-permute-start | bytes 884744 | tf_op jit(solution)/shard_map/ppermute | solution.py:328
  44.1 10.4 %collective-permute-start.1 = (bf16[128,1152]{1,0:T(8,128)(2,1)}, bf16[128,1152]{1,0:T(8,128)(2,1)S(1)}, u32[]{:S(2)}, u32[]{:S(2)}) collective-permute-start(bf16[128,1152]{1,0:T(8,128)(2,1)} %get-tuple-element.39), channel_id=1, source_target_pairs={{0,16},{2,18},{16,0},{18,2},{1,17},{3,19},{17,1},{19,3},{4,20},{6,... | collective-permute-start | bytes 884744 | tf_op jit(solution)/shard_map/ppermute | solution.py:328
  45.8 15.7 %copy-start = (bf16[128,1152]{1,0:T(8,128)(2,1)S(1)}, bf16[128,1152]{1,0:T(8,128)(2,1)}, u32[]{:S(2)}) copy-start(bf16[128,1152]{1,0:T(8,128)(2,1)} %get-tuple-element.37.refs_0_) | copy-start | bytes 884740
  45.8 15.7 %collective-permute-start.2 = (bf16[128,1152]{1,0:T(8,128)(2,1)}, bf16[128,1152]{1,0:T(8,128)(2,1)S(1)}, u32[]{:S(2)}, u32[]{:S(2)}) collective-permute-start(bf16[128,1152]{1,0:T(8,128)(2,1)} %get-tuple-element.40), channel_id=1, source_target_pairs={{0,18},{2,16},{16,2},{18,0},{1,19},{3,17},{17,3},{19,1},{4,22},{6,... | collective-permute-start | bytes 884744 | tf_op jit(solution)/shard_map/ppermute | solution.py:328
  63.1 5.0 %copy-start.10 = (s32[128]{0:T(128)S(1)}, s32[128]{0:T(128)}, u32[]{:S(2)}) copy-start(s32[128]{0:T(128)} %param.21) | copy-start | bytes 1540
  63.1 1.4 %collective-permute-start.3 = (f32[256,128]{1,0:T(8,128)S(1)}, f32[256,128]{1,0:T(8,128)S(1)}, u32[]{:S(2)}, u32[]{:S(2)}) collective-permute-start(f32[256,128]{1,0:T(8,128)S(1)} %shard_map.113), channel_id=1, source_target_pairs={{0,1},{1,0},{2,3},{3,2},{4,5},{5,4},{6,7},{7,6},{8,9},{9,8},{10,11... | collective-permute-start | bytes 393224 | tf_op jit(solution)/shard_map/ppermute | solution.py:366
  64.5 5.8 %collective-permute-start.6 = (bf16[256,128]{1,0:T(8,128)(2,1)S(1)}, bf16[256,128]{1,0:T(8,128)(2,1)S(1)}, u32[]{:S(2)}, u32[]{:S(2)}) collective-permute-start(bf16[256,128]{1,0:T(8,128)(2,1)S(1)} %add_convert_fusion.refs_4_), channel_id=1, source_target_pairs={{0,18},{2,16},{16,2},{18,0},{1,19},{3,17},{17,3},{19,1},{4,22},{6,... | collective-permute-start | bytes 196616 | tf_op jit(solution)/shard_map/ppermute | solution.py:328
  65.0 5.3 %collective-permute-start.5 = (bf16[256,128]{1,0:T(8,128)(2,1)S(1)}, bf16[256,128]{1,0:T(8,128)(2,1)S(1)}, u32[]{:S(2)}, u32[]{:S(2)}) collective-permute-start(bf16[256,128]{1,0:T(8,128)(2,1)S(1)} %add_convert_fusion.refs_4_), channel_id=1, source_target_pairs={{0,16},{2,18},{16,0},{18,2},{1,17},{3,19},{17,1},{19,3},{4,20},{6,... | collective-permute-start | bytes 196616 | tf_op jit(solution)/shard_map/ppermute | solution.py:328
  66.7 4.3 %collective-permute-start.4 = (bf16[256,128]{1,0:T(8,128)(2,1)S(1)}, bf16[256,128]{1,0:T(8,128)(2,1)S(1)}, u32[]{:S(2)}, u32[]{:S(2)}) collective-permute-start(bf16[256,128]{1,0:T(8,128)(2,1)S(1)} %add_convert_fusion.refs_4_), channel_id=1, source_target_pairs={{0,2},{2,0},{16,18},{18,16},{1,3},{3,1},{17,19},{19,17},{4,6},{6,4... | collective-permute-start | bytes 196616 | tf_op jit(solution)/shard_map/ppermute | solution.py:328
  68.2 15.6 %copy-start.1 = (bf16[128,16,256]{2,1,0:T(8,128)(2,1)S(1)}, bf16[128,16,256]{2,1,0:T(8,128)(2,1)}, u32[]{:S(2)}) copy-start(bf16[128,16,256]{2,1,0:T(8,128)(2,1)} %get-tuple-element.35.refs_3_) | copy-start | bytes 3145732
  68.2 15.6 %copy-start.3 = (bf16[128,2048]{1,0:T(8,128)(2,1)S(1)}, bf16[128,2048]{1,0:T(8,128)(2,1)}, u32[]{:S(2)}) copy-start(bf16[128,2048]{1,0:T(8,128)(2,1)} %get-tuple-element.32.refs_0_) | copy-start | bytes 1572868
  70.3 0.6 copy-start.6
  71.0 0.6 copy-start.8
  71.6 0.8 copy-start.7
  72.5 0.8 copy-start.9
  74.5 5.6 %collective-permute-start.7 = (bf16[128,512]{1,0:T(8,128)(2,1)}, bf16[128,512]{1,0:T(8,128)(2,1)S(1)}, u32[]{:S(2)}, u32[]{:S(2)}) collective-permute-start(bf16[128,512]{1,0:T(8,128)(2,1)} %get-tuple-element.44), channel_id=1, source_target_pairs={{0,2},{2,0},{16,18},{18,16},{1,3},{3,1},{17,19},{19,17},{4,6},{6,4... | collective-permute-start | bytes 393224 | tf_op jit(solution)/shard_map/ppermute | solution.py:328
  75.8 8.0 %collective-permute-start.8 = (bf16[128,512]{1,0:T(8,128)(2,1)}, bf16[128,512]{1,0:T(8,128)(2,1)S(1)}, u32[]{:S(2)}, u32[]{:S(2)}) collective-permute-start(bf16[128,512]{1,0:T(8,128)(2,1)} %get-tuple-element.45), channel_id=1, source_target_pairs={{0,16},{2,18},{16,0},{18,2},{1,17},{3,19},{17,1},{19,3},{4,20},{6,... | collective-permute-start | bytes 393224 | tf_op jit(solution)/shard_map/ppermute | solution.py:328
  76.5 7.3 %copy-start.4 = (bf16[128,256]{1,0:T(8,128)(2,1)S(1)}, bf16[128,256]{1,0:T(8,128)(2,1)}, u32[]{:S(2)}) copy-start(bf16[128,256]{1,0:T(8,128)(2,1)} %get-tuple-element.33.refs_1_) | copy-start | bytes 196612
  76.5 7.3 %copy-start.5 = (bf16[128,256]{1,0:T(8,128)(2,1)S(1)}, bf16[128,256]{1,0:T(8,128)(2,1)}, u32[]{:S(2)}) copy-start(bf16[128,256]{1,0:T(8,128)(2,1)} %get-tuple-element.34.refs_2_) | copy-start | bytes 196612
  76.5 7.3 %collective-permute-start.9 = (bf16[128,512]{1,0:T(8,128)(2,1)}, bf16[128,512]{1,0:T(8,128)(2,1)S(1)}, u32[]{:S(2)}, u32[]{:S(2)}) collective-permute-start(bf16[128,512]{1,0:T(8,128)(2,1)} %get-tuple-element.46), channel_id=1, source_target_pairs={{0,18},{2,16},{16,2},{18,0},{1,19},{3,17},{17,3},{19,1},{4,22},{6,... | collective-permute-start | bytes 393224 | tf_op jit(solution)/shard_map/ppermute | solution.py:328
  83.8 1.2 %copy-start.2 = (bf16[128,16,256]{2,1,0:T(8,128)(2,1)S(1)}, bf16[128,16,256]{2,1,0:T(8,128)(2,1)}, u32[]{:S(2)}) copy-start(bf16[128,16,256]{2,1,0:T(8,128)(2,1)} %get-tuple-element.36.refs_4_) | copy-start | bytes 3145732

commit v10 on v9

--- a/solution.py
+++ b/solution.py
@@ -46,10 +46,6 @@
     run_copies(moves, sems)
 
 
-def load_kernel(count, *refs):
-    run_copies(list(zip(refs[:count], refs[count : 2 * count])), refs[-1])
-
-
 def row_kernel(parts, me_ref, map_ref, ids_ref, hidden_ref, *refs):
     out_refs, sems = refs[:parts], refs[parts]
     requests, wide = hidden_ref.shape
@@ -73,9 +69,8 @@
     run_copies(moves, sems, owners)
 
 
-def owner_mask(rows_ref, first, count, rank):
-    features = rows_ref.shape[1] - LANES
-    owners = rows_ref[:, features:].astype(jnp.float32).astype(jnp.int32)
+def owner_mask(owners, first, count, rank):
+    owners = owners.astype(jnp.float32).astype(jnp.int32)
     wide = jnp.concatenate([owners] * (count * rank // LANES), axis=1)
     return wide == lax.broadcasted_iota(jnp.int32, (1, count * rank), 1) // rank + first
 
@@ -92,7 +87,7 @@
         sums = lax.dot_general(
             ref[:, :features], weight, NT, preferred_element_type=jnp.float32
         )
-        sums = jnp.where(owner_mask(ref, step * count, count, rank), sums, 0.0)
+        sums = jnp.where(owner_mask(ref[:, features:], step * count, count, rank), sums, 0.0)
         total = sums[:, :LANES]
         for k in range(1, count * rank // LANES):
             total = total + sums[:, k * LANES : (k + 1) * LANES]
@@ -109,10 +104,10 @@
 
 
 def expand_kernel(parts, *refs):
-    row_refs, low_refs, weight_ref = refs[:parts], refs[parts : 2 * parts], refs[2 * parts]
+    owner_refs, low_refs, weight_ref = refs[:parts], refs[parts : 2 * parts], refs[2 * parts]
     out_refs, total_ref = refs[2 * parts + 1 : 3 * parts + 1], refs[3 * parts + 1]
     count, rank, outputs = weight_ref.shape
-    requests = row_refs[0].shape[0]
+    requests = owner_refs[0].shape[0]
     step, last = pl.program_id(0), pl.num_programs(0) - 1
     weight = weight_ref[...].reshape(count * rank, outputs)
     half = parts // 2
@@ -130,7 +125,8 @@
         for part in (s, s + half):
             first, other = (straight, turned) if part < half else (turned, straight)
             wide = jnp.concatenate([jnp.where(low, first, other)] * (count * rank // LANES), axis=1)
-            wide = jnp.where(owner_mask(row_refs[part], step * count, count, rank), wide, 0.0)
+            mask = owner_mask(owner_refs[part][...], step * count, count, rank)
+            wide = jnp.where(mask, wide, 0.0)
             product = jnp.dot(
                 wide.astype(jnp.bfloat16), weight, preferred_element_type=jnp.float32
             )
@@ -151,9 +147,7 @@
 def attend_kernel(parts, me_ref, len_ref, *refs):
     base_ref, nk_ref, nv_ref, ck_ref, cv_ref, *delta_refs, out_ref = refs
     me = me_ref[0]
-    block = STEP * BATCH
-    steps = base_ref.shape[0] // block
-    requests, columns = base_ref.shape
+    columns = base_ref.shape[1]
     width = columns // parts
     groups = nk_ref.shape[1] // HEAD
     slots = ck_ref.shape[1]
@@ -179,10 +173,11 @@
     scale = 1.0 / math.sqrt(HEAD)
     ones = jnp.ones((keys_in, HEAD), jnp.bfloat16)
 
-    for step in range(steps):
+    if True:
+        step = pl.program_id(0)
         units = []
         for j in range(BATCH):
-            start = step * block + j * STEP
+            start = j * STEP
             at = pl.ds(start, STEP)
             pieces = []
             for s in range(parts):
@@ -249,13 +244,15 @@
     kv = new_key.shape[1]
     slots = cache_keys.shape[1]
     lengths = jnp.tile(lengths.reshape(requests // HALF, HALF), (1, columns // HEAD))
+    block = STEP * BATCH
+    rows2 = lambda a: pl.BlockSpec((block,) + a.shape[1:], lambda i: (i,) + (0,) * (a.ndim - 1))
     arrays = [base, new_key, new_value, cache_keys, cache_values, *deltas]
     return pl.pallas_call(
         functools.partial(attend_kernel, len(deltas)),
         out_shape=jax.ShapeDtypeStruct((requests, columns), jnp.bfloat16),
-        in_specs=[SMEM] + [VMEM] * (1 + len(arrays)),
-        out_specs=VMEM,
-        compiler_params=PARAMS,
+        grid=(requests // block,),
+        in_specs=[SMEM, whole(lengths), *map(rows2, arrays)],
+        out_specs=rows2(base),
         cost_estimate=pl.CostEstimate(
             flops=4 * requests * HALF * slots * columns,
             bytes_accessed=4 * requests * (columns + slots * kv),
@@ -290,15 +287,16 @@
 def expand_rows(rows, lows, weight):
     parts, requests, outputs = len(rows), rows[0].shape[0], weight.shape[2]
     steps, spec = in_chunks(weight)
+    last_lanes = rows[0].shape[1] // LANES - 1
+    owners = pl.BlockSpec((requests, LANES), lambda i: (0, last_lanes))
     out = jax.ShapeDtypeStruct((requests, outputs), jnp.bfloat16)
     return pl.pallas_call(
         functools.partial(expand_kernel, parts),
         out_shape=[out] * parts,
         grid=(steps,),
-        in_specs=[*map(whole, rows), *map(whole, lows), spec],
+        in_specs=[owners] * parts + [*map(whole, lows), spec],
         out_specs=[whole(out)] * parts,
         scratch_shapes=[pltpu.VMEM((parts, requests, outputs), jnp.float32)],
-        compiler_params=PARAMS,
     )(*rows, *lows, weight)
 
 
@@ -350,17 +348,7 @@
         scratch_shapes=[pltpu.SemaphoreType.DMA((square,))],
     )(me[None], owner_map, adapter_ids.T, hidden)
     rows = [rows[0]] + [swap(rows[s], s) for s in range(1, square)]
-    arrays = [query_base, new_key, new_value, cache_keys, cache_values]
-    arrays = pl.pallas_call(
-        functools.partial(load_kernel, len(arrays)),
-        out_shape=[jax.ShapeDtypeStruct(a.shape, a.dtype) for a in arrays],
-        in_specs=[HBM] * len(arrays),
-        out_specs=[VMEM] * len(arrays),
-        scratch_shapes=[pltpu.SemaphoreType.DMA((len(arrays),))],
-    )(*arrays)
-    rows[0], *arrays = lax.optimization_barrier((rows[0], *arrays))
-
-    expand, shrink = to_pool(expand_factors, shrink)
+    expand, rows = to_pool(expand_factors, rows)
     partial = shrink_rows(rows, shrink)
     for c in range(1, tp):
         partial = partial + lax.ppermute(partial, "tp", [(t, t ^ c) for t in range(tp)])
@@ -368,7 +356,9 @@
     lows = [partial] + [swap(partial, s) for s in range(1, square)]
     deltas = expand_rows(rows, lows, expand)
     deltas = [deltas[0]] + [swap(deltas[s], s) for s in range(1, square)]
-    return attend(me[None], *arrays, lengths, deltas)
+    return attend(
+        me[None], query_base, new_key, new_value, cache_keys, cache_values, lengths, deltas
+    )
 
 
 def solution(mesh):

time: 88.5 us -> 75.1 us (0.85)
  waiting for transfers between devices: 45.2 us -> 32.2 us
  local copies, waits for them, and re-layouts: 4.36 us -> 2.94 us
  starting transfers between devices: 21.8 us -> 22.8 us
    all_to_all x2, waiting for transfers between devices: 23.6 us -> 7.64 us  [to_pool(): lax.all_to_all(send, ('level', 'side'), split_axis=0, concat_axis=0, tile...]
    pallas_call x1 -> x0, Pallas kernels: 3.33 us -> none  [per_device(): pl.pallas_call(functools.partial(load_kernel, len(arrays)), out_shape=[ja...]
    ppermute x9, waiting for transfers between devices: 20.3 us -> 23.2 us  [swap(): return lax.ppermute(a, ('rep', 'side'), pairs)]
    pallas_call x1, Pallas kernels: 2.86 us -> 5.08 us  [attend(): pl.pallas_call(functools.partial(attend_kernel, len(deltas)), out_shape=j...]
    unnamed x22 -> x26, local copies, waits for them, and re-layouts: 4.16 us -> 2.12 us
    pallas_call x1, Pallas kernels: 1.22 us -> 2.5 us  [expand_rows(): pl.pallas_call(functools.partial(expand_kernel, parts), out_shape=[out] *...]
    all_to_all x2, starting transfers between devices: 10.9 us -> 11.9 us  [to_pool(): lax.all_to_all(send, ('level', 'side'), split_axis=0, concat_axis=0, tile...]
  transfers between devices with their start and end apart: 12 -> 12, of which waited for: 8 -> 6; matrix products, arithmetic and copies ran while one was open for 0% -> 1% of each run, Pallas kernels for 11% -> 9%
where the time goes in v10:
time: 75.1 us; the launch traced here: 74.6 us
  waiting for transfers between devices  32.2 us (43%)
  starting transfers between devices  22.8 us (30%)
  Pallas kernels  16.5 us (22%)
  local copies, waits for them, and re-layouts  2.94 us (4%)
    ppermute x9, waiting for transfers between devices, swap(): return lax.ppermute(a, ('rep', 'side'), pairs)  23.2 us
    all_to_all x2, starting transfers between devices, to_pool(): lax.all_to_all(send, ('level', 'side'), split_axis=0, concat_axis=0, tile...  11.9 us
    ppermute x9, starting transfers between devices, swap(): return lax.ppermute(a, ('rep', 'side'), pairs)  10.8 us
    all_to_all x2, waiting for transfers between devices, to_pool(): lax.all_to_all(send, ('level', 'side'), split_axis=0, concat_axis=0, tile...  7.64 us
    pallas_call x1, Pallas kernels, attend(): pl.pallas_call(functools.partial(attend_kernel, len(deltas)), out_shape=j...  5.08 us
    pallas_call x2, Pallas kernels, to_pool(): pl.pallas_call(functools.partial(factor_kernel, sides, levels), out_shape...  4.53 us
    pallas_call x1, Pallas kernels, per_device(): pl.pallas_call(functools.partial(row_kernel, square), out_shape=[jax.Shap...  2.91 us
    pallas_call x1, Pallas kernels, expand_rows(): pl.pallas_call(functools.partial(expand_kernel, parts), out_shape=[out] *...  2.5 us
  transfers between devices with their start and end apart: 12, of which 6 were waited for; matrix products, arithmetic and copies ran while one was open for 1% of the time, Pallas kernels for 9%

profile of v10, /device:TPU:0, one launch (start us, length us, event | category | flops | bytes accessed | tf_op | source)
XLA Modules:
  0.0 74.6 jit_solution(16360427169203085431)
XLA Ops:
  0.0 2.4 %shard_map.111 = bf16[8,64,1024]{2,1,0:T(8,128)(2,1)} custom-call(s32[1]{0:T(128)} %bitcast.2.rep_ref, bf16[1,64,4096]{2,1,0:T(8,128)(2,1)} %bitcast.6), custom_call_target="tpu_custom_call" | custom-call | tf_op jit(solution)/shard_map/pallas_call | solution.py:330
  2.4 7.3 %all-to-all-start = ((bf16[8,64,1024]{2,1,0:T(8,128)(2,1)}), bf16[8,64,1024]{2,1,0:T(8,128)(2,1)S(1)}, u32[]{:S(2)}, u32[]{:S(2)}) async-start(bf16[8,64,1024]{2,1,0:T(8,128)(2,1)} %shard_map.111), calls=%async_computation | async-start | bytes 2097152 | tf_op jit(solution)/shard_map/all_to_all | solution.py:339
  9.7 2.9 %shard_map.110 = (bf16[128,1152]{1,0:T(8,128)(2,1)}, bf16[128,1152]{1,0:T(8,128)(2,1)}, bf16[128,1152]{1,0:T(8,128)(2,1)}, bf16[128,1152]{1,0:T(8,128)(2,1)}) custom-call(s32[1]{0:T(128)} %bitcast.me_ref, s32[8]{0:T(128)} %map_ref.1, s32[1,128]{1,0:T(1,128)} %bitcast.7, bf16[128,4096]{1,0:T(8,128)(2,1)} %hidden_ref.1), custom_call_target="tpu_custom_call" | custom-call | tf_op jit(solution)/shard_map/pallas_call | solution.py:343
  12.6 2.1 %collective-permute-start = (bf16[128,1152]{1,0:T(8,128)(2,1)}, bf16[128,1152]{1,0:T(8,128)(2,1)S(1)}, u32[]{:S(2)}, u32[]{:S(2)}) collective-permute-start(bf16[128,1152]{1,0:T(8,128)(2,1)} %get-tuple-element.19), channel_id=1, source_target_pairs={{0,2},{2,0},{16,18},{18,16},{1,3},{3,1},{17,19},{19,17},{4,6},{6,4... | collective-permute-start | bytes 884744 | tf_op jit(solution)/shard_map/ppermute | solution.py:326
  14.7 1.7 %collective-permute-start.1 = (bf16[128,1152]{1,0:T(8,128)(2,1)}, bf16[128,1152]{1,0:T(8,128)(2,1)S(1)}, u32[]{:S(2)}, u32[]{:S(2)}) collective-permute-start(bf16[128,1152]{1,0:T(8,128)(2,1)} %get-tuple-element.20), channel_id=1, source_target_pairs={{0,16},{2,18},{16,0},{18,2},{1,17},{3,19},{17,1},{19,3},{4,20},{6,... | collective-permute-start | bytes 884744 | tf_op jit(solution)/shard_map/ppermute | solution.py:326
  16.4 2.1 %shard_map.109 = bf16[8,64,512]{2,1,0:T(8,128)(2,1)} custom-call(s32[1]{0:T(128)} %bitcast.2.rep_ref, bf16[1,64,2048]{2,1,0:T(8,128)(2,1)} %factor_ref.1), custom_call_target="tpu_custom_call" | custom-call | tf_op jit(solution)/shard_map/pallas_call | solution.py:330
  18.5 11.9 %collective-permute-done.refs_1_ = bf16[128,1152]{1,0:T(8,128)(2,1)S(1)} collective-permute-done((bf16[128,1152]{1,0:T(8,128)(2,1)}, bf16[128,1152]{1,0:T(8,128)(2,1)S(1)}, u32[]{:S(2)}, u32[]{:S(2)}) %collective-permute-start) | collective-permute-done | bytes 294944 | tf_op jit(solution)/shard_map/ppermute | solution.py:326
  30.4 6.7 %collective-permute-done.2.refs_3_ = bf16[128,1152]{1,0:T(8,128)(2,1)S(1)} collective-permute-done((bf16[128,1152]{1,0:T(8,128)(2,1)}, bf16[128,1152]{1,0:T(8,128)(2,1)S(1)}, u32[]{:S(2)}, u32[]{:S(2)}) %collective-permute-start.2) | collective-permute-done | bytes 294944 | tf_op jit(solution)/shard_map/ppermute | solution.py:326
  37.1 4.7 %all-to-all-start.1 = ((bf16[8,64,512]{2,1,0:T(8,128)(2,1)}), bf16[8,64,512]{2,1,0:T(8,128)(2,1)S(1)}, u32[]{:S(2)}, u32[]{:S(2)}) async-start(bf16[8,64,512]{2,1,0:T(8,128)(2,1)} %shard_map.109), calls=%async_computation.1 | async-start | bytes 1048576 | tf_op jit(solution)/shard_map/all_to_all | solution.py:339
  41.8 1.5 %shard_map.112 = f32[256,128]{1,0:T(8,128)S(1)} custom-call(bf16[128,1152]{1,0:T(8,128)(2,1)S(1)} %copy-done, bf16[128,1152]{1,0:T(8,128)(2,1)S(1)} %collective-permute-done.refs_1_, bf16[128,1152]{1,0:T(8,128)(2,1)S(1)} %collective-permute-done.1.refs_2_, bf16[128,1152]{1,0:T(8,128)(2,1)S(1)} %collective-permute-done.2.refs_3_, ...), custom_call_target="tpu_custom_call" | custom-call | tf_op jit(solution)/shard_map/pallas_call | solution.py:277
  43.4 1.3 %collective-permute-done.3 = f32[256,128]{1,0:T(8,128)S(1)} collective-permute-done((f32[256,128]{1,0:T(8,128)S(1)}, f32[256,128]{1,0:T(8,128)S(1)}, u32[]{:S(2)}, u32[]{:S(2)}) %collective-permute-start.3) | collective-permute-done | bytes 131104 | tf_op jit(solution)/shard_map/ppermute | solution.py:354
  44.8 1.9 %collective-permute-start.6 = (bf16[256,128]{1,0:T(8,128)(2,1)S(1)}, bf16[256,128]{1,0:T(8,128)(2,1)S(1)}, u32[]{:S(2)}, u32[]{:S(2)}) collective-permute-start(bf16[256,128]{1,0:T(8,128)(2,1)S(1)} %add_convert_fusion.refs_4_), channel_id=1, source_target_pairs={{0,18},{2,16},{16,2},{18,0},{1,19},{3,17},{17,3},{19,1},{4,22},{6,... | collective-permute-start | bytes 196616 | tf_op jit(solution)/shard_map/ppermute | solution.py:326
  46.6 1.7 %collective-permute-start.5 = (bf16[256,128]{1,0:T(8,128)(2,1)S(1)}, bf16[256,128]{1,0:T(8,128)(2,1)S(1)}, u32[]{:S(2)}, u32[]{:S(2)}) collective-permute-start(bf16[256,128]{1,0:T(8,128)(2,1)S(1)} %add_convert_fusion.refs_4_), channel_id=1, source_target_pairs={{0,16},{2,18},{16,0},{18,2},{1,17},{3,19},{17,1},{19,3},{4,20},{6,... | collective-permute-start | bytes 196616 | tf_op jit(solution)/shard_map/ppermute | solution.py:326
  48.5 7.6 %all-to-all-done.1.refs_8_ = bf16[8,64,512]{2,1,0:T(8,128)(2,1)S(1)} async-done(((bf16[8,64,512]{2,1,0:T(8,128)(2,1)}), bf16[8,64,512]{2,1,0:T(8,128)(2,1)S(1)}, u32[]{:S(2)}, u32[]{:S(2)}) %all-to-all-start.1) | async-done | bytes 524320 | tf_op jit(solution)/shard_map/all_to_all | solution.py:339
  56.2 0.7 %copy-done.4 = bf16[8,64,512]{2,1,0:T(8,128)(2,1)} copy-done((bf16[8,64,512]{2,1,0:T(8,128)(2,1)}, bf16[8,64,512]{2,1,0:T(8,128)(2,1)S(1)}, u32[]{:S(2)}) %copy-start.4) | copy-done | bytes 524312
  56.9 0.6 copy-done.11
  57.6 2.5 %shard_map.113 = (bf16[128,512]{1,0:T(8,128)(2,1)}, bf16[128,512]{1,0:T(8,128)(2,1)}, bf16[128,512]{1,0:T(8,128)(2,1)}, bf16[128,512]{1,0:T(8,128)(2,1)}) custom-call(bf16[128,1152]{1,0:T(8,128)(2,1)} %get-tuple-element.22.refs_0_, bf16[128,1152]{1,0:T(8,128)(2,1)} %copy-done.1, bf16[128,1152]{1,0:T(8,128)(2,1)} %copy-done.2, bf16[128,1152]{1,0:T(8,128)(2,1)} %copy-done.3, ...), custom_call_target="tpu_custom_call" | custom-call | tf_op jit(solution)/shard_map/pallas_call | solution.py:293
  60.1 1.5 %collective-permute-start.7 = (bf16[128,512]{1,0:T(8,128)(2,1)}, bf16[128,512]{1,0:T(8,128)(2,1)S(1)}, u32[]{:S(2)}, u32[]{:S(2)}) collective-permute-start(bf16[128,512]{1,0:T(8,128)(2,1)} %get-tuple-element.28), channel_id=1, source_target_pairs={{0,2},{2,0},{16,18},{18,16},{1,3},{3,1},{17,19},{19,17},{4,6},{6,4... | collective-permute-start | bytes 393224 | tf_op jit(solution)/shard_map/ppermute | solution.py:326
  61.9 1.7 %collective-permute-start.9 = (bf16[128,512]{1,0:T(8,128)(2,1)}, bf16[128,512]{1,0:T(8,128)(2,1)S(1)}, u32[]{:S(2)}, u32[]{:S(2)}) collective-permute-start(bf16[128,512]{1,0:T(8,128)(2,1)} %get-tuple-element.30), channel_id=1, source_target_pairs={{0,18},{2,16},{16,2},{18,0},{1,19},{3,17},{17,3},{19,1},{4,22},{6,... | collective-permute-start | bytes 393224 | tf_op jit(solution)/shard_map/ppermute | solution.py:326
  63.6 0.7 copy.13.len_ref
  64.2 2.1 %collective-permute-done.7.refs_6_ = bf16[128,512]{1,0:T(8,128)(2,1)S(1)} collective-permute-done((bf16[128,512]{1,0:T(8,128)(2,1)}, bf16[128,512]{1,0:T(8,128)(2,1)S(1)}, u32[]{:S(2)}, u32[]{:S(2)}) %collective-permute-start.7) | collective-permute-done | bytes 131104 | tf_op jit(solution)/shard_map/ppermute | solution.py:326
  66.3 2.6 %collective-permute-done.8.refs_7_ = bf16[128,512]{1,0:T(8,128)(2,1)S(1)} collective-permute-done((bf16[128,512]{1,0:T(8,128)(2,1)}, bf16[128,512]{1,0:T(8,128)(2,1)S(1)}, u32[]{:S(2)}, u32[]{:S(2)}) %collective-permute-start.8) | collective-permute-done | bytes 131104 | tf_op jit(solution)/shard_map/ppermute | solution.py:326
  68.9 0.6 copy-done.7
  69.6 5.1 %shard_map.114 = bf16[128,2048]{1,0:T(8,128)(2,1)} custom-call(s32[1]{0:T(128)} %bitcast.me_ref, s32[16,128]{1,0:T(8,128)} %copy.13.len_ref, bf16[128,2048]{1,0:T(8,128)(2,1)} %refs_0_.1, bf16[128,256]{1,0:T(8,128)(2,1)} %refs_1_.1, bf16[128,256]{1,0:T(8,128)(2,1)} %refs_2_.1, bf16[128,16,256]{2,1,0:T(8,128)(2,1)} %refs_3_.1, bf16[128,16,256]{2,1,0:T(8,128)(2,1)} %refs_4_.1, ...), custom_call_target="tpu_custom_call" | custom-call | flops 134217728 | bytes 3145728 | tf_op jit(solution)/shard_map/pallas_call | solution.py:250
  (37 shorter events, 0.7 us)
Async XLA Ops:
  2.4 34.6 %all-to-all-start = ((bf16[8,64,1024]{2,1,0:T(8,128)(2,1)}), bf16[8,64,1024]{2,1,0:T(8,128)(2,1)S(1)}, u32[]{:S(2)}, u32[]{:S(2)}) async-start(bf16[8,64,1024]{2,1,0:T(8,128)(2,1)} %shard_map.111), calls=%async_computation | async-start | bytes 2097152 | tf_op jit(solution)/shard_map/all_to_all | solution.py:339
  12.6 17.8 %collective-permute-start = (bf16[128,1152]{1,0:T(8,128)(2,1)}, bf16[128,1152]{1,0:T(8,128)(2,1)S(1)}, u32[]{:S(2)}, u32[]{:S(2)}) collective-permute-start(bf16[128,1152]{1,0:T(8,128)(2,1)} %get-tuple-element.19), channel_id=1, source_target_pairs={{0,2},{2,0},{16,18},{18,16},{1,3},{3,1},{17,19},{19,17},{4,6},{6,4... | collective-permute-start | bytes 884744 | tf_op jit(solution)/shard_map/ppermute | solution.py:326
  14.7 15.7 %collective-permute-start.1 = (bf16[128,1152]{1,0:T(8,128)(2,1)}, bf16[128,1152]{1,0:T(8,128)(2,1)S(1)}, u32[]{:S(2)}, u32[]{:S(2)}) collective-permute-start(bf16[128,1152]{1,0:T(8,128)(2,1)} %get-tuple-element.20), channel_id=1, source_target_pairs={{0,16},{2,18},{16,0},{18,2},{1,17},{3,19},{17,1},{19,3},{4,20},{6,... | collective-permute-start | bytes 884744 | tf_op jit(solution)/shard_map/ppermute | solution.py:326
  16.4 20.7 %collective-permute-start.2 = (bf16[128,1152]{1,0:T(8,128)(2,1)}, bf16[128,1152]{1,0:T(8,128)(2,1)S(1)}, u32[]{:S(2)}, u32[]{:S(2)}) collective-permute-start(bf16[128,1152]{1,0:T(8,128)(2,1)} %get-tuple-element.21), channel_id=1, source_target_pairs={{0,18},{2,16},{16,2},{18,0},{1,19},{3,17},{17,3},{19,1},{4,22},{6,... | collective-permute-start | bytes 884744 | tf_op jit(solution)/shard_map/ppermute | solution.py:326
  30.4 11.3 %copy-start.1 = (bf16[128,1152]{1,0:T(8,128)(2,1)}, bf16[128,1152]{1,0:T(8,128)(2,1)S(1)}, u32[]{:S(2)}) copy-start(bf16[128,1152]{1,0:T(8,128)(2,1)S(1)} %collective-permute-done.refs_1_) | copy-start | bytes 884740
  30.4 11.3 %copy-start.2 = (bf16[128,1152]{1,0:T(8,128)(2,1)}, bf16[128,1152]{1,0:T(8,128)(2,1)S(1)}, u32[]{:S(2)}) copy-start(bf16[128,1152]{1,0:T(8,128)(2,1)S(1)} %collective-permute-done.1.refs_2_) | copy-start | bytes 884740
  37.1 4.7 %copy-start.3 = (bf16[128,1152]{1,0:T(8,128)(2,1)}, bf16[128,1152]{1,0:T(8,128)(2,1)S(1)}, u32[]{:S(2)}) copy-start(bf16[128,1152]{1,0:T(8,128)(2,1)S(1)} %collective-permute-done.2.refs_3_) | copy-start | bytes 884740
  37.1 4.7 %copy-start = (bf16[128,1152]{1,0:T(8,128)(2,1)S(1)}, bf16[128,1152]{1,0:T(8,128)(2,1)}, u32[]{:S(2)}) copy-start(bf16[128,1152]{1,0:T(8,128)(2,1)} %get-tuple-element.22.refs_0_) | copy-start | bytes 884740
  37.1 19.1 %all-to-all-start.1 = ((bf16[8,64,512]{2,1,0:T(8,128)(2,1)}), bf16[8,64,512]{2,1,0:T(8,128)(2,1)S(1)}, u32[]{:S(2)}, u32[]{:S(2)}) async-start(bf16[8,64,512]{2,1,0:T(8,128)(2,1)} %shard_map.109), calls=%async_computation.1 | async-start | bytes 1048576 | tf_op jit(solution)/shard_map/all_to_all | solution.py:339
  43.3 5.0 %copy-start.12 = (s32[128]{0:T(128)S(1)}, s32[128]{0:T(128)}, u32[]{:S(2)}) copy-start(s32[128]{0:T(128)} %param.21) | copy-start | bytes 1540
  43.3 1.4 %collective-permute-start.3 = (f32[256,128]{1,0:T(8,128)S(1)}, f32[256,128]{1,0:T(8,128)S(1)}, u32[]{:S(2)}, u32[]{:S(2)}) collective-permute-start(f32[256,128]{1,0:T(8,128)S(1)} %shard_map.112), channel_id=1, source_target_pairs={{0,1},{1,0},{2,3},{3,2},{4,5},{5,4},{6,7},{7,6},{8,9},{9,8},{10,11... | collective-permute-start | bytes 393224 | tf_op jit(solution)/shard_map/ppermute | solution.py:354
  44.8 11.4 %copy-start.5 = (bf16[256,128]{1,0:T(8,128)(2,1)}, bf16[256,128]{1,0:T(8,128)(2,1)S(1)}, u32[]{:S(2)}) copy-start(bf16[256,128]{1,0:T(8,128)(2,1)S(1)} %add_convert_fusion.refs_4_) | copy-start | bytes 196612
  44.8 11.4 %collective-permute-start.6 = (bf16[256,128]{1,0:T(8,128)(2,1)S(1)}, bf16[256,128]{1,0:T(8,128)(2,1)S(1)}, u32[]{:S(2)}, u32[]{:S(2)}) collective-permute-start(bf16[256,128]{1,0:T(8,128)(2,1)S(1)} %add_convert_fusion.refs_4_), channel_id=1, source_target_pairs={{0,18},{2,16},{16,2},{18,0},{1,19},{3,17},{17,3},{19,1},{4,22},{6,... | collective-permute-start | bytes 196616 | tf_op jit(solution)/shard_map/ppermute | solution.py:326
  46.6 9.5 %collective-permute-start.5 = (bf16[256,128]{1,0:T(8,128)(2,1)S(1)}, bf16[256,128]{1,0:T(8,128)(2,1)S(1)}, u32[]{:S(2)}, u32[]{:S(2)}) collective-permute-start(bf16[256,128]{1,0:T(8,128)(2,1)S(1)} %add_convert_fusion.refs_4_), channel_id=1, source_target_pairs={{0,16},{2,18},{16,0},{18,2},{1,17},{3,19},{17,1},{19,3},{4,20},{6,... | collective-permute-start | bytes 196616 | tf_op jit(solution)/shard_map/ppermute | solution.py:326
  48.3 7.8 %collective-permute-start.4 = (bf16[256,128]{1,0:T(8,128)(2,1)S(1)}, bf16[256,128]{1,0:T(8,128)(2,1)S(1)}, u32[]{:S(2)}, u32[]{:S(2)}) collective-permute-start(bf16[256,128]{1,0:T(8,128)(2,1)S(1)} %add_convert_fusion.refs_4_), channel_id=1, source_target_pairs={{0,2},{2,0},{16,18},{18,16},{1,3},{3,1},{17,19},{19,17},{4,6},{6,4... | collective-permute-start | bytes 196616 | tf_op jit(solution)/shard_map/ppermute | solution.py:326
  56.1 0.8 %copy-start.4 = (bf16[8,64,512]{2,1,0:T(8,128)(2,1)}, bf16[8,64,512]{2,1,0:T(8,128)(2,1)S(1)}, u32[]{:S(2)}) copy-start(bf16[8,64,512]{2,1,0:T(8,128)(2,1)S(1)} %all-to-all-done.1.refs_8_) | copy-start | bytes 1572868
  56.1 0.8 %copy-start.9 = (bf16[256,128]{1,0:T(8,128)(2,1)}, bf16[256,128]{1,0:T(8,128)(2,1)S(1)}, u32[]{:S(2)}) copy-start(bf16[256,128]{1,0:T(8,128)(2,1)S(1)} %collective-permute-done.6.refs_7_) | copy-start | bytes 196612
  56.1 0.8 %copy-start.10 = (bf16[256,128]{1,0:T(8,128)(2,1)}, bf16[256,128]{1,0:T(8,128)(2,1)S(1)}, u32[]{:S(2)}) copy-start(bf16[256,128]{1,0:T(8,128)(2,1)S(1)} %collective-permute-done.5.refs_6_) | copy-start | bytes 196612
  60.1 6.2 %collective-permute-start.7 = (bf16[128,512]{1,0:T(8,128)(2,1)}, bf16[128,512]{1,0:T(8,128)(2,1)S(1)}, u32[]{:S(2)}, u32[]{:S(2)}) collective-permute-start(bf16[128,512]{1,0:T(8,128)(2,1)} %get-tuple-element.28), channel_id=1, source_target_pairs={{0,2},{2,0},{16,18},{18,16},{1,3},{3,1},{17,19},{19,17},{4,6},{6,4... | collective-permute-start | bytes 393224 | tf_op jit(solution)/shard_map/ppermute | solution.py:326
  61.5 7.3 %collective-permute-start.8 = (bf16[128,512]{1,0:T(8,128)(2,1)}, bf16[128,512]{1,0:T(8,128)(2,1)S(1)}, u32[]{:S(2)}, u32[]{:S(2)}) collective-permute-start(bf16[128,512]{1,0:T(8,128)(2,1)} %get-tuple-element.29), channel_id=1, source_target_pairs={{0,16},{2,18},{16,0},{18,2},{1,17},{3,19},{17,1},{19,3},{4,20},{6,... | collective-permute-start | bytes 393224 | tf_op jit(solution)/shard_map/ppermute | solution.py:326
  61.9 7.0 %collective-permute-start.9 = (bf16[128,512]{1,0:T(8,128)(2,1)}, bf16[128,512]{1,0:T(8,128)(2,1)S(1)}, u32[]{:S(2)}, u32[]{:S(2)}) collective-permute-start(bf16[128,512]{1,0:T(8,128)(2,1)} %get-tuple-element.30), channel_id=1, source_target_pairs={{0,18},{2,16},{16,2},{18,0},{1,19},{3,17},{17,3},{19,1},{4,22},{6,... | collective-permute-start | bytes 393224 | tf_op jit(solution)/shard_map/ppermute | solution.py:326
  66.3 2.6 %copy-start.6 = (bf16[128,512]{1,0:T(8,128)(2,1)}, bf16[128,512]{1,0:T(8,128)(2,1)S(1)}, u32[]{:S(2)}) copy-start(bf16[128,512]{1,0:T(8,128)(2,1)S(1)} %collective-permute-done.7.refs_6_) | copy-start | bytes 393220
  68.9 0.7 copy-start.7
  68.9 0.7 copy-start.8
  (1 other events, 0.6 us)

commit v11 on v10

--- a/solution.py
+++ b/solution.py
@@ -37,12 +37,16 @@
         copy.wait()
 
 
-def factor_kernel(sides, levels, rep_ref, factor_ref, send_ref, sems):
-    width = send_ref.shape[2]
+def factor_kernel(parts, me_ref, shrink_ref, expand_ref, own_ref, other_ref, sems):
+    features, outputs = shrink_ref.shape[2] // parts, expand_ref.shape[2] // parts
+    me = me_ref[0]
     moves = []
-    for side in range(sides):
-        share = factor_ref.at[0, :, columns(rep_ref[0] * sides + side, width)]
-        moves += [(share, send_ref.at[level * sides + side]) for level in range(levels)]
+    for at, ref in ((me, own_ref), (me ^ 1, other_ref)):
+        shrink = shrink_ref.at[0, :, columns(at, features)]
+        expand = expand_ref.at[0, :, columns(at, outputs)]
+        for k in range(ref.shape[0]):
+            moves.append((shrink, ref.at[k, :, :features]))
+            moves.append((expand, ref.at[k, :, features:]))
     run_copies(moves, sems)
 
 
@@ -69,31 +73,43 @@
     run_copies(moves, sems, owners)
 
 
-def owner_mask(owners, first, count, rank):
+def owner_mask(owners, ids, rank):
+    lane = lax.broadcasted_iota(jnp.int32, (1, len(ids) * rank), 1) // rank
+    named = jnp.full_like(lane, -1)
+    for k, owner in enumerate(ids):
+        named = jnp.where(lane == k, owner, named)
     owners = owners.astype(jnp.float32).astype(jnp.int32)
-    wide = jnp.concatenate([owners] * (count * rank // LANES), axis=1)
-    return wide == lax.broadcasted_iota(jnp.int32, (1, count * rank), 1) // rank + first
-
-
-def shrink_kernel(parts, *refs):
-    row_refs, weight_ref, out_ref = refs[:parts], refs[parts], refs[parts + 1]
-    count, rank, features = weight_ref.shape
-    requests = row_refs[0].shape[0]
-    step = pl.program_id(0)
-    weight = weight_ref[...].reshape(count * rank, features)
+    return jnp.concatenate([owners] * (len(ids) * rank // LANES), axis=1) == named
+
+
+def stacked(refs, lanes):
+    return jnp.concatenate([r[k, :, lanes] for r in refs for k in range(r.shape[0])], axis=0)
+
+
+def step_ids(ids_ref, refs):
+    count = sum(r.shape[0] for r in refs)
+    return [ids_ref[pl.program_id(0) * count + k] for k in range(count)]
+
+
+def shrink_kernel(parts, ids_ref, *refs):
+    row_refs, factor_refs, out_ref = refs[:parts], refs[parts:-1], refs[-1]
+    rank = factor_refs[0].shape[1]
+    requests, features = row_refs[0].shape[0], row_refs[0].shape[1] - LANES
+    ids = step_ids(ids_ref, factor_refs)
+    weight = stacked(factor_refs, slice(0, features))
     low = lax.broadcasted_iota(jnp.int32, (requests, LANES), 1) < rank
     folded = []
     for ref in row_refs:
         sums = lax.dot_general(
             ref[:, :features], weight, NT, preferred_element_type=jnp.float32
         )
-        sums = jnp.where(owner_mask(ref[:, features:], step * count, count, rank), sums, 0.0)
+        sums = jnp.where(owner_mask(ref[:, features:], ids, rank), sums, 0.0)
         total = sums[:, :LANES]
-        for k in range(1, count * rank // LANES):
+        for k in range(1, len(ids) * rank // LANES):
             total = total + sums[:, k * LANES : (k + 1) * LANES]
         folded.append(total + pltpu.roll(total, rank, 1))
 
-    @pl.when(step == 0)
+    @pl.when(pl.program_id(0) == 0)
     def _():
         out_ref[...] = jnp.zeros_like(out_ref)
 
@@ -103,13 +119,14 @@
         out_ref[rows, :] += jnp.where(low, folded[s], folded[s + half])
 
 
-def expand_kernel(parts, *refs):
-    owner_refs, low_refs, weight_ref = refs[:parts], refs[parts : 2 * parts], refs[2 * parts]
-    out_refs, total_ref = refs[2 * parts + 1 : 3 * parts + 1], refs[3 * parts + 1]
-    count, rank, outputs = weight_ref.shape
-    requests = owner_refs[0].shape[0]
+def expand_kernel(parts, ids_ref, *refs):
+    owner_refs, low_refs, factor_refs = refs[:parts], refs[parts : 2 * parts], refs[2 * parts : -parts - 1]
+    out_refs, total_ref = refs[-parts - 1 : -1], refs[-1]
+    rank, width = factor_refs[0].shape[1:]
+    requests, outputs = out_refs[0].shape
     step, last = pl.program_id(0), pl.num_programs(0) - 1
-    weight = weight_ref[...].reshape(count * rank, outputs)
+    ids = step_ids(ids_ref, factor_refs)
+    weight = stacked(factor_refs, slice(width - outputs, width))
     half = parts // 2
     low = lax.broadcasted_iota(jnp.int32, (requests, LANES), 1) < rank
     held = [[0.0] * half for _ in range(2)]
@@ -124,9 +141,9 @@
         turned = pltpu.roll(straight, rank, 1)
         for part in (s, s + half):
             first, other = (straight, turned) if part < half else (turned, straight)
-            wide = jnp.concatenate([jnp.where(low, first, other)] * (count * rank // LANES), axis=1)
-            mask = owner_mask(owner_refs[part][...], step * count, count, rank)
-            wide = jnp.where(mask, wide, 0.0)
+            both = jnp.where(low, first, other)
+            wide = jnp.concatenate([both] * (len(ids) * rank // LANES), axis=1)
+            wide = jnp.where(owner_mask(owner_refs[part][...], ids, rank), wide, 0.0)
             product = jnp.dot(
                 wide.astype(jnp.bfloat16), weight, preferred_element_type=jnp.float32
             )
@@ -265,28 +282,30 @@
     return pl.BlockSpec(array.shape, lambda *_: (0,) * len(array.shape))
 
 
-def in_chunks(weight):
-    chunk = math.gcd(weight.shape[0], 8)
-    return weight.shape[0] // chunk, pl.BlockSpec((chunk,) + weight.shape[1:], lambda i: (i, 0, 0))
-
-
-def shrink_rows(rows, weight):
+def in_chunks(factors):
+    chunk = [math.gcd(f.shape[0], 4) for f in factors]
+    return factors[0].shape[0] // chunk[0], [
+        pl.BlockSpec((c,) + f.shape[1:], lambda i: (i, 0, 0)) for c, f in zip(chunk, factors)
+    ]
+
+
+def shrink_rows(ids, rows, factors):
     parts, requests = len(rows), rows[0].shape[0]
-    steps, spec = in_chunks(weight)
+    steps, specs = in_chunks(factors)
     out = jax.ShapeDtypeStruct((parts // 2 * requests, LANES), jnp.float32)
     return pl.pallas_call(
         functools.partial(shrink_kernel, parts),
         out_shape=out,
         grid=(steps,),
-        in_specs=[*map(whole, rows), spec],
+        in_specs=[SMEM, *map(whole, rows), *specs],
         out_specs=whole(out),
         compiler_params=PARAMS,
-    )(*rows, weight)
-
-
-def expand_rows(rows, lows, weight):
-    parts, requests, outputs = len(rows), rows[0].shape[0], weight.shape[2]
-    steps, spec = in_chunks(weight)
+    )(ids, *rows, *factors)
+
+
+def expand_rows(ids, rows, lows, factors, outputs):
+    parts, requests = len(rows), rows[0].shape[0]
+    steps, specs = in_chunks(factors)
     last_lanes = rows[0].shape[1] // LANES - 1
     owners = pl.BlockSpec((requests, LANES), lambda i: (0, last_lanes))
     out = jax.ShapeDtypeStruct((requests, outputs), jnp.bfloat16)
@@ -294,10 +313,11 @@
         functools.partial(expand_kernel, parts),
         out_shape=[out] * parts,
         grid=(steps,),
-        in_specs=[owners] * parts + [*map(whole, lows), spec],
+        in_specs=[SMEM] + [owners] * parts + [*map(whole, lows), *specs],
         out_specs=[whole(out)] * parts,
         scratch_shapes=[pltpu.VMEM((parts, requests, outputs), jnp.float32)],
-    )(*rows, *lows, weight)
+        compiler_params=PARAMS,
+    )(ids, *rows, *lows, *factors)
 
 
 def per_device(
@@ -314,47 +334,54 @@
     lengths,
 ):
     reps, levels, sides, tp = (lax.axis_size(a) for a in ("rep", "level", "side", "tp"))
-    pool = levels * sides
     requests, wide = hidden.shape
     rank = shrink_factors.shape[2]
     square = reps * sides
-    rep = lax.axis_index("rep")
-    me = rep * sides + lax.axis_index("side")
+    features, outputs = wide // square, query_base.shape[1] // square
+    level, side = lax.axis_index("level"), lax.axis_index("side")
+    me = lax.axis_index("rep") * sides + side
 
     def swap(a, s):
         pairs = [(c, c ^ s) for c in range(square)]
         return lax.ppermute(a, ("rep", "side"), pairs)
 
-    def to_pool(factor, after=None):
-        width = factor.shape[2] // square
-        send = pl.pallas_call(
-            functools.partial(factor_kernel, sides, levels),
-            out_shape=jax.ShapeDtypeStruct((pool, rank, width), jnp.bfloat16),
-            in_specs=[SMEM, HBM],
-            out_specs=VMEM,
-            scratch_shapes=[pltpu.SemaphoreType.DMA((pool,))],
-        )(rep[None], factor)
-        if after is not None:
-            send, after = lax.optimization_barrier((send, after))
-        got = lax.all_to_all(send, ("level", "side"), split_axis=0, concat_axis=0, tiled=True)
-        return got, after
-
-    shrink, _ = to_pool(shrink_factors.swapaxes(1, 2))
+    block = (rank, features + outputs)
+    own, other = pl.pallas_call(
+        functools.partial(factor_kernel, square),
+        out_shape=[jax.ShapeDtypeStruct((k,) + block, jnp.bfloat16) for k in (levels, 1)],
+        in_specs=[SMEM, HBM, HBM],
+        out_specs=[VMEM] * 2,
+        scratch_shapes=[pltpu.SemaphoreType.DMA((2 * levels + 2,))],
+    )(me[None], shrink_factors.swapaxes(1, 2), expand_factors)
+    own = lax.all_to_all(own, "level", split_axis=0, concat_axis=0, tiled=True)
+    other = swap(other, 1)
     rows = pl.pallas_call(
         functools.partial(row_kernel, square),
-        out_shape=[jax.ShapeDtypeStruct((requests, wide // square + LANES), jnp.bfloat16)] * square,
+        out_shape=[jax.ShapeDtypeStruct((requests, features + LANES), jnp.bfloat16)] * square,
         in_specs=[SMEM, SMEM, VMEM, HBM],
         out_specs=[VMEM] * square,
         scratch_shapes=[pltpu.SemaphoreType.DMA((square,))],
     )(me[None], owner_map, adapter_ids.T, hidden)
     rows = [rows[0]] + [swap(rows[s], s) for s in range(1, square)]
-    expand, rows = to_pool(expand_factors, rows)
-    partial = shrink_rows(rows, shrink)
+    order = jnp.arange(levels, dtype=jnp.int32)
+    if levels == 4:
+        pairs = [[(i, i ^ k) for i in range(levels)] for k in range(levels)]
+        other = [other] + [lax.ppermute(other, "level", pairs[k]) for k in range(1, levels)]
+        other_at = level ^ order
+    else:
+        other = jnp.broadcast_to(other, (levels,) + block)
+        other = [lax.all_to_all(other, "level", split_axis=0, concat_axis=0, tiled=True)]
+        other_at = order
+    factors = [own, *other]
+    ids = [a.reshape(-1, 4) for a in (order * sides + side, other_at * sides + (side ^ 1))]
+    ids = jnp.concatenate(ids, axis=1).reshape(-1)
+
+    partial = shrink_rows(ids, rows, factors)
     for c in range(1, tp):
         partial = partial + lax.ppermute(partial, "tp", [(t, t ^ c) for t in range(tp)])
     partial = partial.astype(jnp.bfloat16)
     lows = [partial] + [swap(partial, s) for s in range(1, square)]
-    deltas = expand_rows(rows, lows, expand)
+    deltas = expand_rows(ids, rows, lows, factors, outputs)
     deltas = [deltas[0]] + [swap(deltas[s], s) for s in range(1, square)]
     return attend(
         me[None], query_base, new_key, new_value, cache_keys, cache_values, lengths, deltas

time: 75.1 us -> 74.1 us (0.987)
  Pallas kernels: 16.5 us -> 13.8 us
  waiting for transfers between devices: 32.2 us -> 33.7 us
    ppermute x0 -> x3, waiting for transfers between devices: none -> 13.7 us  [per_device(): lax.ppermute(other, 'level', pairs[k])]
    all_to_all x2 -> x1, waiting for transfers between devices: 7.64 us -> 0.01 us  [per_device(): own = lax.all_to_all(own, 'level', split_axis=0, concat_axis=0, tiled=True)]
    all_to_all x2 -> x1, starting transfers between devices: 11.9 us -> 6.33 us  [per_device(): own = lax.all_to_all(own, 'level', split_axis=0, concat_axis=0, tiled=True)]
    ppermute x9 -> x10, waiting for transfers between devices: 23.2 us -> 18.7 us  [swap(): return lax.ppermute(a, ('rep', 'side'), pairs)]
    ppermute x0 -> x3, starting transfers between devices: none -> 4.41 us  [per_device(): lax.ppermute(other, 'level', pairs[k])]
    pallas_call x2 -> x1, Pallas kernels: 4.53 us -> 2.48 us  [per_device(): pl.pallas_call(functools.partial(factor_kernel, square), out_shape=[jax.S...]
    pallas_call x1, Pallas kernels: 2.5 us -> 1.13 us  [expand_rows(): pl.pallas_call(functools.partial(expand_kernel, parts), out_shape=[out] *...]
    ppermute x9 -> x10, starting transfers between devices: 10.8 us -> 12.1 us  [swap(): return lax.ppermute(a, ('rep', 'side'), pairs)]
  transfers between devices with their start and end apart: 12 -> 15, of which waited for: 6 -> 10; matrix products, arithmetic and copies ran while one was open for 1% -> 1% of each run, Pallas kernels for 9% -> 4%
where the time goes in v11:
time: 74.1 us; the launch traced here: 73.7 us
  waiting for transfers between devices  33.7 us (45%)
  starting transfers between devices  22.9 us (31%)
  Pallas kernels  13.8 us (19%)
  local copies, waits for them, and re-layouts  3.13 us (4%)
    ppermute x10, waiting for transfers between devices, swap(): return lax.ppermute(a, ('rep', 'side'), pairs)  18.7 us
    ppermute x3, waiting for transfers between devices, per_device(): lax.ppermute(other, 'level', pairs[k])  13.7 us
    ppermute x10, starting transfers between devices, swap(): return lax.ppermute(a, ('rep', 'side'), pairs)  12.1 us
    all_to_all x1, starting transfers between devices, per_device(): own = lax.all_to_all(own, 'level', split_axis=0, concat_axis=0, tiled=True)  6.33 us
    pallas_call x1, Pallas kernels, attend(): pl.pallas_call(functools.partial(attend_kernel, len(deltas)), out_shape=j...  5.08 us
    ppermute x3, starting transfers between devices, per_device(): lax.ppermute(other, 'level', pairs[k])  4.41 us
    pallas_call x1, Pallas kernels, per_device(): pl.pallas_call(functools.partial(row_kernel, square), out_shape=[jax.Shap...  3.03 us
    pallas_call x1, Pallas kernels, per_device(): pl.pallas_call(functools.partial(factor_kernel, square), out_shape=[jax.S...  2.48 us
  transfers between devices with their start and end apart: 15, of which 10 were waited for; matrix products, arithmetic and copies ran while one was open for 1% of the time, Pallas kernels for 4%

profile of v11, /device:TPU:0, one launch (start us, length us, event | category | flops | bytes accessed | tf_op | source)
XLA Modules:
  0.0 73.7 jit_solution(5521482836022555508)
XLA Ops:
  0.0 2.5 %shard_map.110 = (bf16[4,64,1536]{2,1,0:T(8,128)(2,1)}, bf16[1,64,1536]{2,1,0:T(8,128)(2,1)}) custom-call(s32[1]{0:T(128)} %bitcast.me_ref, bf16[1,64,4096]{2,1,0:T(8,128)(2,1)} %bitcast.7, bf16[1,64,2048]{2,1,0:T(8,128)(2,1)} %expand_ref.1), custom_call_target="tpu_custom_call" | custom-call | tf_op jit(solution)/shard_map/pallas_call | solution.py:349
  2.5 6.3 %all-to-all-start = ((bf16[4,64,1536]{2,1,0:T(8,128)(2,1)}), bf16[4,64,1536]{2,1,0:T(8,128)(2,1)S(1)}, u32[]{:S(2)}, u32[]{:S(2)}) async-start(bf16[4,64,1536]{2,1,0:T(8,128)(2,1)} %get-tuple-element.19), calls=%async_computation | async-start | bytes 1572864 | tf_op jit(solution)/shard_map/all_to_all | solution.py:356
  8.8 3.0 %shard_map.109 = (bf16[128,1152]{1,0:T(8,128)(2,1)}, bf16[128,1152]{1,0:T(8,128)(2,1)}, bf16[128,1152]{1,0:T(8,128)(2,1)}, bf16[128,1152]{1,0:T(8,128)(2,1)}) custom-call(s32[1]{0:T(128)} %bitcast.me_ref, s32[8]{0:T(128)} %map_ref.1, s32[1,128]{1,0:T(1,128)} %bitcast.8, bf16[128,4096]{1,0:T(8,128)(2,1)} %hidden_ref.1), custom_call_target="tpu_custom_call" | custom-call | tf_op jit(solution)/shard_map/pallas_call | solution.py:358
  11.9 1.5 %collective-permute-start = (bf16[128,1152]{1,0:T(8,128)(2,1)}, bf16[128,1152]{1,0:T(8,128)(2,1)S(1)}, u32[]{:S(2)}, u32[]{:S(2)}) collective-permute-start(bf16[128,1152]{1,0:T(8,128)(2,1)} %get-tuple-element.16), channel_id=1, source_target_pairs={{0,2},{2,0},{16,18},{18,16},{1,3},{3,1},{17,19},{19,17},{4,6},{6,4... | collective-permute-start | bytes 884744 | tf_op jit(solution)/shard_map/ppermute | solution.py:346
  14.0 1.5 %collective-permute-start.1 = (bf16[128,1152]{1,0:T(8,128)(2,1)}, bf16[128,1152]{1,0:T(8,128)(2,1)S(1)}, u32[]{:S(2)}, u32[]{:S(2)}) collective-permute-start(bf16[128,1152]{1,0:T(8,128)(2,1)} %get-tuple-element.17), channel_id=1, source_target_pairs={{0,16},{2,18},{16,0},{18,2},{1,17},{3,19},{17,1},{19,3},{4,20},{6,... | collective-permute-start | bytes 884744 | tf_op jit(solution)/shard_map/ppermute | solution.py:346
  15.5 1.4 %collective-permute-start.2 = (bf16[128,1152]{1,0:T(8,128)(2,1)}, bf16[128,1152]{1,0:T(8,128)(2,1)S(1)}, u32[]{:S(2)}, u32[]{:S(2)}) collective-permute-start(bf16[128,1152]{1,0:T(8,128)(2,1)} %get-tuple-element.18), channel_id=1, source_target_pairs={{0,18},{2,16},{16,2},{18,0},{1,19},{3,17},{17,3},{19,1},{4,22},{6,... | collective-permute-start | bytes 884744 | tf_op jit(solution)/shard_map/ppermute | solution.py:346
  16.9 9.4 %collective-permute-done.3.refs_5_.refs_9_ = bf16[1,64,1536]{2,1,0:T(8,128)(2,1)S(1)} collective-permute-done((bf16[1,64,1536]{2,1,0:T(8,128)(2,1)S(1)}, bf16[1,64,1536]{2,1,0:T(8,128)(2,1)S(1)}, u32[]{:S(2)}, u32[]{:S(2)}) %collective-permute-start.3) | collective-permute-done | bytes 196640 | tf_op jit(solution)/shard_map/ppermute | solution.py:346
  26.3 3.8 %collective-permute-start.6 = (bf16[1,64,1536]{2,1,0:T(8,128)(2,1)S(1)}, bf16[1,64,1536]{2,1,0:T(8,128)(2,1)S(1)}, u32[]{:S(2)}, u32[]{:S(2)}) collective-permute-start(bf16[1,64,1536]{2,1,0:T(8,128)(2,1)S(1)} %collective-permute-done.3.refs_5_.refs_9_), channel_id=1, source_target_pairs={{0,12},{4,8},{8,4},{12,0},{1,13},{5,9},{9,5},{13,1},{2,14},{6,10},... | collective-permute-start | bytes 589832 | tf_op jit(solution)/shard_map/ppermute | solution.py:369
  30.8 1.3 %collective-permute-done.2.refs_3_ = bf16[128,1152]{1,0:T(8,128)(2,1)S(1)} collective-permute-done((bf16[128,1152]{1,0:T(8,128)(2,1)}, bf16[128,1152]{1,0:T(8,128)(2,1)S(1)}, u32[]{:S(2)}, u32[]{:S(2)}) %collective-permute-start.2) | collective-permute-done | bytes 294944 | tf_op jit(solution)/shard_map/ppermute | solution.py:346
  32.1 3.9 %collective-permute-done.6.refs_8_.refs_12_ = bf16[1,64,1536]{2,1,0:T(8,128)(2,1)S(1)} collective-permute-done((bf16[1,64,1536]{2,1,0:T(8,128)(2,1)S(1)}, bf16[1,64,1536]{2,1,0:T(8,128)(2,1)S(1)}, u32[]{:S(2)}, u32[]{:S(2)}) %collective-permute-start.6) | collective-permute-done | bytes 196640 | tf_op jit(solution)/shard_map/ppermute | solution.py:369
  35.9 9.8 %collective-permute-done.5.refs_7_.refs_11_ = bf16[1,64,1536]{2,1,0:T(8,128)(2,1)S(1)} collective-permute-done((bf16[1,64,1536]{2,1,0:T(8,128)(2,1)S(1)}, bf16[1,64,1536]{2,1,0:T(8,128)(2,1)S(1)}, u32[]{:S(2)}, u32[]{:S(2)}) %collective-permute-start.5) | collective-permute-done | bytes 196640 | tf_op jit(solution)/shard_map/ppermute | solution.py:369
  45.8 1.0 %copy-done = bf16[128,1152]{1,0:T(8,128)(2,1)S(1)} copy-done((bf16[128,1152]{1,0:T(8,128)(2,1)S(1)}, bf16[128,1152]{1,0:T(8,128)(2,1)}, u32[]{:S(2)}) %copy-start) | copy-done | bytes 294936
  46.8 2.1 %shard_map.111 = f32[256,128]{1,0:T(8,128)S(1)} custom-call(s32[8]{0:T(128)S(1)} %add_bitcast_fusion.ids_ref, bf16[128,1152]{1,0:T(8,128)(2,1)S(1)} %copy-done, bf16[128,1152]{1,0:T(8,128)(2,1)S(1)} %collective-permute-done.refs_1_, bf16[128,1152]{1,0:T(8,128)(2,1)S(1)} %collective-permute-done.1.refs_2_, ...), custom_call_target="tpu_custom_call" | custom-call | tf_op jit(solution)/shard_map/pallas_call | solution.py:296
  49.0 1.3 %collective-permute-done.7 = f32[256,128]{1,0:T(8,128)S(1)} collective-permute-done((f32[256,128]{1,0:T(8,128)S(1)}, f32[256,128]{1,0:T(8,128)S(1)}, u32[]{:S(2)}, u32[]{:S(2)}) %collective-permute-start.7) | collective-permute-done | bytes 131104 | tf_op jit(solution)/shard_map/ppermute | solution.py:381
  50.3 2.6 %collective-permute-start.10 = (bf16[256,128]{1,0:T(8,128)(2,1)S(1)}, bf16[256,128]{1,0:T(8,128)(2,1)S(1)}, u32[]{:S(2)}, u32[]{:S(2)}) collective-permute-start(bf16[256,128]{1,0:T(8,128)(2,1)S(1)} %add_convert_fusion.refs_4_), channel_id=1, source_target_pairs={{0,18},{2,16},{16,2},{18,0},{1,19},{3,17},{17,3},{19,1},{4,22},{6,... | collective-permute-start | bytes 196616 | tf_op jit(solution)/shard_map/ppermute | solution.py:346
  54.0 1.5 %collective-permute-done.10.refs_7_ = bf16[256,128]{1,0:T(8,128)(2,1)S(1)} collective-permute-done((bf16[256,128]{1,0:T(8,128)(2,1)S(1)}, bf16[256,128]{1,0:T(8,128)(2,1)S(1)}, u32[]{:S(2)}, u32[]{:S(2)}) %collective-permute-start.10) | collective-permute-done | bytes 65568 | tf_op jit(solution)/shard_map/ppermute | solution.py:346
  55.6 1.6 %collective-permute-done.9.refs_6_ = bf16[256,128]{1,0:T(8,128)(2,1)S(1)} collective-permute-done((bf16[256,128]{1,0:T(8,128)(2,1)S(1)}, bf16[256,128]{1,0:T(8,128)(2,1)S(1)}, u32[]{:S(2)}, u32[]{:S(2)}) %collective-permute-start.9) | collective-permute-done | bytes 65568 | tf_op jit(solution)/shard_map/ppermute | solution.py:346
  57.6 1.1 %shard_map.112 = (bf16[128,512]{1,0:T(8,128)(2,1)S(1)}, bf16[128,512]{1,0:T(8,128)(2,1)S(1)}, bf16[128,512]{1,0:T(8,128)(2,1)S(1)}, bf16[128,512]{1,0:T(8,128)(2,1)S(1)}) custom-call(s32[8]{0:T(128)S(1)} %add_bitcast_fusion.ids_ref, bf16[128,1152]{1,0:T(8,128)(2,1)S(1)} %copy-done.1, bf16[128,1152]{1,0:T(8,128)(2,1)S(1)} %collective-permute-done.refs_1_, ...), custom_call_target="tpu_custom_call" | custom-call | tf_op jit(solution)/shard_map/pallas_call | solution.py:312
  59.4 0.9 %collective-permute-start.11 = (bf16[128,512]{1,0:T(8,128)(2,1)S(1)}, bf16[128,512]{1,0:T(8,128)(2,1)S(1)}, u32[]{:S(2)}, u32[]{:S(2)}) collective-permute-start(bf16[128,512]{1,0:T(8,128)(2,1)S(1)} %get-tuple-element.22), channel_id=1, source_target_pairs={{0,2},{2,0},{16,18},{18,16},{1,3},{3,1},{17,19},{19,17},{4,6},{6,4... | collective-permute-start | bytes 393224 | tf_op jit(solution)/shard_map/ppermute | solution.py:346
  60.2 1.2 %collective-permute-start.12 = (bf16[128,512]{1,0:T(8,128)(2,1)S(1)}, bf16[128,512]{1,0:T(8,128)(2,1)S(1)}, u32[]{:S(2)}, u32[]{:S(2)}) collective-permute-start(bf16[128,512]{1,0:T(8,128)(2,1)S(1)} %get-tuple-element.23), channel_id=1, source_target_pairs={{0,16},{2,18},{16,0},{18,2},{1,17},{3,19},{17,1},{19,3},{4,20},{6,... | collective-permute-start | bytes 393224 | tf_op jit(solution)/shard_map/ppermute | solution.py:346
  61.4 1.4 %collective-permute-start.13 = (bf16[128,512]{1,0:T(8,128)(2,1)S(1)}, bf16[128,512]{1,0:T(8,128)(2,1)S(1)}, u32[]{:S(2)}, u32[]{:S(2)}) collective-permute-start(bf16[128,512]{1,0:T(8,128)(2,1)S(1)} %get-tuple-element.24), channel_id=1, source_target_pairs={{0,18},{2,16},{16,2},{18,0},{1,19},{3,17},{17,3},{19,1},{4,22},{6,... | collective-permute-start | bytes 393224 | tf_op jit(solution)/shard_map/ppermute | solution.py:346
  63.5 1.7 %collective-permute-done.11.refs_6_ = bf16[128,512]{1,0:T(8,128)(2,1)S(1)} collective-permute-done((bf16[128,512]{1,0:T(8,128)(2,1)S(1)}, bf16[128,512]{1,0:T(8,128)(2,1)S(1)}, u32[]{:S(2)}, u32[]{:S(2)}) %collective-permute-start.11) | collective-permute-done | bytes 131104 | tf_op jit(solution)/shard_map/ppermute | solution.py:346
  65.2 2.8 %collective-permute-done.12.refs_7_ = bf16[128,512]{1,0:T(8,128)(2,1)S(1)} collective-permute-done((bf16[128,512]{1,0:T(8,128)(2,1)S(1)}, bf16[128,512]{1,0:T(8,128)(2,1)S(1)}, u32[]{:S(2)}, u32[]{:S(2)}) %collective-permute-start.12) | collective-permute-done | bytes 131104 | tf_op jit(solution)/shard_map/ppermute | solution.py:346
  68.7 5.1 %shard_map.113 = bf16[128,2048]{1,0:T(8,128)(2,1)} custom-call(s32[1]{0:T(128)} %bitcast.me_ref, s32[16,128]{1,0:T(8,128)} %copy.13.len_ref, bf16[128,2048]{1,0:T(8,128)(2,1)} %refs_0_.1, bf16[128,256]{1,0:T(8,128)(2,1)} %refs_1_.1, bf16[128,256]{1,0:T(8,128)(2,1)} %refs_2_.1, bf16[128,16,256]{2,1,0:T(8,128)(2,1)} %refs_3_.1, bf16[128,16,256]{2,1,0:T(8,128)(2,1)} %refs_4_.1, ...), custom_call_target="tpu_custom_call" | custom-call | flops 134217728 | bytes 3145728 | tf_op jit(solution)/shard_map/pallas_call | solution.py:267
  (34 shorter events, 4.9 us)
Async XLA Ops:
  2.5 43.3 %all-to-all-start = ((bf16[4,64,1536]{2,1,0:T(8,128)(2,1)}), bf16[4,64,1536]{2,1,0:T(8,128)(2,1)S(1)}, u32[]{:S(2)}, u32[]{:S(2)}) async-start(bf16[4,64,1536]{2,1,0:T(8,128)(2,1)} %get-tuple-element.19), calls=%async_computation | async-start | bytes 1572864 | tf_op jit(solution)/shard_map/all_to_all | solution.py:356
  8.8 4.6 %copy-start.7 = (bf16[1,64,1536]{2,1,0:T(8,128)(2,1)S(1)}, bf16[1,64,1536]{2,1,0:T(8,128)(2,1)}, u32[]{:S(2)}) copy-start(bf16[1,64,1536]{2,1,0:T(8,128)(2,1)} %get-tuple-element.20) | copy-start | bytes 589828
  11.9 18.3 %collective-permute-start = (bf16[128,1152]{1,0:T(8,128)(2,1)}, bf16[128,1152]{1,0:T(8,128)(2,1)S(1)}, u32[]{:S(2)}, u32[]{:S(2)}) collective-permute-start(bf16[128,1152]{1,0:T(8,128)(2,1)} %get-tuple-element.16), channel_id=1, source_target_pairs={{0,2},{2,0},{16,18},{18,16},{1,3},{3,1},{17,19},{19,17},{4,6},{6,4... | collective-permute-start | bytes 884744 | tf_op jit(solution)/shard_map/ppermute | solution.py:346
  13.4 12.9 %collective-permute-start.3 = (bf16[1,64,1536]{2,1,0:T(8,128)(2,1)S(1)}, bf16[1,64,1536]{2,1,0:T(8,128)(2,1)S(1)}, u32[]{:S(2)}, u32[]{:S(2)}) collective-permute-start(bf16[1,64,1536]{2,1,0:T(8,128)(2,1)S(1)} %copy-done.7), channel_id=1, source_target_pairs={{0,2},{2,0},{16,18},{18,16},{1,3},{3,1},{17,19},{19,17},{4,6},{6,4... | collective-permute-start | bytes 589832 | tf_op jit(solution)/shard_map/ppermute | solution.py:346
  14.0 16.8 %collective-permute-start.1 = (bf16[128,1152]{1,0:T(8,128)(2,1)}, bf16[128,1152]{1,0:T(8,128)(2,1)S(1)}, u32[]{:S(2)}, u32[]{:S(2)}) collective-permute-start(bf16[128,1152]{1,0:T(8,128)(2,1)} %get-tuple-element.17), channel_id=1, source_target_pairs={{0,16},{2,18},{16,0},{18,2},{1,17},{3,19},{17,1},{19,3},{4,20},{6,... | collective-permute-start | bytes 884744 | tf_op jit(solution)/shard_map/ppermute | solution.py:346
  15.5 16.6 %collective-permute-start.2 = (bf16[128,1152]{1,0:T(8,128)(2,1)}, bf16[128,1152]{1,0:T(8,128)(2,1)S(1)}, u32[]{:S(2)}, u32[]{:S(2)}) collective-permute-start(bf16[128,1152]{1,0:T(8,128)(2,1)} %get-tuple-element.18), channel_id=1, source_target_pairs={{0,18},{2,16},{16,2},{18,0},{1,19},{3,17},{17,3},{19,1},{4,22},{6,... | collective-permute-start | bytes 884744 | tf_op jit(solution)/shard_map/ppermute | solution.py:346
  26.3 9.7 %collective-permute-start.6 = (bf16[1,64,1536]{2,1,0:T(8,128)(2,1)S(1)}, bf16[1,64,1536]{2,1,0:T(8,128)(2,1)S(1)}, u32[]{:S(2)}, u32[]{:S(2)}) collective-permute-start(bf16[1,64,1536]{2,1,0:T(8,128)(2,1)S(1)} %collective-permute-done.3.refs_5_.refs_9_), channel_id=1, source_target_pairs={{0,12},{4,8},{8,4},{12,0},{1,13},{5,9},{9,5},{13,1},{2,14},{6,10},... | collective-permute-start | bytes 589832 | tf_op jit(solution)/shard_map/ppermute | solution.py:369
  30.1 15.7 %collective-permute-start.5 = (bf16[1,64,1536]{2,1,0:T(8,128)(2,1)S(1)}, bf16[1,64,1536]{2,1,0:T(8,128)(2,1)S(1)}, u32[]{:S(2)}, u32[]{:S(2)}) collective-permute-start(bf16[1,64,1536]{2,1,0:T(8,128)(2,1)S(1)} %collective-permute-done.3.refs_5_.refs_9_), channel_id=1, source_target_pairs={{0,8},{4,12},{8,0},{12,4},{1,9},{5,13},{9,1},{13,5},{2,10},{6,14},... | collective-permute-start | bytes 589832 | tf_op jit(solution)/shard_map/ppermute | solution.py:369
  30.1 15.7 %collective-permute-start.4 = (bf16[1,64,1536]{2,1,0:T(8,128)(2,1)S(1)}, bf16[1,64,1536]{2,1,0:T(8,128)(2,1)S(1)}, u32[]{:S(2)}, u32[]{:S(2)}) collective-permute-start(bf16[1,64,1536]{2,1,0:T(8,128)(2,1)S(1)} %collective-permute-done.3.refs_5_.refs_9_), channel_id=1, source_target_pairs={{0,4},{4,0},{8,12},{12,8},{1,5},{5,1},{9,13},{13,9},{2,6},{6,2},{1... | collective-permute-start | bytes 589832 | tf_op jit(solution)/shard_map/ppermute | solution.py:369
  45.8 1.0 %copy-start = (bf16[128,1152]{1,0:T(8,128)(2,1)S(1)}, bf16[128,1152]{1,0:T(8,128)(2,1)}, u32[]{:S(2)}) copy-start(bf16[128,1152]{1,0:T(8,128)(2,1)} %get-tuple-element.15.refs_0_) | copy-start | bytes 884740
  48.9 5.0 %copy-start.6 = (s32[128]{0:T(128)S(1)}, s32[128]{0:T(128)}, u32[]{:S(2)}) copy-start(s32[128]{0:T(128)} %param.21) | copy-start | bytes 1540
  48.9 8.7 %copy-start.1 = (bf16[128,1152]{1,0:T(8,128)(2,1)S(1)}, bf16[128,1152]{1,0:T(8,128)(2,1)}, u32[]{:S(2)}) copy-start(bf16[128,1152]{1,0:T(8,128)(2,1)} %get-tuple-element.15.refs_0_) | copy-start | bytes 884740
  48.9 1.4 %collective-permute-start.7 = (f32[256,128]{1,0:T(8,128)S(1)}, f32[256,128]{1,0:T(8,128)S(1)}, u32[]{:S(2)}, u32[]{:S(2)}) collective-permute-start(f32[256,128]{1,0:T(8,128)S(1)} %shard_map.111), channel_id=1, source_target_pairs={{0,1},{1,0},{2,3},{3,2},{4,5},{5,4},{6,7},{7,6},{8,9},{9,8},{10,11... | collective-permute-start | bytes 393224 | tf_op jit(solution)/shard_map/ppermute | solution.py:381
  50.3 5.2 %collective-permute-start.10 = (bf16[256,128]{1,0:T(8,128)(2,1)S(1)}, bf16[256,128]{1,0:T(8,128)(2,1)S(1)}, u32[]{:S(2)}, u32[]{:S(2)}) collective-permute-start(bf16[256,128]{1,0:T(8,128)(2,1)S(1)} %add_convert_fusion.refs_4_), channel_id=1, source_target_pairs={{0,18},{2,16},{16,2},{18,0},{1,19},{3,17},{17,3},{19,1},{4,22},{6,... | collective-permute-start | bytes 196616 | tf_op jit(solution)/shard_map/ppermute | solution.py:346
  52.9 4.3 %collective-permute-start.9 = (bf16[256,128]{1,0:T(8,128)(2,1)S(1)}, bf16[256,128]{1,0:T(8,128)(2,1)S(1)}, u32[]{:S(2)}, u32[]{:S(2)}) collective-permute-start(bf16[256,128]{1,0:T(8,128)(2,1)S(1)} %add_convert_fusion.refs_4_), channel_id=1, source_target_pairs={{0,16},{2,18},{16,0},{18,2},{1,17},{3,19},{17,1},{19,3},{4,20},{6,... | collective-permute-start | bytes 196616 | tf_op jit(solution)/shard_map/ppermute | solution.py:346
  53.3 4.3 %collective-permute-start.8 = (bf16[256,128]{1,0:T(8,128)(2,1)S(1)}, bf16[256,128]{1,0:T(8,128)(2,1)S(1)}, u32[]{:S(2)}, u32[]{:S(2)}) collective-permute-start(bf16[256,128]{1,0:T(8,128)(2,1)S(1)} %add_convert_fusion.refs_4_), channel_id=1, source_target_pairs={{0,2},{2,0},{16,18},{18,16},{1,3},{3,1},{17,19},{19,17},{4,6},{6,4... | collective-permute-start | bytes 196616 | tf_op jit(solution)/shard_map/ppermute | solution.py:346
  58.7 0.6 copy-start.2
  59.4 5.8 %collective-permute-start.11 = (bf16[128,512]{1,0:T(8,128)(2,1)S(1)}, bf16[128,512]{1,0:T(8,128)(2,1)S(1)}, u32[]{:S(2)}, u32[]{:S(2)}) collective-permute-start(bf16[128,512]{1,0:T(8,128)(2,1)S(1)} %get-tuple-element.22), channel_id=1, source_target_pairs={{0,2},{2,0},{16,18},{18,16},{1,3},{3,1},{17,19},{19,17},{4,6},{6,4... | collective-permute-start | bytes 393224 | tf_op jit(solution)/shard_map/ppermute | solution.py:346
  60.2 7.7 %collective-permute-start.12 = (bf16[128,512]{1,0:T(8,128)(2,1)S(1)}, bf16[128,512]{1,0:T(8,128)(2,1)S(1)}, u32[]{:S(2)}, u32[]{:S(2)}) collective-permute-start(bf16[128,512]{1,0:T(8,128)(2,1)S(1)} %get-tuple-element.23), channel_id=1, source_target_pairs={{0,16},{2,18},{16,0},{18,2},{1,17},{3,19},{17,1},{19,3},{4,20},{6,... | collective-permute-start | bytes 393224 | tf_op jit(solution)/shard_map/ppermute | solution.py:346
  61.4 6.5 %collective-permute-start.13 = (bf16[128,512]{1,0:T(8,128)(2,1)S(1)}, bf16[128,512]{1,0:T(8,128)(2,1)S(1)}, u32[]{:S(2)}, u32[]{:S(2)}) collective-permute-start(bf16[128,512]{1,0:T(8,128)(2,1)S(1)} %get-tuple-element.24), channel_id=1, source_target_pairs={{0,18},{2,16},{16,2},{18,0},{1,19},{3,17},{17,3},{19,1},{4,22},{6,... | collective-permute-start | bytes 393224 | tf_op jit(solution)/shard_map/ppermute | solution.py:346
  65.2 2.8 %copy-start.3 = (bf16[128,512]{1,0:T(8,128)(2,1)}, bf16[128,512]{1,0:T(8,128)(2,1)S(1)}, u32[]{:S(2)}) copy-start(bf16[128,512]{1,0:T(8,128)(2,1)S(1)} %collective-permute-done.11.refs_6_) | copy-start | bytes 393220
  67.9 0.6 copy-start.4
  68.0 0.7 copy-start.5

commit v12 on v11

v12 whole, which is shorter than its diff:
```python
import functools
import math

import jax
import jax.numpy as jnp
from jax import lax
from jax.experimental import pallas as pl
from jax.experimental.pallas import tpu as pltpu
from jax.sharding import Mesh
from jax.sharding import PartitionSpec as P

HEAD = 128
LANES = 128
STEP = 16
HALF = 8
BATCH = 2
DEAD = -1e30
VMEM = pl.BlockSpec(memory_space=pltpu.VMEM)
SMEM = pl.BlockSpec(memory_space=pltpu.SMEM)
HBM = pl.BlockSpec(memory_space=pltpu.HBM)
PARAMS = pltpu.CompilerParams(vmem_limit_bytes=12 * 1024 * 1024)
NT = (((1,), (1,)), ((), ()))
TN = (((0,), (0,)), ((), ()))


def columns(at, width):
    return pl.ds(pl.multiple_of(at * width, width), width)


def run_copies(moves, sems, meanwhile=None):
    copies = [pltpu.make_async_copy(src, dst, sems.at[k]) for k, (src, dst) in enumerate(moves)]
    for copy in copies:
        copy.start()
    if meanwhile is not None:
        meanwhile()
    for copy in copies:
        copy.wait()


def factor_kernel(parts, me_ref, shrink_ref, expand_ref, own_ref, expand_own_ref, other_ref, sems):
    features, outputs = shrink_ref.shape[2] // parts, expand_ref.shape[2] // parts
    me = me_ref[0]
    moves = [
        (shrink_ref.at[:, :, columns(me ^ 1, features)], other_ref.at[:, :, :features]),
        (expand_ref.at[:, :, columns(me ^ 1, outputs)], other_ref.at[:, :, features:]),
        (expand_ref.at[:, :, columns(me, outputs)], expand_own_ref),
    ]
    share = shrink_ref.at[0, :, columns(me, features)]
    moves += [(share, own_ref.at[k]) for k in range(own_ref.shape[0])]
    run_copies(moves, sems)


def row_kernel(parts, me_ref, map_ref, ids_ref, hidden_ref, *refs):
    out_refs, sems = refs[:parts], refs[parts]
    requests, wide = hidden_ref.shape
    features = wide // parts
    moves = [
        (hidden_ref.at[:, columns(me_ref[0] ^ s, features)], out_refs[s].at[:, :features])
        for s in range(parts)
    ]

    def owners():
        ids = ids_ref[...]

        def look(k, found):
            return jnp.where(ids == k, map_ref[k], found)

        found = lax.fori_loop(0, map_ref.shape[0], look, jnp.zeros_like(ids))
        found = jnp.broadcast_to(found.astype(jnp.float32), (LANES, requests)).T
        for s in range(parts):
            out_refs[s][:, features:] = found.astype(jnp.bfloat16)

    run_copies(moves, sems, owners)


def owner_mask(owners, ids, rank):
    lane = lax.broadcasted_iota(jnp.int32, (1, len(ids) * rank), 1) // rank
    named = jnp.full_like(lane, -1)
    for k, owner in enumerate(ids):
        named = jnp.where(lane == k, owner, named)
    owners = owners.astype(jnp.float32).astype(jnp.int32)
    return jnp.concatenate([owners] * (len(ids) * rank // LANES), axis=1) == named


def stacked(refs):
    return jnp.concatenate([r[k] for r in refs for k in range(r.shape[0])], axis=0)


def step_ids(ids_ref, refs):
    count = sum(r.shape[0] for r in refs)
    return [ids_ref[pl.program_id(0) * count + k] for k in range(count)]


def shrink_kernel(parts, ids_ref, *refs):
    row_refs, factor_refs, out_ref = refs[:parts], refs[parts:-1], refs[-1]
    rank = factor_refs[0].shape[1]
    requests, features = row_refs[0].shape[0], row_refs[0].shape[1] - LANES
    ids = step_ids(ids_ref, factor_refs)
    weight = stacked(factor_refs)
    low = lax.broadcasted_iota(jnp.int32, (requests, LANES), 1) < rank
    folded = []
    for ref in row_refs:
        sums = lax.dot_general(
            ref[:, :features], weight, NT, preferred_element_type=jnp.float32
        )
        sums = jnp.where(owner_mask(ref[:, features:], ids, rank), sums, 0.0)
        total = sums[:, :LANES]
        for k in range(1, len(ids) * rank // LANES):
            total = total + sums[:, k * LANES : (k + 1) * LANES]
        folded.append(total + pltpu.roll(total, rank, 1))

    @pl.when(pl.program_id(0) == 0)
    def _():
        out_ref[...] = jnp.zeros_like(out_ref)

    half = parts // 2
    for s in range(half):
        rows = pl.ds(s * requests, requests)
        out_ref[rows, :] += jnp.where(low, folded[s], folded[s + half])


def expand_kernel(parts, ids_ref, *refs):
    owner_refs, low_refs, factor_refs = refs[:parts], refs[parts : 2 * parts], refs[2 * parts : -parts - 1]
    out_refs, total_ref = refs[-parts - 1 : -1], refs[-1]
    rank, outputs = factor_refs[0].shape[1:]
    requests = out_refs[0].shape[0]
    step, last = pl.program_id(0), pl.num_programs(0) - 1
    ids = step_ids(ids_ref, factor_refs)
    weight = stacked(factor_refs)
    half = parts // 2
    low = lax.broadcasted_iota(jnp.int32, (requests, LANES), 1) < rank
    held = [[0.0] * half for _ in range(2)]
    for t in range(parts):
        sums = low_refs[t][...].astype(jnp.float32)
        for s in range(half):
            at = (s ^ t) % half
            piece = sums[at * requests : (at + 1) * requests]
            held[t // half][s] = held[t // half][s] + piece
    for s in range(half):
        straight = held[0][s] + pltpu.roll(held[1][s], rank, 1)
        turned = pltpu.roll(straight, rank, 1)
        for part in (s, s + half):
            first, other = (straight, turned) if part < half else (turned, straight)
            both = jnp.where(low, first, other)
            wide = jnp.concatenate([both] * (len(ids) * rank // LANES), axis=1)
            wide = jnp.where(owner_mask(owner_refs[part][...], ids, rank), wide, 0.0)
            product = jnp.dot(
                wide.astype(jnp.bfloat16), weight, preferred_element_type=jnp.float32
            )

            @pl.when(step == 0)
            def _():
                total_ref[part] = product

            @pl.when(step > 0)
            def _():
                total_ref[part] += product

            @pl.when(step == last)
            def _():
                out_refs[part][...] = total_ref[part].astype(jnp.bfloat16)


def attend_kernel(first, parts, me_ref, len_ref, base_ref, nk_ref, nv_ref, ck_ref, cv_ref, *refs):
    delta_refs, out_ref = refs[:parts], refs[-1]
    block = base_ref.shape[0]
    width = base_ref.shape[1] // parts
    slots = ck_ref.shape[1]
    per_part = width // HEAD
    sets = STEP // HALF
    span = parts * per_part * STEP
    set_span = span // sets
    keys_in = HALF * slots + STEP
    row = lax.broadcasted_iota(jnp.int32, (keys_in, span), 0)
    lane = lax.broadcasted_iota(jnp.int32, (keys_in, span), 1)
    lane_req = lane % HALF
    lane_set = lane // set_span
    own = row - HALF * slots
    cached = jnp.where(row // slots == lane_req, row % slots, slots)
    fresh = jnp.where(own == lane_req + lane_set * HALF, -1, slots)
    slot_of = jnp.where(own >= 0, fresh, cached)
    lane_set = lax.broadcasted_iota(jnp.int32, (1, span), 1) // set_span
    part_at = [(me_ref[0] ^ (first + s)) % parts for s in range(parts)]
    scale = 1.0 / math.sqrt(HEAD)
    step = pl.program_id(0)
    units = range(block // STEP)

    def rows_of(j):
        return pl.ds(j * STEP, STEP)

    def keys_of(cache_ref, fresh_ref, j, h):
        cache = cache_ref[pl.ds(j * STEP + h * HALF, HALF)].reshape(HALF * slots, HEAD)
        return jnp.concatenate([cache, fresh_ref[rows_of(j), :]], axis=0)

    scores = []
    for j in units:
        pieces = []
        for s in range(parts):
            q = base_ref[rows_of(j), columns(part_at[s], width)].astype(jnp.float32)
            q = q + delta_refs[s][rows_of(j), :].astype(jnp.float32)
            pieces += [q[:, k * HEAD : (k + 1) * HEAD] for k in range(per_part)]
        q = jnp.concatenate(
            [p[h * HALF : (h + 1) * HALF] for h in range(sets) for p in pieces], axis=0
        ).astype(jnp.bfloat16)
        score = None
        for h in range(sets):
            keys = keys_of(ck_ref, nk_ref, j, h)
            whole_score = lax.dot_general(keys, q, NT, preferred_element_type=jnp.float32)
            score = whole_score if h == 0 else jnp.where(lane_set == h, whole_score, score)
        scores.append(score)
    probs = []
    for j, score in zip(units, scores):
        lens = len_ref[pl.ds(step * (block // STEP) + j, 1), :]
        score = jnp.where(slot_of < lens, score, DEAD)
        top = jnp.max(score, axis=0, keepdims=True)
        exps = jnp.exp((score - top) * scale)
        total = jnp.sum(exps, axis=0, keepdims=True)
        probs.append((exps * (1.0 / total)).astype(jnp.bfloat16))
    for j, prob in zip(units, probs):
        mixed = []
        for h in range(sets):
            values = keys_of(cv_ref, nv_ref, j, h)
            got = lax.dot_general(prob, values, TN, preferred_element_type=jnp.float32)
            mixed.append(got[h * set_span : (h + 1) * set_span])
        for s in range(parts):
            out = []
            for k in range(per_part):
                at = (s * per_part + k) * HALF
                out.append(jnp.concatenate([m[at : at + HALF] for m in mixed], axis=0))
            out = jnp.concatenate(out, axis=1).astype(jnp.bfloat16)
            out_ref[rows_of(j), columns(part_at[s], width)] = out


def attend_half(first, me, base, new_key, new_value, cache_keys, cache_values, lengths, deltas, out):
    requests, columns = base.shape
    slots, kv = cache_keys.shape[1:]
    groups = kv // HEAD
    parts = len(deltas)
    block = STEP * BATCH
    group = lambda me: (me[0] ^ first) // parts
    wide = pl.BlockSpec((block, columns // groups), lambda i, me: (i, group(me)))
    fresh = pl.BlockSpec((block, HEAD), lambda i, me: (i, group(me)))
    cache = pl.BlockSpec((block, slots, HEAD), lambda i, me: (i, 0, group(me)))
    part = pl.BlockSpec((block, columns // groups // parts), lambda i, me: (i, 0))
    table = pl.BlockSpec(lengths.shape, lambda i, me: (0, 0))
    earlier = [] if out is None else [out]
    return pl.pallas_call(
        functools.partial(attend_kernel, first, parts),
        out_shape=jax.ShapeDtypeStruct((requests, columns), jnp.bfloat16),
        grid_spec=pltpu.PrefetchScalarGridSpec(
            num_scalar_prefetch=1,
            grid=(requests // block,),
            in_specs=[table, wide, fresh, fresh, cache, cache]
            + [part] * parts
            + [pl.BlockSpec(memory_space=pl.ANY)] * len(earlier),
            out_specs=wide,
        ),
        input_output_aliases={7 + parts: 0} if earlier else {},
        cost_estimate=pl.CostEstimate(
            flops=4 * requests * HALF * slots * columns // groups,
            bytes_accessed=4 * requests * (columns + slots * kv) // groups,
            transcendentals=requests * slots * columns // 16 // groups,
        ),
    )(me, lengths, base, new_key, new_value, cache_keys, cache_values, *deltas, *earlier)


def attend(me, base, new_key, new_value, cache_keys, cache_values, lengths, deltas):
    groups = new_key.shape[1] // HEAD
    heads = base.shape[1] // groups // HEAD
    lengths = lengths.reshape(-1, STEP // HALF, 1, HALF)
    lengths = jnp.broadcast_to(lengths, lengths.shape[:2] + (heads, HALF)).reshape(-1, heads * STEP)
    parts = len(deltas) // groups
    out = None
    for first in range(0, len(deltas), parts):
        mine = deltas[first : first + parts]
        arrays = (base, new_key, new_value, cache_keys, cache_values)
        out = attend_half(first, me, *arrays, lengths, mine, out)
    return out


def whole(array):
    return pl.BlockSpec(array.shape, lambda *_: (0,) * len(array.shape))


def in_chunks(factors, most):
    chunk = [math.gcd(f.shape[0], most) for f in factors]
    return factors[0].shape[0] // chunk[0], [
        pl.BlockSpec((c,) + f.shape[1:], lambda i: (i, 0, 0)) for c, f in zip(chunk, factors)
    ]


def shrink_rows(ids, rows, factors):
    parts, requests = len(rows), rows[0].shape[0]
    steps, specs = in_chunks(factors, 4)
    out = jax.ShapeDtypeStruct((parts // 2 * requests, LANES), jnp.float32)
    return pl.pallas_call(
        functools.partial(shrink_kernel, parts),
        out_shape=out,
        grid=(steps,),
        in_specs=[SMEM, *map(whole, rows), *specs],
        out_specs=whole(out),
        compiler_params=PARAMS,
    )(ids, *rows, *factors)


def expand_rows(ids, rows, lows, factors):
    parts, requests, outputs = len(rows), rows[0].shape[0], factors[0].shape[2]
    steps, specs = in_chunks(factors, 8)
    last_lanes = rows[0].shape[1] // LANES - 1
    owners = pl.BlockSpec((requests, LANES), lambda i: (0, last_lanes))
    out = jax.ShapeDtypeStruct((requests, outputs), jnp.bfloat16)
    return pl.pallas_call(
        functools.partial(expand_kernel, parts),
        out_shape=[out] * parts,
        grid=(steps,),
        in_specs=[SMEM] + [owners] * parts + [*map(whole, lows), *specs],
        out_specs=[whole(out)] * parts,
        scratch_shapes=[pltpu.VMEM((parts, requests, outputs), jnp.float32)],
        compiler_params=PARAMS,
    )(ids, *rows, *lows, *factors)


def per_device(
    hidden,
    adapter_ids,
    owner_map,
    shrink_factors,
    expand_factors,
    query_base,
    new_key,
    new_value,
    cache_keys,
    cache_values,
    lengths,
):
    reps, levels, sides, tp = (lax.axis_size(a) for a in ("rep", "level", "side", "tp"))
    requests, wide = hidden.shape
    rank = shrink_factors.shape[2]
    square = reps * sides
    features, outputs = wide // square, query_base.shape[1] // square
    level, side = lax.axis_index("level"), lax.axis_index("side")
    me = lax.axis_index("rep") * sides + side

    def swap(a, s):
        pairs = [(c, c ^ s) for c in range(square)]
        return lax.ppermute(a, ("rep", "side"), pairs)

    shapes = [(levels, rank, features), (1, rank, outputs), (1, rank, features + outputs)]
    own, expand_own, other = pl.pallas_call(
        functools.partial(factor_kernel, square),
        out_shape=[jax.ShapeDtypeStruct(shape, jnp.bfloat16) for shape in shapes],
        in_specs=[SMEM, HBM, HBM],
        out_specs=[VMEM] * 3,
        scratch_shapes=[pltpu.SemaphoreType.DMA((levels + 3,))],
    )(me[None], shrink_factors.swapaxes(1, 2), expand_factors)

    def to_levels(a):
        return lax.all_to_all(a, "level", split_axis=0, concat_axis=0, tiled=True)

    own = to_levels(own)
    other = swap(other, 1)
    rows = pl.pallas_call(
        functools.partial(row_kernel, square),
        out_shape=[jax.ShapeDtypeStruct((requests, features + LANES), jnp.bfloat16)] * square,
        in_specs=[SMEM, SMEM, VMEM, HBM],
        out_specs=[VMEM] * square,
        scratch_shapes=[pltpu.SemaphoreType.DMA((square,))],
    )(me[None], owner_map, adapter_ids.T, hidden)
    *rows, other = lax.optimization_barrier((*rows, other))
    rows = [rows[0]] + [swap(rows[s], s) for s in range(1, square)]
    other, expand_next = other[:, :, :features], other[:, :, features:]
    order = jnp.arange(levels, dtype=jnp.int32)
    if levels == 4:
        pairs = [[(i, i ^ k) for i in range(levels)] for k in range(levels)]
        other = [other] + [lax.ppermute(other, "level", pairs[k]) for k in range(1, levels)]
        other_at = level ^ order
    else:
        other = [to_levels(jnp.broadcast_to(other, own.shape))]
        other_at = order
    ids = [a.reshape(-1, 4) for a in (order * sides + side, other_at * sides + (side ^ 1))]
    ids = jnp.concatenate(ids, axis=1).reshape(-1)
    expand = jnp.concatenate([expand_own, expand_next], axis=1)
    expand = jnp.broadcast_to(expand, (levels,) + expand.shape[1:])
    expand, *rows = lax.optimization_barrier((expand, *rows))
    expand = to_levels(expand).reshape(levels * sides, rank, outputs)
    expand_ids = (order[:, None] * sides + jnp.stack([side, side ^ 1])[None, :]).reshape(-1)

    partial = shrink_rows(ids, rows, [own, *other])
    for c in range(1, tp):
        partial = partial + lax.ppermute(partial, "tp", [(t, t ^ c) for t in range(tp)])
    partial = partial.astype(jnp.bfloat16)
    lows = [partial] + [swap(partial, s) for s in range(1, square)]
    deltas = expand_rows(expand_ids, rows, lows, [expand])
    deltas = [deltas[0]] + [swap(deltas[s], s) for s in range(1, square)]
    return attend(
        me[None], query_base, new_key, new_value, cache_keys, cache_values, lengths, deltas
    )


def solution(mesh):
    reps, pool, tp = (mesh.shape[a] for a in ("rep", "pool", "tp"))
    finer = Mesh(mesh.devices.reshape(reps, pool // 2, 2, tp), ("rep", "level", "side", "tp"))
    pooled = ("level", "side")
    requests = ("rep", "level", "side")
    in_specs = (
        P(requests, "tp"),
        P(requests, None),
        P(),
        P(pooled, "tp", None),
        P(pooled, None, "tp"),
        P(requests, "tp"),
        P(requests, "tp"),
        P(requests, "tp"),
        P(requests, None, "tp"),
        P(requests, None, "tp"),
        P(requests),
    )
    return jax.shard_map(
        per_device, mesh=finer, in_specs=in_specs, out_specs=P(requests, "tp"), check_vma=False
    )
```

time: 74.1 us -> 65.9 us (0.89)
  waiting for transfers between devices: 33.7 us -> 15.5 us
  starting transfers between devices: 22.9 us -> 28.6 us
  Pallas kernels: 13.8 us -> 17.4 us
    ppermute x3, waiting for transfers between devices: 13.7 us -> 0.01 us  [per_device(): lax.ppermute(other, 'level', pairs[k])]
    ppermute x10, waiting for transfers between devices: 18.7 us -> 13.1 us  [swap(): return lax.ppermute(a, ('rep', 'side'), pairs)]
    all_to_all x1 -> x2, starting transfers between devices: 6.33 us -> 11.1 us  [to_levels(): return lax.all_to_all(a, 'level', split_axis=0, concat_axis=0, tiled=True)]
    pallas_call x1 -> x2, Pallas kernels: 5.08 us -> 9.11 us  [attend_half(): pl.pallas_call(functools.partial(attend_kernel, first, parts), out_shape=...]
    all_to_all x1 -> x2, waiting for transfers between devices: 0.01 us -> 1.18 us  [to_levels(): return lax.all_to_all(a, 'level', split_axis=0, concat_axis=0, tiled=True)]
    ppermute x3, starting transfers between devices: 4.41 us -> 5.35 us  [per_device(): lax.ppermute(other, 'level', pairs[k])]
    broadcast_in_dim x0 -> x3, local copies, waits for them, and re-layouts: none -> 0.94 us  [the longest x1 0.84 us: per_device(): expand = jnp.broadcast_to(expand, (levels,) + expand.shape[1:])]
    another operation x4 -> x0, local copies, waits for them, and re-layouts: 0.82 us -> none  [attend(): jnp.tile(lengths.reshape(requests // HALF, HALF), (1, columns // HEAD))]
  transfers between devices with their start and end apart: 15 -> 16, of which waited for: 10 -> 9; matrix products, arithmetic and copies ran while one was open for 1% -> 3% of each run, Pallas kernels for 4% -> 15%
where the time goes in v12:
time: 65.9 us; the launch traced here: 65.5 us
  starting transfers between devices  28.6 us (43%)
  Pallas kernels  17.4 us (26%)
  waiting for transfers between devices  15.5 us (24%)
  local copies, waits for them, and re-layouts  3.64 us (6%)
    ppermute x10, waiting for transfers between devices, swap(): return lax.ppermute(a, ('rep', 'side'), pairs)  13.1 us
    ppermute x10, starting transfers between devices, swap(): return lax.ppermute(a, ('rep', 'side'), pairs)  12.1 us
    all_to_all x2, starting transfers between devices, to_levels(): return lax.all_to_all(a, 'level', split_axis=0, concat_axis=0, tiled=True)  11.1 us
    pallas_call x2, Pallas kernels, attend_half(): pl.pallas_call(functools.partial(attend_kernel, first, parts), out_shape=...  9.11 us
    ppermute x3, starting transfers between devices, per_device(): lax.ppermute(other, 'level', pairs[k])  5.35 us
    pallas_call x1, Pallas kernels, per_device(): pl.pallas_call(functools.partial(row_kernel, square), out_shape=[jax.Shap...  2.92 us
    pallas_call x1, Pallas kernels, per_device(): pl.pallas_call(functools.partial(factor_kernel, square), out_shape=[jax.S...  2.14 us
    pallas_call x1, Pallas kernels, shrink_rows(): pl.pallas_call(functools.partial(shrink_kernel, parts), out_shape=out, gr...  2.08 us
  transfers between devices with their start and end apart: 16, of which 9 were waited for; matrix products, arithmetic and copies ran while one was open for 3% of the time, Pallas kernels for 15%

profile of v12, /device:TPU:0, one launch (start us, length us, event | category | flops | bytes accessed | tf_op | source)
XLA Modules:
  0.0 65.5 jit_solution(9813256165907857437)
XLA Ops:
  0.0 2.1 %shard_map.109 = (bf16[4,64,1024]{2,1,0:T(8,128)(2,1)}, bf16[1,64,512]{2,1,0:T(8,128)(2,1)}, bf16[1,64,1536]{2,1,0:T(8,128)(2,1)}) custom-call(s32[1]{0:T(128)} %bitcast.me_ref, bf16[1,64,4096]{2,1,0:T(8,128)(2,1)} %bitcast.13, bf16[1,64,2048]{2,1,0:T(8,128)(2,1)} %expand_ref.1), custom_call_target="tpu_custom_call" | custom-call | tf_op jit(solution)/shard_map/pallas_call | solution.py:349
  2.2 6.5 %all-to-all-start = ((bf16[4,64,1024]{2,1,0:T(8,128)(2,1)}), bf16[4,64,1024]{2,1,0:T(8,128)(2,1)S(1)}, u32[]{:S(2)}, u32[]{:S(2)}) async-start(bf16[4,64,1024]{2,1,0:T(8,128)(2,1)} %get-tuple-element.41), calls=%async_computation | async-start | bytes 1048576 | tf_op jit(solution)/shard_map/all_to_all | solution.py:358
  8.6 1.5 %collective-permute-start = (bf16[1,64,1536]{2,1,0:T(8,128)(2,1)S(1)}, bf16[1,64,1536]{2,1,0:T(8,128)(2,1)S(1)}, u32[]{:S(2)}, u32[]{:S(2)}) collective-permute-start(bf16[1,64,1536]{2,1,0:T(8,128)(2,1)S(1)} %copy-done.7), channel_id=1, source_target_pairs={{0,2},{2,0},{16,18},{18,16},{1,3},{3,1},{17,19},{19,17},{4,6},{6,4... | collective-permute-start | bytes 589832 | tf_op jit(solution)/shard_map/ppermute | solution.py:346
  10.1 2.9 %shard_map.110 = (bf16[128,1152]{1,0:T(8,128)(2,1)}, bf16[128,1152]{1,0:T(8,128)(2,1)}, bf16[128,1152]{1,0:T(8,128)(2,1)}, bf16[128,1152]{1,0:T(8,128)(2,1)}) custom-call(s32[1]{0:T(128)} %bitcast.me_ref, s32[8]{0:T(128)} %map_ref.1, s32[1,128]{1,0:T(1,128)} %bitcast.14, bf16[128,4096]{1,0:T(8,128)(2,1)} %hidden_ref.1), custom_call_target="tpu_custom_call" | custom-call | tf_op jit(solution)/shard_map/pallas_call | solution.py:362
  13.0 2.0 %collective-permute-done = bf16[1,64,1536]{2,1,0:T(8,128)(2,1)S(1)} collective-permute-done((bf16[1,64,1536]{2,1,0:T(8,128)(2,1)S(1)}, bf16[1,64,1536]{2,1,0:T(8,128)(2,1)S(1)}, u32[]{:S(2)}, u32[]{:S(2)}) %collective-permute-start) | collective-permute-done | bytes 196640 | tf_op jit(solution)/shard_map/ppermute | solution.py:346
  15.0 1.5 %collective-permute-start.1 = (bf16[128,1152]{1,0:T(8,128)(2,1)}, bf16[128,1152]{1,0:T(8,128)(2,1)S(1)}, u32[]{:S(2)}, u32[]{:S(2)}) collective-permute-start(bf16[128,1152]{1,0:T(8,128)(2,1)} %get-tuple-element.34), channel_id=1, source_target_pairs={{0,2},{2,0},{16,18},{18,16},{1,3},{3,1},{17,19},{19,17},{4,6},{6,4... | collective-permute-start | bytes 884744 | tf_op jit(solution)/shard_map/ppermute | solution.py:346
  16.5 1.5 %collective-permute-start.2 = (bf16[128,1152]{1,0:T(8,128)(2,1)}, bf16[128,1152]{1,0:T(8,128)(2,1)S(1)}, u32[]{:S(2)}, u32[]{:S(2)}) collective-permute-start(bf16[128,1152]{1,0:T(8,128)(2,1)} %get-tuple-element.35), channel_id=1, source_target_pairs={{0,16},{2,18},{16,0},{18,2},{1,17},{3,19},{17,1},{19,3},{4,20},{6,... | collective-permute-start | bytes 884744 | tf_op jit(solution)/shard_map/ppermute | solution.py:346
  18.5 3.6 %collective-permute-start.6 = (bf16[1,64,1024]{2,1,0:T(8,128)(2,1)S(1)}, bf16[1,64,1024]{2,1,0:T(8,128)(2,1)S(1)}, u32[]{:S(2)}, u32[]{:S(2)}) collective-permute-start(bf16[1,64,1024]{2,1,0:T(8,128)(2,1)S(1)} %slice.7.refs_5_), channel_id=1, source_target_pairs={{0,12},{4,8},{8,4},{12,0},{1,13},{5,9},{9,5},{13,1},{2,14},{6,10},... | collective-permute-start | bytes 393224 | tf_op jit(solution)/shard_map/ppermute | solution.py:375
  22.1 3.0 %collective-permute-done.1.refs_1_ = bf16[128,1152]{1,0:T(8,128)(2,1)S(1)} collective-permute-done((bf16[128,1152]{1,0:T(8,128)(2,1)}, bf16[128,1152]{1,0:T(8,128)(2,1)S(1)}, u32[]{:S(2)}, u32[]{:S(2)}) %collective-permute-start.1) | collective-permute-done | bytes 294944 | tf_op jit(solution)/shard_map/ppermute | solution.py:346
  25.1 1.7 %collective-permute-start.4 = (bf16[1,64,1024]{2,1,0:T(8,128)(2,1)S(1)}, bf16[1,64,1024]{2,1,0:T(8,128)(2,1)S(1)}, u32[]{:S(2)}, u32[]{:S(2)}) collective-permute-start(bf16[1,64,1024]{2,1,0:T(8,128)(2,1)S(1)} %slice.7.refs_5_), channel_id=1, source_target_pairs={{0,4},{4,0},{8,12},{12,8},{1,5},{5,1},{9,13},{13,9},{2,6},{6,2},{1... | collective-permute-start | bytes 393224 | tf_op jit(solution)/shard_map/ppermute | solution.py:375
  26.9 3.4 %collective-permute-done.2.refs_2_ = bf16[128,1152]{1,0:T(8,128)(2,1)S(1)} collective-permute-done((bf16[128,1152]{1,0:T(8,128)(2,1)}, bf16[128,1152]{1,0:T(8,128)(2,1)S(1)}, u32[]{:S(2)}, u32[]{:S(2)}) %collective-permute-start.2) | collective-permute-done | bytes 294944 | tf_op jit(solution)/shard_map/ppermute | solution.py:346
  31.1 4.6 %all-to-all-start.1 = ((bf16[4,128,512]{2,1,0:T(8,128)(2,1)}), bf16[4,128,512]{2,1,0:T(8,128)(2,1)S(1)}, u32[]{:S(2)}, u32[]{:S(2)}) async-start(bf16[4,128,512]{2,1,0:T(8,128)(2,1)} %broadcast_in_dim.25), calls=%async_computation.1 | async-start | bytes 1048576 | tf_op jit(solution)/shard_map/all_to_all | solution.py:358
  35.9 2.1 %shard_map.111 = f32[256,128]{1,0:T(8,128)S(1)} custom-call(s32[8]{0:T(128)S(1)} %add_bitcast_fusion.ids_ref, bf16[128,1152]{1,0:T(8,128)(2,1)S(1)} %copy-done, bf16[128,1152]{1,0:T(8,128)(2,1)S(1)} %collective-permute-done.1.refs_1_, bf16[128,1152]{1,0:T(8,128)(2,1)S(1)} %collective-permute-done.2.refs_2_, ...), custom_call_target="tpu_custom_call" | custom-call | tf_op jit(solution)/shard_map/pallas_call | solution.py:296
  38.1 1.2 %collective-permute-done.7 = f32[256,128]{1,0:T(8,128)S(1)} collective-permute-done((f32[256,128]{1,0:T(8,128)S(1)}, f32[256,128]{1,0:T(8,128)S(1)}, u32[]{:S(2)}, u32[]{:S(2)}) %collective-permute-start.7) | collective-permute-done | bytes 131104 | tf_op jit(solution)/shard_map/ppermute | solution.py:390
  39.4 1.6 %collective-permute-start.10 = (bf16[256,128]{1,0:T(8,128)(2,1)S(1)}, bf16[256,128]{1,0:T(8,128)(2,1)S(1)}, u32[]{:S(2)}, u32[]{:S(2)}) collective-permute-start(bf16[256,128]{1,0:T(8,128)(2,1)S(1)} %add_convert_fusion.refs_4_), channel_id=1, source_target_pairs={{0,18},{2,16},{16,2},{18,0},{1,19},{3,17},{17,3},{19,1},{4,22},{6,... | collective-permute-start | bytes 196616 | tf_op jit(solution)/shard_map/ppermute | solution.py:346
  41.0 1.2 %collective-permute-start.9 = (bf16[256,128]{1,0:T(8,128)(2,1)S(1)}, bf16[256,128]{1,0:T(8,128)(2,1)S(1)}, u32[]{:S(2)}, u32[]{:S(2)}) collective-permute-start(bf16[256,128]{1,0:T(8,128)(2,1)S(1)} %add_convert_fusion.refs_4_), channel_id=1, source_target_pairs={{0,16},{2,18},{16,0},{18,2},{1,17},{3,19},{17,1},{19,3},{4,20},{6,... | collective-permute-start | bytes 196616 | tf_op jit(solution)/shard_map/ppermute | solution.py:346
  43.1 1.6 %collective-permute-done.10.refs_7_ = bf16[256,128]{1,0:T(8,128)(2,1)S(1)} collective-permute-done((bf16[256,128]{1,0:T(8,128)(2,1)S(1)}, bf16[256,128]{1,0:T(8,128)(2,1)S(1)}, u32[]{:S(2)}, u32[]{:S(2)}) %collective-permute-start.10) | collective-permute-done | bytes 65568 | tf_op jit(solution)/shard_map/ppermute | solution.py:346
  44.7 1.2 %collective-permute-done.9.refs_6_ = bf16[256,128]{1,0:T(8,128)(2,1)S(1)} collective-permute-done((bf16[256,128]{1,0:T(8,128)(2,1)S(1)}, bf16[256,128]{1,0:T(8,128)(2,1)S(1)}, u32[]{:S(2)}, u32[]{:S(2)}) %collective-permute-start.9) | collective-permute-done | bytes 65568 | tf_op jit(solution)/shard_map/ppermute | solution.py:346
  46.4 1.2 %all-to-all-done.1 = bf16[4,128,512]{2,1,0:T(8,128)(2,1)S(1)} async-done(((bf16[4,128,512]{2,1,0:T(8,128)(2,1)}), bf16[4,128,512]{2,1,0:T(8,128)(2,1)S(1)}, u32[]{:S(2)}, u32[]{:S(2)}) %all-to-all-start.1) | async-done | bytes 524320 | tf_op jit(solution)/shard_map/all_to_all | solution.py:358
  48.7 1.6 %collective-permute-start.13 = (bf16[128,512]{1,0:T(8,128)(2,1)S(1)}, bf16[128,512]{1,0:T(8,128)(2,1)S(1)}, u32[]{:S(2)}, u32[]{:S(2)}) collective-permute-start(bf16[128,512]{1,0:T(8,128)(2,1)S(1)} %get-tuple-element.46), channel_id=1, source_target_pairs={{0,2},{2,0},{16,18},{18,16},{1,3},{3,1},{17,19},{19,17},{4,6},{6,4... | collective-permute-start | bytes 393224 | tf_op jit(solution)/shard_map/ppermute | solution.py:346
  50.8 1.5 %collective-permute-start.12 = (bf16[128,512]{1,0:T(8,128)(2,1)S(1)}, bf16[128,512]{1,0:T(8,128)(2,1)S(1)}, u32[]{:S(2)}, u32[]{:S(2)}) collective-permute-start(bf16[128,512]{1,0:T(8,128)(2,1)S(1)} %get-tuple-element.44), channel_id=1, source_target_pairs={{0,18},{2,16},{16,2},{18,0},{1,19},{3,17},{17,3},{19,1},{4,22},{6,... | collective-permute-start | bytes 393224 | tf_op jit(solution)/shard_map/ppermute | solution.py:346
  53.1 1.4 %collective-permute-done.13.refs_1_ = bf16[128,512]{1,0:T(8,128)(2,1)S(1)} collective-permute-done((bf16[128,512]{1,0:T(8,128)(2,1)S(1)}, bf16[128,512]{1,0:T(8,128)(2,1)S(1)}, u32[]{:S(2)}, u32[]{:S(2)}) %collective-permute-start.13) | collective-permute-done | bytes 131104 | tf_op jit(solution)/shard_map/ppermute | solution.py:346
  55.1 4.6 %shard_map.113.refs_2_ = bf16[128,2048]{1,0:T(8,128)(2,1)} custom-call(s32[1]{0:T(128)} %bitcast.me_ref, s32[8,128]{1,0:T(8,128)} %reshape.46.len_ref, bf16[128,2048]{1,0:T(8,128)(2,1)} %base_ref.3, bf16[128,256]{1,0:T(8,128)(2,1)} %nk_ref.3, bf16[128,256]{1,0:T(8,128)(2,1)} %nv_ref.3, bf16[128,16,256]{2,1,0:T(8,128)(2,1)} %ck_ref.3, ...), custom_call_target="tpu_custom_call" | custom-call | flops 67108864 | bytes 1572864 | tf_op jit(solution)/shard_map/pallas_call | solution.py:247
  61.0 4.6 %shard_map.114 = bf16[128,2048]{1,0:T(8,128)(2,1)} custom-call(s32[1]{0:T(128)} %bitcast.me_ref, s32[8,128]{1,0:T(8,128)} %reshape.46.len_ref, bf16[128,2048]{1,0:T(8,128)(2,1)} %base_ref.3, bf16[128,256]{1,0:T(8,128)(2,1)} %nk_ref.3, bf16[128,256]{1,0:T(8,128)(2,1)} %nv_ref.3, bf16[128,16,256]{2,1,0:T(8,128)(2,1)} %ck_ref.3, ...), custom_call_target="tpu_custom_call", output_to_operand_aliasing={{}: (9, {})} | custom-call | flops 67108864 | bytes 1572864 | tf_op jit(solution)/shard_map/pallas_call | solution.py:247
  (44 shorter events, 7.4 us)
Async XLA Ops:
  2.1 6.5 %copy-start.7 = (bf16[1,64,1536]{2,1,0:T(8,128)(2,1)S(1)}, bf16[1,64,1536]{2,1,0:T(8,128)(2,1)}, u32[]{:S(2)}) copy-start(bf16[1,64,1536]{2,1,0:T(8,128)(2,1)} %get-tuple-element.31) | copy-start | bytes 589828
  2.2 29.0 %all-to-all-start = ((bf16[4,64,1024]{2,1,0:T(8,128)(2,1)}), bf16[4,64,1024]{2,1,0:T(8,128)(2,1)S(1)}, u32[]{:S(2)}, u32[]{:S(2)}) async-start(bf16[4,64,1024]{2,1,0:T(8,128)(2,1)} %get-tuple-element.41), calls=%async_computation | async-start | bytes 1048576 | tf_op jit(solution)/shard_map/all_to_all | solution.py:358
  8.6 6.4 %collective-permute-start = (bf16[1,64,1536]{2,1,0:T(8,128)(2,1)S(1)}, bf16[1,64,1536]{2,1,0:T(8,128)(2,1)S(1)}, u32[]{:S(2)}, u32[]{:S(2)}) collective-permute-start(bf16[1,64,1536]{2,1,0:T(8,128)(2,1)S(1)} %copy-done.7), channel_id=1, source_target_pairs={{0,2},{2,0},{16,18},{18,16},{1,3},{3,1},{17,19},{19,17},{4,6},{6,4... | collective-permute-start | bytes 589832 | tf_op jit(solution)/shard_map/ppermute | solution.py:346
  15.0 10.2 %collective-permute-start.1 = (bf16[128,1152]{1,0:T(8,128)(2,1)}, bf16[128,1152]{1,0:T(8,128)(2,1)S(1)}, u32[]{:S(2)}, u32[]{:S(2)}) collective-permute-start(bf16[128,1152]{1,0:T(8,128)(2,1)} %get-tuple-element.34), channel_id=1, source_target_pairs={{0,2},{2,0},{16,18},{18,16},{1,3},{3,1},{17,19},{19,17},{4,6},{6,4... | collective-permute-start | bytes 884744 | tf_op jit(solution)/shard_map/ppermute | solution.py:346
  16.5 13.8 %collective-permute-start.2 = (bf16[128,1152]{1,0:T(8,128)(2,1)}, bf16[128,1152]{1,0:T(8,128)(2,1)S(1)}, u32[]{:S(2)}, u32[]{:S(2)}) collective-permute-start(bf16[128,1152]{1,0:T(8,128)(2,1)} %get-tuple-element.35), channel_id=1, source_target_pairs={{0,16},{2,18},{16,0},{18,2},{1,17},{3,19},{17,1},{19,3},{4,20},{6,... | collective-permute-start | bytes 884744 | tf_op jit(solution)/shard_map/ppermute | solution.py:346
  18.0 12.3 %collective-permute-start.3 = (bf16[128,1152]{1,0:T(8,128)(2,1)}, bf16[128,1152]{1,0:T(8,128)(2,1)S(1)}, u32[]{:S(2)}, u32[]{:S(2)}) collective-permute-start(bf16[128,1152]{1,0:T(8,128)(2,1)} %get-tuple-element.36), channel_id=1, source_target_pairs={{0,18},{2,16},{16,2},{18,0},{1,19},{3,17},{17,3},{19,1},{4,22},{6,... | collective-permute-start | bytes 884744 | tf_op jit(solution)/shard_map/ppermute | solution.py:346
  18.5 8.4 %copy-start.5 = (bf16[1,64,512]{2,1,0:T(8,128)(2,1)S(1)}, bf16[1,64,512]{2,1,0:T(8,128)(2,1)}, u32[]{:S(2)}) copy-start(bf16[1,64,512]{2,1,0:T(8,128)(2,1)} %get-tuple-element.26) | copy-start | bytes 196612
  18.5 17.3 %collective-permute-start.6 = (bf16[1,64,1024]{2,1,0:T(8,128)(2,1)S(1)}, bf16[1,64,1024]{2,1,0:T(8,128)(2,1)S(1)}, u32[]{:S(2)}, u32[]{:S(2)}) collective-permute-start(bf16[1,64,1024]{2,1,0:T(8,128)(2,1)S(1)} %slice.7.refs_5_), channel_id=1, source_target_pairs={{0,12},{4,8},{8,4},{12,0},{1,13},{5,9},{9,5},{13,1},{2,14},{6,10},... | collective-permute-start | bytes 393224 | tf_op jit(solution)/shard_map/ppermute | solution.py:375
  22.1 13.7 %collective-permute-start.5 = (bf16[1,64,1024]{2,1,0:T(8,128)(2,1)S(1)}, bf16[1,64,1024]{2,1,0:T(8,128)(2,1)S(1)}, u32[]{:S(2)}, u32[]{:S(2)}) collective-permute-start(bf16[1,64,1024]{2,1,0:T(8,128)(2,1)S(1)} %slice.7.refs_5_), channel_id=1, source_target_pairs={{0,8},{4,12},{8,0},{12,4},{1,9},{5,13},{9,1},{13,5},{2,10},{6,14},... | collective-permute-start | bytes 393224 | tf_op jit(solution)/shard_map/ppermute | solution.py:375
  25.1 10.7 %collective-permute-start.4 = (bf16[1,64,1024]{2,1,0:T(8,128)(2,1)S(1)}, bf16[1,64,1024]{2,1,0:T(8,128)(2,1)S(1)}, u32[]{:S(2)}, u32[]{:S(2)}) collective-permute-start(bf16[1,64,1024]{2,1,0:T(8,128)(2,1)S(1)} %slice.7.refs_5_), channel_id=1, source_target_pairs={{0,4},{4,0},{8,12},{12,8},{1,5},{5,1},{9,13},{13,9},{2,6},{6,2},{1... | collective-permute-start | bytes 393224 | tf_op jit(solution)/shard_map/ppermute | solution.py:375
  31.1 4.7 %copy-start = (bf16[128,1152]{1,0:T(8,128)(2,1)S(1)}, bf16[128,1152]{1,0:T(8,128)(2,1)}, u32[]{:S(2)}) copy-start(bf16[128,1152]{1,0:T(8,128)(2,1)} %get-tuple-element.37.refs_0_) | copy-start | bytes 884740
  31.1 16.5 %all-to-all-start.1 = ((bf16[4,128,512]{2,1,0:T(8,128)(2,1)}), bf16[4,128,512]{2,1,0:T(8,128)(2,1)S(1)}, u32[]{:S(2)}, u32[]{:S(2)}) async-start(bf16[4,128,512]{2,1,0:T(8,128)(2,1)} %broadcast_in_dim.25), calls=%async_computation.1 | async-start | bytes 1048576 | tf_op jit(solution)/shard_map/all_to_all | solution.py:358
  38.0 1.4 %collective-permute-start.7 = (f32[256,128]{1,0:T(8,128)S(1)}, f32[256,128]{1,0:T(8,128)S(1)}, u32[]{:S(2)}, u32[]{:S(2)}) collective-permute-start(f32[256,128]{1,0:T(8,128)S(1)} %shard_map.111), channel_id=1, source_target_pairs={{0,1},{1,0},{2,3},{3,2},{4,5},{5,4},{6,7},{7,6},{8,9},{9,8},{10,11... | collective-permute-start | bytes 393224 | tf_op jit(solution)/shard_map/ppermute | solution.py:390
  39.4 5.3 %collective-permute-start.10 = (bf16[256,128]{1,0:T(8,128)(2,1)S(1)}, bf16[256,128]{1,0:T(8,128)(2,1)S(1)}, u32[]{:S(2)}, u32[]{:S(2)}) collective-permute-start(bf16[256,128]{1,0:T(8,128)(2,1)S(1)} %add_convert_fusion.refs_4_), channel_id=1, source_target_pairs={{0,18},{2,16},{16,2},{18,0},{1,19},{3,17},{17,3},{19,1},{4,22},{6,... | collective-permute-start | bytes 196616 | tf_op jit(solution)/shard_map/ppermute | solution.py:346
  41.0 5.0 %collective-permute-start.9 = (bf16[256,128]{1,0:T(8,128)(2,1)S(1)}, bf16[256,128]{1,0:T(8,128)(2,1)S(1)}, u32[]{:S(2)}, u32[]{:S(2)}) collective-permute-start(bf16[256,128]{1,0:T(8,128)(2,1)S(1)} %add_convert_fusion.refs_4_), channel_id=1, source_target_pairs={{0,16},{2,18},{16,0},{18,2},{1,17},{3,19},{17,1},{19,3},{4,20},{6,... | collective-permute-start | bytes 196616 | tf_op jit(solution)/shard_map/ppermute | solution.py:346
  42.2 4.3 %collective-permute-start.8 = (bf16[256,128]{1,0:T(8,128)(2,1)S(1)}, bf16[256,128]{1,0:T(8,128)(2,1)S(1)}, u32[]{:S(2)}, u32[]{:S(2)}) collective-permute-start(bf16[256,128]{1,0:T(8,128)(2,1)S(1)} %add_convert_fusion.refs_4_), channel_id=1, source_target_pairs={{0,2},{2,0},{16,18},{18,16},{1,3},{3,1},{17,19},{19,17},{4,6},{6,4... | collective-permute-start | bytes 196616 | tf_op jit(solution)/shard_map/ppermute | solution.py:346
  48.7 5.8 %copy-start.1 = (bf16[128,512]{1,0:T(8,128)(2,1)}, bf16[128,512]{1,0:T(8,128)(2,1)S(1)}, u32[]{:S(2)}) copy-start(bf16[128,512]{1,0:T(8,128)(2,1)S(1)} %get-tuple-element.45.refs_0_) | copy-start | bytes 393220
  48.7 5.8 %collective-permute-start.13 = (bf16[128,512]{1,0:T(8,128)(2,1)S(1)}, bf16[128,512]{1,0:T(8,128)(2,1)S(1)}, u32[]{:S(2)}, u32[]{:S(2)}) collective-permute-start(bf16[128,512]{1,0:T(8,128)(2,1)S(1)} %get-tuple-element.46), channel_id=1, source_target_pairs={{0,2},{2,0},{16,18},{18,16},{1,3},{3,1},{17,19},{19,17},{4,6},{6,4... | collective-permute-start | bytes 393224 | tf_op jit(solution)/shard_map/ppermute | solution.py:346
  50.3 2.0 %copy-start.6 = (s32[128]{0:T(128)S(1)}, s32[128]{0:T(128)}, u32[]{:S(2)}) copy-start(s32[128]{0:T(128)} %param.21) | copy-start | bytes 1540
  50.3 9.4 %collective-permute-start.11 = (bf16[128,512]{1,0:T(8,128)(2,1)S(1)}, bf16[128,512]{1,0:T(8,128)(2,1)S(1)}, u32[]{:S(2)}, u32[]{:S(2)}) collective-permute-start(bf16[128,512]{1,0:T(8,128)(2,1)S(1)} %get-tuple-element.43), channel_id=1, source_target_pairs={{0,16},{2,18},{16,0},{18,2},{1,17},{3,19},{17,1},{19,3},{4,20},{6,... | collective-permute-start | bytes 393224 | tf_op jit(solution)/shard_map/ppermute | solution.py:346
  50.8 8.9 %collective-permute-start.12 = (bf16[128,512]{1,0:T(8,128)(2,1)S(1)}, bf16[128,512]{1,0:T(8,128)(2,1)S(1)}, u32[]{:S(2)}, u32[]{:S(2)}) collective-permute-start(bf16[128,512]{1,0:T(8,128)(2,1)S(1)} %get-tuple-element.44), channel_id=1, source_target_pairs={{0,18},{2,16},{16,2},{18,0},{1,19},{3,17},{17,3},{19,1},{4,22},{6,... | collective-permute-start | bytes 393224 | tf_op jit(solution)/shard_map/ppermute | solution.py:346
  54.5 0.6 copy-start.4
  59.7 0.7 copy-start.2
  60.3 0.6 copy-start.3

commit v13 on v12

--- a/solution.py
+++ b/solution.py
@@ -13,7 +13,7 @@
 LANES = 128
 STEP = 16
 HALF = 8
-BATCH = 2
+BATCH = 4
 DEAD = -1e30
 VMEM = pl.BlockSpec(memory_space=pltpu.VMEM)
 SMEM = pl.BlockSpec(memory_space=pltpu.SMEM)
@@ -37,16 +37,16 @@
         copy.wait()
 
 
-def factor_kernel(parts, me_ref, shrink_ref, expand_ref, own_ref, expand_own_ref, other_ref, sems):
-    features, outputs = shrink_ref.shape[2] // parts, expand_ref.shape[2] // parts
+def factor_kernel(sides, me_ref, shrink_ref, expand_ref, own_ref, other_ref, expand_send_ref, sems):
+    features, outputs = own_ref.shape[2], expand_send_ref.shape[2]
+    levels = own_ref.shape[0]
     me = me_ref[0]
-    moves = [
-        (shrink_ref.at[:, :, columns(me ^ 1, features)], other_ref.at[:, :, :features]),
-        (expand_ref.at[:, :, columns(me ^ 1, outputs)], other_ref.at[:, :, features:]),
-        (expand_ref.at[:, :, columns(me, outputs)], expand_own_ref),
-    ]
+    moves = [(shrink_ref.at[:, :, columns(me ^ 1, features)], other_ref)]
     share = shrink_ref.at[0, :, columns(me, features)]
-    moves += [(share, own_ref.at[k]) for k in range(own_ref.shape[0])]
+    moves += [(share, own_ref.at[k]) for k in range(levels)]
+    for side in range(sides):
+        share = expand_ref.at[0, :, columns(me // sides * sides + side, outputs)]
+        moves += [(share, expand_send_ref.at[k * sides + side]) for k in range(levels)]
     run_copies(moves, sems)
 
 
@@ -264,11 +264,14 @@
     )(me, lengths, base, new_key, new_value, cache_keys, cache_values, *deltas, *earlier)
 
 
+def length_table(lengths, heads):
+    lengths = lengths.reshape(-1, STEP // HALF, 1, HALF)
+    lengths = jnp.broadcast_to(lengths, lengths.shape[:2] + (heads, HALF))
+    return lengths.reshape(-1, heads * STEP)
+
+
 def attend(me, base, new_key, new_value, cache_keys, cache_values, lengths, deltas):
     groups = new_key.shape[1] // HEAD
-    heads = base.shape[1] // groups // HEAD
-    lengths = lengths.reshape(-1, STEP // HALF, 1, HALF)
-    lengths = jnp.broadcast_to(lengths, lengths.shape[:2] + (heads, HALF)).reshape(-1, heads * STEP)
     parts = len(deltas) // groups
     out = None
     for first in range(0, len(deltas), parts):
@@ -345,13 +348,13 @@
         pairs = [(c, c ^ s) for c in range(square)]
         return lax.ppermute(a, ("rep", "side"), pairs)
 
-    shapes = [(levels, rank, features), (1, rank, outputs), (1, rank, features + outputs)]
-    own, expand_own, other = pl.pallas_call(
-        functools.partial(factor_kernel, square),
+    shapes = [(levels, rank, features), (1, rank, features), (levels * sides, rank, outputs)]
+    own, other, expand = pl.pallas_call(
+        functools.partial(factor_kernel, sides),
         out_shape=[jax.ShapeDtypeStruct(shape, jnp.bfloat16) for shape in shapes],
         in_specs=[SMEM, HBM, HBM],
         out_specs=[VMEM] * 3,
-        scratch_shapes=[pltpu.SemaphoreType.DMA((levels + 3,))],
+        scratch_shapes=[pltpu.SemaphoreType.DMA((levels * (sides + 1) + 1,))],
     )(me[None], shrink_factors.swapaxes(1, 2), expand_factors)
 
     def to_levels(a):
@@ -366,9 +369,10 @@
         out_specs=[VMEM] * square,
         scratch_shapes=[pltpu.SemaphoreType.DMA((square,))],
     )(me[None], owner_map, adapter_ids.T, hidden)
-    *rows, other = lax.optimization_barrier((*rows, other))
+    table = length_table(lengths, outputs * square // new_key.shape[1])
+    *rows, other, table = lax.optimization_barrier((*rows, other, table))
     rows = [rows[0]] + [swap(rows[s], s) for s in range(1, square)]
-    other, expand_next = other[:, :, :features], other[:, :, features:]
+
     order = jnp.arange(levels, dtype=jnp.int32)
     if levels == 4:
         pairs = [[(i, i ^ k) for i in range(levels)] for k in range(levels)]
@@ -379,11 +383,10 @@
         other_at = order
     ids = [a.reshape(-1, 4) for a in (order * sides + side, other_at * sides + (side ^ 1))]
     ids = jnp.concatenate(ids, axis=1).reshape(-1)
-    expand = jnp.concatenate([expand_own, expand_next], axis=1)
-    expand = jnp.broadcast_to(expand, (levels,) + expand.shape[1:])
     expand, *rows = lax.optimization_barrier((expand, *rows))
-    expand = to_levels(expand).reshape(levels * sides, rank, outputs)
-    expand_ids = (order[:, None] * sides + jnp.stack([side, side ^ 1])[None, :]).reshape(-1)
+    pooled = ("level", "side")
+    expand = lax.all_to_all(expand, pooled, split_axis=0, concat_axis=0, tiled=True)
+    expand_ids = jnp.arange(levels * sides, dtype=jnp.int32)
 
     partial = shrink_rows(ids, rows, [own, *other])
     for c in range(1, tp):
@@ -393,7 +396,7 @@
     deltas = expand_rows(expand_ids, rows, lows, [expand])
     deltas = [deltas[0]] + [swap(deltas[s], s) for s in range(1, square)]
     return attend(
-        me[None], query_base, new_key, new_value, cache_keys, cache_values, lengths, deltas
+        me[None], query_base, new_key, new_value, cache_keys, cache_values, table, deltas
     )
 
 

time: 65.9 us -> 84.4 us (1.28)
  waiting for transfers between devices: 15.5 us -> 37 us
  Pallas kernels: 17.4 us -> 15.2 us
    ppermute x3, waiting for transfers between devices: 0.01 us -> 17.9 us  [per_device(): lax.ppermute(other, 'level', pairs[k])]
    all_to_all x0 -> x1, starting transfers between devices: none -> 5.32 us  [per_device(): lax.all_to_all(expand, pooled, split_axis=0, concat_axis=0, tiled=True)]
    ppermute x10, waiting for transfers between devices: 13.1 us -> 17.8 us  [swap(): return lax.ppermute(a, ('rep', 'side'), pairs)]
    all_to_all x2 -> x1, starting transfers between devices: 11.1 us -> 6.46 us  [to_levels(): return lax.all_to_all(a, 'level', split_axis=0, concat_axis=0, tiled=True)]
    pallas_call x2, Pallas kernels: 9.11 us -> 6.35 us  [attend_half(): pl.pallas_call(functools.partial(attend_kernel, first, parts), out_shape=...]
    all_to_all x2 -> x1, waiting for transfers between devices: 1.18 us -> 0.01 us  [to_levels(): return lax.all_to_all(a, 'level', split_axis=0, concat_axis=0, tiled=True)]
    ppermute x3, starting transfers between devices: 5.35 us -> 4.41 us  [per_device(): lax.ppermute(other, 'level', pairs[k])]
    unnamed x16 -> x14, local copies, waits for them, and re-layouts: 1.92 us -> 2.61 us
  transfers between devices with their start and end apart: 16 -> 16, of which waited for: 9 -> 10; matrix products, arithmetic and copies ran while one was open for 3% -> 1% of each run, Pallas kernels for 15% -> 10%
where the time goes in v13:
time: 84.4 us; the launch traced here: 84 us
  waiting for transfers between devices  37 us (44%)
  starting transfers between devices  28.2 us (33%)
  Pallas kernels  15.2 us (18%)
  local copies, waits for them, and re-layouts  3.39 us (4%)
    ppermute x3, waiting for transfers between devices, per_device(): lax.ppermute(other, 'level', pairs[k])  17.9 us
    ppermute x10, waiting for transfers between devices, swap(): return lax.ppermute(a, ('rep', 'side'), pairs)  17.8 us
    ppermute x10, starting transfers between devices, swap(): return lax.ppermute(a, ('rep', 'side'), pairs)  12 us
    all_to_all x1, starting transfers between devices, to_levels(): return lax.all_to_all(a, 'level', split_axis=0, concat_axis=0, tiled=True)  6.46 us
    pallas_call x2, Pallas kernels, attend_half(): pl.pallas_call(functools.partial(attend_kernel, first, parts), out_shape=...  6.35 us
    all_to_all x1, starting transfers between devices, per_device(): lax.all_to_all(expand, pooled, split_axis=0, concat_axis=0, tiled=True)  5.32 us
    ppermute x3, starting transfers between devices, per_device(): lax.ppermute(other, 'level', pairs[k])  4.41 us
    pallas_call x1, Pallas kernels, per_device(): pl.pallas_call(functools.partial(row_kernel, square), out_shape=[jax.Shap...  2.93 us
  transfers between devices with their start and end apart: 16, of which 10 were waited for; matrix products, arithmetic and copies ran while one was open for 1% of the time, Pallas kernels for 10%

profile of v13, /device:TPU:0, one launch (start us, length us, event | category | flops | bytes accessed | tf_op | source)
XLA Modules:
  0.0 84.0 jit_solution(13346864428718605686)
XLA Ops:
  0.0 2.7 %shard_map.110 = (bf16[4,64,1024]{2,1,0:T(8,128)(2,1)}, bf16[1,64,1024]{2,1,0:T(8,128)(2,1)}, bf16[8,64,512]{2,1,0:T(8,128)(2,1)}) custom-call(s32[1]{0:T(128)} %bitcast.me_ref, bf16[1,64,4096]{2,1,0:T(8,128)(2,1)} %bitcast.7, bf16[1,64,2048]{2,1,0:T(8,128)(2,1)} %expand_ref.1), custom_call_target="tpu_custom_call" | custom-call | tf_op jit(solution)/shard_map/pallas_call | solution.py:352
  2.7 6.5 %all-to-all-start = ((bf16[4,64,1024]{2,1,0:T(8,128)(2,1)}), bf16[4,64,1024]{2,1,0:T(8,128)(2,1)S(1)}, u32[]{:S(2)}, u32[]{:S(2)}) async-start(bf16[4,64,1024]{2,1,0:T(8,128)(2,1)} %get-tuple-element.42), calls=%async_computation | async-start | bytes 1048576 | tf_op jit(solution)/shard_map/all_to_all | solution.py:361
  9.2 1.4 %collective-permute-start = (bf16[1,64,1024]{2,1,0:T(8,128)(2,1)S(1)}, bf16[1,64,1024]{2,1,0:T(8,128)(2,1)S(1)}, u32[]{:S(2)}, u32[]{:S(2)}) collective-permute-start(bf16[1,64,1024]{2,1,0:T(8,128)(2,1)S(1)} %copy-done.6), channel_id=1, source_target_pairs={{0,2},{2,0},{16,18},{18,16},{1,3},{3,1},{17,19},{19,17},{4,6},{6,4... | collective-permute-start | bytes 393224 | tf_op jit(solution)/shard_map/ppermute | solution.py:349
  11.3 2.9 %shard_map.109 = (bf16[128,1152]{1,0:T(8,128)(2,1)}, bf16[128,1152]{1,0:T(8,128)(2,1)}, bf16[128,1152]{1,0:T(8,128)(2,1)}, bf16[128,1152]{1,0:T(8,128)(2,1)}) custom-call(s32[1]{0:T(128)} %bitcast.me_ref, s32[8]{0:T(128)} %map_ref.1, s32[1,128]{1,0:T(1,128)} %bitcast.8, bf16[128,4096]{1,0:T(8,128)(2,1)} %hidden_ref.1), custom_call_target="tpu_custom_call" | custom-call | tf_op jit(solution)/shard_map/pallas_call | solution.py:365
  14.3 1.2 %collective-permute-start.1 = (bf16[128,1152]{1,0:T(8,128)(2,1)}, bf16[128,1152]{1,0:T(8,128)(2,1)S(1)}, u32[]{:S(2)}, u32[]{:S(2)}) collective-permute-start(bf16[128,1152]{1,0:T(8,128)(2,1)} %get-tuple-element.35), channel_id=1, source_target_pairs={{0,2},{2,0},{16,18},{18,16},{1,3},{3,1},{17,19},{19,17},{4,6},{6,4... | collective-permute-start | bytes 884744 | tf_op jit(solution)/shard_map/ppermute | solution.py:349
  15.5 1.7 %collective-permute-start.2 = (bf16[128,1152]{1,0:T(8,128)(2,1)}, bf16[128,1152]{1,0:T(8,128)(2,1)S(1)}, u32[]{:S(2)}, u32[]{:S(2)}) collective-permute-start(bf16[128,1152]{1,0:T(8,128)(2,1)} %get-tuple-element.36), channel_id=1, source_target_pairs={{0,16},{2,18},{16,0},{18,2},{1,17},{3,19},{17,1},{19,3},{4,20},{6,... | collective-permute-start | bytes 884744 | tf_op jit(solution)/shard_map/ppermute | solution.py:349
  17.8 6.7 %collective-permute-done.1.refs_1_ = bf16[128,1152]{1,0:T(8,128)(2,1)S(1)} collective-permute-done((bf16[128,1152]{1,0:T(8,128)(2,1)}, bf16[128,1152]{1,0:T(8,128)(2,1)S(1)}, u32[]{:S(2)}, u32[]{:S(2)}) %collective-permute-start.1) | collective-permute-done | bytes 294944 | tf_op jit(solution)/shard_map/ppermute | solution.py:349
  24.5 4.6 %collective-permute-done.2.refs_2_ = bf16[128,1152]{1,0:T(8,128)(2,1)S(1)} collective-permute-done((bf16[128,1152]{1,0:T(8,128)(2,1)}, bf16[128,1152]{1,0:T(8,128)(2,1)S(1)}, u32[]{:S(2)}, u32[]{:S(2)}) %collective-permute-start.2) | collective-permute-done | bytes 294944 | tf_op jit(solution)/shard_map/ppermute | solution.py:349
  29.1 1.2 %collective-permute-done.3.refs_3_ = bf16[128,1152]{1,0:T(8,128)(2,1)S(1)} collective-permute-done((bf16[128,1152]{1,0:T(8,128)(2,1)}, bf16[128,1152]{1,0:T(8,128)(2,1)S(1)}, u32[]{:S(2)}, u32[]{:S(2)}) %collective-permute-start.3) | collective-permute-done | bytes 294944 | tf_op jit(solution)/shard_map/ppermute | solution.py:349
  30.2 5.3 %all-to-all-start.1 = ((bf16[8,64,512]{2,1,0:T(8,128)(2,1)}), bf16[8,64,512]{2,1,0:T(8,128)(2,1)S(1)}, u32[]{:S(2)}, u32[]{:S(2)}) async-start(bf16[8,64,512]{2,1,0:T(8,128)(2,1)} %get-tuple-element.44), calls=%async_computation.1 | async-start | bytes 1048576 | tf_op jit(solution)/shard_map/all_to_all | solution.py:388
  35.6 2.0 %collective-permute-start.4 = (bf16[1,64,1024]{2,1,0:T(8,128)(2,1)S(1)}, bf16[1,64,1024]{2,1,0:T(8,128)(2,1)S(1)}, u32[]{:S(2)}, u32[]{:S(2)}) collective-permute-start(bf16[1,64,1024]{2,1,0:T(8,128)(2,1)S(1)} %collective-permute-done.refs_5_), channel_id=1, source_target_pairs={{0,4},{4,0},{8,12},{12,8},{1,5},{5,1},{9,13},{13,9},{2,6},{6,2},{1... | collective-permute-start | bytes 393224 | tf_op jit(solution)/shard_map/ppermute | solution.py:379
  37.6 2.4 %collective-permute-start.5 = (bf16[1,64,1024]{2,1,0:T(8,128)(2,1)S(1)}, bf16[1,64,1024]{2,1,0:T(8,128)(2,1)S(1)}, u32[]{:S(2)}, u32[]{:S(2)}) collective-permute-start(bf16[1,64,1024]{2,1,0:T(8,128)(2,1)S(1)} %collective-permute-done.refs_5_), channel_id=1, source_target_pairs={{0,8},{4,12},{8,0},{12,4},{1,9},{5,13},{9,1},{13,5},{2,10},{6,14},... | collective-permute-start | bytes 393224 | tf_op jit(solution)/shard_map/ppermute | solution.py:379
  40.1 7.8 %collective-permute-done.4.refs_6_ = bf16[1,64,1024]{2,1,0:T(8,128)(2,1)S(1)} collective-permute-done((bf16[1,64,1024]{2,1,0:T(8,128)(2,1)S(1)}, bf16[1,64,1024]{2,1,0:T(8,128)(2,1)S(1)}, u32[]{:S(2)}, u32[]{:S(2)}) %collective-permute-start.4) | collective-permute-done | bytes 131104 | tf_op jit(solution)/shard_map/ppermute | solution.py:379
  47.8 10.1 %collective-permute-done.5.refs_7_ = bf16[1,64,1024]{2,1,0:T(8,128)(2,1)S(1)} collective-permute-done((bf16[1,64,1024]{2,1,0:T(8,128)(2,1)S(1)}, bf16[1,64,1024]{2,1,0:T(8,128)(2,1)S(1)}, u32[]{:S(2)}, u32[]{:S(2)}) %collective-permute-start.5) | collective-permute-done | bytes 131104 | tf_op jit(solution)/shard_map/ppermute | solution.py:379
  57.9 2.1 %shard_map.111 = f32[256,128]{1,0:T(8,128)S(1)} custom-call(s32[8]{0:T(128)S(1)} %add_bitcast_fusion.ids_ref, bf16[128,1152]{1,0:T(8,128)(2,1)S(1)} %copy-done, bf16[128,1152]{1,0:T(8,128)(2,1)S(1)} %collective-permute-done.1.refs_1_, bf16[128,1152]{1,0:T(8,128)(2,1)S(1)} %collective-permute-done.2.refs_2_, ...), custom_call_target="tpu_custom_call" | custom-call | tf_op jit(solution)/shard_map/pallas_call | solution.py:299
  60.1 1.3 %collective-permute-done.7 = f32[256,128]{1,0:T(8,128)S(1)} collective-permute-done((f32[256,128]{1,0:T(8,128)S(1)}, f32[256,128]{1,0:T(8,128)S(1)}, u32[]{:S(2)}, u32[]{:S(2)}) %collective-permute-start.7) | collective-permute-done | bytes 131104 | tf_op jit(solution)/shard_map/ppermute | solution.py:393
  61.4 1.5 %collective-permute-start.8 = (bf16[256,128]{1,0:T(8,128)(2,1)S(1)}, bf16[256,128]{1,0:T(8,128)(2,1)S(1)}, u32[]{:S(2)}, u32[]{:S(2)}) collective-permute-start(bf16[256,128]{1,0:T(8,128)(2,1)S(1)} %add_convert_fusion.refs_4_), channel_id=1, source_target_pairs={{0,2},{2,0},{16,18},{18,16},{1,3},{3,1},{17,19},{19,17},{4,6},{6,4... | collective-permute-start | bytes 196616 | tf_op jit(solution)/shard_map/ppermute | solution.py:349
  63.3 1.7 %collective-permute-start.10 = (bf16[256,128]{1,0:T(8,128)(2,1)S(1)}, bf16[256,128]{1,0:T(8,128)(2,1)S(1)}, u32[]{:S(2)}, u32[]{:S(2)}) collective-permute-start(bf16[256,128]{1,0:T(8,128)(2,1)S(1)} %add_convert_fusion.refs_4_), channel_id=1, source_target_pairs={{0,18},{2,16},{16,2},{18,0},{1,19},{3,17},{17,3},{19,1},{4,22},{6,... | collective-permute-start | bytes 196616 | tf_op jit(solution)/shard_map/ppermute | solution.py:349
  65.8 2.0 %collective-permute-done.9.refs_6_ = bf16[256,128]{1,0:T(8,128)(2,1)S(1)} collective-permute-done((bf16[256,128]{1,0:T(8,128)(2,1)S(1)}, bf16[256,128]{1,0:T(8,128)(2,1)S(1)}, u32[]{:S(2)}, u32[]{:S(2)}) %collective-permute-start.9) | collective-permute-done | bytes 65568 | tf_op jit(solution)/shard_map/ppermute | solution.py:349
  70.9 1.7 %collective-permute-start.11 = (bf16[128,512]{1,0:T(8,128)(2,1)S(1)}, bf16[128,512]{1,0:T(8,128)(2,1)S(1)}, u32[]{:S(2)}, u32[]{:S(2)}) collective-permute-start(bf16[128,512]{1,0:T(8,128)(2,1)S(1)} %get-tuple-element.45), channel_id=1, source_target_pairs={{0,16},{2,18},{16,0},{18,2},{1,17},{3,19},{17,1},{19,3},{4,20},{6,... | collective-permute-start | bytes 393224 | tf_op jit(solution)/shard_map/ppermute | solution.py:349
  72.5 1.2 %collective-permute-start.12 = (bf16[128,512]{1,0:T(8,128)(2,1)S(1)}, bf16[128,512]{1,0:T(8,128)(2,1)S(1)}, u32[]{:S(2)}, u32[]{:S(2)}) collective-permute-start(bf16[128,512]{1,0:T(8,128)(2,1)S(1)} %get-tuple-element.46), channel_id=1, source_target_pairs={{0,18},{2,16},{16,2},{18,0},{1,19},{3,17},{17,3},{19,1},{4,22},{6,... | collective-permute-start | bytes 393224 | tf_op jit(solution)/shard_map/ppermute | solution.py:349
  73.7 2.0 %collective-permute-done.13.refs_1_ = bf16[128,512]{1,0:T(8,128)(2,1)S(1)} collective-permute-done((bf16[128,512]{1,0:T(8,128)(2,1)S(1)}, bf16[128,512]{1,0:T(8,128)(2,1)S(1)}, u32[]{:S(2)}, u32[]{:S(2)}) %collective-permute-start.13) | collective-permute-done | bytes 131104 | tf_op jit(solution)/shard_map/ppermute | solution.py:349
  76.3 3.2 %shard_map.113.refs_2_ = bf16[128,2048]{1,0:T(8,128)(2,1)} custom-call(s32[1]{0:T(128)} %bitcast.me_ref, s32[8,128]{1,0:T(8,128)} %reshape.33.len_ref, bf16[128,2048]{1,0:T(8,128)(2,1)} %base_ref.3, bf16[128,256]{1,0:T(8,128)(2,1)} %nk_ref.3, bf16[128,256]{1,0:T(8,128)(2,1)} %nv_ref.3, bf16[128,16,256]{2,1,0:T(8,128)(2,1)} %ck_ref.3, ...), custom_call_target="tpu_custom_call" | custom-call | flops 67108864 | bytes 1572864 | tf_op jit(solution)/shard_map/pallas_call | solution.py:247
  80.8 3.2 %shard_map.114 = bf16[128,2048]{1,0:T(8,128)(2,1)} custom-call(s32[1]{0:T(128)} %bitcast.me_ref, s32[8,128]{1,0:T(8,128)} %reshape.33.len_ref, bf16[128,2048]{1,0:T(8,128)(2,1)} %base_ref.3, bf16[128,256]{1,0:T(8,128)(2,1)} %nk_ref.3, bf16[128,256]{1,0:T(8,128)(2,1)} %nv_ref.3, bf16[128,16,256]{2,1,0:T(8,128)(2,1)} %ck_ref.3, ...), custom_call_target="tpu_custom_call", output_to_operand_aliasing={{}: (9, {})} | custom-call | flops 67108864 | bytes 1572864 | tf_op jit(solution)/shard_map/pallas_call | solution.py:247
  (35 shorter events, 7.7 us)
Async XLA Ops:
  2.7 6.5 %copy-start.6 = (bf16[1,64,1024]{2,1,0:T(8,128)(2,1)S(1)}, bf16[1,64,1024]{2,1,0:T(8,128)(2,1)}, u32[]{:S(2)}) copy-start(bf16[1,64,1024]{2,1,0:T(8,128)(2,1)} %get-tuple-element.31) | copy-start | bytes 393220
  2.7 27.5 %all-to-all-start = ((bf16[4,64,1024]{2,1,0:T(8,128)(2,1)}), bf16[4,64,1024]{2,1,0:T(8,128)(2,1)S(1)}, u32[]{:S(2)}, u32[]{:S(2)}) async-start(bf16[4,64,1024]{2,1,0:T(8,128)(2,1)} %get-tuple-element.42), calls=%async_computation | async-start | bytes 1048576 | tf_op jit(solution)/shard_map/all_to_all | solution.py:361
  9.2 1.4 %copy-start.5 = (s32[128]{0:T(128)S(1)}, s32[128]{0:T(128)}, u32[]{:S(2)}) copy-start(s32[128]{0:T(128)} %param.21) | copy-start | bytes 1540
  9.2 5.1 %collective-permute-start = (bf16[1,64,1024]{2,1,0:T(8,128)(2,1)S(1)}, bf16[1,64,1024]{2,1,0:T(8,128)(2,1)S(1)}, u32[]{:S(2)}, u32[]{:S(2)}) collective-permute-start(bf16[1,64,1024]{2,1,0:T(8,128)(2,1)S(1)} %copy-done.6), channel_id=1, source_target_pairs={{0,2},{2,0},{16,18},{18,16},{1,3},{3,1},{17,19},{19,17},{4,6},{6,4... | collective-permute-start | bytes 393224 | tf_op jit(solution)/shard_map/ppermute | solution.py:349
  14.3 10.2 %collective-permute-start.1 = (bf16[128,1152]{1,0:T(8,128)(2,1)}, bf16[128,1152]{1,0:T(8,128)(2,1)S(1)}, u32[]{:S(2)}, u32[]{:S(2)}) collective-permute-start(bf16[128,1152]{1,0:T(8,128)(2,1)} %get-tuple-element.35), channel_id=1, source_target_pairs={{0,2},{2,0},{16,18},{18,16},{1,3},{3,1},{17,19},{19,17},{4,6},{6,4... | collective-permute-start | bytes 884744 | tf_op jit(solution)/shard_map/ppermute | solution.py:349
  15.5 13.5 %collective-permute-start.2 = (bf16[128,1152]{1,0:T(8,128)(2,1)}, bf16[128,1152]{1,0:T(8,128)(2,1)S(1)}, u32[]{:S(2)}, u32[]{:S(2)}) collective-permute-start(bf16[128,1152]{1,0:T(8,128)(2,1)} %get-tuple-element.36), channel_id=1, source_target_pairs={{0,16},{2,18},{16,0},{18,2},{1,17},{3,19},{17,1},{19,3},{4,20},{6,... | collective-permute-start | bytes 884744 | tf_op jit(solution)/shard_map/ppermute | solution.py:349
  17.2 13.0 %collective-permute-start.3 = (bf16[128,1152]{1,0:T(8,128)(2,1)}, bf16[128,1152]{1,0:T(8,128)(2,1)S(1)}, u32[]{:S(2)}, u32[]{:S(2)}) collective-permute-start(bf16[128,1152]{1,0:T(8,128)(2,1)} %get-tuple-element.37), channel_id=1, source_target_pairs={{0,18},{2,16},{16,2},{18,0},{1,19},{3,17},{17,3},{19,1},{4,22},{6,... | collective-permute-start | bytes 884744 | tf_op jit(solution)/shard_map/ppermute | solution.py:349
  30.2 27.7 %copy-start = (bf16[128,1152]{1,0:T(8,128)(2,1)S(1)}, bf16[128,1152]{1,0:T(8,128)(2,1)}, u32[]{:S(2)}) copy-start(bf16[128,1152]{1,0:T(8,128)(2,1)} %get-tuple-element.38.refs_0_) | copy-start | bytes 884740
  30.2 38.2 %all-to-all-start.1 = ((bf16[8,64,512]{2,1,0:T(8,128)(2,1)}), bf16[8,64,512]{2,1,0:T(8,128)(2,1)S(1)}, u32[]{:S(2)}, u32[]{:S(2)}) async-start(bf16[8,64,512]{2,1,0:T(8,128)(2,1)} %get-tuple-element.44), calls=%async_computation.1 | async-start | bytes 1048576 | tf_op jit(solution)/shard_map/all_to_all | solution.py:388
  35.6 12.3 %collective-permute-start.4 = (bf16[1,64,1024]{2,1,0:T(8,128)(2,1)S(1)}, bf16[1,64,1024]{2,1,0:T(8,128)(2,1)S(1)}, u32[]{:S(2)}, u32[]{:S(2)}) collective-permute-start(bf16[1,64,1024]{2,1,0:T(8,128)(2,1)S(1)} %collective-permute-done.refs_5_), channel_id=1, source_target_pairs={{0,4},{4,0},{8,12},{12,8},{1,5},{5,1},{9,13},{13,9},{2,6},{6,2},{1... | collective-permute-start | bytes 393224 | tf_op jit(solution)/shard_map/ppermute | solution.py:379
  37.6 20.3 %collective-permute-start.5 = (bf16[1,64,1024]{2,1,0:T(8,128)(2,1)S(1)}, bf16[1,64,1024]{2,1,0:T(8,128)(2,1)S(1)}, u32[]{:S(2)}, u32[]{:S(2)}) collective-permute-start(bf16[1,64,1024]{2,1,0:T(8,128)(2,1)S(1)} %collective-permute-done.refs_5_), channel_id=1, source_target_pairs={{0,8},{4,12},{8,0},{12,4},{1,9},{5,13},{9,1},{13,5},{2,10},{6,14},... | collective-permute-start | bytes 393224 | tf_op jit(solution)/shard_map/ppermute | solution.py:379
  39.9 18.0 %collective-permute-start.6 = (bf16[1,64,1024]{2,1,0:T(8,128)(2,1)S(1)}, bf16[1,64,1024]{2,1,0:T(8,128)(2,1)S(1)}, u32[]{:S(2)}, u32[]{:S(2)}) collective-permute-start(bf16[1,64,1024]{2,1,0:T(8,128)(2,1)S(1)} %collective-permute-done.refs_5_), channel_id=1, source_target_pairs={{0,12},{4,8},{8,4},{12,0},{1,13},{5,9},{9,5},{13,1},{2,14},{6,10},... | collective-permute-start | bytes 393224 | tf_op jit(solution)/shard_map/ppermute | solution.py:379
  60.0 1.4 %collective-permute-start.7 = (f32[256,128]{1,0:T(8,128)S(1)}, f32[256,128]{1,0:T(8,128)S(1)}, u32[]{:S(2)}, u32[]{:S(2)}) collective-permute-start(f32[256,128]{1,0:T(8,128)S(1)} %shard_map.111), channel_id=1, source_target_pairs={{0,1},{1,0},{2,3},{3,2},{4,5},{5,4},{6,7},{7,6},{8,9},{9,8},{10,11... | collective-permute-start | bytes 393224 | tf_op jit(solution)/shard_map/ppermute | solution.py:393
  61.4 4.3 %collective-permute-start.8 = (bf16[256,128]{1,0:T(8,128)(2,1)S(1)}, bf16[256,128]{1,0:T(8,128)(2,1)S(1)}, u32[]{:S(2)}, u32[]{:S(2)}) collective-permute-start(bf16[256,128]{1,0:T(8,128)(2,1)S(1)} %add_convert_fusion.refs_4_), channel_id=1, source_target_pairs={{0,2},{2,0},{16,18},{18,16},{1,3},{3,1},{17,19},{19,17},{4,6},{6,4... | collective-permute-start | bytes 196616 | tf_op jit(solution)/shard_map/ppermute | solution.py:349
  63.0 4.8 %collective-permute-start.9 = (bf16[256,128]{1,0:T(8,128)(2,1)S(1)}, bf16[256,128]{1,0:T(8,128)(2,1)S(1)}, u32[]{:S(2)}, u32[]{:S(2)}) collective-permute-start(bf16[256,128]{1,0:T(8,128)(2,1)S(1)} %add_convert_fusion.refs_4_), channel_id=1, source_target_pairs={{0,16},{2,18},{16,0},{18,2},{1,17},{3,19},{17,1},{19,3},{4,20},{6,... | collective-permute-start | bytes 196616 | tf_op jit(solution)/shard_map/ppermute | solution.py:349
  63.3 5.2 %collective-permute-start.10 = (bf16[256,128]{1,0:T(8,128)(2,1)S(1)}, bf16[256,128]{1,0:T(8,128)(2,1)S(1)}, u32[]{:S(2)}, u32[]{:S(2)}) collective-permute-start(bf16[256,128]{1,0:T(8,128)(2,1)S(1)} %add_convert_fusion.refs_4_), channel_id=1, source_target_pairs={{0,18},{2,16},{16,2},{18,0},{1,19},{3,17},{17,3},{19,1},{4,22},{6,... | collective-permute-start | bytes 196616 | tf_op jit(solution)/shard_map/ppermute | solution.py:349
  69.6 0.7 copy-start.1
  70.2 5.4 %collective-permute-start.13 = (bf16[128,512]{1,0:T(8,128)(2,1)S(1)}, bf16[128,512]{1,0:T(8,128)(2,1)S(1)}, u32[]{:S(2)}, u32[]{:S(2)}) collective-permute-start(bf16[128,512]{1,0:T(8,128)(2,1)S(1)} %get-tuple-element.48), channel_id=1, source_target_pairs={{0,2},{2,0},{16,18},{18,16},{1,3},{3,1},{17,19},{19,17},{4,6},{6,4... | collective-permute-start | bytes 393224 | tf_op jit(solution)/shard_map/ppermute | solution.py:349
  70.9 8.7 %collective-permute-start.11 = (bf16[128,512]{1,0:T(8,128)(2,1)S(1)}, bf16[128,512]{1,0:T(8,128)(2,1)S(1)}, u32[]{:S(2)}, u32[]{:S(2)}) collective-permute-start(bf16[128,512]{1,0:T(8,128)(2,1)S(1)} %get-tuple-element.45), channel_id=1, source_target_pairs={{0,16},{2,18},{16,0},{18,2},{1,17},{3,19},{17,1},{19,3},{4,20},{6,... | collective-permute-start | bytes 393224 | tf_op jit(solution)/shard_map/ppermute | solution.py:349
  72.5 7.0 %collective-permute-start.12 = (bf16[128,512]{1,0:T(8,128)(2,1)S(1)}, bf16[128,512]{1,0:T(8,128)(2,1)S(1)}, u32[]{:S(2)}, u32[]{:S(2)}) collective-permute-start(bf16[128,512]{1,0:T(8,128)(2,1)S(1)} %get-tuple-element.46), channel_id=1, source_target_pairs={{0,18},{2,16},{16,2},{18,0},{1,19},{3,17},{17,3},{19,1},{4,22},{6,... | collective-permute-start | bytes 393224 | tf_op jit(solution)/shard_map/ppermute | solution.py:349
  75.7 0.6 copy-start.4
  79.5 0.7 copy-start.2
  80.2 0.6 copy-start.3

commit v14 on v13

--- a/solution.py
+++ b/solution.py
@@ -383,7 +383,7 @@
         other_at = order
     ids = [a.reshape(-1, 4) for a in (order * sides + side, other_at * sides + (side ^ 1))]
     ids = jnp.concatenate(ids, axis=1).reshape(-1)
-    expand, *rows = lax.optimization_barrier((expand, *rows))
+    expand, other, rows = lax.optimization_barrier((expand, other, rows))
     pooled = ("level", "side")
     expand = lax.all_to_all(expand, pooled, split_axis=0, concat_axis=0, tiled=True)
     expand_ids = jnp.arange(levels * sides, dtype=jnp.int32)

time: 84.4 us -> 72 us (0.85)
  waiting for transfers between devices: 37 us -> 18.7 us
  starting transfers between devices: 28.2 us -> 34.2 us
    ppermute x10, waiting for transfers between devices: 17.8 us -> 6.55 us  [swap(): return lax.ppermute(a, ('rep', 'side'), pairs)]
    ppermute x3, waiting for transfers between devices: 17.9 us -> 8.07 us  [per_device(): lax.ppermute(other, 'level', pairs[k])]
    ppermute x3, starting transfers between devices: 4.41 us -> 11.5 us  [per_device(): lax.ppermute(other, 'level', pairs[k])]
    all_to_all x1, waiting for transfers between devices: 0.01 us -> 2.7 us  [per_device(): lax.all_to_all(expand, pooled, split_axis=0, concat_axis=0, tiled=True)]
    all_to_all x1, starting transfers between devices: 5.32 us -> 3.82 us  [per_device(): lax.all_to_all(expand, pooled, split_axis=0, concat_axis=0, tiled=True)]
  transfers between devices with their start and end apart: 16 -> 16, of which waited for: 10 -> 8; matrix products, arithmetic and copies ran while one was open for 1% -> 1% of each run, Pallas kernels for 10% -> 11%
where the time goes in v14:
time: 72 us; the launch traced here: 71.6 us
  starting transfers between devices  34.2 us (48%)
  waiting for transfers between devices  18.7 us (26%)
  Pallas kernels  15.2 us (21%)
  local copies, waits for them, and re-layouts  3.39 us (5%)
    ppermute x10, starting transfers between devices, swap(): return lax.ppermute(a, ('rep', 'side'), pairs)  12.3 us
    ppermute x3, starting transfers between devices, per_device(): lax.ppermute(other, 'level', pairs[k])  11.5 us
    ppermute x3, waiting for transfers between devices, per_device(): lax.ppermute(other, 'level', pairs[k])  8.07 us
    ppermute x10, waiting for transfers between devices, swap(): return lax.ppermute(a, ('rep', 'side'), pairs)  6.55 us
    all_to_all x1, starting transfers between devices, to_levels(): return lax.all_to_all(a, 'level', split_axis=0, concat_axis=0, tiled=True)  6.46 us
    pallas_call x2, Pallas kernels, attend_half(): pl.pallas_call(functools.partial(attend_kernel, first, parts), out_shape=...  6.35 us
    all_to_all x1, starting transfers between devices, per_device(): lax.all_to_all(expand, pooled, split_axis=0, concat_axis=0, tiled=True)  3.82 us
    pallas_call x1, Pallas kernels, per_device(): pl.pallas_call(functools.partial(row_kernel, square), out_shape=[jax.Shap...  2.93 us
  transfers between devices with their start and end apart: 16, of which 8 were waited for; matrix products, arithmetic and copies ran while one was open for 1% of the time, Pallas kernels for 11%

profile of v14, /device:TPU:0, one launch (start us, length us, event | category | flops | bytes accessed | tf_op | source)
XLA Modules:
  0.0 71.6 jit_solution(14461540197823694732)
XLA Ops:
  0.0 2.7 %shard_map.110 = (bf16[4,64,1024]{2,1,0:T(8,128)(2,1)}, bf16[1,64,1024]{2,1,0:T(8,128)(2,1)}, bf16[8,64,512]{2,1,0:T(8,128)(2,1)}) custom-call(s32[1]{0:T(128)} %bitcast.me_ref, bf16[1,64,4096]{2,1,0:T(8,128)(2,1)} %bitcast.7, bf16[1,64,2048]{2,1,0:T(8,128)(2,1)} %expand_ref.1), custom_call_target="tpu_custom_call" | custom-call | tf_op jit(solution)/shard_map/pallas_call | solution.py:352
  2.7 6.5 %all-to-all-start = ((bf16[4,64,1024]{2,1,0:T(8,128)(2,1)}), bf16[4,64,1024]{2,1,0:T(8,128)(2,1)S(1)}, u32[]{:S(2)}, u32[]{:S(2)}) async-start(bf16[4,64,1024]{2,1,0:T(8,128)(2,1)} %get-tuple-element.47), calls=%async_computation | async-start | bytes 1048576 | tf_op jit(solution)/shard_map/all_to_all | solution.py:361
  9.2 1.4 %collective-permute-start = (bf16[1,64,1024]{2,1,0:T(8,128)(2,1)S(1)}, bf16[1,64,1024]{2,1,0:T(8,128)(2,1)S(1)}, u32[]{:S(2)}, u32[]{:S(2)}) collective-permute-start(bf16[1,64,1024]{2,1,0:T(8,128)(2,1)S(1)} %copy-done.6), channel_id=1, source_target_pairs={{0,2},{2,0},{16,18},{18,16},{1,3},{3,1},{17,19},{19,17},{4,6},{6,4... | collective-permute-start | bytes 393224 | tf_op jit(solution)/shard_map/ppermute | solution.py:349
  10.7 0.7 reshape.33.len_ref
  11.3 2.9 %shard_map.109 = (bf16[128,1152]{1,0:T(8,128)(2,1)}, bf16[128,1152]{1,0:T(8,128)(2,1)}, bf16[128,1152]{1,0:T(8,128)(2,1)}, bf16[128,1152]{1,0:T(8,128)(2,1)}) custom-call(s32[1]{0:T(128)} %bitcast.me_ref, s32[8]{0:T(128)} %map_ref.1, s32[1,128]{1,0:T(1,128)} %bitcast.8, bf16[128,4096]{1,0:T(8,128)(2,1)} %hidden_ref.1), custom_call_target="tpu_custom_call" | custom-call | tf_op jit(solution)/shard_map/pallas_call | solution.py:365
  14.3 1.2 %collective-permute-start.4 = (bf16[128,1152]{1,0:T(8,128)(2,1)}, bf16[128,1152]{1,0:T(8,128)(2,1)S(1)}, u32[]{:S(2)}, u32[]{:S(2)}) collective-permute-start(bf16[128,1152]{1,0:T(8,128)(2,1)} %get-tuple-element.40), channel_id=1, source_target_pairs={{0,2},{2,0},{16,18},{18,16},{1,3},{3,1},{17,19},{19,17},{4,6},{6,4... | collective-permute-start | bytes 884744 | tf_op jit(solution)/shard_map/ppermute | solution.py:349
  15.5 1.7 %collective-permute-start.5 = (bf16[128,1152]{1,0:T(8,128)(2,1)}, bf16[128,1152]{1,0:T(8,128)(2,1)S(1)}, u32[]{:S(2)}, u32[]{:S(2)}) collective-permute-start(bf16[128,1152]{1,0:T(8,128)(2,1)} %get-tuple-element.41), channel_id=1, source_target_pairs={{0,16},{2,18},{16,0},{18,2},{1,17},{3,19},{17,1},{19,3},{4,20},{6,... | collective-permute-start | bytes 884744 | tf_op jit(solution)/shard_map/ppermute | solution.py:349
  17.8 3.8 %collective-permute-start.3 = (bf16[1,64,1024]{2,1,0:T(8,128)(2,1)S(1)}, bf16[1,64,1024]{2,1,0:T(8,128)(2,1)S(1)}, u32[]{:S(2)}, u32[]{:S(2)}) collective-permute-start(bf16[1,64,1024]{2,1,0:T(8,128)(2,1)S(1)} %collective-permute-done.refs_5_), channel_id=1, source_target_pairs={{0,12},{4,8},{8,4},{12,0},{1,13},{5,9},{9,5},{13,1},{2,14},{6,10},... | collective-permute-start | bytes 393224 | tf_op jit(solution)/shard_map/ppermute | solution.py:379
  21.7 4.4 %collective-permute-done.3.refs_8_ = bf16[1,64,1024]{2,1,0:T(8,128)(2,1)S(1)} collective-permute-done((bf16[1,64,1024]{2,1,0:T(8,128)(2,1)S(1)}, bf16[1,64,1024]{2,1,0:T(8,128)(2,1)S(1)}, u32[]{:S(2)}, u32[]{:S(2)}) %collective-permute-start.3) | collective-permute-done | bytes 131104 | tf_op jit(solution)/shard_map/ppermute | solution.py:379
  26.0 7.7 %collective-permute-start.1 = (bf16[1,64,1024]{2,1,0:T(8,128)(2,1)S(1)}, bf16[1,64,1024]{2,1,0:T(8,128)(2,1)S(1)}, u32[]{:S(2)}, u32[]{:S(2)}) collective-permute-start(bf16[1,64,1024]{2,1,0:T(8,128)(2,1)S(1)} %collective-permute-done.refs_5_), channel_id=1, source_target_pairs={{0,4},{4,0},{8,12},{12,8},{1,5},{5,1},{9,13},{13,9},{2,6},{6,2},{1... | collective-permute-start | bytes 393224 | tf_op jit(solution)/shard_map/ppermute | solution.py:379
  33.7 1.3 %collective-permute-done.2.refs_7_ = bf16[1,64,1024]{2,1,0:T(8,128)(2,1)S(1)} collective-permute-done((bf16[1,64,1024]{2,1,0:T(8,128)(2,1)S(1)}, bf16[1,64,1024]{2,1,0:T(8,128)(2,1)S(1)}, u32[]{:S(2)}, u32[]{:S(2)}) %collective-permute-start.2) | collective-permute-done | bytes 131104 | tf_op jit(solution)/shard_map/ppermute | solution.py:379
  35.0 2.4 %collective-permute-done.1.refs_6_ = bf16[1,64,1024]{2,1,0:T(8,128)(2,1)S(1)} collective-permute-done((bf16[1,64,1024]{2,1,0:T(8,128)(2,1)S(1)}, bf16[1,64,1024]{2,1,0:T(8,128)(2,1)S(1)}, u32[]{:S(2)}, u32[]{:S(2)}) %collective-permute-start.1) | collective-permute-done | bytes 131104 | tf_op jit(solution)/shard_map/ppermute | solution.py:379
  37.5 3.8 %all-to-all-start.1 = ((bf16[8,64,512]{2,1,0:T(8,128)(2,1)}), bf16[8,64,512]{2,1,0:T(8,128)(2,1)S(1)}, u32[]{:S(2)}, u32[]{:S(2)}) async-start(bf16[8,64,512]{2,1,0:T(8,128)(2,1)} %get-tuple-element.52), calls=%async_computation.1 | async-start | bytes 1048576 | tf_op jit(solution)/shard_map/all_to_all | solution.py:388
  41.4 2.1 %shard_map.111 = f32[256,128]{1,0:T(8,128)S(1)} custom-call(s32[8]{0:T(128)S(1)} %add_bitcast_fusion.ids_ref, bf16[128,1152]{1,0:T(8,128)(2,1)S(1)} %copy-done, bf16[128,1152]{1,0:T(8,128)(2,1)S(1)} %collective-permute-done.4.refs_1_, bf16[128,1152]{1,0:T(8,128)(2,1)S(1)} %collective-permute-done.5.refs_2_, ...), custom_call_target="tpu_custom_call" | custom-call | tf_op jit(solution)/shard_map/pallas_call | solution.py:299
  43.5 1.3 %collective-permute-done.7 = f32[256,128]{1,0:T(8,128)S(1)} collective-permute-done((f32[256,128]{1,0:T(8,128)S(1)}, f32[256,128]{1,0:T(8,128)S(1)}, u32[]{:S(2)}, u32[]{:S(2)}) %collective-permute-start.7) | collective-permute-done | bytes 131104 | tf_op jit(solution)/shard_map/ppermute | solution.py:393
  44.9 3.2 %collective-permute-start.10 = (bf16[256,128]{1,0:T(8,128)(2,1)S(1)}, bf16[256,128]{1,0:T(8,128)(2,1)S(1)}, u32[]{:S(2)}, u32[]{:S(2)}) collective-permute-start(bf16[256,128]{1,0:T(8,128)(2,1)S(1)} %add_convert_fusion.refs_4_), channel_id=1, source_target_pairs={{0,18},{2,16},{16,2},{18,0},{1,19},{3,17},{17,3},{19,1},{4,22},{6,... | collective-permute-start | bytes 196616 | tf_op jit(solution)/shard_map/ppermute | solution.py:349
  48.8 3.4 %collective-permute-done.10.refs_7_ = bf16[256,128]{1,0:T(8,128)(2,1)S(1)} collective-permute-done((bf16[256,128]{1,0:T(8,128)(2,1)S(1)}, bf16[256,128]{1,0:T(8,128)(2,1)S(1)}, u32[]{:S(2)}, u32[]{:S(2)}) %collective-permute-start.10) | collective-permute-done | bytes 65568 | tf_op jit(solution)/shard_map/ppermute | solution.py:349
  52.7 2.7 %all-to-all-done.1.refs_8_ = bf16[8,64,512]{2,1,0:T(8,128)(2,1)S(1)} async-done(((bf16[8,64,512]{2,1,0:T(8,128)(2,1)}), bf16[8,64,512]{2,1,0:T(8,128)(2,1)S(1)}, u32[]{:S(2)}, u32[]{:S(2)}) %all-to-all-start.1) | async-done | bytes 524320 | tf_op jit(solution)/shard_map/all_to_all | solution.py:388
  55.4 1.1 %shard_map.112 = (bf16[128,512]{1,0:T(8,128)(2,1)S(1)}, bf16[128,512]{1,0:T(8,128)(2,1)S(1)}, bf16[128,512]{1,0:T(8,128)(2,1)S(1)}, bf16[128,512]{1,0:T(8,128)(2,1)S(1)}) custom-call(s32[8]{0:T(128)S(1)} %iota.10.ids_ref, bf16[128,1152]{1,0:T(8,128)(2,1)S(1)} %copy-done, bf16[128,1152]{1,0:T(8,128)(2,1)S(1)} %collective-permute-done.4.refs_1_, ...), custom_call_target="tpu_custom_call" | custom-call | tf_op jit(solution)/shard_map/pallas_call | solution.py:315
  57.2 1.4 %collective-permute-start.13 = (bf16[128,512]{1,0:T(8,128)(2,1)S(1)}, bf16[128,512]{1,0:T(8,128)(2,1)S(1)}, u32[]{:S(2)}, u32[]{:S(2)}) collective-permute-start(bf16[128,512]{1,0:T(8,128)(2,1)S(1)} %get-tuple-element.56), channel_id=1, source_target_pairs={{0,2},{2,0},{16,18},{18,16},{1,3},{3,1},{17,19},{19,17},{4,6},{6,4... | collective-permute-start | bytes 393224 | tf_op jit(solution)/shard_map/ppermute | solution.py:349
  58.6 1.5 %collective-permute-start.11 = (bf16[128,512]{1,0:T(8,128)(2,1)S(1)}, bf16[128,512]{1,0:T(8,128)(2,1)S(1)}, u32[]{:S(2)}, u32[]{:S(2)}) collective-permute-start(bf16[128,512]{1,0:T(8,128)(2,1)S(1)} %get-tuple-element.53), channel_id=1, source_target_pairs={{0,16},{2,18},{16,0},{18,2},{1,17},{3,19},{17,1},{19,3},{4,20},{6,... | collective-permute-start | bytes 393224 | tf_op jit(solution)/shard_map/ppermute | solution.py:349
  60.7 2.6 %collective-permute-done.13.refs_1_ = bf16[128,512]{1,0:T(8,128)(2,1)S(1)} collective-permute-done((bf16[128,512]{1,0:T(8,128)(2,1)S(1)}, bf16[128,512]{1,0:T(8,128)(2,1)S(1)}, u32[]{:S(2)}, u32[]{:S(2)}) %collective-permute-start.13) | collective-permute-done | bytes 131104 | tf_op jit(solution)/shard_map/ppermute | solution.py:349
  63.9 3.2 %shard_map.113.refs_2_ = bf16[128,2048]{1,0:T(8,128)(2,1)} custom-call(s32[1]{0:T(128)} %bitcast.me_ref, s32[8,128]{1,0:T(8,128)} %reshape.33.len_ref, bf16[128,2048]{1,0:T(8,128)(2,1)} %base_ref.3, bf16[128,256]{1,0:T(8,128)(2,1)} %nk_ref.3, bf16[128,256]{1,0:T(8,128)(2,1)} %nv_ref.3, bf16[128,16,256]{2,1,0:T(8,128)(2,1)} %ck_ref.3, ...), custom_call_target="tpu_custom_call" | custom-call | flops 67108864 | bytes 1572864 | tf_op jit(solution)/shard_map/pallas_call | solution.py:247
  68.5 3.2 %shard_map.114 = bf16[128,2048]{1,0:T(8,128)(2,1)} custom-call(s32[1]{0:T(128)} %bitcast.me_ref, s32[8,128]{1,0:T(8,128)} %reshape.33.len_ref, bf16[128,2048]{1,0:T(8,128)(2,1)} %base_ref.3, bf16[128,256]{1,0:T(8,128)(2,1)} %nk_ref.3, bf16[128,256]{1,0:T(8,128)(2,1)} %nv_ref.3, bf16[128,16,256]{2,1,0:T(8,128)(2,1)} %ck_ref.3, ...), custom_call_target="tpu_custom_call", output_to_operand_aliasing={{}: (9, {})} | custom-call | flops 67108864 | bytes 1572864 | tf_op jit(solution)/shard_map/pallas_call | solution.py:247
  (35 shorter events, 5.2 us)
Async XLA Ops:
  2.7 6.5 %copy-start.6 = (bf16[1,64,1024]{2,1,0:T(8,128)(2,1)S(1)}, bf16[1,64,1024]{2,1,0:T(8,128)(2,1)}, u32[]{:S(2)}) copy-start(bf16[1,64,1024]{2,1,0:T(8,128)(2,1)} %get-tuple-element.35) | copy-start | bytes 393220
  2.7 34.7 %all-to-all-start = ((bf16[4,64,1024]{2,1,0:T(8,128)(2,1)}), bf16[4,64,1024]{2,1,0:T(8,128)(2,1)S(1)}, u32[]{:S(2)}, u32[]{:S(2)}) async-start(bf16[4,64,1024]{2,1,0:T(8,128)(2,1)} %get-tuple-element.47), calls=%async_computation | async-start | bytes 1048576 | tf_op jit(solution)/shard_map/all_to_all | solution.py:361
  9.2 1.4 %copy-start.5 = (s32[128]{0:T(128)S(1)}, s32[128]{0:T(128)}, u32[]{:S(2)}) copy-start(s32[128]{0:T(128)} %param.21) | copy-start | bytes 1540
  9.2 5.1 %collective-permute-start = (bf16[1,64,1024]{2,1,0:T(8,128)(2,1)S(1)}, bf16[1,64,1024]{2,1,0:T(8,128)(2,1)S(1)}, u32[]{:S(2)}, u32[]{:S(2)}) collective-permute-start(bf16[1,64,1024]{2,1,0:T(8,128)(2,1)S(1)} %copy-done.6), channel_id=1, source_target_pairs={{0,2},{2,0},{16,18},{18,16},{1,3},{3,1},{17,19},{19,17},{4,6},{6,4... | collective-permute-start | bytes 393224 | tf_op jit(solution)/shard_map/ppermute | solution.py:349
  14.3 23.1 %collective-permute-start.4 = (bf16[128,1152]{1,0:T(8,128)(2,1)}, bf16[128,1152]{1,0:T(8,128)(2,1)S(1)}, u32[]{:S(2)}, u32[]{:S(2)}) collective-permute-start(bf16[128,1152]{1,0:T(8,128)(2,1)} %get-tuple-element.40), channel_id=1, source_target_pairs={{0,2},{2,0},{16,18},{18,16},{1,3},{3,1},{17,19},{19,17},{4,6},{6,4... | collective-permute-start | bytes 884744 | tf_op jit(solution)/shard_map/ppermute | solution.py:349
  15.5 21.9 %collective-permute-start.5 = (bf16[128,1152]{1,0:T(8,128)(2,1)}, bf16[128,1152]{1,0:T(8,128)(2,1)S(1)}, u32[]{:S(2)}, u32[]{:S(2)}) collective-permute-start(bf16[128,1152]{1,0:T(8,128)(2,1)} %get-tuple-element.41), channel_id=1, source_target_pairs={{0,16},{2,18},{16,0},{18,2},{1,17},{3,19},{17,1},{19,3},{4,20},{6,... | collective-permute-start | bytes 884744 | tf_op jit(solution)/shard_map/ppermute | solution.py:349
  17.2 20.2 %collective-permute-start.6 = (bf16[128,1152]{1,0:T(8,128)(2,1)}, bf16[128,1152]{1,0:T(8,128)(2,1)S(1)}, u32[]{:S(2)}, u32[]{:S(2)}) collective-permute-start(bf16[128,1152]{1,0:T(8,128)(2,1)} %get-tuple-element.42), channel_id=1, source_target_pairs={{0,18},{2,16},{16,2},{18,0},{1,19},{3,17},{17,3},{19,1},{4,22},{6,... | collective-permute-start | bytes 884744 | tf_op jit(solution)/shard_map/ppermute | solution.py:349
  17.8 8.2 %collective-permute-start.3 = (bf16[1,64,1024]{2,1,0:T(8,128)(2,1)S(1)}, bf16[1,64,1024]{2,1,0:T(8,128)(2,1)S(1)}, u32[]{:S(2)}, u32[]{:S(2)}) collective-permute-start(bf16[1,64,1024]{2,1,0:T(8,128)(2,1)S(1)} %collective-permute-done.refs_5_), channel_id=1, source_target_pairs={{0,12},{4,8},{8,4},{12,0},{1,13},{5,9},{9,5},{13,1},{2,14},{6,10},... | collective-permute-start | bytes 393224 | tf_op jit(solution)/shard_map/ppermute | solution.py:379
  21.7 13.4 %collective-permute-start.2 = (bf16[1,64,1024]{2,1,0:T(8,128)(2,1)S(1)}, bf16[1,64,1024]{2,1,0:T(8,128)(2,1)S(1)}, u32[]{:S(2)}, u32[]{:S(2)}) collective-permute-start(bf16[1,64,1024]{2,1,0:T(8,128)(2,1)S(1)} %collective-permute-done.refs_5_), channel_id=1, source_target_pairs={{0,8},{4,12},{8,0},{12,4},{1,9},{5,13},{9,1},{13,5},{2,10},{6,14},... | collective-permute-start | bytes 393224 | tf_op jit(solution)/shard_map/ppermute | solution.py:379
  26.0 11.4 %collective-permute-start.1 = (bf16[1,64,1024]{2,1,0:T(8,128)(2,1)S(1)}, bf16[1,64,1024]{2,1,0:T(8,128)(2,1)S(1)}, u32[]{:S(2)}, u32[]{:S(2)}) collective-permute-start(bf16[1,64,1024]{2,1,0:T(8,128)(2,1)S(1)} %collective-permute-done.refs_5_), channel_id=1, source_target_pairs={{0,4},{4,0},{8,12},{12,8},{1,5},{5,1},{9,13},{13,9},{2,6},{6,2},{1... | collective-permute-start | bytes 393224 | tf_op jit(solution)/shard_map/ppermute | solution.py:379
  37.5 3.9 %copy-start = (bf16[128,1152]{1,0:T(8,128)(2,1)S(1)}, bf16[128,1152]{1,0:T(8,128)(2,1)}, u32[]{:S(2)}) copy-start(bf16[128,1152]{1,0:T(8,128)(2,1)} %get-tuple-element.43.refs_0_) | copy-start | bytes 884740
  37.5 18.0 %all-to-all-start.1 = ((bf16[8,64,512]{2,1,0:T(8,128)(2,1)}), bf16[8,64,512]{2,1,0:T(8,128)(2,1)S(1)}, u32[]{:S(2)}, u32[]{:S(2)}) async-start(bf16[8,64,512]{2,1,0:T(8,128)(2,1)} %get-tuple-element.52), calls=%async_computation.1 | async-start | bytes 1048576 | tf_op jit(solution)/shard_map/all_to_all | solution.py:388
  43.5 1.4 %collective-permute-start.7 = (f32[256,128]{1,0:T(8,128)S(1)}, f32[256,128]{1,0:T(8,128)S(1)}, u32[]{:S(2)}, u32[]{:S(2)}) collective-permute-start(f32[256,128]{1,0:T(8,128)S(1)} %shard_map.111), channel_id=1, source_target_pairs={{0,1},{1,0},{2,3},{3,2},{4,5},{5,4},{6,7},{7,6},{8,9},{9,8},{10,11... | collective-permute-start | bytes 393224 | tf_op jit(solution)/shard_map/ppermute | solution.py:393
  44.9 7.3 %collective-permute-start.10 = (bf16[256,128]{1,0:T(8,128)(2,1)S(1)}, bf16[256,128]{1,0:T(8,128)(2,1)S(1)}, u32[]{:S(2)}, u32[]{:S(2)}) collective-permute-start(bf16[256,128]{1,0:T(8,128)(2,1)S(1)} %add_convert_fusion.refs_4_), channel_id=1, source_target_pairs={{0,18},{2,16},{16,2},{18,0},{1,19},{3,17},{17,3},{19,1},{4,22},{6,... | collective-permute-start | bytes 196616 | tf_op jit(solution)/shard_map/ppermute | solution.py:349
  48.1 4.6 %collective-permute-start.9 = (bf16[256,128]{1,0:T(8,128)(2,1)S(1)}, bf16[256,128]{1,0:T(8,128)(2,1)S(1)}, u32[]{:S(2)}, u32[]{:S(2)}) collective-permute-start(bf16[256,128]{1,0:T(8,128)(2,1)S(1)} %add_convert_fusion.refs_4_), channel_id=1, source_target_pairs={{0,16},{2,18},{16,0},{18,2},{1,17},{3,19},{17,1},{19,3},{4,20},{6,... | collective-permute-start | bytes 196616 | tf_op jit(solution)/shard_map/ppermute | solution.py:349
  48.5 4.3 %collective-permute-start.8 = (bf16[256,128]{1,0:T(8,128)(2,1)S(1)}, bf16[256,128]{1,0:T(8,128)(2,1)S(1)}, u32[]{:S(2)}, u32[]{:S(2)}) collective-permute-start(bf16[256,128]{1,0:T(8,128)(2,1)S(1)} %add_convert_fusion.refs_4_), channel_id=1, source_target_pairs={{0,2},{2,0},{16,18},{18,16},{1,3},{3,1},{17,19},{19,17},{4,6},{6,4... | collective-permute-start | bytes 196616 | tf_op jit(solution)/shard_map/ppermute | solution.py:349
  56.6 0.7 copy-start.1
  57.2 6.1 %collective-permute-start.13 = (bf16[128,512]{1,0:T(8,128)(2,1)S(1)}, bf16[128,512]{1,0:T(8,128)(2,1)S(1)}, u32[]{:S(2)}, u32[]{:S(2)}) collective-permute-start(bf16[128,512]{1,0:T(8,128)(2,1)S(1)} %get-tuple-element.56), channel_id=1, source_target_pairs={{0,2},{2,0},{16,18},{18,16},{1,3},{3,1},{17,19},{19,17},{4,6},{6,4... | collective-permute-start | bytes 393224 | tf_op jit(solution)/shard_map/ppermute | solution.py:349
  58.6 8.5 %collective-permute-start.11 = (bf16[128,512]{1,0:T(8,128)(2,1)S(1)}, bf16[128,512]{1,0:T(8,128)(2,1)S(1)}, u32[]{:S(2)}, u32[]{:S(2)}) collective-permute-start(bf16[128,512]{1,0:T(8,128)(2,1)S(1)} %get-tuple-element.53), channel_id=1, source_target_pairs={{0,16},{2,18},{16,0},{18,2},{1,17},{3,19},{17,1},{19,3},{4,20},{6,... | collective-permute-start | bytes 393224 | tf_op jit(solution)/shard_map/ppermute | solution.py:349
  60.1 7.0 %collective-permute-start.12 = (bf16[128,512]{1,0:T(8,128)(2,1)S(1)}, bf16[128,512]{1,0:T(8,128)(2,1)S(1)}, u32[]{:S(2)}, u32[]{:S(2)}) collective-permute-start(bf16[128,512]{1,0:T(8,128)(2,1)S(1)} %get-tuple-element.54), channel_id=1, source_target_pairs={{0,18},{2,16},{16,2},{18,0},{1,19},{3,17},{17,3},{19,1},{4,22},{6,... | collective-permute-start | bytes 393224 | tf_op jit(solution)/shard_map/ppermute | solution.py:349
  63.3 0.6 copy-start.4
  67.1 0.7 copy-start.2
  67.8 0.6 copy-start.3

commit v15 on v12

--- a/solution.py
+++ b/solution.py
@@ -13,7 +13,7 @@
 LANES = 128
 STEP = 16
 HALF = 8
-BATCH = 2
+BATCH = 4
 DEAD = -1e30
 VMEM = pl.BlockSpec(memory_space=pltpu.VMEM)
 SMEM = pl.BlockSpec(memory_space=pltpu.SMEM)
@@ -264,11 +264,14 @@
     )(me, lengths, base, new_key, new_value, cache_keys, cache_values, *deltas, *earlier)
 
 
+def length_table(lengths, heads):
+    lengths = lengths.reshape(-1, STEP // HALF, 1, HALF)
+    lengths = jnp.broadcast_to(lengths, lengths.shape[:2] + (heads, HALF))
+    return lengths.reshape(-1, heads * STEP)
+
+
 def attend(me, base, new_key, new_value, cache_keys, cache_values, lengths, deltas):
     groups = new_key.shape[1] // HEAD
-    heads = base.shape[1] // groups // HEAD
-    lengths = lengths.reshape(-1, STEP // HALF, 1, HALF)
-    lengths = jnp.broadcast_to(lengths, lengths.shape[:2] + (heads, HALF)).reshape(-1, heads * STEP)
     parts = len(deltas) // groups
     out = None
     for first in range(0, len(deltas), parts):
@@ -366,7 +369,8 @@
         out_specs=[VMEM] * square,
         scratch_shapes=[pltpu.SemaphoreType.DMA((square,))],
     )(me[None], owner_map, adapter_ids.T, hidden)
-    *rows, other = lax.optimization_barrier((*rows, other))
+    table = length_table(lengths, outputs * square // new_key.shape[1])
+    *rows, other, table = lax.optimization_barrier((*rows, other, table))
     rows = [rows[0]] + [swap(rows[s], s) for s in range(1, square)]
     other, expand_next = other[:, :, :features], other[:, :, features:]
     order = jnp.arange(levels, dtype=jnp.int32)
@@ -393,7 +397,7 @@
     deltas = expand_rows(expand_ids, rows, lows, [expand])
     deltas = [deltas[0]] + [swap(deltas[s], s) for s in range(1, square)]
     return attend(
-        me[None], query_base, new_key, new_value, cache_keys, cache_values, lengths, deltas
+        me[None], query_base, new_key, new_value, cache_keys, cache_values, table, deltas
     )
 
 

time: 65.9 us -> 63.7 us (0.967)
  Pallas kernels: 17.4 us -> 14.6 us
    pallas_call x2, Pallas kernels: 9.11 us -> 6.35 us  [attend_half(): pl.pallas_call(functools.partial(attend_kernel, first, parts), out_shape=...]
  transfers between devices with their start and end apart: 16 -> 16, of which waited for: 9 -> 9; matrix products, arithmetic and copies ran while one was open for 3% -> 3% of each run, Pallas kernels for 15% -> 13%
where the time goes in v15:
time: 63.7 us; the launch traced here: 63.3 us
  starting transfers between devices  28.5 us (45%)
  waiting for transfers between devices  15.5 us (24%)
  Pallas kernels  14.6 us (23%)
  local copies, waits for them, and re-layouts  4.28 us (7%)
    ppermute x10, waiting for transfers between devices, swap(): return lax.ppermute(a, ('rep', 'side'), pairs)  13.1 us
    ppermute x10, starting transfers between devices, swap(): return lax.ppermute(a, ('rep', 'side'), pairs)  12 us
    all_to_all x2, starting transfers between devices, to_levels(): return lax.all_to_all(a, 'level', split_axis=0, concat_axis=0, tiled=True)  11.1 us
    pallas_call x2, Pallas kernels, attend_half(): pl.pallas_call(functools.partial(attend_kernel, first, parts), out_shape=...  6.35 us
    ppermute x3, starting transfers between devices, per_device(): lax.ppermute(other, 'level', pairs[k])  5.35 us
    pallas_call x1, Pallas kernels, per_device(): pl.pallas_call(functools.partial(row_kernel, square), out_shape=[jax.Shap...  2.91 us
    unnamed x16, local copies, waits for them, and re-layouts  2.57 us
    pallas_call x1, Pallas kernels, per_device(): pl.pallas_call(functools.partial(factor_kernel, square), out_shape=[jax.S...  2.14 us
  transfers between devices with their start and end apart: 16, of which 9 were waited for; matrix products, arithmetic and copies ran while one was open for 3% of the time, Pallas kernels for 13%

profile of v15, /device:TPU:0, one launch (start us, length us, event | category | flops | bytes accessed | tf_op | source)
XLA Modules:
  0.0 63.3 jit_solution(10376254985079288894)
XLA Ops:
  0.0 2.1 %shard_map.110 = (bf16[4,64,1024]{2,1,0:T(8,128)(2,1)}, bf16[1,64,512]{2,1,0:T(8,128)(2,1)}, bf16[1,64,1536]{2,1,0:T(8,128)(2,1)}) custom-call(s32[1]{0:T(128)} %bitcast.me_ref, bf16[1,64,4096]{2,1,0:T(8,128)(2,1)} %bitcast.13, bf16[1,64,2048]{2,1,0:T(8,128)(2,1)} %expand_ref.1), custom_call_target="tpu_custom_call" | custom-call | tf_op jit(solution)/shard_map/pallas_call | solution.py:352
  2.2 6.5 %all-to-all-start = ((bf16[4,64,1024]{2,1,0:T(8,128)(2,1)}), bf16[4,64,1024]{2,1,0:T(8,128)(2,1)S(1)}, u32[]{:S(2)}, u32[]{:S(2)}) async-start(bf16[4,64,1024]{2,1,0:T(8,128)(2,1)} %get-tuple-element.43), calls=%async_computation | async-start | bytes 1048576 | tf_op jit(solution)/shard_map/all_to_all | solution.py:361
  8.6 1.5 %collective-permute-start = (bf16[1,64,1536]{2,1,0:T(8,128)(2,1)S(1)}, bf16[1,64,1536]{2,1,0:T(8,128)(2,1)S(1)}, u32[]{:S(2)}, u32[]{:S(2)}) collective-permute-start(bf16[1,64,1536]{2,1,0:T(8,128)(2,1)S(1)} %copy-done.7), channel_id=1, source_target_pairs={{0,2},{2,0},{16,18},{18,16},{1,3},{3,1},{17,19},{19,17},{4,6},{6,4... | collective-permute-start | bytes 589832 | tf_op jit(solution)/shard_map/ppermute | solution.py:349
  10.9 2.9 %shard_map.109 = (bf16[128,1152]{1,0:T(8,128)(2,1)}, bf16[128,1152]{1,0:T(8,128)(2,1)}, bf16[128,1152]{1,0:T(8,128)(2,1)}, bf16[128,1152]{1,0:T(8,128)(2,1)}) custom-call(s32[1]{0:T(128)} %bitcast.me_ref, s32[8]{0:T(128)} %map_ref.1, s32[1,128]{1,0:T(1,128)} %bitcast.14, bf16[128,4096]{1,0:T(8,128)(2,1)} %hidden_ref.1), custom_call_target="tpu_custom_call" | custom-call | tf_op jit(solution)/shard_map/pallas_call | solution.py:365
  13.8 1.2 %collective-permute-done = bf16[1,64,1536]{2,1,0:T(8,128)(2,1)S(1)} collective-permute-done((bf16[1,64,1536]{2,1,0:T(8,128)(2,1)S(1)}, bf16[1,64,1536]{2,1,0:T(8,128)(2,1)S(1)}, u32[]{:S(2)}, u32[]{:S(2)}) %collective-permute-start) | collective-permute-done | bytes 196640 | tf_op jit(solution)/shard_map/ppermute | solution.py:349
  15.0 1.5 %collective-permute-start.1 = (bf16[128,1152]{1,0:T(8,128)(2,1)}, bf16[128,1152]{1,0:T(8,128)(2,1)S(1)}, u32[]{:S(2)}, u32[]{:S(2)}) collective-permute-start(bf16[128,1152]{1,0:T(8,128)(2,1)} %get-tuple-element.36), channel_id=1, source_target_pairs={{0,2},{2,0},{16,18},{18,16},{1,3},{3,1},{17,19},{19,17},{4,6},{6,4... | collective-permute-start | bytes 884744 | tf_op jit(solution)/shard_map/ppermute | solution.py:349
  16.5 1.5 %collective-permute-start.2 = (bf16[128,1152]{1,0:T(8,128)(2,1)}, bf16[128,1152]{1,0:T(8,128)(2,1)S(1)}, u32[]{:S(2)}, u32[]{:S(2)}) collective-permute-start(bf16[128,1152]{1,0:T(8,128)(2,1)} %get-tuple-element.37), channel_id=1, source_target_pairs={{0,16},{2,18},{16,0},{18,2},{1,17},{3,19},{17,1},{19,3},{4,20},{6,... | collective-permute-start | bytes 884744 | tf_op jit(solution)/shard_map/ppermute | solution.py:349
  18.5 3.6 %collective-permute-start.6 = (bf16[1,64,1024]{2,1,0:T(8,128)(2,1)S(1)}, bf16[1,64,1024]{2,1,0:T(8,128)(2,1)S(1)}, u32[]{:S(2)}, u32[]{:S(2)}) collective-permute-start(bf16[1,64,1024]{2,1,0:T(8,128)(2,1)S(1)} %slice.7.refs_5_), channel_id=1, source_target_pairs={{0,12},{4,8},{8,4},{12,0},{1,13},{5,9},{9,5},{13,1},{2,14},{6,10},... | collective-permute-start | bytes 393224 | tf_op jit(solution)/shard_map/ppermute | solution.py:379
  22.1 3.0 %collective-permute-done.1.refs_1_ = bf16[128,1152]{1,0:T(8,128)(2,1)S(1)} collective-permute-done((bf16[128,1152]{1,0:T(8,128)(2,1)}, bf16[128,1152]{1,0:T(8,128)(2,1)S(1)}, u32[]{:S(2)}, u32[]{:S(2)}) %collective-permute-start.1) | collective-permute-done | bytes 294944 | tf_op jit(solution)/shard_map/ppermute | solution.py:349
  25.1 1.7 %collective-permute-start.4 = (bf16[1,64,1024]{2,1,0:T(8,128)(2,1)S(1)}, bf16[1,64,1024]{2,1,0:T(8,128)(2,1)S(1)}, u32[]{:S(2)}, u32[]{:S(2)}) collective-permute-start(bf16[1,64,1024]{2,1,0:T(8,128)(2,1)S(1)} %slice.7.refs_5_), channel_id=1, source_target_pairs={{0,4},{4,0},{8,12},{12,8},{1,5},{5,1},{9,13},{13,9},{2,6},{6,2},{1... | collective-permute-start | bytes 393224 | tf_op jit(solution)/shard_map/ppermute | solution.py:379
  26.9 3.4 %collective-permute-done.2.refs_2_ = bf16[128,1152]{1,0:T(8,128)(2,1)S(1)} collective-permute-done((bf16[128,1152]{1,0:T(8,128)(2,1)}, bf16[128,1152]{1,0:T(8,128)(2,1)S(1)}, u32[]{:S(2)}, u32[]{:S(2)}) %collective-permute-start.2) | collective-permute-done | bytes 294944 | tf_op jit(solution)/shard_map/ppermute | solution.py:349
  31.1 4.6 %all-to-all-start.1 = ((bf16[4,128,512]{2,1,0:T(8,128)(2,1)}), bf16[4,128,512]{2,1,0:T(8,128)(2,1)S(1)}, u32[]{:S(2)}, u32[]{:S(2)}) async-start(bf16[4,128,512]{2,1,0:T(8,128)(2,1)} %broadcast_in_dim.25), calls=%async_computation.1 | async-start | bytes 1048576 | tf_op jit(solution)/shard_map/all_to_all | solution.py:361
  35.9 2.1 %shard_map.111 = f32[256,128]{1,0:T(8,128)S(1)} custom-call(s32[8]{0:T(128)S(1)} %add_bitcast_fusion.ids_ref, bf16[128,1152]{1,0:T(8,128)(2,1)S(1)} %copy-done, bf16[128,1152]{1,0:T(8,128)(2,1)S(1)} %collective-permute-done.1.refs_1_, bf16[128,1152]{1,0:T(8,128)(2,1)S(1)} %collective-permute-done.2.refs_2_, ...), custom_call_target="tpu_custom_call" | custom-call | tf_op jit(solution)/shard_map/pallas_call | solution.py:299
  38.1 1.2 %collective-permute-done.7 = f32[256,128]{1,0:T(8,128)S(1)} collective-permute-done((f32[256,128]{1,0:T(8,128)S(1)}, f32[256,128]{1,0:T(8,128)S(1)}, u32[]{:S(2)}, u32[]{:S(2)}) %collective-permute-start.7) | collective-permute-done | bytes 131104 | tf_op jit(solution)/shard_map/ppermute | solution.py:394
  39.4 1.6 %collective-permute-start.10 = (bf16[256,128]{1,0:T(8,128)(2,1)S(1)}, bf16[256,128]{1,0:T(8,128)(2,1)S(1)}, u32[]{:S(2)}, u32[]{:S(2)}) collective-permute-start(bf16[256,128]{1,0:T(8,128)(2,1)S(1)} %add_convert_fusion.refs_4_), channel_id=1, source_target_pairs={{0,18},{2,16},{16,2},{18,0},{1,19},{3,17},{17,3},{19,1},{4,22},{6,... | collective-permute-start | bytes 196616 | tf_op jit(solution)/shard_map/ppermute | solution.py:349
  40.9 1.2 %collective-permute-start.9 = (bf16[256,128]{1,0:T(8,128)(2,1)S(1)}, bf16[256,128]{1,0:T(8,128)(2,1)S(1)}, u32[]{:S(2)}, u32[]{:S(2)}) collective-permute-start(bf16[256,128]{1,0:T(8,128)(2,1)S(1)} %add_convert_fusion.refs_4_), channel_id=1, source_target_pairs={{0,16},{2,18},{16,0},{18,2},{1,17},{3,19},{17,1},{19,3},{4,20},{6,... | collective-permute-start | bytes 196616 | tf_op jit(solution)/shard_map/ppermute | solution.py:349
  43.1 1.6 %collective-permute-done.10.refs_7_ = bf16[256,128]{1,0:T(8,128)(2,1)S(1)} collective-permute-done((bf16[256,128]{1,0:T(8,128)(2,1)S(1)}, bf16[256,128]{1,0:T(8,128)(2,1)S(1)}, u32[]{:S(2)}, u32[]{:S(2)}) %collective-permute-start.10) | collective-permute-done | bytes 65568 | tf_op jit(solution)/shard_map/ppermute | solution.py:349
  44.7 1.2 %collective-permute-done.9.refs_6_ = bf16[256,128]{1,0:T(8,128)(2,1)S(1)} collective-permute-done((bf16[256,128]{1,0:T(8,128)(2,1)S(1)}, bf16[256,128]{1,0:T(8,128)(2,1)S(1)}, u32[]{:S(2)}, u32[]{:S(2)}) %collective-permute-start.9) | collective-permute-done | bytes 65568 | tf_op jit(solution)/shard_map/ppermute | solution.py:349
  46.4 1.2 %all-to-all-done.1 = bf16[4,128,512]{2,1,0:T(8,128)(2,1)S(1)} async-done(((bf16[4,128,512]{2,1,0:T(8,128)(2,1)}), bf16[4,128,512]{2,1,0:T(8,128)(2,1)S(1)}, u32[]{:S(2)}, u32[]{:S(2)}) %all-to-all-start.1) | async-done | bytes 524320 | tf_op jit(solution)/shard_map/all_to_all | solution.py:361
  49.4 1.5 %collective-permute-start.13 = (bf16[128,512]{1,0:T(8,128)(2,1)S(1)}, bf16[128,512]{1,0:T(8,128)(2,1)S(1)}, u32[]{:S(2)}, u32[]{:S(2)}) collective-permute-start(bf16[128,512]{1,0:T(8,128)(2,1)S(1)} %get-tuple-element.48), channel_id=1, source_target_pairs={{0,2},{2,0},{16,18},{18,16},{1,3},{3,1},{17,19},{19,17},{4,6},{6,4... | collective-permute-start | bytes 393224 | tf_op jit(solution)/shard_map/ppermute | solution.py:349
  51.4 1.5 %collective-permute-start.12 = (bf16[128,512]{1,0:T(8,128)(2,1)S(1)}, bf16[128,512]{1,0:T(8,128)(2,1)S(1)}, u32[]{:S(2)}, u32[]{:S(2)}) collective-permute-start(bf16[128,512]{1,0:T(8,128)(2,1)S(1)} %get-tuple-element.46), channel_id=1, source_target_pairs={{0,18},{2,16},{16,2},{18,0},{1,19},{3,17},{17,3},{19,1},{4,22},{6,... | collective-permute-start | bytes 393224 | tf_op jit(solution)/shard_map/ppermute | solution.py:349
  52.8 2.2 %collective-permute-done.13.refs_1_ = bf16[128,512]{1,0:T(8,128)(2,1)S(1)} collective-permute-done((bf16[128,512]{1,0:T(8,128)(2,1)S(1)}, bf16[128,512]{1,0:T(8,128)(2,1)S(1)}, u32[]{:S(2)}, u32[]{:S(2)}) %collective-permute-start.13) | collective-permute-done | bytes 131104 | tf_op jit(solution)/shard_map/ppermute | solution.py:349
  55.7 3.2 %shard_map.113.refs_2_ = bf16[128,2048]{1,0:T(8,128)(2,1)} custom-call(s32[1]{0:T(128)} %bitcast.me_ref, s32[8,128]{1,0:T(8,128)} %reshape.46.len_ref, bf16[128,2048]{1,0:T(8,128)(2,1)} %base_ref.3, bf16[128,256]{1,0:T(8,128)(2,1)} %nk_ref.3, bf16[128,256]{1,0:T(8,128)(2,1)} %nv_ref.3, bf16[128,16,256]{2,1,0:T(8,128)(2,1)} %ck_ref.3, ...), custom_call_target="tpu_custom_call" | custom-call | flops 67108864 | bytes 1572864 | tf_op jit(solution)/shard_map/pallas_call | solution.py:247
  60.2 3.2 %shard_map.114 = bf16[128,2048]{1,0:T(8,128)(2,1)} custom-call(s32[1]{0:T(128)} %bitcast.me_ref, s32[8,128]{1,0:T(8,128)} %reshape.46.len_ref, bf16[128,2048]{1,0:T(8,128)(2,1)} %base_ref.3, bf16[128,256]{1,0:T(8,128)(2,1)} %nk_ref.3, bf16[128,256]{1,0:T(8,128)(2,1)} %nv_ref.3, bf16[128,16,256]{2,1,0:T(8,128)(2,1)} %ck_ref.3, ...), custom_call_target="tpu_custom_call", output_to_operand_aliasing={{}: (9, {})} | custom-call | flops 67108864 | bytes 1572864 | tf_op jit(solution)/shard_map/pallas_call | solution.py:247
  (44 shorter events, 8.0 us)
Async XLA Ops:
  2.1 6.5 %copy-start.7 = (bf16[1,64,1536]{2,1,0:T(8,128)(2,1)S(1)}, bf16[1,64,1536]{2,1,0:T(8,128)(2,1)}, u32[]{:S(2)}) copy-start(bf16[1,64,1536]{2,1,0:T(8,128)(2,1)} %get-tuple-element.31) | copy-start | bytes 589828
  2.2 29.0 %all-to-all-start = ((bf16[4,64,1024]{2,1,0:T(8,128)(2,1)}), bf16[4,64,1024]{2,1,0:T(8,128)(2,1)S(1)}, u32[]{:S(2)}, u32[]{:S(2)}) async-start(bf16[4,64,1024]{2,1,0:T(8,128)(2,1)} %get-tuple-element.43), calls=%async_computation | async-start | bytes 1048576 | tf_op jit(solution)/shard_map/all_to_all | solution.py:361
  8.6 1.5 %copy-start.6 = (s32[128]{0:T(128)S(1)}, s32[128]{0:T(128)}, u32[]{:S(2)}) copy-start(s32[128]{0:T(128)} %param.21) | copy-start | bytes 1540
  8.6 6.4 %collective-permute-start = (bf16[1,64,1536]{2,1,0:T(8,128)(2,1)S(1)}, bf16[1,64,1536]{2,1,0:T(8,128)(2,1)S(1)}, u32[]{:S(2)}, u32[]{:S(2)}) collective-permute-start(bf16[1,64,1536]{2,1,0:T(8,128)(2,1)S(1)} %copy-done.7), channel_id=1, source_target_pairs={{0,2},{2,0},{16,18},{18,16},{1,3},{3,1},{17,19},{19,17},{4,6},{6,4... | collective-permute-start | bytes 589832 | tf_op jit(solution)/shard_map/ppermute | solution.py:349
  15.0 10.2 %collective-permute-start.1 = (bf16[128,1152]{1,0:T(8,128)(2,1)}, bf16[128,1152]{1,0:T(8,128)(2,1)S(1)}, u32[]{:S(2)}, u32[]{:S(2)}) collective-permute-start(bf16[128,1152]{1,0:T(8,128)(2,1)} %get-tuple-element.36), channel_id=1, source_target_pairs={{0,2},{2,0},{16,18},{18,16},{1,3},{3,1},{17,19},{19,17},{4,6},{6,4... | collective-permute-start | bytes 884744 | tf_op jit(solution)/shard_map/ppermute | solution.py:349
  16.5 13.8 %collective-permute-start.2 = (bf16[128,1152]{1,0:T(8,128)(2,1)}, bf16[128,1152]{1,0:T(8,128)(2,1)S(1)}, u32[]{:S(2)}, u32[]{:S(2)}) collective-permute-start(bf16[128,1152]{1,0:T(8,128)(2,1)} %get-tuple-element.37), channel_id=1, source_target_pairs={{0,16},{2,18},{16,0},{18,2},{1,17},{3,19},{17,1},{19,3},{4,20},{6,... | collective-permute-start | bytes 884744 | tf_op jit(solution)/shard_map/ppermute | solution.py:349
  18.0 12.3 %collective-permute-start.3 = (bf16[128,1152]{1,0:T(8,128)(2,1)}, bf16[128,1152]{1,0:T(8,128)(2,1)S(1)}, u32[]{:S(2)}, u32[]{:S(2)}) collective-permute-start(bf16[128,1152]{1,0:T(8,128)(2,1)} %get-tuple-element.38), channel_id=1, source_target_pairs={{0,18},{2,16},{16,2},{18,0},{1,19},{3,17},{17,3},{19,1},{4,22},{6,... | collective-permute-start | bytes 884744 | tf_op jit(solution)/shard_map/ppermute | solution.py:349
  18.5 8.4 %copy-start.5 = (bf16[1,64,512]{2,1,0:T(8,128)(2,1)S(1)}, bf16[1,64,512]{2,1,0:T(8,128)(2,1)}, u32[]{:S(2)}) copy-start(bf16[1,64,512]{2,1,0:T(8,128)(2,1)} %get-tuple-element.33) | copy-start | bytes 196612
  18.5 17.3 %collective-permute-start.6 = (bf16[1,64,1024]{2,1,0:T(8,128)(2,1)S(1)}, bf16[1,64,1024]{2,1,0:T(8,128)(2,1)S(1)}, u32[]{:S(2)}, u32[]{:S(2)}) collective-permute-start(bf16[1,64,1024]{2,1,0:T(8,128)(2,1)S(1)} %slice.7.refs_5_), channel_id=1, source_target_pairs={{0,12},{4,8},{8,4},{12,0},{1,13},{5,9},{9,5},{13,1},{2,14},{6,10},... | collective-permute-start | bytes 393224 | tf_op jit(solution)/shard_map/ppermute | solution.py:379
  22.1 13.7 %collective-permute-start.5 = (bf16[1,64,1024]{2,1,0:T(8,128)(2,1)S(1)}, bf16[1,64,1024]{2,1,0:T(8,128)(2,1)S(1)}, u32[]{:S(2)}, u32[]{:S(2)}) collective-permute-start(bf16[1,64,1024]{2,1,0:T(8,128)(2,1)S(1)} %slice.7.refs_5_), channel_id=1, source_target_pairs={{0,8},{4,12},{8,0},{12,4},{1,9},{5,13},{9,1},{13,5},{2,10},{6,14},... | collective-permute-start | bytes 393224 | tf_op jit(solution)/shard_map/ppermute | solution.py:379
  25.1 10.7 %collective-permute-start.4 = (bf16[1,64,1024]{2,1,0:T(8,128)(2,1)S(1)}, bf16[1,64,1024]{2,1,0:T(8,128)(2,1)S(1)}, u32[]{:S(2)}, u32[]{:S(2)}) collective-permute-start(bf16[1,64,1024]{2,1,0:T(8,128)(2,1)S(1)} %slice.7.refs_5_), channel_id=1, source_target_pairs={{0,4},{4,0},{8,12},{12,8},{1,5},{5,1},{9,13},{13,9},{2,6},{6,2},{1... | collective-permute-start | bytes 393224 | tf_op jit(solution)/shard_map/ppermute | solution.py:379
  31.1 4.7 %copy-start = (bf16[128,1152]{1,0:T(8,128)(2,1)S(1)}, bf16[128,1152]{1,0:T(8,128)(2,1)}, u32[]{:S(2)}) copy-start(bf16[128,1152]{1,0:T(8,128)(2,1)} %get-tuple-element.39.refs_0_) | copy-start | bytes 884740
  31.1 16.5 %all-to-all-start.1 = ((bf16[4,128,512]{2,1,0:T(8,128)(2,1)}), bf16[4,128,512]{2,1,0:T(8,128)(2,1)S(1)}, u32[]{:S(2)}, u32[]{:S(2)}) async-start(bf16[4,128,512]{2,1,0:T(8,128)(2,1)} %broadcast_in_dim.25), calls=%async_computation.1 | async-start | bytes 1048576 | tf_op jit(solution)/shard_map/all_to_all | solution.py:361
  38.0 1.4 %collective-permute-start.7 = (f32[256,128]{1,0:T(8,128)S(1)}, f32[256,128]{1,0:T(8,128)S(1)}, u32[]{:S(2)}, u32[]{:S(2)}) collective-permute-start(f32[256,128]{1,0:T(8,128)S(1)} %shard_map.111), channel_id=1, source_target_pairs={{0,1},{1,0},{2,3},{3,2},{4,5},{5,4},{6,7},{7,6},{8,9},{9,8},{10,11... | collective-permute-start | bytes 393224 | tf_op jit(solution)/shard_map/ppermute | solution.py:394
  39.4 5.3 %collective-permute-start.10 = (bf16[256,128]{1,0:T(8,128)(2,1)S(1)}, bf16[256,128]{1,0:T(8,128)(2,1)S(1)}, u32[]{:S(2)}, u32[]{:S(2)}) collective-permute-start(bf16[256,128]{1,0:T(8,128)(2,1)S(1)} %add_convert_fusion.refs_4_), channel_id=1, source_target_pairs={{0,18},{2,16},{16,2},{18,0},{1,19},{3,17},{17,3},{19,1},{4,22},{6,... | collective-permute-start | bytes 196616 | tf_op jit(solution)/shard_map/ppermute | solution.py:349
  40.9 5.0 %collective-permute-start.9 = (bf16[256,128]{1,0:T(8,128)(2,1)S(1)}, bf16[256,128]{1,0:T(8,128)(2,1)S(1)}, u32[]{:S(2)}, u32[]{:S(2)}) collective-permute-start(bf16[256,128]{1,0:T(8,128)(2,1)S(1)} %add_convert_fusion.refs_4_), channel_id=1, source_target_pairs={{0,16},{2,18},{16,0},{18,2},{1,17},{3,19},{17,1},{19,3},{4,20},{6,... | collective-permute-start | bytes 196616 | tf_op jit(solution)/shard_map/ppermute | solution.py:349
  42.2 4.3 %collective-permute-start.8 = (bf16[256,128]{1,0:T(8,128)(2,1)S(1)}, bf16[256,128]{1,0:T(8,128)(2,1)S(1)}, u32[]{:S(2)}, u32[]{:S(2)}) collective-permute-start(bf16[256,128]{1,0:T(8,128)(2,1)S(1)} %add_convert_fusion.refs_4_), channel_id=1, source_target_pairs={{0,2},{2,0},{16,18},{18,16},{1,3},{3,1},{17,19},{19,17},{4,6},{6,4... | collective-permute-start | bytes 196616 | tf_op jit(solution)/shard_map/ppermute | solution.py:349
  48.7 0.7 %copy-start.1 = (bf16[128,512]{1,0:T(8,128)(2,1)}, bf16[128,512]{1,0:T(8,128)(2,1)S(1)}, u32[]{:S(2)}) copy-start(bf16[128,512]{1,0:T(8,128)(2,1)S(1)} %get-tuple-element.47.refs_0_) | copy-start | bytes 393220
  49.4 5.7 %collective-permute-start.13 = (bf16[128,512]{1,0:T(8,128)(2,1)S(1)}, bf16[128,512]{1,0:T(8,128)(2,1)S(1)}, u32[]{:S(2)}, u32[]{:S(2)}) collective-permute-start(bf16[128,512]{1,0:T(8,128)(2,1)S(1)} %get-tuple-element.48), channel_id=1, source_target_pairs={{0,2},{2,0},{16,18},{18,16},{1,3},{3,1},{17,19},{19,17},{4,6},{6,4... | collective-permute-start | bytes 393224 | tf_op jit(solution)/shard_map/ppermute | solution.py:349
  50.8 8.0 %collective-permute-start.11 = (bf16[128,512]{1,0:T(8,128)(2,1)S(1)}, bf16[128,512]{1,0:T(8,128)(2,1)S(1)}, u32[]{:S(2)}, u32[]{:S(2)}) collective-permute-start(bf16[128,512]{1,0:T(8,128)(2,1)S(1)} %get-tuple-element.45), channel_id=1, source_target_pairs={{0,16},{2,18},{16,0},{18,2},{1,17},{3,19},{17,1},{19,3},{4,20},{6,... | collective-permute-start | bytes 393224 | tf_op jit(solution)/shard_map/ppermute | solution.py:349
  51.4 7.5 %collective-permute-start.12 = (bf16[128,512]{1,0:T(8,128)(2,1)S(1)}, bf16[128,512]{1,0:T(8,128)(2,1)S(1)}, u32[]{:S(2)}, u32[]{:S(2)}) collective-permute-start(bf16[128,512]{1,0:T(8,128)(2,1)S(1)} %get-tuple-element.46), channel_id=1, source_target_pairs={{0,18},{2,16},{16,2},{18,0},{1,19},{3,17},{17,3},{19,1},{4,22},{6,... | collective-permute-start | bytes 393224 | tf_op jit(solution)/shard_map/ppermute | solution.py:349
  55.1 0.6 %copy-start.4 = (bf16[128,512]{1,0:T(8,128)(2,1)}, bf16[128,512]{1,0:T(8,128)(2,1)S(1)}, u32[]{:S(2)}) copy-start(bf16[128,512]{1,0:T(8,128)(2,1)S(1)} %collective-permute-done.13.refs_1_) | copy-start | bytes 393220
  58.9 0.7 %copy-start.2 = (bf16[128,512]{1,0:T(8,128)(2,1)}, bf16[128,512]{1,0:T(8,128)(2,1)S(1)}, u32[]{:S(2)}) copy-start(bf16[128,512]{1,0:T(8,128)(2,1)S(1)} %collective-permute-done.11.refs_0_) | copy-start | bytes 393220
  59.5 0.6 %copy-start.3 = (bf16[128,512]{1,0:T(8,128)(2,1)}, bf16[128,512]{1,0:T(8,128)(2,1)S(1)}, u32[]{:S(2)}) copy-start(bf16[128,512]{1,0:T(8,128)(2,1)S(1)} %collective-permute-done.12.refs_1_) | copy-start | bytes 393220

commit v16 on v15

--- a/solution.py
+++ b/solution.py
@@ -373,6 +373,9 @@
     *rows, other, table = lax.optimization_barrier((*rows, other, table))
     rows = [rows[0]] + [swap(rows[s], s) for s in range(1, square)]
     other, expand_next = other[:, :, :features], other[:, :, features:]
+    expand = jnp.concatenate([expand_own, expand_next], axis=1)
+    expand = jnp.broadcast_to(expand, (levels,) + expand.shape[1:])
+    other, expand = lax.optimization_barrier((other, expand))
     order = jnp.arange(levels, dtype=jnp.int32)
     if levels == 4:
         pairs = [[(i, i ^ k) for i in range(levels)] for k in range(levels)]
@@ -383,8 +386,6 @@
         other_at = order
     ids = [a.reshape(-1, 4) for a in (order * sides + side, other_at * sides + (side ^ 1))]
     ids = jnp.concatenate(ids, axis=1).reshape(-1)
-    expand = jnp.concatenate([expand_own, expand_next], axis=1)
-    expand = jnp.broadcast_to(expand, (levels,) + expand.shape[1:])
     expand, *rows = lax.optimization_barrier((expand, *rows))
     expand = to_levels(expand).reshape(levels * sides, rank, outputs)
     expand_ids = (order[:, None] * sides + jnp.stack([side, side ^ 1])[None, :]).reshape(-1)

time: 63.7 us -> 62.8 us (0.986)
  waiting for transfers between devices: 15.5 us -> 13.9 us
  local copies, waits for them, and re-layouts: 4.28 us -> 5.13 us
    ppermute x10, waiting for transfers between devices: 13.1 us -> 11.5 us  [swap(): return lax.ppermute(a, ('rep', 'side'), pairs)]
    unnamed x16, local copies, waits for them, and re-layouts: 2.57 us -> 3.4 us
where the time goes in v16:
time: 62.8 us; the launch traced here: 62.4 us
  starting transfers between devices  28.3 us (45%)
  Pallas kernels  14.6 us (23%)
  waiting for transfers between devices  13.9 us (22%)
  local copies, waits for them, and re-layouts  5.13 us (8%)
    ppermute x10, starting transfers between devices, swap(): return lax.ppermute(a, ('rep', 'side'), pairs)  12 us
    ppermute x10, waiting for transfers between devices, swap(): return lax.ppermute(a, ('rep', 'side'), pairs)  11.5 us
    all_to_all x2, starting transfers between devices, to_levels(): return lax.all_to_all(a, 'level', split_axis=0, concat_axis=0, tiled=True)  11 us
    pallas_call x2, Pallas kernels, attend_half(): pl.pallas_call(functools.partial(attend_kernel, first, parts), out_shape=...  6.36 us
    ppermute x3, starting transfers between devices, per_device(): lax.ppermute(other, 'level', pairs[k])  5.29 us
    unnamed x16, local copies, waits for them, and re-layouts  3.4 us
    pallas_call x1, Pallas kernels, per_device(): pl.pallas_call(functools.partial(row_kernel, square), out_shape=[jax.Shap...  2.94 us
    pallas_call x1, Pallas kernels, per_device(): pl.pallas_call(functools.partial(factor_kernel, square), out_shape=[jax.S...  2.15 us
  transfers between devices with their start and end apart: 16, of which 9 were waited for; matrix products, arithmetic and copies ran while one was open for 3% of the time, Pallas kernels for 13%

profile of v16, /device:TPU:0, one launch (start us, length us, event | category | flops | bytes accessed | tf_op | source)
XLA Modules:
  0.0 62.4 jit_solution(4761979296398038002)
XLA Ops:
  0.0 2.1 %shard_map.110 = (bf16[4,64,1024]{2,1,0:T(8,128)(2,1)}, bf16[1,64,512]{2,1,0:T(8,128)(2,1)}, bf16[1,64,1536]{2,1,0:T(8,128)(2,1)}) custom-call(s32[1]{0:T(128)} %bitcast.me_ref, bf16[1,64,4096]{2,1,0:T(8,128)(2,1)} %bitcast.13, bf16[1,64,2048]{2,1,0:T(8,128)(2,1)} %expand_ref.1), custom_call_target="tpu_custom_call" | custom-call | tf_op jit(solution)/shard_map/pallas_call | solution.py:352
  2.2 6.5 %all-to-all-start = ((bf16[4,64,1024]{2,1,0:T(8,128)(2,1)}), bf16[4,64,1024]{2,1,0:T(8,128)(2,1)S(1)}, u32[]{:S(2)}, u32[]{:S(2)}) async-start(bf16[4,64,1024]{2,1,0:T(8,128)(2,1)} %get-tuple-element.46), calls=%async_computation | async-start | bytes 1048576 | tf_op jit(solution)/shard_map/all_to_all | solution.py:361
  8.6 1.5 %collective-permute-start = (bf16[1,64,1536]{2,1,0:T(8,128)(2,1)S(1)}, bf16[1,64,1536]{2,1,0:T(8,128)(2,1)S(1)}, u32[]{:S(2)}, u32[]{:S(2)}) collective-permute-start(bf16[1,64,1536]{2,1,0:T(8,128)(2,1)S(1)} %copy-done.7), channel_id=1, source_target_pairs={{0,2},{2,0},{16,18},{18,16},{1,3},{3,1},{17,19},{19,17},{4,6},{6,4... | collective-permute-start | bytes 589832 | tf_op jit(solution)/shard_map/ppermute | solution.py:349
  10.9 2.9 %shard_map.109 = (bf16[128,1152]{1,0:T(8,128)(2,1)}, bf16[128,1152]{1,0:T(8,128)(2,1)}, bf16[128,1152]{1,0:T(8,128)(2,1)}, bf16[128,1152]{1,0:T(8,128)(2,1)}) custom-call(s32[1]{0:T(128)} %bitcast.me_ref, s32[8]{0:T(128)} %map_ref.1, s32[1,128]{1,0:T(1,128)} %bitcast.14, bf16[128,4096]{1,0:T(8,128)(2,1)} %hidden_ref.1), custom_call_target="tpu_custom_call" | custom-call | tf_op jit(solution)/shard_map/pallas_call | solution.py:365
  13.9 1.1 %collective-permute-done = bf16[1,64,1536]{2,1,0:T(8,128)(2,1)S(1)} collective-permute-done((bf16[1,64,1536]{2,1,0:T(8,128)(2,1)S(1)}, bf16[1,64,1536]{2,1,0:T(8,128)(2,1)S(1)}, u32[]{:S(2)}, u32[]{:S(2)}) %collective-permute-start) | collective-permute-done | bytes 196640 | tf_op jit(solution)/shard_map/ppermute | solution.py:349
  15.0 1.5 %collective-permute-start.1 = (bf16[128,1152]{1,0:T(8,128)(2,1)}, bf16[128,1152]{1,0:T(8,128)(2,1)S(1)}, u32[]{:S(2)}, u32[]{:S(2)}) collective-permute-start(bf16[128,1152]{1,0:T(8,128)(2,1)} %get-tuple-element.39), channel_id=1, source_target_pairs={{0,2},{2,0},{16,18},{18,16},{1,3},{3,1},{17,19},{19,17},{4,6},{6,4... | collective-permute-start | bytes 884744 | tf_op jit(solution)/shard_map/ppermute | solution.py:349
  16.5 1.5 %collective-permute-start.2 = (bf16[128,1152]{1,0:T(8,128)(2,1)}, bf16[128,1152]{1,0:T(8,128)(2,1)S(1)}, u32[]{:S(2)}, u32[]{:S(2)}) collective-permute-start(bf16[128,1152]{1,0:T(8,128)(2,1)} %get-tuple-element.40), channel_id=1, source_target_pairs={{0,16},{2,18},{16,0},{18,2},{1,17},{3,19},{17,1},{19,3},{4,20},{6,... | collective-permute-start | bytes 884744 | tf_op jit(solution)/shard_map/ppermute | solution.py:349
  20.2 3.5 %collective-permute-start.6 = (bf16[1,64,1024]{2,1,0:T(8,128)(2,1)S(1)}, bf16[1,64,1024]{2,1,0:T(8,128)(2,1)S(1)}, u32[]{:S(2)}, u32[]{:S(2)}) collective-permute-start(bf16[1,64,1024]{2,1,0:T(8,128)(2,1)S(1)} %slice.6.refs_5_), channel_id=1, source_target_pairs={{0,12},{4,8},{8,4},{12,0},{1,13},{5,9},{9,5},{13,1},{2,14},{6,10},... | collective-permute-start | bytes 393224 | tf_op jit(solution)/shard_map/ppermute | solution.py:382
  23.7 1.4 %collective-permute-done.1.refs_1_ = bf16[128,1152]{1,0:T(8,128)(2,1)S(1)} collective-permute-done((bf16[128,1152]{1,0:T(8,128)(2,1)}, bf16[128,1152]{1,0:T(8,128)(2,1)S(1)}, u32[]{:S(2)}, u32[]{:S(2)}) %collective-permute-start.1) | collective-permute-done | bytes 294944 | tf_op jit(solution)/shard_map/ppermute | solution.py:349
  25.2 1.7 %collective-permute-start.4 = (bf16[1,64,1024]{2,1,0:T(8,128)(2,1)S(1)}, bf16[1,64,1024]{2,1,0:T(8,128)(2,1)S(1)}, u32[]{:S(2)}, u32[]{:S(2)}) collective-permute-start(bf16[1,64,1024]{2,1,0:T(8,128)(2,1)S(1)} %slice.6.refs_5_), channel_id=1, source_target_pairs={{0,4},{4,0},{8,12},{12,8},{1,5},{5,1},{9,13},{13,9},{2,6},{6,2},{1... | collective-permute-start | bytes 393224 | tf_op jit(solution)/shard_map/ppermute | solution.py:382
  26.9 3.4 %collective-permute-done.2.refs_2_ = bf16[128,1152]{1,0:T(8,128)(2,1)S(1)} collective-permute-done((bf16[128,1152]{1,0:T(8,128)(2,1)}, bf16[128,1152]{1,0:T(8,128)(2,1)S(1)}, u32[]{:S(2)}, u32[]{:S(2)}) %collective-permute-start.2) | collective-permute-done | bytes 294944 | tf_op jit(solution)/shard_map/ppermute | solution.py:349
  30.3 4.5 %all-to-all-start.1 = ((bf16[4,128,512]{2,1,0:T(8,128)(2,1)}), bf16[4,128,512]{2,1,0:T(8,128)(2,1)S(1)}, u32[]{:S(2)}, u32[]{:S(2)}) async-start(bf16[4,128,512]{2,1,0:T(8,128)(2,1)} %broadcast_in_dim.25), calls=%async_computation.1 | async-start | bytes 1048576 | tf_op jit(solution)/shard_map/all_to_all | solution.py:361
  34.9 2.1 %shard_map.111 = f32[256,128]{1,0:T(8,128)S(1)} custom-call(s32[8]{0:T(128)S(1)} %add_bitcast_fusion.ids_ref, bf16[128,1152]{1,0:T(8,128)(2,1)S(1)} %copy-done, bf16[128,1152]{1,0:T(8,128)(2,1)S(1)} %collective-permute-done.1.refs_1_, bf16[128,1152]{1,0:T(8,128)(2,1)S(1)} %collective-permute-done.2.refs_2_, ...), custom_call_target="tpu_custom_call" | custom-call | tf_op jit(solution)/shard_map/pallas_call | solution.py:299
  37.2 1.2 %collective-permute-done.7 = f32[256,128]{1,0:T(8,128)S(1)} collective-permute-done((f32[256,128]{1,0:T(8,128)S(1)}, f32[256,128]{1,0:T(8,128)S(1)}, u32[]{:S(2)}, u32[]{:S(2)}) %collective-permute-start.7) | collective-permute-done | bytes 131104 | tf_op jit(solution)/shard_map/ppermute | solution.py:395
  38.4 2.0 %collective-permute-start.10 = (bf16[256,128]{1,0:T(8,128)(2,1)S(1)}, bf16[256,128]{1,0:T(8,128)(2,1)S(1)}, u32[]{:S(2)}, u32[]{:S(2)}) collective-permute-start(bf16[256,128]{1,0:T(8,128)(2,1)S(1)} %add_convert_fusion.refs_4_), channel_id=1, source_target_pairs={{0,18},{2,16},{16,2},{18,0},{1,19},{3,17},{17,3},{19,1},{4,22},{6,... | collective-permute-start | bytes 196616 | tf_op jit(solution)/shard_map/ppermute | solution.py:349
  42.1 1.6 %collective-permute-done.10.refs_7_ = bf16[256,128]{1,0:T(8,128)(2,1)S(1)} collective-permute-done((bf16[256,128]{1,0:T(8,128)(2,1)S(1)}, bf16[256,128]{1,0:T(8,128)(2,1)S(1)}, u32[]{:S(2)}, u32[]{:S(2)}) %collective-permute-start.10) | collective-permute-done | bytes 65568 | tf_op jit(solution)/shard_map/ppermute | solution.py:349
  43.8 1.3 %collective-permute-done.9.refs_6_ = bf16[256,128]{1,0:T(8,128)(2,1)S(1)} collective-permute-done((bf16[256,128]{1,0:T(8,128)(2,1)S(1)}, bf16[256,128]{1,0:T(8,128)(2,1)S(1)}, u32[]{:S(2)}, u32[]{:S(2)}) %collective-permute-start.9) | collective-permute-done | bytes 65568 | tf_op jit(solution)/shard_map/ppermute | solution.py:349
  45.5 1.2 %all-to-all-done.1 = bf16[4,128,512]{2,1,0:T(8,128)(2,1)S(1)} async-done(((bf16[4,128,512]{2,1,0:T(8,128)(2,1)}), bf16[4,128,512]{2,1,0:T(8,128)(2,1)S(1)}, u32[]{:S(2)}, u32[]{:S(2)}) %all-to-all-start.1) | async-done | bytes 524320 | tf_op jit(solution)/shard_map/all_to_all | solution.py:361
  46.6 1.1 %shard_map.112 = (bf16[128,512]{1,0:T(8,128)(2,1)S(1)}, bf16[128,512]{1,0:T(8,128)(2,1)S(1)}, bf16[128,512]{1,0:T(8,128)(2,1)S(1)}, bf16[128,512]{1,0:T(8,128)(2,1)S(1)}) custom-call(s32[8]{0:T(128)S(1)} %add.53.ids_ref, bf16[128,1152]{1,0:T(8,128)(2,1)S(1)} %copy-done, bf16[128,1152]{1,0:T(8,128)(2,1)S(1)} %collective-permute-done.1.refs_1_, ...), custom_call_target="tpu_custom_call" | custom-call | tf_op jit(solution)/shard_map/pallas_call | solution.py:315
  48.4 1.5 %collective-permute-start.13 = (bf16[128,512]{1,0:T(8,128)(2,1)S(1)}, bf16[128,512]{1,0:T(8,128)(2,1)S(1)}, u32[]{:S(2)}, u32[]{:S(2)}) collective-permute-start(bf16[128,512]{1,0:T(8,128)(2,1)S(1)} %get-tuple-element.52), channel_id=1, source_target_pairs={{0,2},{2,0},{16,18},{18,16},{1,3},{3,1},{17,19},{19,17},{4,6},{6,4... | collective-permute-start | bytes 393224 | tf_op jit(solution)/shard_map/ppermute | solution.py:349
  50.4 1.5 %collective-permute-start.12 = (bf16[128,512]{1,0:T(8,128)(2,1)S(1)}, bf16[128,512]{1,0:T(8,128)(2,1)S(1)}, u32[]{:S(2)}, u32[]{:S(2)}) collective-permute-start(bf16[128,512]{1,0:T(8,128)(2,1)S(1)} %get-tuple-element.50), channel_id=1, source_target_pairs={{0,18},{2,16},{16,2},{18,0},{1,19},{3,17},{17,3},{19,1},{4,22},{6,... | collective-permute-start | bytes 393224 | tf_op jit(solution)/shard_map/ppermute | solution.py:349
  51.9 2.2 %collective-permute-done.13.refs_1_ = bf16[128,512]{1,0:T(8,128)(2,1)S(1)} collective-permute-done((bf16[128,512]{1,0:T(8,128)(2,1)S(1)}, bf16[128,512]{1,0:T(8,128)(2,1)S(1)}, u32[]{:S(2)}, u32[]{:S(2)}) %collective-permute-start.13) | collective-permute-done | bytes 131104 | tf_op jit(solution)/shard_map/ppermute | solution.py:349
  54.7 3.2 %shard_map.113.refs_2_ = bf16[128,2048]{1,0:T(8,128)(2,1)} custom-call(s32[1]{0:T(128)} %bitcast.me_ref, s32[8,128]{1,0:T(8,128)} %reshape.46.len_ref, bf16[128,2048]{1,0:T(8,128)(2,1)} %base_ref.3, bf16[128,256]{1,0:T(8,128)(2,1)} %nk_ref.3, bf16[128,256]{1,0:T(8,128)(2,1)} %nv_ref.3, bf16[128,16,256]{2,1,0:T(8,128)(2,1)} %ck_ref.3, ...), custom_call_target="tpu_custom_call" | custom-call | flops 67108864 | bytes 1572864 | tf_op jit(solution)/shard_map/pallas_call | solution.py:247
  59.2 3.2 %shard_map.114 = bf16[128,2048]{1,0:T(8,128)(2,1)} custom-call(s32[1]{0:T(128)} %bitcast.me_ref, s32[8,128]{1,0:T(8,128)} %reshape.46.len_ref, bf16[128,2048]{1,0:T(8,128)(2,1)} %base_ref.3, bf16[128,256]{1,0:T(8,128)(2,1)} %nk_ref.3, bf16[128,256]{1,0:T(8,128)(2,1)} %nv_ref.3, bf16[128,16,256]{2,1,0:T(8,128)(2,1)} %ck_ref.3, ...), custom_call_target="tpu_custom_call", output_to_operand_aliasing={{}: (9, {})} | custom-call | flops 67108864 | bytes 1572864 | tf_op jit(solution)/shard_map/pallas_call | solution.py:247
  (44 shorter events, 8.4 us)
Async XLA Ops:
  2.2 6.5 %copy-start.7 = (bf16[1,64,1536]{2,1,0:T(8,128)(2,1)S(1)}, bf16[1,64,1536]{2,1,0:T(8,128)(2,1)}, u32[]{:S(2)}) copy-start(bf16[1,64,1536]{2,1,0:T(8,128)(2,1)} %get-tuple-element.33) | copy-start | bytes 589828
  2.2 28.1 %all-to-all-start = ((bf16[4,64,1024]{2,1,0:T(8,128)(2,1)}), bf16[4,64,1024]{2,1,0:T(8,128)(2,1)S(1)}, u32[]{:S(2)}, u32[]{:S(2)}) async-start(bf16[4,64,1024]{2,1,0:T(8,128)(2,1)} %get-tuple-element.46), calls=%async_computation | async-start | bytes 1048576 | tf_op jit(solution)/shard_map/all_to_all | solution.py:361
  8.6 1.5 %copy-start.6 = (s32[128]{0:T(128)S(1)}, s32[128]{0:T(128)}, u32[]{:S(2)}) copy-start(s32[128]{0:T(128)} %param.21) | copy-start | bytes 1540
  8.6 6.4 %collective-permute-start = (bf16[1,64,1536]{2,1,0:T(8,128)(2,1)S(1)}, bf16[1,64,1536]{2,1,0:T(8,128)(2,1)S(1)}, u32[]{:S(2)}, u32[]{:S(2)}) collective-permute-start(bf16[1,64,1536]{2,1,0:T(8,128)(2,1)S(1)} %copy-done.7), channel_id=1, source_target_pairs={{0,2},{2,0},{16,18},{18,16},{1,3},{3,1},{17,19},{19,17},{4,6},{6,4... | collective-permute-start | bytes 589832 | tf_op jit(solution)/shard_map/ppermute | solution.py:349
  15.0 10.2 %collective-permute-start.1 = (bf16[128,1152]{1,0:T(8,128)(2,1)}, bf16[128,1152]{1,0:T(8,128)(2,1)S(1)}, u32[]{:S(2)}, u32[]{:S(2)}) collective-permute-start(bf16[128,1152]{1,0:T(8,128)(2,1)} %get-tuple-element.39), channel_id=1, source_target_pairs={{0,2},{2,0},{16,18},{18,16},{1,3},{3,1},{17,19},{19,17},{4,6},{6,4... | collective-permute-start | bytes 884744 | tf_op jit(solution)/shard_map/ppermute | solution.py:349
  16.5 13.8 %collective-permute-start.2 = (bf16[128,1152]{1,0:T(8,128)(2,1)}, bf16[128,1152]{1,0:T(8,128)(2,1)S(1)}, u32[]{:S(2)}, u32[]{:S(2)}) collective-permute-start(bf16[128,1152]{1,0:T(8,128)(2,1)} %get-tuple-element.40), channel_id=1, source_target_pairs={{0,16},{2,18},{16,0},{18,2},{1,17},{3,19},{17,1},{19,3},{4,20},{6,... | collective-permute-start | bytes 884744 | tf_op jit(solution)/shard_map/ppermute | solution.py:349
  18.0 12.3 %collective-permute-start.3 = (bf16[128,1152]{1,0:T(8,128)(2,1)}, bf16[128,1152]{1,0:T(8,128)(2,1)S(1)}, u32[]{:S(2)}, u32[]{:S(2)}) collective-permute-start(bf16[128,1152]{1,0:T(8,128)(2,1)} %get-tuple-element.41), channel_id=1, source_target_pairs={{0,18},{2,16},{16,2},{18,0},{1,19},{3,17},{17,3},{19,1},{4,22},{6,... | collective-permute-start | bytes 884744 | tf_op jit(solution)/shard_map/ppermute | solution.py:349
  18.5 0.8 %copy-start.5 = (bf16[1,64,512]{2,1,0:T(8,128)(2,1)S(1)}, bf16[1,64,512]{2,1,0:T(8,128)(2,1)}, u32[]{:S(2)}) copy-start(bf16[1,64,512]{2,1,0:T(8,128)(2,1)} %get-tuple-element.36) | copy-start | bytes 196612
  20.2 14.7 %collective-permute-start.6 = (bf16[1,64,1024]{2,1,0:T(8,128)(2,1)S(1)}, bf16[1,64,1024]{2,1,0:T(8,128)(2,1)S(1)}, u32[]{:S(2)}, u32[]{:S(2)}) collective-permute-start(bf16[1,64,1024]{2,1,0:T(8,128)(2,1)S(1)} %slice.6.refs_5_), channel_id=1, source_target_pairs={{0,12},{4,8},{8,4},{12,0},{1,13},{5,9},{9,5},{13,1},{2,14},{6,10},... | collective-permute-start | bytes 393224 | tf_op jit(solution)/shard_map/ppermute | solution.py:382
  23.7 11.2 %collective-permute-start.5 = (bf16[1,64,1024]{2,1,0:T(8,128)(2,1)S(1)}, bf16[1,64,1024]{2,1,0:T(8,128)(2,1)S(1)}, u32[]{:S(2)}, u32[]{:S(2)}) collective-permute-start(bf16[1,64,1024]{2,1,0:T(8,128)(2,1)S(1)} %slice.6.refs_5_), channel_id=1, source_target_pairs={{0,8},{4,12},{8,0},{12,4},{1,9},{5,13},{9,1},{13,5},{2,10},{6,14},... | collective-permute-start | bytes 393224 | tf_op jit(solution)/shard_map/ppermute | solution.py:382
  25.2 9.7 %collective-permute-start.4 = (bf16[1,64,1024]{2,1,0:T(8,128)(2,1)S(1)}, bf16[1,64,1024]{2,1,0:T(8,128)(2,1)S(1)}, u32[]{:S(2)}, u32[]{:S(2)}) collective-permute-start(bf16[1,64,1024]{2,1,0:T(8,128)(2,1)S(1)} %slice.6.refs_5_), channel_id=1, source_target_pairs={{0,4},{4,0},{8,12},{12,8},{1,5},{5,1},{9,13},{13,9},{2,6},{6,2},{1... | collective-permute-start | bytes 393224 | tf_op jit(solution)/shard_map/ppermute | solution.py:382
  26.9 8.0 %copy-start = (bf16[128,1152]{1,0:T(8,128)(2,1)S(1)}, bf16[128,1152]{1,0:T(8,128)(2,1)}, u32[]{:S(2)}) copy-start(bf16[128,1152]{1,0:T(8,128)(2,1)} %get-tuple-element.42.refs_0_) | copy-start | bytes 884740
  30.3 16.3 %all-to-all-start.1 = ((bf16[4,128,512]{2,1,0:T(8,128)(2,1)}), bf16[4,128,512]{2,1,0:T(8,128)(2,1)S(1)}, u32[]{:S(2)}, u32[]{:S(2)}) async-start(bf16[4,128,512]{2,1,0:T(8,128)(2,1)} %broadcast_in_dim.25), calls=%async_computation.1 | async-start | bytes 1048576 | tf_op jit(solution)/shard_map/all_to_all | solution.py:361
  37.0 1.4 %collective-permute-start.7 = (f32[256,128]{1,0:T(8,128)S(1)}, f32[256,128]{1,0:T(8,128)S(1)}, u32[]{:S(2)}, u32[]{:S(2)}) collective-permute-start(f32[256,128]{1,0:T(8,128)S(1)} %shard_map.111), channel_id=1, source_target_pairs={{0,1},{1,0},{2,3},{3,2},{4,5},{5,4},{6,7},{7,6},{8,9},{9,8},{10,11... | collective-permute-start | bytes 393224 | tf_op jit(solution)/shard_map/ppermute | solution.py:395
  38.4 5.3 %collective-permute-start.10 = (bf16[256,128]{1,0:T(8,128)(2,1)S(1)}, bf16[256,128]{1,0:T(8,128)(2,1)S(1)}, u32[]{:S(2)}, u32[]{:S(2)}) collective-permute-start(bf16[256,128]{1,0:T(8,128)(2,1)S(1)} %add_convert_fusion.refs_4_), channel_id=1, source_target_pairs={{0,18},{2,16},{16,2},{18,0},{1,19},{3,17},{17,3},{19,1},{4,22},{6,... | collective-permute-start | bytes 196616 | tf_op jit(solution)/shard_map/ppermute | solution.py:349
  40.5 4.6 %collective-permute-start.9 = (bf16[256,128]{1,0:T(8,128)(2,1)S(1)}, bf16[256,128]{1,0:T(8,128)(2,1)S(1)}, u32[]{:S(2)}, u32[]{:S(2)}) collective-permute-start(bf16[256,128]{1,0:T(8,128)(2,1)S(1)} %add_convert_fusion.refs_4_), channel_id=1, source_target_pairs={{0,16},{2,18},{16,0},{18,2},{1,17},{3,19},{17,1},{19,3},{4,20},{6,... | collective-permute-start | bytes 196616 | tf_op jit(solution)/shard_map/ppermute | solution.py:349
  41.2 4.3 %collective-permute-start.8 = (bf16[256,128]{1,0:T(8,128)(2,1)S(1)}, bf16[256,128]{1,0:T(8,128)(2,1)S(1)}, u32[]{:S(2)}, u32[]{:S(2)}) collective-permute-start(bf16[256,128]{1,0:T(8,128)(2,1)S(1)} %add_convert_fusion.refs_4_), channel_id=1, source_target_pairs={{0,2},{2,0},{16,18},{18,16},{1,3},{3,1},{17,19},{19,17},{4,6},{6,4... | collective-permute-start | bytes 196616 | tf_op jit(solution)/shard_map/ppermute | solution.py:349
  47.7 0.7 %copy-start.1 = (bf16[128,512]{1,0:T(8,128)(2,1)}, bf16[128,512]{1,0:T(8,128)(2,1)S(1)}, u32[]{:S(2)}) copy-start(bf16[128,512]{1,0:T(8,128)(2,1)S(1)} %get-tuple-element.51.refs_0_) | copy-start | bytes 393220
  48.4 5.7 %collective-permute-start.13 = (bf16[128,512]{1,0:T(8,128)(2,1)S(1)}, bf16[128,512]{1,0:T(8,128)(2,1)S(1)}, u32[]{:S(2)}, u32[]{:S(2)}) collective-permute-start(bf16[128,512]{1,0:T(8,128)(2,1)S(1)} %get-tuple-element.52), channel_id=1, source_target_pairs={{0,2},{2,0},{16,18},{18,16},{1,3},{3,1},{17,19},{19,17},{4,6},{6,4... | collective-permute-start | bytes 393224 | tf_op jit(solution)/shard_map/ppermute | solution.py:349
  49.9 8.0 %collective-permute-start.11 = (bf16[128,512]{1,0:T(8,128)(2,1)S(1)}, bf16[128,512]{1,0:T(8,128)(2,1)S(1)}, u32[]{:S(2)}, u32[]{:S(2)}) collective-permute-start(bf16[128,512]{1,0:T(8,128)(2,1)S(1)} %get-tuple-element.49), channel_id=1, source_target_pairs={{0,16},{2,18},{16,0},{18,2},{1,17},{3,19},{17,1},{19,3},{4,20},{6,... | collective-permute-start | bytes 393224 | tf_op jit(solution)/shard_map/ppermute | solution.py:349
  50.4 7.6 %collective-permute-start.12 = (bf16[128,512]{1,0:T(8,128)(2,1)S(1)}, bf16[128,512]{1,0:T(8,128)(2,1)S(1)}, u32[]{:S(2)}, u32[]{:S(2)}) collective-permute-start(bf16[128,512]{1,0:T(8,128)(2,1)S(1)} %get-tuple-element.50), channel_id=1, source_target_pairs={{0,18},{2,16},{16,2},{18,0},{1,19},{3,17},{17,3},{19,1},{4,22},{6,... | collective-permute-start | bytes 393224 | tf_op jit(solution)/shard_map/ppermute | solution.py:349
  54.1 0.6 %copy-start.4 = (bf16[128,512]{1,0:T(8,128)(2,1)}, bf16[128,512]{1,0:T(8,128)(2,1)S(1)}, u32[]{:S(2)}) copy-start(bf16[128,512]{1,0:T(8,128)(2,1)S(1)} %collective-permute-done.13.refs_1_) | copy-start | bytes 393220
  57.9 0.7 %copy-start.2 = (bf16[128,512]{1,0:T(8,128)(2,1)}, bf16[128,512]{1,0:T(8,128)(2,1)S(1)}, u32[]{:S(2)}) copy-start(bf16[128,512]{1,0:T(8,128)(2,1)S(1)} %collective-permute-done.11.refs_0_) | copy-start | bytes 393220
  58.6 0.6 %copy-start.3 = (bf16[128,512]{1,0:T(8,128)(2,1)}, bf16[128,512]{1,0:T(8,128)(2,1)S(1)}, u32[]{:S(2)}) copy-start(bf16[128,512]{1,0:T(8,128)(2,1)S(1)} %collective-permute-done.12.refs_1_) | copy-start | bytes 393220

commit v17 on v16

--- a/solution.py
+++ b/solution.py
@@ -13,7 +13,7 @@
 LANES = 128
 STEP = 16
 HALF = 8
-BATCH = 4
+BATCH = 8
 DEAD = -1e30
 VMEM = pl.BlockSpec(memory_space=pltpu.VMEM)
 SMEM = pl.BlockSpec(memory_space=pltpu.SMEM)

time: 62.8 us -> 62.1 us (0.989)
    pallas_call x2, Pallas kernels: 6.36 us -> 5.69 us  [attend_half(): pl.pallas_call(functools.partial(attend_kernel, first, parts), out_shape=...]
where the time goes in v17:
time: 62.1 us; the launch traced here: 61.7 us
  starting transfers between devices  28.3 us (46%)
  Pallas kernels  14 us (23%)
  waiting for transfers between devices  13.9 us (22%)
  local copies, waits for them, and re-layouts  5.15 us (8%)
    ppermute x10, starting transfers between devices, swap(): return lax.ppermute(a, ('rep', 'side'), pairs)  12 us
    ppermute x10, waiting for transfers between devices, swap(): return lax.ppermute(a, ('rep', 'side'), pairs)  11.5 us
    all_to_all x2, starting transfers between devices, to_levels(): return lax.all_to_all(a, 'level', split_axis=0, concat_axis=0, tiled=True)  11 us
    pallas_call x2, Pallas kernels, attend_half(): pl.pallas_call(functools.partial(attend_kernel, first, parts), out_shape=...  5.69 us
    ppermute x3, starting transfers between devices, per_device(): lax.ppermute(other, 'level', pairs[k])  5.29 us
    unnamed x16, local copies, waits for them, and re-layouts  3.41 us
    pallas_call x1, Pallas kernels, per_device(): pl.pallas_call(functools.partial(row_kernel, square), out_shape=[jax.Shap...  2.94 us
    pallas_call x1, Pallas kernels, per_device(): pl.pallas_call(functools.partial(factor_kernel, square), out_shape=[jax.S...  2.15 us
  transfers between devices with their start and end apart: 16, of which 9 were waited for; matrix products, arithmetic and copies ran while one was open for 3% of the time, Pallas kernels for 13%

profile of v17, /device:TPU:0, one launch (start us, length us, event | category | flops | bytes accessed | tf_op | source)
XLA Modules:
  0.0 61.7 jit_solution(4034030390471601345)
XLA Ops:
  0.0 2.1 %shard_map.110 = (bf16[4,64,1024]{2,1,0:T(8,128)(2,1)}, bf16[1,64,512]{2,1,0:T(8,128)(2,1)}, bf16[1,64,1536]{2,1,0:T(8,128)(2,1)}) custom-call(s32[1]{0:T(128)} %bitcast.me_ref, bf16[1,64,4096]{2,1,0:T(8,128)(2,1)} %bitcast.13, bf16[1,64,2048]{2,1,0:T(8,128)(2,1)} %expand_ref.1), custom_call_target="tpu_custom_call" | custom-call | tf_op jit(solution)/shard_map/pallas_call | solution.py:352
  2.2 6.5 %all-to-all-start = ((bf16[4,64,1024]{2,1,0:T(8,128)(2,1)}), bf16[4,64,1024]{2,1,0:T(8,128)(2,1)S(1)}, u32[]{:S(2)}, u32[]{:S(2)}) async-start(bf16[4,64,1024]{2,1,0:T(8,128)(2,1)} %get-tuple-element.46), calls=%async_computation | async-start | bytes 1048576 | tf_op jit(solution)/shard_map/all_to_all | solution.py:361
  8.6 1.5 %collective-permute-start = (bf16[1,64,1536]{2,1,0:T(8,128)(2,1)S(1)}, bf16[1,64,1536]{2,1,0:T(8,128)(2,1)S(1)}, u32[]{:S(2)}, u32[]{:S(2)}) collective-permute-start(bf16[1,64,1536]{2,1,0:T(8,128)(2,1)S(1)} %copy-done.7), channel_id=1, source_target_pairs={{0,2},{2,0},{16,18},{18,16},{1,3},{3,1},{17,19},{19,17},{4,6},{6,4... | collective-permute-start | bytes 589832 | tf_op jit(solution)/shard_map/ppermute | solution.py:349
  10.9 2.9 %shard_map.109 = (bf16[128,1152]{1,0:T(8,128)(2,1)}, bf16[128,1152]{1,0:T(8,128)(2,1)}, bf16[128,1152]{1,0:T(8,128)(2,1)}, bf16[128,1152]{1,0:T(8,128)(2,1)}) custom-call(s32[1]{0:T(128)} %bitcast.me_ref, s32[8]{0:T(128)} %map_ref.1, s32[1,128]{1,0:T(1,128)} %bitcast.14, bf16[128,4096]{1,0:T(8,128)(2,1)} %hidden_ref.1), custom_call_target="tpu_custom_call" | custom-call | tf_op jit(solution)/shard_map/pallas_call | solution.py:365
  13.9 1.1 %collective-permute-done = bf16[1,64,1536]{2,1,0:T(8,128)(2,1)S(1)} collective-permute-done((bf16[1,64,1536]{2,1,0:T(8,128)(2,1)S(1)}, bf16[1,64,1536]{2,1,0:T(8,128)(2,1)S(1)}, u32[]{:S(2)}, u32[]{:S(2)}) %collective-permute-start) | collective-permute-done | bytes 196640 | tf_op jit(solution)/shard_map/ppermute | solution.py:349
  15.0 1.5 %collective-permute-start.1 = (bf16[128,1152]{1,0:T(8,128)(2,1)}, bf16[128,1152]{1,0:T(8,128)(2,1)S(1)}, u32[]{:S(2)}, u32[]{:S(2)}) collective-permute-start(bf16[128,1152]{1,0:T(8,128)(2,1)} %get-tuple-element.39), channel_id=1, source_target_pairs={{0,2},{2,0},{16,18},{18,16},{1,3},{3,1},{17,19},{19,17},{4,6},{6,4... | collective-permute-start | bytes 884744 | tf_op jit(solution)/shard_map/ppermute | solution.py:349
  16.5 1.5 %collective-permute-start.2 = (bf16[128,1152]{1,0:T(8,128)(2,1)}, bf16[128,1152]{1,0:T(8,128)(2,1)S(1)}, u32[]{:S(2)}, u32[]{:S(2)}) collective-permute-start(bf16[128,1152]{1,0:T(8,128)(2,1)} %get-tuple-element.40), channel_id=1, source_target_pairs={{0,16},{2,18},{16,0},{18,2},{1,17},{3,19},{17,1},{19,3},{4,20},{6,... | collective-permute-start | bytes 884744 | tf_op jit(solution)/shard_map/ppermute | solution.py:349
  20.2 3.5 %collective-permute-start.6 = (bf16[1,64,1024]{2,1,0:T(8,128)(2,1)S(1)}, bf16[1,64,1024]{2,1,0:T(8,128)(2,1)S(1)}, u32[]{:S(2)}, u32[]{:S(2)}) collective-permute-start(bf16[1,64,1024]{2,1,0:T(8,128)(2,1)S(1)} %slice.6.refs_5_), channel_id=1, source_target_pairs={{0,12},{4,8},{8,4},{12,0},{1,13},{5,9},{9,5},{13,1},{2,14},{6,10},... | collective-permute-start | bytes 393224 | tf_op jit(solution)/shard_map/ppermute | solution.py:382
  23.7 1.4 %collective-permute-done.1.refs_1_ = bf16[128,1152]{1,0:T(8,128)(2,1)S(1)} collective-permute-done((bf16[128,1152]{1,0:T(8,128)(2,1)}, bf16[128,1152]{1,0:T(8,128)(2,1)S(1)}, u32[]{:S(2)}, u32[]{:S(2)}) %collective-permute-start.1) | collective-permute-done | bytes 294944 | tf_op jit(solution)/shard_map/ppermute | solution.py:349
  25.2 1.7 %collective-permute-start.4 = (bf16[1,64,1024]{2,1,0:T(8,128)(2,1)S(1)}, bf16[1,64,1024]{2,1,0:T(8,128)(2,1)S(1)}, u32[]{:S(2)}, u32[]{:S(2)}) collective-permute-start(bf16[1,64,1024]{2,1,0:T(8,128)(2,1)S(1)} %slice.6.refs_5_), channel_id=1, source_target_pairs={{0,4},{4,0},{8,12},{12,8},{1,5},{5,1},{9,13},{13,9},{2,6},{6,2},{1... | collective-permute-start | bytes 393224 | tf_op jit(solution)/shard_map/ppermute | solution.py:382
  26.9 3.4 %collective-permute-done.2.refs_2_ = bf16[128,1152]{1,0:T(8,128)(2,1)S(1)} collective-permute-done((bf16[128,1152]{1,0:T(8,128)(2,1)}, bf16[128,1152]{1,0:T(8,128)(2,1)S(1)}, u32[]{:S(2)}, u32[]{:S(2)}) %collective-permute-start.2) | collective-permute-done | bytes 294944 | tf_op jit(solution)/shard_map/ppermute | solution.py:349
  30.3 4.5 %all-to-all-start.1 = ((bf16[4,128,512]{2,1,0:T(8,128)(2,1)}), bf16[4,128,512]{2,1,0:T(8,128)(2,1)S(1)}, u32[]{:S(2)}, u32[]{:S(2)}) async-start(bf16[4,128,512]{2,1,0:T(8,128)(2,1)} %broadcast_in_dim.25), calls=%async_computation.1 | async-start | bytes 1048576 | tf_op jit(solution)/shard_map/all_to_all | solution.py:361
  34.9 2.1 %shard_map.111 = f32[256,128]{1,0:T(8,128)S(1)} custom-call(s32[8]{0:T(128)S(1)} %add_bitcast_fusion.ids_ref, bf16[128,1152]{1,0:T(8,128)(2,1)S(1)} %copy-done, bf16[128,1152]{1,0:T(8,128)(2,1)S(1)} %collective-permute-done.1.refs_1_, bf16[128,1152]{1,0:T(8,128)(2,1)S(1)} %collective-permute-done.2.refs_2_, ...), custom_call_target="tpu_custom_call" | custom-call | tf_op jit(solution)/shard_map/pallas_call | solution.py:299
  37.2 1.2 %collective-permute-done.7 = f32[256,128]{1,0:T(8,128)S(1)} collective-permute-done((f32[256,128]{1,0:T(8,128)S(1)}, f32[256,128]{1,0:T(8,128)S(1)}, u32[]{:S(2)}, u32[]{:S(2)}) %collective-permute-start.7) | collective-permute-done | bytes 131104 | tf_op jit(solution)/shard_map/ppermute | solution.py:395
  38.4 2.0 %collective-permute-start.10 = (bf16[256,128]{1,0:T(8,128)(2,1)S(1)}, bf16[256,128]{1,0:T(8,128)(2,1)S(1)}, u32[]{:S(2)}, u32[]{:S(2)}) collective-permute-start(bf16[256,128]{1,0:T(8,128)(2,1)S(1)} %add_convert_fusion.refs_4_), channel_id=1, source_target_pairs={{0,18},{2,16},{16,2},{18,0},{1,19},{3,17},{17,3},{19,1},{4,22},{6,... | collective-permute-start | bytes 196616 | tf_op jit(solution)/shard_map/ppermute | solution.py:349
  42.1 1.6 %collective-permute-done.10.refs_7_ = bf16[256,128]{1,0:T(8,128)(2,1)S(1)} collective-permute-done((bf16[256,128]{1,0:T(8,128)(2,1)S(1)}, bf16[256,128]{1,0:T(8,128)(2,1)S(1)}, u32[]{:S(2)}, u32[]{:S(2)}) %collective-permute-start.10) | collective-permute-done | bytes 65568 | tf_op jit(solution)/shard_map/ppermute | solution.py:349
  43.8 1.3 %collective-permute-done.9.refs_6_ = bf16[256,128]{1,0:T(8,128)(2,1)S(1)} collective-permute-done((bf16[256,128]{1,0:T(8,128)(2,1)S(1)}, bf16[256,128]{1,0:T(8,128)(2,1)S(1)}, u32[]{:S(2)}, u32[]{:S(2)}) %collective-permute-start.9) | collective-permute-done | bytes 65568 | tf_op jit(solution)/shard_map/ppermute | solution.py:349
  45.5 1.2 %all-to-all-done.1 = bf16[4,128,512]{2,1,0:T(8,128)(2,1)S(1)} async-done(((bf16[4,128,512]{2,1,0:T(8,128)(2,1)}), bf16[4,128,512]{2,1,0:T(8,128)(2,1)S(1)}, u32[]{:S(2)}, u32[]{:S(2)}) %all-to-all-start.1) | async-done | bytes 524320 | tf_op jit(solution)/shard_map/all_to_all | solution.py:361
  46.6 1.1 %shard_map.112 = (bf16[128,512]{1,0:T(8,128)(2,1)S(1)}, bf16[128,512]{1,0:T(8,128)(2,1)S(1)}, bf16[128,512]{1,0:T(8,128)(2,1)S(1)}, bf16[128,512]{1,0:T(8,128)(2,1)S(1)}) custom-call(s32[8]{0:T(128)S(1)} %add.53.ids_ref, bf16[128,1152]{1,0:T(8,128)(2,1)S(1)} %copy-done, bf16[128,1152]{1,0:T(8,128)(2,1)S(1)} %collective-permute-done.1.refs_1_, ...), custom_call_target="tpu_custom_call" | custom-call | tf_op jit(solution)/shard_map/pallas_call | solution.py:315
  48.4 1.5 %collective-permute-start.13 = (bf16[128,512]{1,0:T(8,128)(2,1)S(1)}, bf16[128,512]{1,0:T(8,128)(2,1)S(1)}, u32[]{:S(2)}, u32[]{:S(2)}) collective-permute-start(bf16[128,512]{1,0:T(8,128)(2,1)S(1)} %get-tuple-element.52), channel_id=1, source_target_pairs={{0,2},{2,0},{16,18},{18,16},{1,3},{3,1},{17,19},{19,17},{4,6},{6,4... | collective-permute-start | bytes 393224 | tf_op jit(solution)/shard_map/ppermute | solution.py:349
  50.4 1.5 %collective-permute-start.12 = (bf16[128,512]{1,0:T(8,128)(2,1)S(1)}, bf16[128,512]{1,0:T(8,128)(2,1)S(1)}, u32[]{:S(2)}, u32[]{:S(2)}) collective-permute-start(bf16[128,512]{1,0:T(8,128)(2,1)S(1)} %get-tuple-element.50), channel_id=1, source_target_pairs={{0,18},{2,16},{16,2},{18,0},{1,19},{3,17},{17,3},{19,1},{4,22},{6,... | collective-permute-start | bytes 393224 | tf_op jit(solution)/shard_map/ppermute | solution.py:349
  51.9 2.2 %collective-permute-done.13.refs_1_ = bf16[128,512]{1,0:T(8,128)(2,1)S(1)} collective-permute-done((bf16[128,512]{1,0:T(8,128)(2,1)S(1)}, bf16[128,512]{1,0:T(8,128)(2,1)S(1)}, u32[]{:S(2)}, u32[]{:S(2)}) %collective-permute-start.13) | collective-permute-done | bytes 131104 | tf_op jit(solution)/shard_map/ppermute | solution.py:349
  54.7 2.8 %shard_map.113.refs_2_ = bf16[128,2048]{1,0:T(8,128)(2,1)} custom-call(s32[1]{0:T(128)} %bitcast.me_ref, s32[8,128]{1,0:T(8,128)} %reshape.46.len_ref, bf16[128,2048]{1,0:T(8,128)(2,1)} %base_ref.3, bf16[128,256]{1,0:T(8,128)(2,1)} %nk_ref.3, bf16[128,256]{1,0:T(8,128)(2,1)} %nv_ref.3, bf16[128,16,256]{2,1,0:T(8,128)(2,1)} %ck_ref.3, ...), custom_call_target="tpu_custom_call" | custom-call | flops 67108864 | bytes 1572864 | tf_op jit(solution)/shard_map/pallas_call | solution.py:247
  58.9 2.8 %shard_map.114 = bf16[128,2048]{1,0:T(8,128)(2,1)} custom-call(s32[1]{0:T(128)} %bitcast.me_ref, s32[8,128]{1,0:T(8,128)} %reshape.46.len_ref, bf16[128,2048]{1,0:T(8,128)(2,1)} %base_ref.3, bf16[128,256]{1,0:T(8,128)(2,1)} %nk_ref.3, bf16[128,256]{1,0:T(8,128)(2,1)} %nv_ref.3, bf16[128,16,256]{2,1,0:T(8,128)(2,1)} %ck_ref.3, ...), custom_call_target="tpu_custom_call", output_to_operand_aliasing={{}: (9, {})} | custom-call | flops 67108864 | bytes 1572864 | tf_op jit(solution)/shard_map/pallas_call | solution.py:247
  (44 shorter events, 8.4 us)
Async XLA Ops:
  2.2 6.5 %copy-start.7 = (bf16[1,64,1536]{2,1,0:T(8,128)(2,1)S(1)}, bf16[1,64,1536]{2,1,0:T(8,128)(2,1)}, u32[]{:S(2)}) copy-start(bf16[1,64,1536]{2,1,0:T(8,128)(2,1)} %get-tuple-element.33) | copy-start | bytes 589828
  2.2 28.1 %all-to-all-start = ((bf16[4,64,1024]{2,1,0:T(8,128)(2,1)}), bf16[4,64,1024]{2,1,0:T(8,128)(2,1)S(1)}, u32[]{:S(2)}, u32[]{:S(2)}) async-start(bf16[4,64,1024]{2,1,0:T(8,128)(2,1)} %get-tuple-element.46), calls=%async_computation | async-start | bytes 1048576 | tf_op jit(solution)/shard_map/all_to_all | solution.py:361
  8.6 1.5 %copy-start.6 = (s32[128]{0:T(128)S(1)}, s32[128]{0:T(128)}, u32[]{:S(2)}) copy-start(s32[128]{0:T(128)} %param.21) | copy-start | bytes 1540
  8.6 6.4 %collective-permute-start = (bf16[1,64,1536]{2,1,0:T(8,128)(2,1)S(1)}, bf16[1,64,1536]{2,1,0:T(8,128)(2,1)S(1)}, u32[]{:S(2)}, u32[]{:S(2)}) collective-permute-start(bf16[1,64,1536]{2,1,0:T(8,128)(2,1)S(1)} %copy-done.7), channel_id=1, source_target_pairs={{0,2},{2,0},{16,18},{18,16},{1,3},{3,1},{17,19},{19,17},{4,6},{6,4... | collective-permute-start | bytes 589832 | tf_op jit(solution)/shard_map/ppermute | solution.py:349
  15.0 10.2 %collective-permute-start.1 = (bf16[128,1152]{1,0:T(8,128)(2,1)}, bf16[128,1152]{1,0:T(8,128)(2,1)S(1)}, u32[]{:S(2)}, u32[]{:S(2)}) collective-permute-start(bf16[128,1152]{1,0:T(8,128)(2,1)} %get-tuple-element.39), channel_id=1, source_target_pairs={{0,2},{2,0},{16,18},{18,16},{1,3},{3,1},{17,19},{19,17},{4,6},{6,4... | collective-permute-start | bytes 884744 | tf_op jit(solution)/shard_map/ppermute | solution.py:349
  16.5 13.8 %collective-permute-start.2 = (bf16[128,1152]{1,0:T(8,128)(2,1)}, bf16[128,1152]{1,0:T(8,128)(2,1)S(1)}, u32[]{:S(2)}, u32[]{:S(2)}) collective-permute-start(bf16[128,1152]{1,0:T(8,128)(2,1)} %get-tuple-element.40), channel_id=1, source_target_pairs={{0,16},{2,18},{16,0},{18,2},{1,17},{3,19},{17,1},{19,3},{4,20},{6,... | collective-permute-start | bytes 884744 | tf_op jit(solution)/shard_map/ppermute | solution.py:349
  18.0 12.3 %collective-permute-start.3 = (bf16[128,1152]{1,0:T(8,128)(2,1)}, bf16[128,1152]{1,0:T(8,128)(2,1)S(1)}, u32[]{:S(2)}, u32[]{:S(2)}) collective-permute-start(bf16[128,1152]{1,0:T(8,128)(2,1)} %get-tuple-element.41), channel_id=1, source_target_pairs={{0,18},{2,16},{16,2},{18,0},{1,19},{3,17},{17,3},{19,1},{4,22},{6,... | collective-permute-start | bytes 884744 | tf_op jit(solution)/shard_map/ppermute | solution.py:349
  18.5 0.8 %copy-start.5 = (bf16[1,64,512]{2,1,0:T(8,128)(2,1)S(1)}, bf16[1,64,512]{2,1,0:T(8,128)(2,1)}, u32[]{:S(2)}) copy-start(bf16[1,64,512]{2,1,0:T(8,128)(2,1)} %get-tuple-element.36) | copy-start | bytes 196612
  20.2 14.7 %collective-permute-start.6 = (bf16[1,64,1024]{2,1,0:T(8,128)(2,1)S(1)}, bf16[1,64,1024]{2,1,0:T(8,128)(2,1)S(1)}, u32[]{:S(2)}, u32[]{:S(2)}) collective-permute-start(bf16[1,64,1024]{2,1,0:T(8,128)(2,1)S(1)} %slice.6.refs_5_), channel_id=1, source_target_pairs={{0,12},{4,8},{8,4},{12,0},{1,13},{5,9},{9,5},{13,1},{2,14},{6,10},... | collective-permute-start | bytes 393224 | tf_op jit(solution)/shard_map/ppermute | solution.py:382
  23.7 11.2 %collective-permute-start.5 = (bf16[1,64,1024]{2,1,0:T(8,128)(2,1)S(1)}, bf16[1,64,1024]{2,1,0:T(8,128)(2,1)S(1)}, u32[]{:S(2)}, u32[]{:S(2)}) collective-permute-start(bf16[1,64,1024]{2,1,0:T(8,128)(2,1)S(1)} %slice.6.refs_5_), channel_id=1, source_target_pairs={{0,8},{4,12},{8,0},{12,4},{1,9},{5,13},{9,1},{13,5},{2,10},{6,14},... | collective-permute-start | bytes 393224 | tf_op jit(solution)/shard_map/ppermute | solution.py:382
  25.2 9.7 %collective-permute-start.4 = (bf16[1,64,1024]{2,1,0:T(8,128)(2,1)S(1)}, bf16[1,64,1024]{2,1,0:T(8,128)(2,1)S(1)}, u32[]{:S(2)}, u32[]{:S(2)}) collective-permute-start(bf16[1,64,1024]{2,1,0:T(8,128)(2,1)S(1)} %slice.6.refs_5_), channel_id=1, source_target_pairs={{0,4},{4,0},{8,12},{12,8},{1,5},{5,1},{9,13},{13,9},{2,6},{6,2},{1... | collective-permute-start | bytes 393224 | tf_op jit(solution)/shard_map/ppermute | solution.py:382
  26.9 8.0 %copy-start = (bf16[128,1152]{1,0:T(8,128)(2,1)S(1)}, bf16[128,1152]{1,0:T(8,128)(2,1)}, u32[]{:S(2)}) copy-start(bf16[128,1152]{1,0:T(8,128)(2,1)} %get-tuple-element.42.refs_0_) | copy-start | bytes 884740
  30.3 16.3 %all-to-all-start.1 = ((bf16[4,128,512]{2,1,0:T(8,128)(2,1)}), bf16[4,128,512]{2,1,0:T(8,128)(2,1)S(1)}, u32[]{:S(2)}, u32[]{:S(2)}) async-start(bf16[4,128,512]{2,1,0:T(8,128)(2,1)} %broadcast_in_dim.25), calls=%async_computation.1 | async-start | bytes 1048576 | tf_op jit(solution)/shard_map/all_to_all | solution.py:361
  37.0 1.4 %collective-permute-start.7 = (f32[256,128]{1,0:T(8,128)S(1)}, f32[256,128]{1,0:T(8,128)S(1)}, u32[]{:S(2)}, u32[]{:S(2)}) collective-permute-start(f32[256,128]{1,0:T(8,128)S(1)} %shard_map.111), channel_id=1, source_target_pairs={{0,1},{1,0},{2,3},{3,2},{4,5},{5,4},{6,7},{7,6},{8,9},{9,8},{10,11... | collective-permute-start | bytes 393224 | tf_op jit(solution)/shard_map/ppermute | solution.py:395
  38.4 5.3 %collective-permute-start.10 = (bf16[256,128]{1,0:T(8,128)(2,1)S(1)}, bf16[256,128]{1,0:T(8,128)(2,1)S(1)}, u32[]{:S(2)}, u32[]{:S(2)}) collective-permute-start(bf16[256,128]{1,0:T(8,128)(2,1)S(1)} %add_convert_fusion.refs_4_), channel_id=1, source_target_pairs={{0,18},{2,16},{16,2},{18,0},{1,19},{3,17},{17,3},{19,1},{4,22},{6,... | collective-permute-start | bytes 196616 | tf_op jit(solution)/shard_map/ppermute | solution.py:349
  40.5 4.6 %collective-permute-start.9 = (bf16[256,128]{1,0:T(8,128)(2,1)S(1)}, bf16[256,128]{1,0:T(8,128)(2,1)S(1)}, u32[]{:S(2)}, u32[]{:S(2)}) collective-permute-start(bf16[256,128]{1,0:T(8,128)(2,1)S(1)} %add_convert_fusion.refs_4_), channel_id=1, source_target_pairs={{0,16},{2,18},{16,0},{18,2},{1,17},{3,19},{17,1},{19,3},{4,20},{6,... | collective-permute-start | bytes 196616 | tf_op jit(solution)/shard_map/ppermute | solution.py:349
  41.2 4.3 %collective-permute-start.8 = (bf16[256,128]{1,0:T(8,128)(2,1)S(1)}, bf16[256,128]{1,0:T(8,128)(2,1)S(1)}, u32[]{:S(2)}, u32[]{:S(2)}) collective-permute-start(bf16[256,128]{1,0:T(8,128)(2,1)S(1)} %add_convert_fusion.refs_4_), channel_id=1, source_target_pairs={{0,2},{2,0},{16,18},{18,16},{1,3},{3,1},{17,19},{19,17},{4,6},{6,4... | collective-permute-start | bytes 196616 | tf_op jit(solution)/shard_map/ppermute | solution.py:349
  47.7 0.7 %copy-start.1 = (bf16[128,512]{1,0:T(8,128)(2,1)}, bf16[128,512]{1,0:T(8,128)(2,1)S(1)}, u32[]{:S(2)}) copy-start(bf16[128,512]{1,0:T(8,128)(2,1)S(1)} %get-tuple-element.51.refs_0_) | copy-start | bytes 393220
  48.4 5.7 %collective-permute-start.13 = (bf16[128,512]{1,0:T(8,128)(2,1)S(1)}, bf16[128,512]{1,0:T(8,128)(2,1)S(1)}, u32[]{:S(2)}, u32[]{:S(2)}) collective-permute-start(bf16[128,512]{1,0:T(8,128)(2,1)S(1)} %get-tuple-element.52), channel_id=1, source_target_pairs={{0,2},{2,0},{16,18},{18,16},{1,3},{3,1},{17,19},{19,17},{4,6},{6,4... | collective-permute-start | bytes 393224 | tf_op jit(solution)/shard_map/ppermute | solution.py:349
  49.9 7.7 %collective-permute-start.11 = (bf16[128,512]{1,0:T(8,128)(2,1)S(1)}, bf16[128,512]{1,0:T(8,128)(2,1)S(1)}, u32[]{:S(2)}, u32[]{:S(2)}) collective-permute-start(bf16[128,512]{1,0:T(8,128)(2,1)S(1)} %get-tuple-element.49), channel_id=1, source_target_pairs={{0,16},{2,18},{16,0},{18,2},{1,17},{3,19},{17,1},{19,3},{4,20},{6,... | collective-permute-start | bytes 393224 | tf_op jit(solution)/shard_map/ppermute | solution.py:349
  50.4 7.2 %collective-permute-start.12 = (bf16[128,512]{1,0:T(8,128)(2,1)S(1)}, bf16[128,512]{1,0:T(8,128)(2,1)S(1)}, u32[]{:S(2)}, u32[]{:S(2)}) collective-permute-start(bf16[128,512]{1,0:T(8,128)(2,1)S(1)} %get-tuple-element.50), channel_id=1, source_target_pairs={{0,18},{2,16},{16,2},{18,0},{1,19},{3,17},{17,3},{19,1},{4,22},{6,... | collective-permute-start | bytes 393224 | tf_op jit(solution)/shard_map/ppermute | solution.py:349
  54.1 0.6 %copy-start.4 = (bf16[128,512]{1,0:T(8,128)(2,1)}, bf16[128,512]{1,0:T(8,128)(2,1)S(1)}, u32[]{:S(2)}) copy-start(bf16[128,512]{1,0:T(8,128)(2,1)S(1)} %collective-permute-done.13.refs_1_) | copy-start | bytes 393220
  57.6 0.7 %copy-start.2 = (bf16[128,512]{1,0:T(8,128)(2,1)}, bf16[128,512]{1,0:T(8,128)(2,1)S(1)}, u32[]{:S(2)}) copy-start(bf16[128,512]{1,0:T(8,128)(2,1)S(1)} %collective-permute-done.11.refs_0_) | copy-start | bytes 393220
  58.2 0.6 %copy-start.3 = (bf16[128,512]{1,0:T(8,128)(2,1)}, bf16[128,512]{1,0:T(8,128)(2,1)S(1)}, u32[]{:S(2)}) copy-start(bf16[128,512]{1,0:T(8,128)(2,1)S(1)} %collective-permute-done.12.refs_1_) | copy-start | bytes 393220
